TPU v7x, 32 devices: a whole 2x2x4 slice. The times are simulated.
32 devices in a mesh: sector: 16 (over z, y, core), span: 2 (over x).
Axes of the slice: x: 2, y: 2, z: 4, core: 2. Of those that a mesh axis runs over, the one named last changes fastest.
Arguments:
- rhs: float32 [11, 7, 32, 16, 128], P(None, None, 'sector', 'span'), may hold values from -6 to 6
- diag_coef: float32 [32, 16, 128], P('sector', 'span'), may hold values from 2 to 4
- face_coef: float32 [3, 32, 16, 128], P(None, 'sector', 'span'), may hold values from 0.2 to 0.6
- time_coef: float32 [32, 16, 128], P('sector', 'span'), may hold values from 0.05 to 0.4
- jac_up: float32 [3, 7, 7], replicated, may hold values from -1.5 to 1.5
- jac_down: float32 [3, 7, 7], replicated, may hold values from -1.5 to 1.5
- wall_mask: int32 [32, 16, 128], P('sector', 'span'), may hold values 0 or 1
- stator_adj: float32 [11, 7, 64, 16], P(None, None, 'sector', 'span'), may hold values from -6 to 6
- owner: int32 [11, 32, 16], P(None, 'sector', 'span'), may hold values from 0 to 62, as said below
- first_panel_share: float32 [11, 32, 16], P(None, 'sector', 'span'), may hold values from 0 to 1
Outputs:
- adjoint_out: float32 [11, 7, 32, 16, 128], P(None, None, 'sector', 'span')
- stator_sens: float32 [11, 7, 64, 16], P(None, None, 'sector', 'span')
Inputs may be any that keep to these rules, and one draw needn't show every extreme that they name: For instance t and an inlet cell in azimuthal block b (cells b * 2 to (b + 1) * 2 - 1), owner and owner + 1 both lie in panel block q = (b + (t * 16) // 10 - t // 10) mod 16, that is between q * 4 and (q + 1) * 4 - 1.
All inputs are finite; a program needn't handle non-finite values. No bound on the sum of `wall_mask` on one device may be relied on, other than what follows from the above.
Results may differ from a plain program's by a relative error of at most 0.0001.
Values sent between devices are 32-bit elements; how exact they have to be, the bound alone decides.
No kernel may reach another device: no remote copies, remote signals or barrier semaphores. Data moves between devices by JAX's collectives and lax.ppermute only.
A program may use at most 64 MiB of HBM per device.

v0:
```python
import functools

import jax
import jax.numpy as jnp
import ml_dtypes
import numpy as np
from jax import lax
from jax.experimental import pallas as pl
from jax.experimental.pallas import tpu as pltpu
from jax.sharding import PartitionSpec as P

SWEEPS = 4
DEPTH = 2
LANES = 128
CHUNK = 256
WINDOW = 8
HIGHEST = lax.Precision.HIGHEST
DOWN_AZ, SPECTRAL, UP_SP, DOWN_SP, UP_AX, DOWN_AX, UP_AZ = range(7)
C_TIME, C_AZ, C_SP, C_UP, C_DOWN, C_MASK = range(6)
RATES = 8
GROUP = 3
AXES = ("sector", "span")


class Plan:
    def __init__(self, rhs, stator_adj, sectors, spans):
        self.insts, self.fields, self.ct, self.rows, self.nax = rhs.shape
        self.panels = stator_adj.shape[2]
        self.sectors, self.spans = sectors, spans
        self.tf = self.insts * self.fields
        self.pad = -(-self.tf // 16) * 16
        self.cells = self.ct * self.rows
        self.slab = self.rows * LANES
        self.width = self.panels * self.rows
        self.shift = [
            ((t * sectors) // (self.insts - 1) - t // (self.insts - 1)) % sectors for t in range(self.insts)
        ]
        assert self.ct == 2 and self.nax == LANES and SWEEPS % DEPTH == 0 and spans > 1
        assert len(set(self.shift)) == self.insts and self.cells * WINDOW == LANES and self.rows >= SWEEPS
        assert self.slab % CHUNK == 0 and 3 * self.pad <= 256 and 2 * self.ct * self.width == LANES
        assert sectors % 2 == 0
        self.ends = 1 if spans == 2 else 2
        self.blocks = [-1, 0, 1]
        self.halves = [0, 1] if spans == 2 else [-1, 0, 1]
        self.tiles = [(k, x) for k in self.blocks for x in self.halves]
        self.slots = [
            [t for t in range(self.insts) if any((k + self.shift[t]) % sectors == o for k in self.blocks)]
            for o in range(sectors)
        ]
        assert max(map(len, self.slots)) * self.width <= LANES

    def spectral(self):
        t = np.arange(self.insts)
        off = t[:, None] - t[None, :]
        sines = np.where(off == 0, 1.0, np.sin(np.pi * off / self.insts))
        table = np.where(off == 0, 0.0, 0.5 * (1.0 - 2.0 * (off % 2)) / sines).astype(np.float32)
        full = np.zeros((self.pad, self.pad), np.float32)
        full[: self.tf, : self.tf] = np.kron(table.T, np.eye(self.fields, dtype=np.float32))
        hi = full.astype(ml_dtypes.bfloat16)
        lo = (full - hi.astype(np.float32)).astype(ml_dtypes.bfloat16)
        return np.concatenate([hi, lo, hi], axis=1)

    def field_rows(self):
        out = np.zeros((self.pad, self.fields), np.float32)
        out[np.arange(self.tf), np.arange(self.tf) % self.fields] = 1.0
        return out

    def field_lanes(self):
        return np.tile(self.field_rows().T, (1, 3))

    def block_diagonal(self):
        block = np.full(self.pad, -1)
        block[: self.tf] = np.arange(self.tf) // self.fields
        same = (block[:, None] == block[None, :]) & (block[:, None] >= 0)
        return np.tile(same.astype(np.float32), (1, 3))

    def inst_rows(self):
        out = np.zeros((self.pad, 16), np.float32)
        out[np.arange(self.tf), np.arange(self.tf) // self.fields] = 1.0
        return out

    def cell_lanes(self):
        out = np.zeros((self.ct, self.rows, self.ct, self.panels, self.rows), np.float32)
        for a in range(self.ct):
            for r in range(self.rows):
                out[a, r, a, :, r] = 1.0
        out = out.reshape(self.cells, -1)
        return np.pad(out, ((0, 0), (0, LANES - out.shape[1])))

    def window_lanes(self):
        out = np.zeros((LANES, LANES), np.float32)
        out[:, ::WINDOW] = self.cell_lanes().T
        return out

    def twice(self, table):
        return np.concatenate([table, table]).astype(ml_dtypes.bfloat16)

    def weight_lanes(self):
        out = np.zeros((LANES, LANES), np.float32)
        half = self.ct * self.width
        out[: self.cells, :half] = self.cell_lanes()[:, :half]
        out[self.cells : 2 * self.cells, half:] = self.cell_lanes()[:, :half]
        return out

    def panel_lanes(self):
        lane = np.arange(LANES)
        return np.where(lane < self.ct * self.width, (lane // self.rows) % self.panels, -9).astype(np.float32)[None]


def call(kernel, out, scratch=(), flops=2_000_000, nbytes=1_000_000):
    return pl.pallas_call(
        kernel,
        out_shape=out,
        scratch_shapes=list(scratch),
        compiler_params=pltpu.CompilerParams(vmem_limit_bytes=40 * 1024 * 1024),
        cost_estimate=pl.CostEstimate(flops=flops, bytes_accessed=nbytes, transcendentals=0),
    )


def f32(*shape):
    return jax.ShapeDtypeStruct(shape, jnp.float32)


def vmem(*shape):
    return pltpu.VMEM(shape, jnp.float32)


def halves_of(x):
    hi = x.astype(jnp.bfloat16)
    return hi, (x - hi.astype(jnp.float32)).astype(jnp.bfloat16)


def dot3(w, x):
    hi, lo = halves_of(x)
    return jnp.dot(w, jnp.concatenate([hi, hi, lo], axis=0), preferred_element_type=jnp.float32)


def pick(x, table2):
    return jnp.dot(jnp.concatenate(halves_of(x), axis=1), table2, preferred_element_type=jnp.float32)


def dot_full(a, b):
    return jnp.dot(a, b, precision=HIGHEST, preferred_element_type=jnp.float32)


def lane_index(rows):
    return lax.broadcasted_iota(jnp.int32, (rows, LANES), 1)


def rolled(x, by):
    by %= LANES
    return pltpu.roll(x, by, axis=1) if by else x


def at(r, count=1, start=0):
    return slice(start + r * LANES, start + (r + count) * LANES)


def parity():
    return lax.rem(lax.axis_index("sector"), 2)


def has_sides(plan):
    span = lax.axis_index("span")
    return jnp.where(span < plan.spans - 1, 1.0, 0.0), jnp.where(span > 0, 1.0, 0.0)


class Layer:
    def __init__(self, plan, ref, start=0, rates=None, seam=None, layer=0):
        self.plan, self.ref, self.start, self.seam, self.layer = plan, ref, start, seam, layer
        self.rates = rates or (ref, start)

    def rate(self, which, r, count=1):
        ref, start = self.rates
        row = self.plan.pad + which
        return ref[row : row + 1, at(r, count, start)]

    def row(self, r):
        value = self.ref[: self.plan.pad, at(r, 1, self.start)]
        if self.seam is None:
            return value
        return value + placed(self.seam, self.layer * self.plan.rows + r) * self.rate(C_MASK, r)

    def chunk(self, c):
        count = CHUNK // LANES
        if self.seam is None:
            return self.ref[: self.plan.pad, at(c * count, count, self.start)]
        return jnp.concatenate([self.row(c * count + part) for part in range(count)], axis=1)


def placed(tile, cell):
    return jnp.where(lane_index(tile.shape[0]) == 0, rolled(tile, -cell * WINDOW), 0.0)


class Products:
    def __init__(self, plan, w_ref, p_ref, first):
        self.plan, self.w, self.p, self.first = plan, w_ref, p_ref, first

    def fill(self, layer):
        for c in range(self.plan.slab // CHUNK):
            self.p[:, c * CHUNK : (c + 1) * CHUNK] = dot3(matrix(self.plan, self.w, self.first, 6), layer.chunk(c))
        self.layer = layer
        return self

    def get(self, block, r):
        row = (block - self.first) * self.plan.pad
        return self.p[row : row + self.plan.pad, at(r)]

    def own_terms(self, r):
        rate = self.layer.rate
        total = rate(C_TIME, r) * self.get(SPECTRAL, r)
        beside = []
        if r + 1 < self.plan.rows:
            beside.append(self.get(UP_SP, r + 1))
        if r > 0:
            beside.append(self.get(DOWN_SP, r - 1))
        total = total + rate(C_SP, r) * sum(beside[1:], beside[0])
        total = total + rate(C_UP, r) * rolled(self.get(UP_AX, r), -1)
        return total + rate(C_DOWN, r) * rolled(self.get(DOWN_AX, r), 1)


def matrix(plan, w_ref, block, count=1):
    return w_ref[block * plan.pad : (block + count) * plan.pad, :]


def two_layers(plan, ref, rates=None, seam=None):
    return [
        Layer(plan, ref, a * plan.slab, (rates, a * plan.slab) if rates is not None else None, seam, a)
        for a in range(plan.ct)
    ]


def inner_rows(plan, w_ref, p_refs, layers, force, g_ref):
    first = Products(plan, w_ref, p_refs[0], DOWN_AZ).fill(layers[0])
    second = Products(plan, w_ref, p_refs[1], SPECTRAL).fill(layers[1])
    for r in range(plan.rows):
        other = second.get(UP_AZ, r), first.get(DOWN_AZ, r)
        for a, products in enumerate((first, second)):
            total = products.own_terms(r) + layers[a].rate(C_AZ, r) * other[a]
            g_ref[:, at(r, 1, a * plan.slab)] = force[a].row(r) - total


def azimuthal(plan, w_ref, block, chunk_of, take):
    for c in range(plan.slab // CHUNK):
        terms = dot3(matrix(plan, w_ref, block), chunk_of(c))
        for part in range(CHUNK // LANES):
            take(c * (CHUNK // LANES) + part, terms[:, at(part)])


def middle_rows(plan, w_ref, p_refs, own, own_force, g_ref, near, near_force, side, corner, y_ref, h_ref, n_refs):
    pad, rows, ct = plan.pad, plan.rows, plan.ct
    outward, inward, last = (UP_SP, DOWN_SP), (DOWN_SP, UP_SP), (rows - 1, 0)
    edge_terms, edge_new, corner_terms = [], [], []
    for n in range(2):
        first, second, edge_force, edge_rate = side(n)
        corners = corner(n)
        every = dot3(w_ref[...], first)
        edge_terms.append(every[outward[n] * pad : (outward[n] + 1) * pad])
        corner_terms.append([dot3(matrix(plan, w_ref, outward[n]), c) for c in corners])
        beyond = dot3(matrix(plan, w_ref, outward[n]), second)
        within = dot3(matrix(plan, w_ref, inward[n]), jnp.concatenate([x.row(last[n]) for x in own], axis=1))
        from_low = dot3(matrix(plan, w_ref, DOWN_AZ), corners[0])
        from_high = dot3(matrix(plan, w_ref, UP_AZ), corners[1])
        new = []
        for a in range(ct):

            def part(block, b=a):
                return every[block * pad : (block + 1) * pad, at(b)]

            around = part(UP_AZ, 1) + from_low if a == 0 else from_high + part(DOWN_AZ, 0)
            total = edge_rate(C_TIME, a) * part(SPECTRAL) + edge_rate(C_AZ, a) * around
            total = total + edge_rate(C_SP, a) * (beyond[:, at(a)] + within[:, at(a)])
            total = total + edge_rate(C_UP, a) * rolled(part(UP_AX), -1)
            total = total + edge_rate(C_DOWN, a) * rolled(part(DOWN_AX), 1)
            new.append(edge_force[:, at(a)] - total)
        edge_new.append(dot3(matrix(plan, w_ref, outward[n]), jnp.concatenate(new, axis=1)))

    products = (
        Products(plan, w_ref, p_refs[0], DOWN_AZ).fill(near[0]), Products(plan, w_ref, p_refs[1], SPECTRAL).fill(near[1]),
    )
    for a, (to_own, to_near) in enumerate(((DOWN_AZ, UP_AZ), (UP_AZ, DOWN_AZ))):

        def take(r, terms):
            total = products[a].own_terms(r) + near[a].rate(C_AZ, r) * terms
            mine = own[a].rate(C_AZ, r) * products[a].get(to_own, r)
            for n in range(2):
                if r == last[n]:
                    total = total + near[a].rate(C_SP, r) * corner_terms[n][a]
                    mine = mine + own[a].rate(C_SP, r) * edge_terms[n][:, at(a)]
            n_refs[a][:, at(r)] = near_force[a].row(r) - total
            lanes = at(r, 1, a * plan.slab)
            y_ref[:, lanes] = g_ref[:, lanes] - mine

        azimuthal(plan, w_ref, to_near, own[a].chunk, take)

    after = [Layer(plan, y_ref, a * plan.slab, own[a].rates) for a in range(ct)]
    inner_rows(plan, w_ref, p_refs, after, own_force, h_ref)
    for a in range(ct):
        for n in range(2):
            lanes = at(last[n], 1, a * plan.slab)
            h_ref[:, lanes] -= own[a].rate(C_SP, last[n]) * edge_new[n][:, at(a)]


def outer_rows(plan, w_ref, own, near, far_chunks, n_refs, h_ref, put):
    count = CHUNK // LANES
    for a, block in enumerate((DOWN_AZ, UP_AZ)):

        def near_chunk(c):
            terms = dot3(matrix(plan, w_ref, block), far_chunks[a](c))
            return n_refs[a][:, at(c * count, count)] - near[a].rate(C_AZ, c * count, count) * terms

        def take(r, terms):
            put(a, r, h_ref[:, at(r, 1, a * plan.slab)] - own[a].rate(C_AZ, r) * terms)

        azimuthal(plan, w_ref, block, near_chunk, take)


def sides_of(plan, side_ref, force_ref, seams_ref):
    pad, ct = plan.pad, plan.ct
    keeps = has_sides(plan)

    def read(n, ref, e, seam):
        i = n if plan.ends == 2 else 0
        value = ref[i, :pad, at(e * ct, ct)]
        if seam:
            r = e if n == 0 else plan.rows - 1 - e
            tile = seams_ref[1, 1 + i]
            scale = ref[i, pad + C_MASK : pad + C_MASK + 1, at(e * ct, ct)]
            value = value + jnp.concatenate([placed(tile, a * plan.rows + r) for a in range(ct)], axis=1) * scale
        return value * keeps[n]

    def side(n):
        i = n if plan.ends == 2 else 0
        same = side_ref is force_ref

        def rate(which, a):
            return force_ref[i, pad + which : pad + which + 1, at(a)] * keeps[n]

        force = read(n, force_ref, 0, True)
        first = force if same else read(n, side_ref, 0, False)
        return first, read(n, side_ref, 1, same), force, rate

    return side


def corners_of(plan, c_refs, seams_ref):
    keeps = has_sides(plan)

    def corner(n):
        i = n if plan.ends == 2 else 0
        out = []
        for a, c_ref in enumerate(c_refs):
            value = c_ref[i, : plan.pad]
            if seams_ref is not None:
                r = 0 if n == 0 else plan.rows - 1
                scale = c_ref[i, plan.pad + C_MASK : plan.pad + C_MASK + 1]
                value = value + placed(seams_ref[2 * a, 1 + i], a * plan.rows + r) * scale
            out.append(value * keeps[n])
        return out

    return corner


def prepare(plan, rhs_ref, diag_ref, face_ref, time_ref, mask_ref, m_ref, side_ref, c0_ref, c1_ref):
    pad = plan.pad
    lane = lane_index(1)
    tail = jnp.zeros((pad - plan.tf, LANES), jnp.float32)
    mirror = parity()
    for cell in range(plan.cells):
        a, r = divmod(cell, plan.rows)
        there = jnp.where(mirror == 0, a, plan.ct - 1 - a) * plan.rows + r
        one = pl.ds(there, 1)
        scale = mask_ref[one, :].astype(jnp.float32) / diag_ref[one, :]
        axial = scale * face_ref[2, one, :]
        rates = [
            scale * time_ref[one, :], scale * face_ref[0, one, :], scale * face_ref[1, one, :],
            jnp.where(lane < LANES - 1, axial, 0.0), jnp.where(lane > 0, axial, 0.0), scale,
            jnp.zeros((RATES - 6, LANES), jnp.float32),
        ]
        field = jnp.concatenate([rhs_ref[pl.ds(there, plan.tf, stride=plan.cells), :], tail], axis=0) * scale
        m_ref[:pad, at(cell)] = field
        m_ref[pad:, at(cell)] = jnp.concatenate(rates, axis=0)
    write_edges(plan, m_ref, side_ref, (c0_ref, c1_ref))


def write_edges(plan, x_ref, side_ref, c_refs):
    first = lax.axis_index("span") == 0
    for a in range(plan.ct):
        for e in range(DEPTH):
            low, high = x_ref[:, at(a * plan.rows + e)], x_ref[:, at((a + 1) * plan.rows - 1 - e)]
            ends = [jnp.where(first, high, low)] if plan.ends == 1 else [low, high]
            for n, end in enumerate(ends):
                side_ref[n, :, at(e * plan.ct + a)] = end
                if e == 0:
                    c_refs[a][n] = end


def stack_matrices(plan, up_ref, down_ref, spectral_ref, rows_ref, lanes_ref, diagonal_ref, out_ref):
    pad = plan.pad
    lane = lax.broadcasted_iota(jnp.int32, (pad, 3 * pad), 1)
    second = (lane >= pad) & (lane < 2 * pad)
    out_ref[SPECTRAL * pad : (SPECTRAL + 1) * pad, :] = spectral_ref[...]
    even = parity() == 0
    for block, small in (
        (DOWN_AZ, jnp.where(even, down_ref[0], up_ref[0])), (UP_AZ, jnp.where(even, up_ref[0], down_ref[0])),
        (UP_SP, up_ref[1]), (DOWN_SP, down_ref[1]), (UP_AX, up_ref[2]), (DOWN_AX, down_ref[2]),
    ):
        full = dot_full(dot_full(rows_ref[...], small), lanes_ref[...]) * diagonal_ref[...]
        hi = full.astype(jnp.bfloat16).astype(jnp.float32)
        out_ref[block * pad : (block + 1) * pad, :] = jnp.where(second, full - hi, hi).astype(jnp.bfloat16)


def send_panels(plan, stator_ref, owner_ref, share_ref, out_ref, panels_ref):
    me = lax.axis_index("sector")
    for f in range(plan.fields):
        panels_ref[pl.ds(f, plan.insts, stride=RATES), : plan.width] = jnp.transpose(stator_ref[f])
    out_ref[...] = jnp.zeros_like(out_ref)
    both = jnp.concatenate([lax.rem(owner_ref[...], plan.panels).astype(jnp.float32), share_ref[...]], axis=1)
    for t in range(plan.insts):
        group, row = divmod(t, GROUP)
        lanes = slice(group * 2 * plan.cells, (group + 1) * 2 * plan.cells)
        row += RATES
        out_ref[:, row : row + 1, lanes] = jnp.broadcast_to(both[t : t + 1][None], (out_ref.shape[0], 1, 2 * plan.cells))
    for o, slots in enumerate(plan.slots):
        to = lax.rem(me + (plan.sectors - o), plan.sectors) * plan.spans
        for slot, t in enumerate(slots):
            lanes = slice(slot * plan.width, (slot + 1) * plan.width)
            panels = panels_ref[t * RATES : t * RATES + plan.fields, : plan.width]
            for x in range(plan.spans):
                out_ref[to + x, : plan.fields, lanes] = panels


def begin(
    plan, w_ref, m_ref, got_ref, inst_rows, weight_table, panel_lanes, sum_table,
    seams_ref, weight_ref, x_ref, g_ref, panels_ref, terms_ref, rows_ref, p0_ref, p1_ref,
):
    pad, insts, fields = plan.pad, plan.insts, plan.fields
    me, span = lax.axis_index("sector"), lax.axis_index("span")
    tiles = plan.tiles
    panels_ref[...] = jnp.zeros_like(panels_ref)
    rows_ref[...] = jnp.zeros_like(rows_ref)
    wide = 2 * plan.cells
    for n, (k, x) in enumerate(tiles):
        at_span = x if plan.spans == 2 else jnp.clip(span + x, 0, plan.spans - 1)
        for t in range(insts):
            o = (k + plan.shift[t]) % plan.sectors
            source = lax.rem(me + o, plan.sectors) * plan.spans + at_span
            tile = rolled(got_ref[source, :RATES], -plan.slots[o].index(t) * plan.width)
            panels_ref[t * fields : (t + 1) * fields, n * LANES : n * LANES + plan.width] = tile[:fields, : plan.width]
        source = lax.rem(me + k + plan.sectors, plan.sectors) * plan.spans + at_span
        table = got_ref[source, RATES:]
        for group in range(-(-insts // GROUP)):
            shifted = rolled(table, -group * wide)
            rows_ref[group * GROUP : (group + 1) * GROUP, n * LANES : n * LANES + wide] = shifted[:GROUP, :wide]
    spread = dot_full(inst_rows[...], rows_ref[...])
    spread = pick(jnp.concatenate([spread[:, at(n)] for n in range(len(tiles))], axis=0), weight_table[...])
    first, share, panel = spread, rolled(spread, plan.ct * plan.width), panel_lanes[...]
    lower = (jnp.abs(first - panel) < 0.5).astype(jnp.float32)
    upper = (jnp.abs(first + 1.0 - panel) < 0.5).astype(jnp.float32)
    weights = share * lower + (1.0 - share) * upper
    for n in range(len(tiles)):
        panels = panels_ref[:, at(n)]
        terms_ref[n * pad : (n + 1) * pad, :] = panels + rolled(panels, plan.width)
    seams = pick(terms_ref[...] * weights, sum_table[...])

    even = parity() == 0
    is_first = span == 0

    def tile(values, k, x):
        n = tiles.index((k, x))
        return values[n * pad : (n + 1) * pad]

    def around(values, k):
        if plan.spans == 2:
            pair = tile(values, k, 0), tile(values, k, 1)
            return [jnp.where(is_first, pair[0], pair[1]), jnp.where(is_first, pair[1], pair[0])]
        return [tile(values, k, x) for x in (0, 1, -1)]

    def mirrored(value):
        return rolled(value, LANES // 2)

    here = around(seams, 0)
    behind, ahead = around(seams, -1), around(seams, 1)
    for i in range(1 + plan.ends):
        seams_ref[0, i] = jnp.where(even, mirrored(behind[i]), ahead[i])
        seams_ref[1, i] = jnp.where(even, here[i], mirrored(here[i]))
        seams_ref[2, i] = jnp.where(even, mirrored(ahead[i]), behind[i])
    weight_ref[...] = around(weights, 0)[0]

    for layer in two_layers(plan, m_ref, seam=seams_ref[1, 0]):
        for r in range(plan.rows):
            x_ref[:, at(r, 1, layer.start)] = layer.row(r)
    layers = two_layers(plan, x_ref, m_ref)
    inner_rows(plan, w_ref, (p0_ref, p1_ref), layers, layers, g_ref)


def first_half(
    plan, w_ref, m_ref, f_ref, g_ref, low_ref, high_ref, side_ref, c_low, c_high, seams_ref,
    x_ref, near_ref, side_out, c0_ref, c1_ref, p0_ref, p1_ref, y_ref, h_ref, n0_ref, n1_ref,
):
    own = two_layers(plan, f_ref, m_ref)
    low = two_layers(plan, low_ref, seam=seams_ref[0, 0])
    high = two_layers(plan, high_ref, seam=seams_ref[2, 0])
    near = low[0], high[1]
    n_refs = n0_ref, n1_ref
    middle_rows(
        plan, w_ref, (p0_ref, p1_ref), own, own, g_ref, near, near, sides_of(plan, side_ref, side_ref, seams_ref),
        corners_of(plan, (c_low, c_high), seams_ref), y_ref, h_ref, n_refs,
    )
    lane = lane_index(plan.pad)
    near_ref[:, plan.slab :] = jnp.zeros((plan.pad, LANES), jnp.float32)

    def put(a, r, value):
        x_ref[:, at(r, 1, a * plan.slab)] = value
        if a == 0:
            near_ref[:, at(r)] = value
        else:
            here = rolled(value, r * WINDOW)
            near_ref[:, plan.slab :] = jnp.where(lane == r * WINDOW, here, near_ref[:, plan.slab :])

    outer_rows(plan, w_ref, own, near, (low[1].chunk, high[0].chunk), n_refs, h_ref, put)
    write_edges(plan, x_ref, side_out, (c0_ref, c1_ref))


def inner(plan, w_ref, m_ref, f_ref, x_ref, c_low, c_high, g_ref, far_ref, p0_ref, p1_ref):
    far_ref[...] = x_ref[:, plan.slab :] + 0.0 * (c_low[0, 0:1, 0:1] + c_high[0, 0:1, 0:1])
    inner_rows(plan, w_ref, (p0_ref, p1_ref), two_layers(plan, x_ref, m_ref), two_layers(plan, f_ref, m_ref), g_ref)


def middle(
    plan, w_ref, m_ref, f_ref, x_ref, g_ref, low_ref, high_ref, side_ref, c_low, c_high,
    low_first, high_first, side_first, seams_ref, weight_ref, spread_table,
    h_ref, n0_ref, n1_ref, send_ref, p0_ref, p1_ref, y_ref, inlet_ref,
):
    pad = plan.pad
    own, force = two_layers(plan, x_ref, m_ref), two_layers(plan, f_ref, m_ref)
    low_force = Layer(plan, low_first, 0, None, seams_ref[0, 0], 0)
    high_force = Layer(plan, high_first, plan.slab, None, seams_ref[2, 0], 1)
    near = Layer(plan, low_ref, 0, low_force.rates), Layer(plan, high_ref, plan.slab, high_force.rates)
    n_refs = n0_ref, n1_ref
    middle_rows(
        plan, w_ref, (p0_ref, p1_ref), own, force, g_ref, near, (low_force, high_force),
        sides_of(plan, side_ref, side_first, seams_ref), corners_of(plan, (c_low, c_high), None), y_ref, h_ref, n_refs,
    )
    lane = lane_index(pad)
    inlet_ref[...] = jnp.zeros_like(inlet_ref)

    def put(a, r, value):
        cell = a * plan.rows + r
        inlet_ref[...] = jnp.where(lane == cell * WINDOW, rolled(value, cell * WINDOW), inlet_ref[...])

    def far_inlet(c):
        tile = low_ref[:, plan.slab :]
        count = CHUNK // LANES
        return jnp.concatenate([placed(tile, c * count + part) for part in range(count)], axis=1)

    outer_rows(plan, w_ref, own, near, (far_inlet, Layer(plan, high_ref).chunk), n_refs, h_ref, put)
    inlet = inlet_ref[...]
    inlet = jnp.where(parity() == 0, inlet, rolled(inlet, LANES // 2))
    back = pick(inlet, spread_table[...]) * weight_ref[...]
    back = back + rolled(back, -plan.width)
    me = lax.axis_index("sector")
    send_ref[...] = jnp.zeros_like(send_ref)
    for t in range(plan.insts):
        to = lax.rem(me + plan.shift[t], plan.sectors)
        send_ref[to, : plan.fields, : plan.width] = back[t * plan.fields : (t + 1) * plan.fields, : plan.width]


def outer(plan, w_ref, m_ref, low_first, high_first, n0_ref, n1_ref, h_ref, low_ref, high_ref, out_ref):
    mirror = parity()
    own = two_layers(plan, m_ref)
    near = Layer(plan, low_first), Layer(plan, high_first, plan.slab)

    def put(a, r, value):
        there = jnp.where(mirror == 0, a, plan.ct - 1 - a) * plan.rows + r
        out_ref[pl.ds(there, plan.tf, stride=plan.cells), :] = value[: plan.tf]

    far = Layer(plan, low_ref).chunk, Layer(plan, high_ref).chunk
    outer_rows(plan, w_ref, own, near, far, (n0_ref, n1_ref), h_ref, put)


def collect_panels(plan, got_ref, out_ref, panels_ref):
    me = lax.axis_index("sector")
    for t in range(plan.insts):
        source = lax.rem(me + (plan.sectors - plan.shift[t]), plan.sectors)
        panels_ref[t * RATES : (t + 1) * RATES, :] = got_ref[source]
    for f in range(plan.fields):
        tile = panels_ref[pl.ds(f, plan.insts, stride=RATES), : plan.width]
        out_ref[f] = jnp.transpose(tile)


def sibling(plan):
    return [s ^ 1 for s in range(plan.sectors)]


def outside(plan):
    return [(s - 1 if s % 2 == 0 else s + 1) % plan.sectors for s in range(plan.sectors)]


def swap(array, partner):
    return lax.ppermute(array, "sector", list(enumerate(partner)))


def beside(plan, array, partner):
    def pairs(step):
        out = []
        for s in range(plan.sectors):
            for x in range(plan.spans):
                to = 1 - x if plan.ends == 1 else x + step
                if 0 <= to < plan.spans:
                    out.append((s * plan.spans + x, partner[s] * plan.spans + to))
        return out

    if plan.ends == 1:
        return lax.ppermute(array, AXES, pairs(0))
    return jnp.concatenate([lax.ppermute(array[:1], AXES, pairs(-1)), lax.ppermute(array[1:], AXES, pairs(1))])


def on_device(
    sectors, spans,
    rhs, diag_coef, face_coef, time_coef, jac_up, jac_down, wall_mask, stator_adj, owner, first_panel_share,
):
    plan = Plan(rhs, stator_adj, sectors, spans)
    pad, cells, slab, insts, fields, ends = plan.pad, plan.cells, plan.slab, plan.insts, plan.fields, plan.ends
    bind = functools.partial
    whole, half = f32(pad, plan.ct * slab), f32(pad, slab)
    products = (vmem(6 * pad, slab),) * 2
    alone, next_chip, next_core = list(range(sectors)), outside(plan), sibling(plan)

    def edges(rows):
        return f32(ends, rows, DEPTH * plan.ct * LANES), f32(ends, rows, LANES), f32(ends, rows, LANES)

    stator = jnp.transpose(stator_adj, (1, 2, 3, 0)).reshape(fields, plan.width, insts)
    sent = call(bind(send_panels, plan), f32(sectors * spans, 2 * RATES, LANES), (vmem(insts * RATES, LANES),))(
        stator, owner.reshape(insts, cells), first_panel_share.reshape(insts, cells)
    )
    got = lax.all_to_all(sent, AXES, 0, 0, tiled=True)
    m, side, c0, c1 = call(bind(prepare, plan), (f32(pad + RATES, plan.ct * slab),) + edges(pad + RATES))(
        rhs.reshape(plan.tf * cells, LANES), diag_coef.reshape(cells, LANES), face_coef.reshape(3, cells, LANES),
        time_coef.reshape(cells, LANES), wall_mask.reshape(cells, LANES),
    )
    low_first, high_first = swap(m, next_chip), swap(m, next_core)
    side_first = beside(plan, side, alone)
    c_low, c_high = beside(plan, c0, next_chip), beside(plan, c1, next_core)
    matrices = call(
        bind(stack_matrices, plan), jax.ShapeDtypeStruct((7 * pad, 3 * pad), jnp.bfloat16)
    )(jac_up, jac_down, plan.spectral(), plan.field_rows(), plan.field_lanes(), plan.block_diagonal())
    tiles = len(plan.tiles)
    seams, weight, force, g = call(
        bind(begin, plan), (f32(3, 1 + ends, pad, LANES), f32(pad, LANES), whole, whole),
        (vmem(pad, tiles * LANES), vmem(tiles * pad, LANES), vmem(16, tiles * LANES)) + products,
        flops=2_000_000_000,
    )(
        matrices, m, got, plan.inst_rows(), plan.twice(plan.weight_lanes()), plan.panel_lanes(),
        plan.twice(plan.window_lanes()),
    )
    x, near, side, c0, c1 = call(
        bind(first_half, plan), (whole, f32(pad, slab + LANES)) + edges(pad),
        products + (vmem(pad, 2 * slab), vmem(pad, 2 * slab), vmem(pad, slab), vmem(pad, slab)), flops=4_000_000_000,
    )(matrices, m, force, g, low_first, high_first, side_first, c_low, c_high, seams)

    low, high = swap(near, next_chip), swap(x, next_core)
    side = beside(plan, side, alone)
    c_low, c_high = beside(plan, c0, next_chip), beside(plan, c1, next_core)
    g, far = call(bind(inner, plan), (whole, half), products, flops=2_000_000_000)(
        matrices, m, force, x, c_low, c_high
    )
    far_low = swap(far, next_chip)
    h, n0, n1, back = call(
        bind(middle, plan), (whole, half, half, f32(sectors, RATES, LANES)),
        products + (vmem(pad, 2 * slab), vmem(pad, LANES)), flops=4_000_000_000,
    )(
        matrices, m, force, x, g, low, high, side, c_low, c_high, low_first, high_first, side_first, seams, weight,
        plan.twice(plan.window_lanes().T),
    )
    returned = lax.all_to_all(back, "sector", 0, 0, tiled=True)
    sens = call(bind(collect_panels, plan), f32(fields, plan.width, insts), (vmem(insts * RATES, LANES),))(returned)
    out = call(bind(outer, plan), f32(plan.tf * cells, LANES))(
        matrices, m, low_first, high_first, n0, n1, h, far_low, high
    )
    sens = jnp.transpose(sens.reshape(fields, plan.panels, plan.rows, insts), (3, 0, 1, 2))
    return out.reshape(rhs.shape), sens


def solution(mesh):
    in_specs = (
        P(None, None, "sector", "span", None),
        P("sector", "span", None),
        P(None, "sector", "span", None),
        P("sector", "span", None),
        P(),
        P(),
        P("sector", "span", None),
        P(None, None, "sector", "span"),
        P(None, "sector", "span"),
        P(None, "sector", "span"),
    )
    out_specs = (P(None, None, "sector", "span", None), P(None, None, "sector", "span"))
    return jax.shard_map(
        functools.partial(on_device, mesh.shape["sector"], mesh.shape["span"]),
        mesh=mesh, in_specs=in_specs, out_specs=out_specs, check_vma=False,
    )
```

profile of v0, /device:TPU:0, one launch (start us, length us, event | category | flops | bytes accessed | tf_op | source)
XLA Modules:
  0.0 69.1 jit_solution(4794957920940528595)
XLA Ops:
  1.3 1.1 %copy-done.2 = f32[11,7,2,8,128]{4,3,2,1,0:T(8,128)S(1)} copy-done((f32[11,7,2,8,128]{4,3,2,1,0:T(8,128)S(1)}, f32[11,7,2,8,128]{4,3,2,1,0:T(8,128)}, u32[]{:S(2)}) %copy-start.2) | copy-done | bytes 630808
  5.3 5.7 %collective-permute-start = (f32[88,2048]{1,0:T(8,128)S(1)}, f32[88,2048]{1,0:T(8,128)S(1)}, u32[]{:S(2)}, u32[]{:S(2)}) collective-permute-start(f32[88,2048]{1,0:T(8,128)S(1)} %get-tuple-element.21.m_ref), channel_id=1, source_target_pairs={{0,30},{2,4},{4,2},{6,8},{8,6},{10,12},{12,10},{14,16},{16,14},{18... | collective-permute-start | bytes 2162696 | tf_op jit(solution)/shard_map/ppermute | solution.py:601
  11.8 0.9 %shard_map.196 = f32[32,16,128]{2,1,0:T(8,128)} custom-call(f32[7,32,11]{2,1,0:T(8,128)S(1)} %bitcast.15, s32[11,16]{1,0:T(8,128)S(1)} %copy.23.owner_ref, f32[11,16]{1,0:T(8,128)S(1)} %copy.24.share_ref), custom_call_target="tpu_custom_call" | custom-call | flops 2000000 | bytes 1000000 | tf_op jit(solution)/shard_map/pallas_call | solution.py:634
  12.8 2.7 %all-to-all-start = ((f32[32,16,128]{2,1,0:T(8,128)}), f32[32,16,128]{2,1,0:T(8,128)S(1)}, u32[]{:S(2)}, u32[]{:S(2)}) async-start(f32[32,16,128]{2,1,0:T(8,128)} %shard_map.196), calls=%async_computation | async-start | bytes 524288 | tf_op jit(solution)/shard_map/all_to_all | solution.py:637
  15.5 5.3 %collective-permute-start.3 = (f32[1,88,128]{2,1,0:T(8,128)S(1)}, f32[1,88,128]{2,1,0:T(8,128)S(1)}, u32[]{:S(2)}, u32[]{:S(2)}) collective-permute-start(f32[1,88,128]{2,1,0:T(8,128)S(1)} %get-tuple-element.25), channel_id=1, source_target_pairs={{0,31},{1,30},{2,5},{3,4},{4,3},{5,2},{6,9},{7,8},{8,7},{9,6},{10,... | collective-permute-start | bytes 135176 | tf_op jit(solution)/shard_map/ppermute | solution.py:615
  21.4 1.1 %shard_map.194.w_ref = bf16[560,240]{1,0:T(8,128)(2,1)S(1)} custom-call(f32[3,7,7]{2,1,0:T(8,128)S(1)} %copy-done.13, f32[3,7,7]{2,1,0:T(8,128)S(1)} %copy-done.14, bf16[80,240]{1,0:T(8,128)(2,1)S(1)} %copy-done.11, f32[80,7]{1,0:T(8,128)S(1)} %copy-done.10, f32[7,240]{1,0:T(8,128)S(1)} %copy-done.18, f32[80,240]{1,0:T(8,128)S(1)} %copy-done.8), custom_call_target="tpu_custom_call" | custom-call | flops 2000000 | bytes 1000000 | tf_op jit(solution)/shard_map/pallas_call | solution.py:645
  22.5 6.2 %all-to-all-done.got_ref = f32[32,16,128]{2,1,0:T(8,128)S(1)} async-done(((f32[32,16,128]{2,1,0:T(8,128)}), f32[32,16,128]{2,1,0:T(8,128)S(1)}, u32[]{:S(2)}, u32[]{:S(2)}) %all-to-all-start) | async-done | bytes 262176 | tf_op jit(solution)/shard_map/all_to_all | solution.py:637
  28.7 0.8 %copy-done.23 = bf16[256,128]{1,0:T(8,128)(2,1)S(1)} copy-done((bf16[256,128]{1,0:T(8,128)(2,1)S(1)}, bf16[256,128]{1,0:T(8,128)(2,1)}, u32[]{:S(2)}) %copy-start.23) | copy-done | bytes 65560
  30.2 1.7 %shard_map.197 = (f32[3,2,80,128]{3,2,1,0:T(8,128)S(1)}, f32[80,128]{1,0:T(8,128)S(1)}, f32[80,2048]{1,0:T(8,128)S(1)}, f32[80,2048]{1,0:T(8,128)S(1)}) custom-call(bf16[560,240]{1,0:T(8,128)(2,1)S(1)} %shard_map.194.w_ref, f32[88,2048]{1,0:T(8,128)S(1)} %get-tuple-element.21.m_ref, f32[32,16,128]{2,1,0:T(8,128)S(1)} %all-to-all-done.got_ref, ...), custom_call_target="tpu_custom_call" | custom-call | flops 2000000000 | bytes 1000000 | tf_op jit(solution)/shard_map/pallas_call | solution.py:649
  32.0 2.8 %shard_map.198 = (f32[80,2048]{1,0:T(8,128)S(1)}, f32[80,1152]{1,0:T(8,128)S(1)}, f32[1,80,512]{2,1,0:T(8,128)S(1)}, f32[1,80,128]{2,1,0:T(8,128)S(1)}, f32[1,80,128]{2,1,0:T(8,128)S(1)}) custom-call(bf16[560,240]{1,0:T(8,128)(2,1)S(1)} %shard_map.194.w_ref, f32[88,2048]{1,0:T(8,128)S(1)} %get-tuple-element.21.m_ref, ...), custom_call_target="tpu_custom_call" | custom-call | flops 4000000000 | bytes 1000000 | tf_op jit(solution)/shard_map/pallas_call | solution.py:657
  34.9 4.6 %collective-permute-start.7 = (f32[80,1152]{1,0:T(8,128)S(1)}, f32[80,1152]{1,0:T(8,128)S(1)}, u32[]{:S(2)}, u32[]{:S(2)}) collective-permute-start(f32[80,1152]{1,0:T(8,128)S(1)} %get-tuple-element.32), channel_id=1, source_target_pairs={{0,30},{2,4},{4,2},{6,8},{8,6},{10,12},{12,10},{14,16},{16,14},{18... | collective-permute-start | bytes 1105928 | tf_op jit(solution)/shard_map/ppermute | solution.py:601
  39.5 1.4 %collective-permute-start.5 = (f32[1,80,128]{2,1,0:T(8,128)S(1)}, f32[1,80,128]{2,1,0:T(8,128)S(1)}, u32[]{:S(2)}, u32[]{:S(2)}) collective-permute-start(f32[1,80,128]{2,1,0:T(8,128)S(1)} %get-tuple-element.29), channel_id=1, source_target_pairs={{0,31},{1,30},{2,5},{3,4},{4,3},{5,2},{6,9},{7,8},{8,7},{9,6},{10,... | collective-permute-start | bytes 122888 | tf_op jit(solution)/shard_map/ppermute | solution.py:615
  41.1 5.6 %collective-permute-done.5.c_low = f32[1,80,128]{2,1,0:T(8,128)S(1)} collective-permute-done((f32[1,80,128]{2,1,0:T(8,128)S(1)}, f32[1,80,128]{2,1,0:T(8,128)S(1)}, u32[]{:S(2)}, u32[]{:S(2)}) %collective-permute-start.5) | collective-permute-done | bytes 40992 | tf_op jit(solution)/shard_map/ppermute | solution.py:615
  46.7 1.5 %shard_map.199 = (f32[80,2048]{1,0:T(8,128)S(1)}, f32[80,1024]{1,0:T(8,128)}) custom-call(bf16[560,240]{1,0:T(8,128)(2,1)S(1)} %shard_map.194.w_ref, f32[88,2048]{1,0:T(8,128)S(1)} %get-tuple-element.21.m_ref, f32[80,2048]{1,0:T(8,128)S(1)} %get-tuple-element.22.f_ref, f32[80,2048]{1,0:T(8,128)S(1)} %get-tuple-element.28.x_ref, ...), custom_call_target="tpu_custom_call" | custom-call | flops 2000000000 | bytes 1000000 | tf_op jit(solution)/shard_map/pallas_call | solution.py:665
  48.1 4.0 %collective-permute-start.10 = (f32[80,1024]{1,0:T(8,128)}, f32[80,1024]{1,0:T(8,128)S(1)}, u32[]{:S(2)}, u32[]{:S(2)}) collective-permute-start(f32[80,1024]{1,0:T(8,128)} %get-tuple-element.38), channel_id=1, source_target_pairs={{0,30},{2,4},{4,2},{6,8},{8,6},{10,12},{12,10},{14,16},{16,14},{18... | collective-permute-start | bytes 983048 | tf_op jit(solution)/shard_map/ppermute | solution.py:601
  52.1 2.9 %shard_map.200 = (f32[80,2048]{1,0:T(8,128)S(1)}, f32[80,1024]{1,0:T(8,128)S(1)}, f32[80,1024]{1,0:T(8,128)S(1)}, f32[16,8,128]{2,1,0:T(8,128)S(1)}) custom-call(bf16[560,240]{1,0:T(8,128)(2,1)S(1)} %shard_map.194.w_ref, f32[88,2048]{1,0:T(8,128)S(1)} %get-tuple-element.21.m_ref, f32[80,2048]{1,0:T(8,128)S(1)} %get-tuple-element.22.f_ref, ...), custom_call_target="tpu_custom_call" | custom-call | flops 4000000000 | bytes 1000000 | tf_op jit(solution)/shard_map/pallas_call | solution.py:669
  55.0 0.8 %copy-done = f32[80,2048]{1,0:T(8,128)} copy-done((f32[80,2048]{1,0:T(8,128)}, f32[80,2048]{1,0:T(8,128)S(1)}, u32[]{:S(2)}) %copy-start) | copy-done | bytes 655384
  58.0 3.5 %all-to-all-start.1 = ((f32[16,8,128]{2,1,0:T(8,128)}), f32[16,8,128]{2,1,0:T(8,128)S(1)}, u32[]{:S(2)}, u32[]{:S(2)}) async-start(f32[16,8,128]{2,1,0:T(8,128)} %copy-done.9), calls=%async_computation.1 | async-start | bytes 131072 | tf_op jit(solution)/shard_map/all_to_all | solution.py:676
  61.5 1.1 %copy-done.1 = f32[80,2048]{1,0:T(8,128)S(1)} copy-done((f32[80,2048]{1,0:T(8,128)S(1)}, f32[80,2048]{1,0:T(8,128)}, u32[]{:S(2)}) %copy-start.1) | copy-done | bytes 655384
  62.6 1.0 %copy-done.4 = f32[80,1024]{1,0:T(8,128)S(1)} copy-done((f32[80,1024]{1,0:T(8,128)S(1)}, f32[80,1024]{1,0:T(8,128)}, u32[]{:S(2)}) %copy-start.4) | copy-done | bytes 327704
  63.5 1.0 %copy-done.6 = f32[80,1024]{1,0:T(8,128)S(1)} copy-done((f32[80,1024]{1,0:T(8,128)S(1)}, f32[80,1024]{1,0:T(8,128)}, u32[]{:S(2)}) %copy-start.6) | copy-done | bytes 327704
  64.5 1.4 %shard_map.201 = f32[1232,128]{1,0:T(8,128)} custom-call(bf16[560,240]{1,0:T(8,128)(2,1)S(1)} %shard_map.194.w_ref, f32[88,2048]{1,0:T(8,128)S(1)} %get-tuple-element.21.m_ref, f32[88,2048]{1,0:T(8,128)S(1)} %collective-permute-done.low_ref.low_first, f32[88,2048]{1,0:T(8,128)S(1)} %collective-permute-done.1.high_ref.high_first, f32[80,1024]{1,0:T(8,128)S(1)} %copy-done.4, ...), custom_call_target="tpu_custom_call" | custom-call | flops 2000000 | bytes 1000000 | tf_op jit(solution)/shard_map/pallas_call | solution.py:678
  66.0 2.4 %all-to-all-done.1.got_ref = f32[16,8,128]{2,1,0:T(8,128)S(1)} async-done(((f32[16,8,128]{2,1,0:T(8,128)}), f32[16,8,128]{2,1,0:T(8,128)S(1)}, u32[]{:S(2)}, u32[]{:S(2)}) %all-to-all-start.1) | async-done | bytes 65568 | tf_op jit(solution)/shard_map/all_to_all | solution.py:676
  68.3 0.8 %shard_map.202 = f32[7,32,11]{2,1,0:T(8,128)} custom-call(f32[16,8,128]{2,1,0:T(8,128)S(1)} %all-to-all-done.1.got_ref), custom_call_target="tpu_custom_call" | custom-call | flops 2000000 | bytes 1000000 | tf_op jit(solution)/shard_map/pallas_call | solution.py:677
  (69 shorter events, 8.1 us)
Async XLA Ops:
  4.5 7.2 %copy-start.7 = (f32[11,7,4,8]{0,3,2,1:T(8,128)S(1)}, f32[11,7,4,8]{0,3,2,1:T(8,128)}, u32[]{:S(2)}) copy-start(f32[11,7,4,8]{0,3,2,1:T(8,128)} %param.26) | copy-start | bytes 29572
  4.8 27.1 %collective-permute-start.1 = (f32[88,2048]{1,0:T(8,128)S(1)}, f32[88,2048]{1,0:T(8,128)S(1)}, u32[]{:S(2)}, u32[]{:S(2)}) collective-permute-start(f32[88,2048]{1,0:T(8,128)S(1)} %get-tuple-element.21.m_ref), channel_id=1, source_target_pairs={{0,2},{2,0},{4,6},{6,4},{8,10},{10,8},{12,14},{14,12},{16,18},{18,... | collective-permute-start | bytes 2162696 | tf_op jit(solution)/shard_map/ppermute | solution.py:601
  5.3 26.6 %collective-permute-start = (f32[88,2048]{1,0:T(8,128)S(1)}, f32[88,2048]{1,0:T(8,128)S(1)}, u32[]{:S(2)}, u32[]{:S(2)}) collective-permute-start(f32[88,2048]{1,0:T(8,128)S(1)} %get-tuple-element.21.m_ref), channel_id=1, source_target_pairs={{0,30},{2,4},{4,2},{6,8},{8,6},{10,12},{12,10},{14,16},{16,14},{18... | collective-permute-start | bytes 2162696 | tf_op jit(solution)/shard_map/ppermute | solution.py:601
  12.7 8.6 %copy-start.8 = (f32[80,240]{1,0:T(8,128)S(1)}, f32[80,240]{1,0:T(8,128)}, u32[]{:S(2)}) copy-start(f32[80,240]{1,0:T(8,128)} %constant.21.clone.diagonal_ref) | copy-start | bytes 230404
  12.7 8.6 %copy-start.10 = (f32[80,7]{1,0:T(8,128)S(1)}, f32[80,7]{1,0:T(8,128)}, u32[]{:S(2)}) copy-start(f32[80,7]{1,0:T(8,128)} %constant.19.clone.rows_ref) | copy-start | bytes 6724
  12.7 8.7 %copy-start.11 = (bf16[80,240]{1,0:T(8,128)(2,1)S(1)}, bf16[80,240]{1,0:T(8,128)(2,1)}, u32[]{:S(2)}) copy-start(bf16[80,240]{1,0:T(8,128)(2,1)} %constant.18.clone.spectral_ref) | copy-start | bytes 115204
  12.7 8.7 %copy-start.13 = (f32[3,7,7]{2,1,0:T(8,128)S(1)}, f32[3,7,7]{2,1,0:T(8,128)}, u32[]{:S(2)}) copy-start(f32[3,7,7]{2,1,0:T(8,128)} %up_ref.1) | copy-start | bytes 1768
  12.7 8.7 %copy-start.14 = (f32[3,7,7]{2,1,0:T(8,128)S(1)}, f32[3,7,7]{2,1,0:T(8,128)}, u32[]{:S(2)}) copy-start(f32[3,7,7]{2,1,0:T(8,128)} %down_ref.1) | copy-start | bytes 1768
  12.7 8.6 %copy-start.18 = (f32[7,240]{1,0:T(8,128)S(1)}, f32[7,240]{1,0:T(8,128)}, u32[]{:S(2)}) copy-start(f32[7,240]{1,0:T(8,128)} %constant.20.clone.lanes_ref) | copy-start | bytes 20164
  12.8 15.9 %all-to-all-start = ((f32[32,16,128]{2,1,0:T(8,128)}), f32[32,16,128]{2,1,0:T(8,128)S(1)}, u32[]{:S(2)}, u32[]{:S(2)}) async-start(f32[32,16,128]{2,1,0:T(8,128)} %shard_map.196), calls=%async_computation | async-start | bytes 524288 | tf_op jit(solution)/shard_map/all_to_all | solution.py:637
  15.5 16.4 %collective-permute-start.3 = (f32[1,88,128]{2,1,0:T(8,128)S(1)}, f32[1,88,128]{2,1,0:T(8,128)S(1)}, u32[]{:S(2)}, u32[]{:S(2)}) collective-permute-start(f32[1,88,128]{2,1,0:T(8,128)S(1)} %get-tuple-element.25), channel_id=1, source_target_pairs={{0,31},{1,30},{2,5},{3,4},{4,3},{5,2},{6,9},{7,8},{8,7},{9,6},{10,... | collective-permute-start | bytes 135176 | tf_op jit(solution)/shard_map/ppermute | solution.py:615
  20.8 11.1 %collective-permute-start.4 = (f32[1,88,128]{2,1,0:T(8,128)S(1)}, f32[1,88,128]{2,1,0:T(8,128)S(1)}, u32[]{:S(2)}, u32[]{:S(2)}) collective-permute-start(f32[1,88,128]{2,1,0:T(8,128)S(1)} %get-tuple-element.26), channel_id=1, source_target_pairs={{0,3},{1,2},{2,1},{3,0},{4,7},{5,6},{6,5},{7,4},{8,11},{9,10},{10,... | collective-permute-start | bytes 135176 | tf_op jit(solution)/shard_map/ppermute | solution.py:615
  20.8 7.9 %copy-start.22 = (bf16[256,128]{1,0:T(8,128)(2,1)S(1)}, bf16[256,128]{1,0:T(8,128)(2,1)}, u32[]{:S(2)}) copy-start(bf16[256,128]{1,0:T(8,128)(2,1)} %constant.25.clone.sum_table) | copy-start | bytes 196612
  20.8 7.9 %copy-start.24 = (f32[80,16]{1,0:T(8,128)S(1)}, f32[80,16]{1,0:T(8,128)}, u32[]{:S(2)}) copy-start(f32[80,16]{1,0:T(8,128)} %constant.22.clone.inst_rows) | copy-start | bytes 15364
  20.8 11.1 %collective-permute-start.2 = (f32[1,88,512]{2,1,0:T(8,128)S(1)}, f32[1,88,512]{2,1,0:T(8,128)S(1)}, u32[]{:S(2)}, u32[]{:S(2)}) collective-permute-start(f32[1,88,512]{2,1,0:T(8,128)S(1)} %get-tuple-element.24), channel_id=1, source_target_pairs={{0,1},{1,0},{2,3},{3,2},{4,5},{5,4},{6,7},{7,6},{8,9},{9,8},{10,11... | collective-permute-start | bytes 540680 | tf_op jit(solution)/shard_map/ppermute | solution.py:615
  34.8 17.3 %collective-permute-start.8 = (f32[80,2048]{1,0:T(8,128)S(1)}, f32[80,2048]{1,0:T(8,128)S(1)}, u32[]{:S(2)}, u32[]{:S(2)}) collective-permute-start(f32[80,2048]{1,0:T(8,128)S(1)} %get-tuple-element.28.x_ref), channel_id=1, source_target_pairs={{0,2},{2,0},{4,6},{6,4},{8,10},{10,8},{12,14},{14,12},{16,18},{18,... | collective-permute-start | bytes 1966088 | tf_op jit(solution)/shard_map/ppermute | solution.py:601
  34.9 17.2 %collective-permute-start.7 = (f32[80,1152]{1,0:T(8,128)S(1)}, f32[80,1152]{1,0:T(8,128)S(1)}, u32[]{:S(2)}, u32[]{:S(2)}) collective-permute-start(f32[80,1152]{1,0:T(8,128)S(1)} %get-tuple-element.32), channel_id=1, source_target_pairs={{0,30},{2,4},{4,2},{6,8},{8,6},{10,12},{12,10},{14,16},{16,14},{18... | collective-permute-start | bytes 1105928 | tf_op jit(solution)/shard_map/ppermute | solution.py:601
  39.5 7.2 %collective-permute-start.5 = (f32[1,80,128]{2,1,0:T(8,128)S(1)}, f32[1,80,128]{2,1,0:T(8,128)S(1)}, u32[]{:S(2)}, u32[]{:S(2)}) collective-permute-start(f32[1,80,128]{2,1,0:T(8,128)S(1)} %get-tuple-element.29), channel_id=1, source_target_pairs={{0,31},{1,30},{2,5},{3,4},{4,3},{5,2},{6,9},{7,8},{8,7},{9,6},{10,... | collective-permute-start | bytes 122888 | tf_op jit(solution)/shard_map/ppermute | solution.py:615
  40.9 5.8 %collective-permute-start.6 = (f32[1,80,128]{2,1,0:T(8,128)S(1)}, f32[1,80,128]{2,1,0:T(8,128)S(1)}, u32[]{:S(2)}, u32[]{:S(2)}) collective-permute-start(f32[1,80,128]{2,1,0:T(8,128)S(1)} %get-tuple-element.30), channel_id=1, source_target_pairs={{0,3},{1,2},{2,1},{3,0},{4,7},{5,6},{6,5},{7,4},{8,11},{9,10},{10,... | collective-permute-start | bytes 122888 | tf_op jit(solution)/shard_map/ppermute | solution.py:615
  40.9 11.3 %copy-start.20 = (f32[1,88,512]{2,1,0:T(8,128)S(1)}, f32[1,88,512]{2,1,0:T(8,128)}, u32[]{:S(2)}) copy-start(f32[1,88,512]{2,1,0:T(8,128)} %copy-done.19) | copy-start | bytes 540676
  40.9 11.3 %copy-start.21 = (bf16[256,128]{1,0:T(8,128)(2,1)S(1)}, bf16[256,128]{1,0:T(8,128)(2,1)}, u32[]{:S(2)}) copy-start(bf16[256,128]{1,0:T(8,128)(2,1)} %constant.26.clone.spread_table) | copy-start | bytes 196612
  40.9 11.2 %collective-permute-start.9 = (f32[1,80,512]{2,1,0:T(8,128)S(1)}, f32[1,80,512]{2,1,0:T(8,128)S(1)}, u32[]{:S(2)}, u32[]{:S(2)}) collective-permute-start(f32[1,80,512]{2,1,0:T(8,128)S(1)} %get-tuple-element.33), channel_id=1, source_target_pairs={{0,1},{1,0},{2,3},{3,2},{4,5},{5,4},{6,7},{7,6},{8,9},{9,8},{10,11... | collective-permute-start | bytes 491528 | tf_op jit(solution)/shard_map/ppermute | solution.py:615
  48.1 13.3 %collective-permute-start.10 = (f32[80,1024]{1,0:T(8,128)}, f32[80,1024]{1,0:T(8,128)S(1)}, u32[]{:S(2)}, u32[]{:S(2)}) collective-permute-start(f32[80,1024]{1,0:T(8,128)} %get-tuple-element.38), channel_id=1, source_target_pairs={{0,30},{2,4},{4,2},{6,8},{8,6},{10,12},{12,10},{14,16},{16,14},{18... | collective-permute-start | bytes 983048 | tf_op jit(solution)/shard_map/ppermute | solution.py:601
  58.0 10.4 %all-to-all-start.1 = ((f32[16,8,128]{2,1,0:T(8,128)}), f32[16,8,128]{2,1,0:T(8,128)S(1)}, u32[]{:S(2)}, u32[]{:S(2)}) async-start(f32[16,8,128]{2,1,0:T(8,128)} %copy-done.9), calls=%async_computation.1 | async-start | bytes 131072 | tf_op jit(solution)/shard_map/all_to_all | solution.py:676
  (17 other events, 21.4 us)
where the time goes:
time: 69.8 us; the launch traced here: 69.1 us
  starting transfers between devices  28.5 us (41%)
  waiting for transfers between devices  14.2 us (20%)
  Pallas kernels  13.4 us (19%)
  local copies, waits for them, and re-layouts  12.2 us (17%)
  between operations  0.86 us (1%)
    ppermute x5, starting transfers between devices, swap(): return lax.ppermute(array, 'sector', list(enumerate(partner)))  14.8 us
    unnamed x56, local copies, waits for them, and re-layouts  12 us
    ppermute x6, starting transfers between devices, beside(): return lax.ppermute(array, AXES, pairs(0))  7.44 us
    all_to_all x1, waiting for transfers between devices, on_device(): got = lax.all_to_all(sent, AXES, 0, 0, tiled=True)  6.19 us
    ppermute x6, waiting for transfers between devices, beside(): return lax.ppermute(array, AXES, pairs(0))  5.61 us
    all_to_all x1, starting transfers between devices, on_device(): returned = lax.all_to_all(back, 'sector', 0, 0, tiled=True)  3.5 us
    pallas_call x1, Pallas kernels, on_device(): call(bind(middle, plan), (whole, half, half, f32(sectors, RATES, LANES)),...  2.88 us
    pallas_call x1, Pallas kernels, on_device(): call(bind(first_half, plan), (whole, f32(pad, slab + LANES)) + edges(pad)...  2.84 us
  transfers between devices with their start and end apart: 13, of which 3 were waited for; matrix products, arithmetic and copies ran while one was open for 0% of the time, Pallas kernels for 14%

commit v1 on v0

--- a/solution.py
+++ b/solution.py
@@ -16,7 +16,7 @@
 WINDOW = 8
 HIGHEST = lax.Precision.HIGHEST
 DOWN_AZ, SPECTRAL, UP_SP, DOWN_SP, UP_AX, DOWN_AX, UP_AZ = range(7)
-C_TIME, C_AZ, C_SP, C_UP, C_DOWN, C_MASK = range(6)
+C_TIME, C_AZ, C_SP, C_UP, C_DOWN, C_MASK, C_OTHER = range(7)
 RATES = 8
 GROUP = 3
 AXES = ("sector", "span")
@@ -107,14 +107,26 @@
         return np.where(lane < self.ct * self.width, (lane // self.rows) % self.panels, -9).astype(np.float32)[None]
 
 
-def call(kernel, out, scratch=(), flops=2_000_000, nbytes=1_000_000):
+def call(kernel, out, scratch=(), flops=2_000_000, nbytes=1_000_000, **specs):
     return pl.pallas_call(
         kernel,
         out_shape=out,
         scratch_shapes=list(scratch),
-        compiler_params=pltpu.CompilerParams(vmem_limit_bytes=40 * 1024 * 1024),
+        compiler_params=pltpu.CompilerParams(vmem_limit_bytes=20 * 1024 * 1024),
         cost_estimate=pl.CostEstimate(flops=flops, bytes_accessed=nbytes, transcendentals=0),
-    )
+        **specs,
+    )
+
+
+def places(count, far=()):
+    return [pl.BlockSpec(memory_space=pltpu.HBM if i in far else pltpu.VMEM) for i in range(count)]
+
+
+def copies(pairs, sems):
+    out = [pltpu.make_async_copy(source, target, sems.at[i]) for i, (source, target) in enumerate(pairs)]
+    for one in out:
+        one.start()
+    return out
 
 
 def f32(*shape):
@@ -166,8 +178,8 @@
 
 
 class Layer:
-    def __init__(self, plan, ref, start=0, rates=None, seam=None, layer=0):
-        self.plan, self.ref, self.start, self.seam, self.layer = plan, ref, start, seam, layer
+    def __init__(self, plan, ref, start=0, rates=None, seam=None, layer=0, scale=C_MASK):
+        self.plan, self.ref, self.start, self.seam, self.layer, self.scale = plan, ref, start, seam, layer, scale
         self.rates = rates or (ref, start)
 
     def rate(self, which, r, count=1):
@@ -179,7 +191,7 @@
         value = self.ref[: self.plan.pad, at(r, 1, self.start)]
         if self.seam is None:
             return value
-        return value + placed(self.seam, self.layer * self.plan.rows + r) * self.rate(C_MASK, r)
+        return value + placed(self.seam, self.layer * self.plan.rows + r) * self.rate(self.scale, r)
 
     def chunk(self, c):
         count = CHUNK // LANES
@@ -361,25 +373,44 @@
     return corner
 
 
-def prepare(plan, rhs_ref, diag_ref, face_ref, time_ref, mask_ref, m_ref, side_ref, c0_ref, c1_ref):
+def prepare(
+    plan, rhs_hbm, diag_hbm, face_hbm, time_hbm, mask_hbm, m_ref, near_ref, side_ref, c0_ref, c1_ref,
+    rhs_ref, diag_ref, face_ref, time_ref, mask_ref, sems,
+):
     pad = plan.pad
+    for one in copies((
+        (rhs_hbm, rhs_ref), (diag_hbm, diag_ref), (face_hbm, face_ref), (time_hbm, time_ref), (mask_hbm, mask_ref),
+    ), sems):
+        one.wait()
     lane = lane_index(1)
     tail = jnp.zeros((pad - plan.tf, LANES), jnp.float32)
     mirror = parity()
-    for cell in range(plan.cells):
-        a, r = divmod(cell, plan.rows)
-        there = jnp.where(mirror == 0, a, plan.ct - 1 - a) * plan.rows + r
-        one = pl.ds(there, 1)
-        scale = mask_ref[one, :].astype(jnp.float32) / diag_ref[one, :]
-        axial = scale * face_ref[2, one, :]
-        rates = [
-            scale * time_ref[one, :], scale * face_ref[0, one, :], scale * face_ref[1, one, :],
-            jnp.where(lane < LANES - 1, axial, 0.0), jnp.where(lane > 0, axial, 0.0), scale,
-            jnp.zeros((RATES - 6, LANES), jnp.float32),
-        ]
-        field = jnp.concatenate([rhs_ref[pl.ds(there, plan.tf, stride=plan.cells), :], tail], axis=0) * scale
-        m_ref[:pad, at(cell)] = field
-        m_ref[pad:, at(cell)] = jnp.concatenate(rates, axis=0)
+
+    def places_of(a, r):
+        return jnp.where(mirror == 0, a, plan.ct - 1 - a) * plan.rows + r
+
+    def scale_of(a, r):
+        one = pl.ds(places_of(a, r), 1)
+        return mask_ref[one, :].astype(jnp.float32) / diag_ref[one, :]
+
+    for r in range(plan.rows):
+        scales = [scale_of(a, r) for a in range(plan.ct)]
+        for a, scale in enumerate(scales):
+            there = places_of(a, r)
+            one = pl.ds(there, 1)
+            axial = scale * face_ref[2, one, :]
+            rates = jnp.concatenate([
+                scale * time_ref[one, :], scale * face_ref[0, one, :], scale * face_ref[1, one, :],
+                jnp.where(lane < LANES - 1, axial, 0.0), jnp.where(lane > 0, axial, 0.0), scale, scales[1 - a],
+                jnp.zeros((RATES - 7, LANES), jnp.float32),
+            ], axis=0)
+            field = jnp.concatenate([rhs_ref[pl.ds(there, plan.tf, stride=plan.cells), :], tail], axis=0) * scale
+            lanes = at(a * plan.rows + r)
+            m_ref[:pad, lanes] = field
+            m_ref[pad:, lanes] = rates
+            if a == 0:
+                near_ref[:pad, lanes] = field
+                near_ref[pad:, lanes] = rates
     write_edges(plan, m_ref, side_ref, (c0_ref, c1_ref))
 
 
@@ -395,8 +426,16 @@
                     c_refs[a][n] = end
 
 
-def stack_matrices(plan, up_ref, down_ref, spectral_ref, rows_ref, lanes_ref, diagonal_ref, out_ref):
+def after(value, *refs):
+    return value + 0.0 * sum(ref[0, 0:1, 0:1] for ref in refs)
+
+
+def stack_matrices(plan, m_ref, side_ref, c_high, up_ref, down_ref, spectral_ref, rows_ref, lanes_ref, diagonal_ref, *refs):
     pad = plan.pad
+    out_ref, far_ref = refs[len(refs) // 2 - 1 : len(refs) // 2 + 1]
+    far_ref[...] = after(m_ref[:pad, plan.slab :], side_ref, c_high)
+    for source, target in zip(refs[: len(refs) // 2 - 1], refs[len(refs) // 2 + 1 :]):
+        target[...] = source[...]
     lane = lax.broadcasted_iota(jnp.int32, (pad, 3 * pad), 1)
     second = (lane >= pad) & (lane < 2 * pad)
     out_ref[SPECTRAL * pad : (SPECTRAL + 1) * pad, :] = spectral_ref[...]
@@ -494,19 +533,28 @@
     inner_rows(plan, w_ref, (p0_ref, p1_ref), layers, layers, g_ref)
 
 
-def first_half(
+def middle_first(
     plan, w_ref, m_ref, f_ref, g_ref, low_ref, high_ref, side_ref, c_low, c_high, seams_ref,
-    x_ref, near_ref, side_out, c0_ref, c1_ref, p0_ref, p1_ref, y_ref, h_ref, n0_ref, n1_ref,
+    h_ref, n0_ref, n1_ref, p0_ref, p1_ref, y_ref,
 ):
     own = two_layers(plan, f_ref, m_ref)
-    low = two_layers(plan, low_ref, seam=seams_ref[0, 0])
-    high = two_layers(plan, high_ref, seam=seams_ref[2, 0])
-    near = low[0], high[1]
-    n_refs = n0_ref, n1_ref
+    near = (
+        Layer(plan, low_ref, 0, None, seams_ref[0, 0], 0), Layer(plan, high_ref, plan.slab, None, seams_ref[2, 0], 1),
+    )
     middle_rows(
         plan, w_ref, (p0_ref, p1_ref), own, own, g_ref, near, near, sides_of(plan, side_ref, side_ref, seams_ref),
-        corners_of(plan, (c_low, c_high), seams_ref), y_ref, h_ref, n_refs,
-    )
+        corners_of(plan, (c_low, c_high), seams_ref), y_ref, h_ref, (n0_ref, n1_ref),
+    )
+
+
+def outer_first(
+    plan, w_ref, m_ref, low_first, high_first, n0_ref, n1_ref, h_ref, far_ref, seams_ref,
+    x_ref, near_ref, side_out, c0_ref, c1_ref,
+):
+    own = two_layers(plan, m_ref)
+    near = Layer(plan, low_first), Layer(plan, high_first, plan.slab)
+    far_low = Layer(plan, far_ref, 0, (low_first, 0), seams_ref[0, 0], 1, C_OTHER)
+    far_high = Layer(plan, high_first, 0, None, seams_ref[2, 0], 0)
     lane = lane_index(plan.pad)
     near_ref[:, plan.slab :] = jnp.zeros((plan.pad, LANES), jnp.float32)
 
@@ -518,19 +566,19 @@
             here = rolled(value, r * WINDOW)
             near_ref[:, plan.slab :] = jnp.where(lane == r * WINDOW, here, near_ref[:, plan.slab :])
 
-    outer_rows(plan, w_ref, own, near, (low[1].chunk, high[0].chunk), n_refs, h_ref, put)
+    outer_rows(plan, w_ref, own, near, (far_low.chunk, far_high.chunk), (n0_ref, n1_ref), h_ref, put)
     write_edges(plan, x_ref, side_out, (c0_ref, c1_ref))
 
 
-def inner(plan, w_ref, m_ref, f_ref, x_ref, c_low, c_high, g_ref, far_ref, p0_ref, p1_ref):
-    far_ref[...] = x_ref[:, plan.slab :] + 0.0 * (c_low[0, 0:1, 0:1] + c_high[0, 0:1, 0:1])
+def inner(plan, w_ref, m_ref, f_ref, x_ref, side_ref, c_high, g_ref, far_ref, p0_ref, p1_ref):
+    far_ref[...] = after(x_ref[:, plan.slab :], side_ref, c_high)
     inner_rows(plan, w_ref, (p0_ref, p1_ref), two_layers(plan, x_ref, m_ref), two_layers(plan, f_ref, m_ref), g_ref)
 
 
 def middle(
     plan, w_ref, m_ref, f_ref, x_ref, g_ref, low_ref, high_ref, side_ref, c_low, c_high,
     low_first, high_first, side_first, seams_ref, weight_ref, spread_table,
-    h_ref, n0_ref, n1_ref, send_ref, p0_ref, p1_ref, y_ref, inlet_ref,
+    h_hbm, n0_hbm, n1_hbm, send_hbm, h_ref, n0_ref, n1_ref, send_ref, p0_ref, p1_ref, y_ref, inlet_ref, sems,
 ):
     pad = plan.pad
     own, force = two_layers(plan, x_ref, m_ref), two_layers(plan, f_ref, m_ref)
@@ -542,6 +590,7 @@
         plan, w_ref, (p0_ref, p1_ref), own, force, g_ref, near, (low_force, high_force),
         sides_of(plan, side_ref, side_first, seams_ref), corners_of(plan, (c_low, c_high), None), y_ref, h_ref, n_refs,
     )
+    started = copies(((h_ref, h_hbm), (n0_ref, n0_hbm), (n1_ref, n1_hbm)), sems)
     lane = lane_index(pad)
     inlet_ref[...] = jnp.zeros_like(inlet_ref)
 
@@ -564,9 +613,18 @@
     for t in range(plan.insts):
         to = lax.rem(me + plan.shift[t], plan.sectors)
         send_ref[to, : plan.fields, : plan.width] = back[t * plan.fields : (t + 1) * plan.fields, : plan.width]
-
-
-def outer(plan, w_ref, m_ref, low_first, high_first, n0_ref, n1_ref, h_ref, low_ref, high_ref, out_ref):
+    started.append(pltpu.make_async_copy(send_ref, send_hbm, sems.at[3]))
+    started[-1].start()
+    for one in started:
+        one.wait()
+
+
+def outer(
+    plan, w_ref, m_ref, low_first, high_first, n0_hbm, n1_hbm, h_hbm, low_ref, high_ref, out_ref,
+    n0_ref, n1_ref, h_ref, sems,
+):
+    for one in copies(((n0_hbm, n0_ref), (n1_hbm, n1_ref), (h_hbm, h_ref)), sems):
+        one.wait()
     mirror = parity()
     own = two_layers(plan, m_ref)
     near = Layer(plan, low_first), Layer(plan, high_first, plan.slab)
@@ -635,49 +693,67 @@
         stator, owner.reshape(insts, cells), first_panel_share.reshape(insts, cells)
     )
     got = lax.all_to_all(sent, AXES, 0, 0, tiled=True)
-    m, side, c0, c1 = call(bind(prepare, plan), (f32(pad + RATES, plan.ct * slab),) + edges(pad + RATES))(
+    m, near, side, c0, c1 = call(
+        bind(prepare, plan), (f32(pad + RATES, plan.ct * slab), f32(pad + RATES, slab)) + edges(pad + RATES),
+        (
+            vmem(plan.tf * cells, LANES), vmem(cells, LANES), vmem(3, cells, LANES), vmem(cells, LANES),
+            pltpu.VMEM((cells, LANES), jnp.int32), pltpu.SemaphoreType.DMA((5,)),
+        ),
+        in_specs=places(5, range(5)),
+    )(
         rhs.reshape(plan.tf * cells, LANES), diag_coef.reshape(cells, LANES), face_coef.reshape(3, cells, LANES),
         time_coef.reshape(cells, LANES), wall_mask.reshape(cells, LANES),
     )
-    low_first, high_first = swap(m, next_chip), swap(m, next_core)
+    low_first, high_first = swap(near, next_chip), swap(m, next_core)
     side_first = beside(plan, side, alone)
     c_low, c_high = beside(plan, c0, next_chip), beside(plan, c1, next_core)
-    matrices = call(
-        bind(stack_matrices, plan), jax.ShapeDtypeStruct((7 * pad, 3 * pad), jnp.bfloat16)
-    )(jac_up, jac_down, plan.spectral(), plan.field_rows(), plan.field_lanes(), plan.block_diagonal())
+    tables = (
+        plan.inst_rows(), plan.twice(plan.weight_lanes()), plan.panel_lanes(), plan.twice(plan.window_lanes()),
+        plan.twice(plan.window_lanes().T),
+    )
+    matrices, far, *tables = call(
+        bind(stack_matrices, plan),
+        [jax.ShapeDtypeStruct((7 * pad, 3 * pad), jnp.bfloat16), half]
+        + [jax.ShapeDtypeStruct(table.shape, table.dtype) for table in tables],
+    )(m, side_first, c_high, jac_up, jac_down, plan.spectral(), plan.field_rows(), plan.field_lanes(), plan.block_diagonal(), *tables)
+    far_low = swap(far, next_chip)
     tiles = len(plan.tiles)
     seams, weight, force, g = call(
         bind(begin, plan), (f32(3, 1 + ends, pad, LANES), f32(pad, LANES), whole, whole),
         (vmem(pad, tiles * LANES), vmem(tiles * pad, LANES), vmem(16, tiles * LANES)) + products,
         flops=2_000_000_000,
-    )(
-        matrices, m, got, plan.inst_rows(), plan.twice(plan.weight_lanes()), plan.panel_lanes(),
-        plan.twice(plan.window_lanes()),
-    )
-    x, near, side, c0, c1 = call(
-        bind(first_half, plan), (whole, f32(pad, slab + LANES)) + edges(pad),
-        products + (vmem(pad, 2 * slab), vmem(pad, 2 * slab), vmem(pad, slab), vmem(pad, slab)), flops=4_000_000_000,
+    )(matrices, m, got, *tables[:4])
+    h, n0, n1 = call(
+        bind(middle_first, plan), (whole, half, half), products + (vmem(pad, 2 * slab),), flops=4_000_000_000
     )(matrices, m, force, g, low_first, high_first, side_first, c_low, c_high, seams)
+    x, near, side, c0, c1 = call(bind(outer_first, plan), (whole, f32(pad, slab + LANES)) + edges(pad))(
+        matrices, m, low_first, high_first, n0, n1, h, far_low, seams
+    )
 
     low, high = swap(near, next_chip), swap(x, next_core)
     side = beside(plan, side, alone)
     c_low, c_high = beside(plan, c0, next_chip), beside(plan, c1, next_core)
     g, far = call(bind(inner, plan), (whole, half), products, flops=2_000_000_000)(
-        matrices, m, force, x, c_low, c_high
+        matrices, m, force, x, side, c_high
     )
     far_low = swap(far, next_chip)
+    copied = (vmem(pad, 2 * slab), vmem(pad, slab), vmem(pad, slab))
     h, n0, n1, back = call(
         bind(middle, plan), (whole, half, half, f32(sectors, RATES, LANES)),
-        products + (vmem(pad, 2 * slab), vmem(pad, LANES)), flops=4_000_000_000,
+        copied + (vmem(sectors, RATES, LANES),) + products
+        + (vmem(pad, 2 * slab), vmem(pad, LANES), pltpu.SemaphoreType.DMA((4,))),
+        flops=4_000_000_000, out_specs=places(4, range(4)),
     )(
         matrices, m, force, x, g, low, high, side, c_low, c_high, low_first, high_first, side_first, seams, weight,
-        plan.twice(plan.window_lanes().T),
+        tables[4],
     )
     returned = lax.all_to_all(back, "sector", 0, 0, tiled=True)
     sens = call(bind(collect_panels, plan), f32(fields, plan.width, insts), (vmem(insts * RATES, LANES),))(returned)
-    out = call(bind(outer, plan), f32(plan.tf * cells, LANES))(
-        matrices, m, low_first, high_first, n0, n1, h, far_low, high
-    )
+    out = call(
+        bind(outer, plan), f32(plan.tf * cells, LANES),
+        (vmem(pad, slab), vmem(pad, slab), vmem(pad, 2 * slab), pltpu.SemaphoreType.DMA((3,))),
+        in_specs=places(9, (4, 5, 6)),
+    )(matrices, m, low_first, high_first, n0, n1, h, far_low, high)
     sens = jnp.transpose(sens.reshape(fields, plan.panels, plan.rows, insts), (3, 0, 1, 2))
     return out.reshape(rhs.shape), sens
 

time: 69.8 us -> 71.8 us (1.029)
  Pallas kernels: 13.4 us -> 19.2 us
  waiting for transfers between devices: 14.2 us -> 8.45 us
  starting transfers between devices: 28.5 us -> 31.3 us
  local copies, waits for them, and re-layouts: 12.2 us -> 11 us
    all_to_all x1, waiting for transfers between devices: 6.19 us -> 0.01 us  [on_device(): got = lax.all_to_all(sent, AXES, 0, 0, tiled=True)]
    pallas_call x4 -> x5, Pallas kernels: 5.66 us -> 9.94 us  [the longest x1 3.31 us: on_device(): call(bind(middle_first, plan), (whole, half, half), products + (vmem(pad,...]
    all_to_all x1, starting transfers between devices: 2.73 us -> 6.97 us  [on_device(): got = lax.all_to_all(sent, AXES, 0, 0, tiled=True)]
    ppermute x6, starting transfers between devices: 7.44 us -> 5.89 us  [beside(): return lax.ppermute(array, AXES, pairs(0))]
    pallas_call x1, Pallas kernels: 2.88 us -> 4.43 us  [on_device(): call(bind(middle, plan), (whole, half, half, f32(sectors, RATES, LANES)),...]
    unnamed x56 -> x58, local copies, waits for them, and re-layouts: 12 us -> 10.8 us
    ppermute x6, waiting for transfers between devices: 5.61 us -> 6.39 us  [beside(): return lax.ppermute(array, AXES, pairs(0))]
    ppermute x5 -> x6, starting transfers between devices: 14.8 us -> 14.9 us  [swap(): return lax.ppermute(array, 'sector', list(enumerate(partner)))]
  transfers between devices with their start and end apart: 13 -> 14, of which waited for: 3 -> 4; matrix products, arithmetic and copies ran while one was open for 0% -> 0% of each run, Pallas kernels for 14% -> 23%
where the time goes in v1:
time: 71.8 us; the launch traced here: 70.9 us
  starting transfers between devices  31.3 us (44%)
  Pallas kernels  19.2 us (27%)
  local copies, waits for them, and re-layouts  11 us (15%)
  waiting for transfers between devices  8.45 us (12%)
  between operations  0.94 us (1%)
    ppermute x6, starting transfers between devices, swap(): return lax.ppermute(array, 'sector', list(enumerate(partner)))  14.9 us
    unnamed x58, local copies, waits for them, and re-layouts  10.8 us
    all_to_all x1, starting transfers between devices, on_device(): got = lax.all_to_all(sent, AXES, 0, 0, tiled=True)  6.97 us
    ppermute x6, waiting for transfers between devices, beside(): return lax.ppermute(array, AXES, pairs(0))  6.39 us
    ppermute x6, starting transfers between devices, beside(): return lax.ppermute(array, AXES, pairs(0))  5.89 us
    pallas_call x1, Pallas kernels, on_device(): call(bind(middle, plan), (whole, half, half, f32(sectors, RATES, LANES)),...  4.43 us
    all_to_all x1, starting transfers between devices, on_device(): returned = lax.all_to_all(back, 'sector', 0, 0, tiled=True)  3.5 us
    pallas_call x1, Pallas kernels, on_device(): call(bind(middle_first, plan), (whole, half, half), products + (vmem(pad,...  3.31 us
  transfers between devices with their start and end apart: 14, of which 4 were waited for; matrix products, arithmetic and copies ran while one was open for 0% of the time, Pallas kernels for 23%

profile of v1, /device:TPU:0, one launch (start us, length us, event | category | flops | bytes accessed | tf_op | source)
XLA Modules:
  0.0 70.9 jit_solution(17544990207856830660)
XLA Ops:
  1.3 1.1 %copy-done = f32[11,7,2,8,128]{4,3,2,1,0:T(8,128)S(1)} copy-done((f32[11,7,2,8,128]{4,3,2,1,0:T(8,128)S(1)}, f32[11,7,2,8,128]{4,3,2,1,0:T(8,128)}, u32[]{:S(2)}) %copy-start) | copy-done | bytes 630808
  4.5 1.2 %shard_map.194 = (f32[88,2048]{1,0:T(8,128)S(1)}, f32[88,1024]{1,0:T(8,128)S(1)}, f32[1,88,512]{2,1,0:T(8,128)S(1)}, f32[1,88,128]{2,1,0:T(8,128)}, f32[1,88,128]{2,1,0:T(8,128)S(1)}) custom-call(f32[1232,128]{1,0:T(8,128)S(1)} %bitcast.14, f32[16,128]{1,0:T(8,128)S(1)} %bitcast.17, f32[3,16,128]{2,1,0:T(8,128)S(1)} %bitcast.16, f32[16,128]{1,0:T(8,128)S(1)} %bitcast.18, ...), custom_call_target="tpu_custom_call" | custom-call | flops 2000000 | bytes 1000000 | tf_op jit(solution)/shard_map/pallas_call | solution.py:696
  7.1 0.9 %shard_map.196 = f32[32,16,128]{2,1,0:T(8,128)} custom-call(f32[7,32,11]{2,1,0:T(8,128)S(1)} %bitcast.15, s32[11,16]{1,0:T(8,128)S(1)} %copy.23.owner_ref, f32[11,16]{1,0:T(8,128)S(1)} %copy.24.share_ref), custom_call_target="tpu_custom_call" | custom-call | flops 2000000 | bytes 1000000 | tf_op jit(solution)/shard_map/pallas_call | solution.py:692
  8.1 7.0 %all-to-all-start = ((f32[32,16,128]{2,1,0:T(8,128)}), f32[32,16,128]{2,1,0:T(8,128)S(1)}, u32[]{:S(2)}, u32[]{:S(2)}) async-start(f32[32,16,128]{2,1,0:T(8,128)} %shard_map.196), calls=%async_computation | async-start | bytes 524288 | tf_op jit(solution)/shard_map/all_to_all | solution.py:695
  15.0 1.8 %collective-permute-start = (f32[1,88,512]{2,1,0:T(8,128)S(1)}, f32[1,88,512]{2,1,0:T(8,128)S(1)}, u32[]{:S(2)}, u32[]{:S(2)}) collective-permute-start(f32[1,88,512]{2,1,0:T(8,128)S(1)} %get-tuple-element.33), channel_id=1, source_target_pairs={{0,1},{1,0},{2,3},{3,2},{4,5},{5,4},{6,7},{7,6},{8,9},{9,8},{10,11... | collective-permute-start | bytes 540680 | tf_op jit(solution)/shard_map/ppermute | solution.py:673
  16.9 3.7 %collective-permute-start.2 = (f32[88,1024]{1,0:T(8,128)S(1)}, f32[88,1024]{1,0:T(8,128)S(1)}, u32[]{:S(2)}, u32[]{:S(2)}) collective-permute-start(f32[88,1024]{1,0:T(8,128)S(1)} %get-tuple-element.36), channel_id=1, source_target_pairs={{0,30},{2,4},{4,2},{6,8},{8,6},{10,12},{12,10},{14,16},{16,14},{18... | collective-permute-start | bytes 1081352 | tf_op jit(solution)/shard_map/ppermute | solution.py:659
  20.6 1.7 %collective-permute-start.4 = (f32[1,88,128]{2,1,0:T(8,128)}, f32[1,88,128]{2,1,0:T(8,128)}, u32[]{:S(2)}, u32[]{:S(2)}) collective-permute-start(f32[1,88,128]{2,1,0:T(8,128)} %get-tuple-element.43), channel_id=1, source_target_pairs={{0,31},{1,30},{2,5},{3,4},{4,3},{5,2},{6,9},{7,8},{8,7},{9,6},{10,... | collective-permute-start | bytes 135176 | tf_op jit(solution)/shard_map/ppermute | solution.py:673
  22.3 2.6 %collective-permute-done.1.c_high = f32[1,88,128]{2,1,0:T(8,128)S(1)} collective-permute-done((f32[1,88,128]{2,1,0:T(8,128)S(1)}, f32[1,88,128]{2,1,0:T(8,128)S(1)}, u32[]{:S(2)}, u32[]{:S(2)}) %collective-permute-start.1) | collective-permute-done | bytes 45088 | tf_op jit(solution)/shard_map/ppermute | solution.py:673
  25.1 1.8 %shard_map.195 = (bf16[560,240]{1,0:T(8,128)(2,1)S(1)}, f32[80,1024]{1,0:T(8,128)}, f32[80,16]{1,0:T(8,128)S(1)}, bf16[256,128]{1,0:T(8,128)(2,1)S(1)}, f32[1,12...) custom-call(f32[88,2048]{1,0:T(8,128)S(1)} %get-tuple-element.32.m_ref, ...), custom_call_target="tpu_custom_call" | custom-call | flops 2000000 | bytes 1000000 | tf_op jit(solution)/shard_map/pallas_call | solution.py:714
  28.1 4.7 %collective-permute-start.5 = (f32[80,1024]{1,0:T(8,128)}, f32[80,1024]{1,0:T(8,128)S(1)}, u32[]{:S(2)}, u32[]{:S(2)}) collective-permute-start(f32[80,1024]{1,0:T(8,128)} %get-tuple-element.48), channel_id=1, source_target_pairs={{0,30},{2,4},{4,2},{6,8},{8,6},{10,12},{12,10},{14,16},{16,14},{18... | collective-permute-start | bytes 983048 | tf_op jit(solution)/shard_map/ppermute | solution.py:659
  34.4 1.7 %shard_map.197 = (f32[3,2,80,128]{3,2,1,0:T(8,128)S(1)}, f32[80,128]{1,0:T(8,128)S(1)}, f32[80,2048]{1,0:T(8,128)S(1)}, f32[80,2048]{1,0:T(8,128)S(1)}) custom-call(bf16[560,240]{1,0:T(8,128)(2,1)S(1)} %get-tuple-element.35.w_ref, f32[88,2048]{1,0:T(8,128)S(1)} %get-tuple-element.32.m_ref, f32[32,16,128]{2,1,0:T(8,128)S(1)} %all-to-all-done.got_ref, ...), custom_call_target="tpu_custom_call" | custom-call | flops 2000000000 | bytes 1000000 | tf_op jit(solution)/shard_map/pallas_call | solution.py:721
  36.2 3.3 %shard_map.198 = (f32[80,2048]{1,0:T(8,128)S(1)}, f32[80,1024]{1,0:T(8,128)S(1)}, f32[80,1024]{1,0:T(8,128)S(1)}) custom-call(bf16[560,240]{1,0:T(8,128)(2,1)S(1)} %get-tuple-element.35.w_ref, f32[88,2048]{1,0:T(8,128)S(1)} %get-tuple-element.32.m_ref, f32[80,2048]{1,0:T(8,128)S(1)} %get-tuple-element.41.f_ref, f32[80,2048]{1,0:T(8,128)S(1)} %get-tuple-element.42.g_ref, ...), custom_call_target="tpu_custom_call" | custom-call | flops 4000000000 | bytes 1000000 | tf_op jit(solution)/shard_map/pallas_call | solution.py:726
  40.3 3.5 %collective-permute-start.8 = (f32[80,1152]{1,0:T(8,128)S(1)}, f32[80,1152]{1,0:T(8,128)S(1)}, u32[]{:S(2)}, u32[]{:S(2)}) collective-permute-start(f32[80,1152]{1,0:T(8,128)S(1)} %get-tuple-element.53), channel_id=1, source_target_pairs={{0,30},{2,4},{4,2},{6,8},{8,6},{10,12},{12,10},{14,16},{16,14},{18... | collective-permute-start | bytes 1105928 | tf_op jit(solution)/shard_map/ppermute | solution.py:659
  43.9 2.3 %collective-permute-start.10 = (f32[1,80,128]{2,1,0:T(8,128)S(1)}, f32[1,80,128]{2,1,0:T(8,128)S(1)}, u32[]{:S(2)}, u32[]{:S(2)}) collective-permute-start(f32[1,80,128]{2,1,0:T(8,128)S(1)} %get-tuple-element.54), channel_id=1, source_target_pairs={{0,31},{1,30},{2,5},{3,4},{4,3},{5,2},{6,9},{7,8},{8,7},{9,6},{10,... | collective-permute-start | bytes 122888 | tf_op jit(solution)/shard_map/ppermute | solution.py:673
  46.2 2.0 %collective-permute-done.7.c_high = f32[1,80,128]{2,1,0:T(8,128)S(1)} collective-permute-done((f32[1,80,128]{2,1,0:T(8,128)S(1)}, f32[1,80,128]{2,1,0:T(8,128)S(1)}, u32[]{:S(2)}, u32[]{:S(2)}) %collective-permute-start.7) | collective-permute-done | bytes 40992 | tf_op jit(solution)/shard_map/ppermute | solution.py:673
  48.3 1.7 %collective-permute-done.6.side_ref = f32[1,80,512]{2,1,0:T(8,128)S(1)} collective-permute-done((f32[1,80,512]{2,1,0:T(8,128)S(1)}, f32[1,80,512]{2,1,0:T(8,128)S(1)}, u32[]{:S(2)}, u32[]{:S(2)}) %collective-permute-start.6) | collective-permute-done | bytes 163872 | tf_op jit(solution)/shard_map/ppermute | solution.py:673
  50.0 1.5 %shard_map.200 = (f32[80,2048]{1,0:T(8,128)S(1)}, f32[80,1024]{1,0:T(8,128)}) custom-call(bf16[560,240]{1,0:T(8,128)(2,1)S(1)} %get-tuple-element.35.w_ref, f32[88,2048]{1,0:T(8,128)S(1)} %get-tuple-element.32.m_ref, f32[80,2048]{1,0:T(8,128)S(1)} %get-tuple-element.41.f_ref, f32[80,2048]{1,0:T(8,128)S(1)} %get-tuple-element.49.x_ref, ...), custom_call_target="tpu_custom_call" | custom-call | flops 2000000000 | bytes 1000000 | tf_op jit(solution)/shard_map/pallas_call | solution.py:736
  51.5 2.4 %collective-permute-start.11 = (f32[80,1024]{1,0:T(8,128)}, f32[80,1024]{1,0:T(8,128)}, u32[]{:S(2)}, u32[]{:S(2)}) collective-permute-start(f32[80,1024]{1,0:T(8,128)} %get-tuple-element.60), channel_id=1, source_target_pairs={{0,30},{2,4},{4,2},{6,8},{8,6},{10,12},{12,10},{14,16},{16,14},{18... | collective-permute-start | bytes 983048 | tf_op jit(solution)/shard_map/ppermute | solution.py:659
  53.9 4.4 %shard_map.201 = (f32[80,2048]{1,0:T(8,128)S(1)}, f32[80,1024]{1,0:T(8,128)S(1)}, f32[80,1024]{1,0:T(8,128)S(1)}, f32[16,8,128]{2,1,0:T(8,128)}) custom-call(bf16[560,240]{1,0:T(8,128)(2,1)S(1)} %get-tuple-element.35.w_ref, f32[88,2048]{1,0:T(8,128)S(1)} %get-tuple-element.32.m_ref, f32[80,2048]{1,0:T(8,128)S(1)} %get-tuple-element.41.f_ref, ...), custom_call_target="tpu_custom_call" | custom-call | flops 4000000000 | bytes 1000000 | tf_op jit(solution)/shard_map/pallas_call | solution.py:741
  59.8 3.5 %all-to-all-start.1 = ((f32[16,8,128]{2,1,0:T(8,128)}), f32[16,8,128]{2,1,0:T(8,128)S(1)}, u32[]{:S(2)}, u32[]{:S(2)}) async-start(f32[16,8,128]{2,1,0:T(8,128)} %get-tuple-element.61), calls=%async_computation.1 | async-start | bytes 131072 | tf_op jit(solution)/shard_map/all_to_all | solution.py:750
  63.3 1.0 %copy-done.2 = f32[80,1024]{1,0:T(8,128)S(1)} copy-done((f32[80,1024]{1,0:T(8,128)S(1)}, f32[80,1024]{1,0:T(8,128)}, u32[]{:S(2)}) %copy-start.2) | copy-done | bytes 327704
  64.3 1.0 %copy-done.4 = f32[80,1024]{1,0:T(8,128)S(1)} copy-done((f32[80,1024]{1,0:T(8,128)S(1)}, f32[80,1024]{1,0:T(8,128)}, u32[]{:S(2)}) %copy-start.4) | copy-done | bytes 327704
  65.3 2.9 %shard_map.202 = f32[1232,128]{1,0:T(8,128)} custom-call(bf16[560,240]{1,0:T(8,128)(2,1)S(1)} %get-tuple-element.35.w_ref, f32[88,2048]{1,0:T(8,128)S(1)} %get-tuple-element.32.m_ref, f32[88,1024]{1,0:T(8,128)S(1)} %collective-permute-done.2.low_ref.low_first, f32[88,2048]{1,0:T(8,128)S(1)} %collective-permute-done.3.high_ref.high_first, ...), custom_call_target="tpu_custom_call" | custom-call | flops 2000000 | bytes 1000000 | tf_op jit(solution)/shard_map/pallas_call | solution.py:752
  68.1 2.0 %all-to-all-done.1.got_ref = f32[16,8,128]{2,1,0:T(8,128)S(1)} async-done(((f32[16,8,128]{2,1,0:T(8,128)}), f32[16,8,128]{2,1,0:T(8,128)S(1)}, u32[]{:S(2)}, u32[]{:S(2)}) %all-to-all-start.1) | async-done | bytes 65568 | tf_op jit(solution)/shard_map/all_to_all | solution.py:750
  (74 shorter events, 10.1 us)
Async XLA Ops:
  5.8 30.4 %collective-permute-start.3 = (f32[88,2048]{1,0:T(8,128)S(1)}, f32[88,2048]{1,0:T(8,128)S(1)}, u32[]{:S(2)}, u32[]{:S(2)}) collective-permute-start(f32[88,2048]{1,0:T(8,128)S(1)} %get-tuple-element.32.m_ref), channel_id=1, source_target_pairs={{0,2},{2,0},{4,6},{6,4},{8,10},{10,8},{12,14},{14,12},{16,18},{18,... | collective-permute-start | bytes 2162696 | tf_op jit(solution)/shard_map/ppermute | solution.py:659
  8.0 17.0 %copy-start.8 = (f32[80,240]{1,0:T(8,128)S(1)}, f32[80,240]{1,0:T(8,128)}, u32[]{:S(2)}) copy-start(f32[80,240]{1,0:T(8,128)} %constant.21.clone.diagonal_ref) | copy-start | bytes 230404
  8.0 17.0 %copy-start.9 = (bf16[256,128]{1,0:T(8,128)(2,1)S(1)}, bf16[256,128]{1,0:T(8,128)(2,1)}, u32[]{:S(2)}) copy-start(bf16[256,128]{1,0:T(8,128)(2,1)} %constant.26.clone.refs_4_) | copy-start | bytes 196612
  8.0 17.0 %copy-start.10 = (bf16[256,128]{1,0:T(8,128)(2,1)S(1)}, bf16[256,128]{1,0:T(8,128)(2,1)}, u32[]{:S(2)}) copy-start(bf16[256,128]{1,0:T(8,128)(2,1)} %constant.25.clone.refs_3_) | copy-start | bytes 196612
  8.0 17.0 %copy-start.11 = (bf16[256,128]{1,0:T(8,128)(2,1)S(1)}, bf16[256,128]{1,0:T(8,128)(2,1)}, u32[]{:S(2)}) copy-start(bf16[256,128]{1,0:T(8,128)(2,1)} %constant.23.clone.refs_1_) | copy-start | bytes 196612
  8.0 17.0 %copy-start.12 = (f32[80,16]{1,0:T(8,128)S(1)}, f32[80,16]{1,0:T(8,128)}, u32[]{:S(2)}) copy-start(f32[80,16]{1,0:T(8,128)} %constant.22.clone.refs_0_) | copy-start | bytes 15364
  8.0 17.0 %copy-start.13 = (f32[80,7]{1,0:T(8,128)S(1)}, f32[80,7]{1,0:T(8,128)}, u32[]{:S(2)}) copy-start(f32[80,7]{1,0:T(8,128)} %constant.19.clone.rows_ref) | copy-start | bytes 6724
  8.0 17.0 %copy-start.14 = (bf16[80,240]{1,0:T(8,128)(2,1)S(1)}, bf16[80,240]{1,0:T(8,128)(2,1)}, u32[]{:S(2)}) copy-start(bf16[80,240]{1,0:T(8,128)(2,1)} %constant.18.clone.spectral_ref) | copy-start | bytes 115204
  8.0 17.0 %copy-start.16 = (f32[3,7,7]{2,1,0:T(8,128)S(1)}, f32[3,7,7]{2,1,0:T(8,128)}, u32[]{:S(2)}) copy-start(f32[3,7,7]{2,1,0:T(8,128)} %up_ref.1) | copy-start | bytes 1768
  8.0 17.0 %copy-start.17 = (f32[3,7,7]{2,1,0:T(8,128)S(1)}, f32[3,7,7]{2,1,0:T(8,128)}, u32[]{:S(2)}) copy-start(f32[3,7,7]{2,1,0:T(8,128)} %down_ref.1) | copy-start | bytes 1768
  8.1 17.0 %copy-start.21 = (f32[7,240]{1,0:T(8,128)S(1)}, f32[7,240]{1,0:T(8,128)}, u32[]{:S(2)}) copy-start(f32[7,240]{1,0:T(8,128)} %constant.20.clone.lanes_ref) | copy-start | bytes 20164
  8.1 24.7 %all-to-all-start = ((f32[32,16,128]{2,1,0:T(8,128)}), f32[32,16,128]{2,1,0:T(8,128)S(1)}, u32[]{:S(2)}, u32[]{:S(2)}) async-start(f32[32,16,128]{2,1,0:T(8,128)} %shard_map.196), calls=%async_computation | async-start | bytes 524288 | tf_op jit(solution)/shard_map/all_to_all | solution.py:695
  15.0 9.9 %collective-permute-start = (f32[1,88,512]{2,1,0:T(8,128)S(1)}, f32[1,88,512]{2,1,0:T(8,128)S(1)}, u32[]{:S(2)}, u32[]{:S(2)}) collective-permute-start(f32[1,88,512]{2,1,0:T(8,128)S(1)} %get-tuple-element.33), channel_id=1, source_target_pairs={{0,1},{1,0},{2,3},{3,2},{4,5},{5,4},{6,7},{7,6},{8,9},{9,8},{10,11... | collective-permute-start | bytes 540680 | tf_op jit(solution)/shard_map/ppermute | solution.py:673
  16.9 19.2 %collective-permute-start.2 = (f32[88,1024]{1,0:T(8,128)S(1)}, f32[88,1024]{1,0:T(8,128)S(1)}, u32[]{:S(2)}, u32[]{:S(2)}) collective-permute-start(f32[88,1024]{1,0:T(8,128)S(1)} %get-tuple-element.36), channel_id=1, source_target_pairs={{0,30},{2,4},{4,2},{6,8},{8,6},{10,12},{12,10},{14,16},{16,14},{18... | collective-permute-start | bytes 1081352 | tf_op jit(solution)/shard_map/ppermute | solution.py:659
  20.6 4.4 %collective-permute-start.1 = (f32[1,88,128]{2,1,0:T(8,128)S(1)}, f32[1,88,128]{2,1,0:T(8,128)S(1)}, u32[]{:S(2)}, u32[]{:S(2)}) collective-permute-start(f32[1,88,128]{2,1,0:T(8,128)S(1)} %get-tuple-element.34), channel_id=1, source_target_pairs={{0,3},{1,2},{2,1},{3,0},{4,7},{5,6},{6,5},{7,4},{8,11},{9,10},{10,... | collective-permute-start | bytes 135176 | tf_op jit(solution)/shard_map/ppermute | solution.py:673
  20.6 15.5 %collective-permute-start.4 = (f32[1,88,128]{2,1,0:T(8,128)}, f32[1,88,128]{2,1,0:T(8,128)}, u32[]{:S(2)}, u32[]{:S(2)}) collective-permute-start(f32[1,88,128]{2,1,0:T(8,128)} %get-tuple-element.43), channel_id=1, source_target_pairs={{0,31},{1,30},{2,5},{3,4},{4,3},{5,2},{6,9},{7,8},{8,7},{9,6},{10,... | collective-permute-start | bytes 135176 | tf_op jit(solution)/shard_map/ppermute | solution.py:673
  28.1 11.4 %collective-permute-start.5 = (f32[80,1024]{1,0:T(8,128)}, f32[80,1024]{1,0:T(8,128)S(1)}, u32[]{:S(2)}, u32[]{:S(2)}) collective-permute-start(f32[80,1024]{1,0:T(8,128)} %get-tuple-element.48), channel_id=1, source_target_pairs={{0,30},{2,4},{4,2},{6,8},{8,6},{10,12},{12,10},{14,16},{16,14},{18... | collective-permute-start | bytes 983048 | tf_op jit(solution)/shard_map/ppermute | solution.py:659
  40.3 13.6 %collective-permute-start.9 = (f32[80,2048]{1,0:T(8,128)S(1)}, f32[80,2048]{1,0:T(8,128)S(1)}, u32[]{:S(2)}, u32[]{:S(2)}) collective-permute-start(f32[80,2048]{1,0:T(8,128)S(1)} %get-tuple-element.49.x_ref), channel_id=1, source_target_pairs={{0,2},{2,0},{4,6},{6,4},{8,10},{10,8},{12,14},{14,12},{16,18},{18,... | collective-permute-start | bytes 1966088 | tf_op jit(solution)/shard_map/ppermute | solution.py:659
  40.3 13.5 %collective-permute-start.8 = (f32[80,1152]{1,0:T(8,128)S(1)}, f32[80,1152]{1,0:T(8,128)S(1)}, u32[]{:S(2)}, u32[]{:S(2)}) collective-permute-start(f32[80,1152]{1,0:T(8,128)S(1)} %get-tuple-element.53), channel_id=1, source_target_pairs={{0,30},{2,4},{4,2},{6,8},{8,6},{10,12},{12,10},{14,16},{16,14},{18... | collective-permute-start | bytes 1105928 | tf_op jit(solution)/shard_map/ppermute | solution.py:659
  43.9 6.1 %collective-permute-start.6 = (f32[1,80,512]{2,1,0:T(8,128)S(1)}, f32[1,80,512]{2,1,0:T(8,128)S(1)}, u32[]{:S(2)}, u32[]{:S(2)}) collective-permute-start(f32[1,80,512]{2,1,0:T(8,128)S(1)} %get-tuple-element.50), channel_id=1, source_target_pairs={{0,1},{1,0},{2,3},{3,2},{4,5},{5,4},{6,7},{7,6},{8,9},{9,8},{10,11... | collective-permute-start | bytes 491528 | tf_op jit(solution)/shard_map/ppermute | solution.py:673
  43.9 4.4 %collective-permute-start.7 = (f32[1,80,128]{2,1,0:T(8,128)S(1)}, f32[1,80,128]{2,1,0:T(8,128)S(1)}, u32[]{:S(2)}, u32[]{:S(2)}) collective-permute-start(f32[1,80,128]{2,1,0:T(8,128)S(1)} %get-tuple-element.51), channel_id=1, source_target_pairs={{0,3},{1,2},{2,1},{3,0},{4,7},{5,6},{6,5},{7,4},{8,11},{9,10},{10,... | collective-permute-start | bytes 122888 | tf_op jit(solution)/shard_map/ppermute | solution.py:673
  43.9 10.0 %collective-permute-start.10 = (f32[1,80,128]{2,1,0:T(8,128)S(1)}, f32[1,80,128]{2,1,0:T(8,128)S(1)}, u32[]{:S(2)}, u32[]{:S(2)}) collective-permute-start(f32[1,80,128]{2,1,0:T(8,128)S(1)} %get-tuple-element.54), channel_id=1, source_target_pairs={{0,31},{1,30},{2,5},{3,4},{4,3},{5,2},{6,9},{7,8},{8,7},{9,6},{10,... | collective-permute-start | bytes 122888 | tf_op jit(solution)/shard_map/ppermute | solution.py:673
  51.5 11.9 %collective-permute-start.11 = (f32[80,1024]{1,0:T(8,128)}, f32[80,1024]{1,0:T(8,128)}, u32[]{:S(2)}, u32[]{:S(2)}) collective-permute-start(f32[80,1024]{1,0:T(8,128)} %get-tuple-element.60), channel_id=1, source_target_pairs={{0,30},{2,4},{4,2},{6,8},{8,6},{10,12},{12,10},{14,16},{16,14},{18... | collective-permute-start | bytes 983048 | tf_op jit(solution)/shard_map/ppermute | solution.py:659
  59.8 10.4 %all-to-all-start.1 = ((f32[16,8,128]{2,1,0:T(8,128)}), f32[16,8,128]{2,1,0:T(8,128)S(1)}, u32[]{:S(2)}, u32[]{:S(2)}) async-start(f32[16,8,128]{2,1,0:T(8,128)} %get-tuple-element.61), calls=%async_computation.1 | async-start | bytes 131072 | tf_op jit(solution)/shard_map/all_to_all | solution.py:750
  (19 other events, 40.7 us)

commit v2 on v0

--- a/solution.py
+++ b/solution.py
@@ -74,37 +74,36 @@
         same = (block[:, None] == block[None, :]) & (block[:, None] >= 0)
         return np.tile(same.astype(np.float32), (1, 3))
 
+
     def inst_rows(self):
-        out = np.zeros((self.pad, 16), np.float32)
-        out[np.arange(self.tf), np.arange(self.tf) // self.fields] = 1.0
-        return out
-
-    def cell_lanes(self):
-        out = np.zeros((self.ct, self.rows, self.ct, self.panels, self.rows), np.float32)
-        for a in range(self.ct):
-            for r in range(self.rows):
-                out[a, r, a, :, r] = 1.0
-        out = out.reshape(self.cells, -1)
-        return np.pad(out, ((0, 0), (0, LANES - out.shape[1])))
+        row, inst = table_index(self.pad, 16)
+        return ((row >= inst * self.fields) & (row < (inst + 1) * self.fields)).astype(jnp.float32)
+
+    def cell_of(self, lane):
+        return lax.div(lane, self.width) * self.rows + lax.rem(lane, self.rows)
 
     def window_lanes(self):
-        out = np.zeros((LANES, LANES), np.float32)
-        out[:, ::WINDOW] = self.cell_lanes().T
-        return out
-
-    def twice(self, table):
-        return np.concatenate([table, table]).astype(ml_dtypes.bfloat16)
+        lane, to = table_index(LANES, LANES)
+        return (lane < self.ct * self.width) & (to == self.cell_of(lane) * WINDOW)
+
+    def window_spread(self):
+        to, lane = table_index(LANES, LANES)
+        return (lane < self.ct * self.width) & (to == self.cell_of(lane) * WINDOW)
 
     def weight_lanes(self):
-        out = np.zeros((LANES, LANES), np.float32)
+        cell, lane = table_index(LANES, LANES)
         half = self.ct * self.width
-        out[: self.cells, :half] = self.cell_lanes()[:, :half]
-        out[self.cells : 2 * self.cells, half:] = self.cell_lanes()[:, :half]
-        return out
+        wanted = jnp.where(lane < half, self.cell_of(lane), self.cells + self.cell_of(lane - half))
+        return cell == wanted
 
     def panel_lanes(self):
-        lane = np.arange(LANES)
-        return np.where(lane < self.ct * self.width, (lane // self.rows) % self.panels, -9).astype(np.float32)[None]
+        lane = lane_index(1)
+        panel = lax.rem(lax.div(lane, self.rows), self.panels)
+        return jnp.where(lane < self.ct * self.width, panel, -9).astype(jnp.float32)
+
+
+def table_index(rows, columns):
+    return [lax.broadcasted_iota(jnp.int32, (rows, columns), axis) for axis in (0, 1)]
 
 
 def call(kernel, out, scratch=(), flops=2_000_000, nbytes=1_000_000):
@@ -112,7 +111,7 @@
         kernel,
         out_shape=out,
         scratch_shapes=list(scratch),
-        compiler_params=pltpu.CompilerParams(vmem_limit_bytes=40 * 1024 * 1024),
+        compiler_params=pltpu.CompilerParams(vmem_limit_bytes=20 * 1024 * 1024),
         cost_estimate=pl.CostEstimate(flops=flops, bytes_accessed=nbytes, transcendentals=0),
     )
 
@@ -135,8 +134,10 @@
     return jnp.dot(w, jnp.concatenate([hi, hi, lo], axis=0), preferred_element_type=jnp.float32)
 
 
-def pick(x, table2):
-    return jnp.dot(jnp.concatenate(halves_of(x), axis=1), table2, preferred_element_type=jnp.float32)
+def pick(x, table):
+    table = table.astype(jnp.float32).astype(jnp.bfloat16)
+    table = jnp.concatenate([table, table], axis=0)
+    return jnp.dot(jnp.concatenate(halves_of(x), axis=1), table, preferred_element_type=jnp.float32)
 
 
 def dot_full(a, b):
@@ -301,9 +302,10 @@
             h_ref[:, lanes] -= own[a].rate(C_SP, last[n]) * edge_new[n][:, at(a)]
 
 
-def outer_rows(plan, w_ref, own, near, far_chunks, n_refs, h_ref, put):
+def outer_rows(plan, w_ref, own, near, far_chunks, n_refs, h_ref, put, layers=(0, 1)):
     count = CHUNK // LANES
-    for a, block in enumerate((DOWN_AZ, UP_AZ)):
+    for a in layers:
+        block = (DOWN_AZ, UP_AZ)[a]
 
         def near_chunk(c):
             terms = dot3(matrix(plan, w_ref, block), far_chunks[a](c))
@@ -361,7 +363,7 @@
     return corner
 
 
-def prepare(plan, rhs_ref, diag_ref, face_ref, time_ref, mask_ref, m_ref, side_ref, c0_ref, c1_ref):
+def prepare(plan, rhs_ref, coef_ref, m_ref, side_ref, c0_ref, c1_ref):
     pad = plan.pad
     lane = lane_index(1)
     tail = jnp.zeros((pad - plan.tf, LANES), jnp.float32)
@@ -369,11 +371,11 @@
     for cell in range(plan.cells):
         a, r = divmod(cell, plan.rows)
         there = jnp.where(mirror == 0, a, plan.ct - 1 - a) * plan.rows + r
-        one = pl.ds(there, 1)
-        scale = mask_ref[one, :].astype(jnp.float32) / diag_ref[one, :]
-        axial = scale * face_ref[2, one, :]
+        mask, diag, time, *face = [coef_ref[pl.ds(there + plan.cells * i, 1), :] for i in range(6)]
+        scale = mask / diag
+        axial = scale * face[2]
         rates = [
-            scale * time_ref[one, :], scale * face_ref[0, one, :], scale * face_ref[1, one, :],
+            scale * time, scale * face[0], scale * face[1],
             jnp.where(lane < LANES - 1, axial, 0.0), jnp.where(lane > 0, axial, 0.0), scale,
             jnp.zeros((RATES - 6, LANES), jnp.float32),
         ]
@@ -395,7 +397,7 @@
                     c_refs[a][n] = end
 
 
-def stack_matrices(plan, up_ref, down_ref, spectral_ref, rows_ref, lanes_ref, diagonal_ref, out_ref):
+def stack_matrices(plan, up_ref, down_ref, spectral_ref, rows_ref, lanes_ref, diagonal_ref, out_ref, down_out):
     pad = plan.pad
     lane = lax.broadcasted_iota(jnp.int32, (pad, 3 * pad), 1)
     second = (lane >= pad) & (lane < 2 * pad)
@@ -408,14 +410,15 @@
         full = dot_full(dot_full(rows_ref[...], small), lanes_ref[...]) * diagonal_ref[...]
         hi = full.astype(jnp.bfloat16).astype(jnp.float32)
         out_ref[block * pad : (block + 1) * pad, :] = jnp.where(second, full - hi, hi).astype(jnp.bfloat16)
-
-
-def send_panels(plan, stator_ref, owner_ref, share_ref, out_ref, panels_ref):
+    down_out[...] = matrix(plan, out_ref, DOWN_AZ)
+
+
+def send_panels(plan, stator_ref, both_ref, out_ref, panels_ref):
     me = lax.axis_index("sector")
     for f in range(plan.fields):
         panels_ref[pl.ds(f, plan.insts, stride=RATES), : plan.width] = jnp.transpose(stator_ref[f])
     out_ref[...] = jnp.zeros_like(out_ref)
-    both = jnp.concatenate([lax.rem(owner_ref[...], plan.panels).astype(jnp.float32), share_ref[...]], axis=1)
+    both = both_ref[...]
     for t in range(plan.insts):
         group, row = divmod(t, GROUP)
         lanes = slice(group * 2 * plan.cells, (group + 1) * 2 * plan.cells)
@@ -431,7 +434,7 @@
 
 
 def begin(
-    plan, w_ref, m_ref, got_ref, inst_rows, weight_table, panel_lanes, sum_table,
+    plan, w_ref, m_ref, got_ref,
     seams_ref, weight_ref, x_ref, g_ref, panels_ref, terms_ref, rows_ref, p0_ref, p1_ref,
 ):
     pad, insts, fields = plan.pad, plan.insts, plan.fields
@@ -452,16 +455,16 @@
         for group in range(-(-insts // GROUP)):
             shifted = rolled(table, -group * wide)
             rows_ref[group * GROUP : (group + 1) * GROUP, n * LANES : n * LANES + wide] = shifted[:GROUP, :wide]
-    spread = dot_full(inst_rows[...], rows_ref[...])
-    spread = pick(jnp.concatenate([spread[:, at(n)] for n in range(len(tiles))], axis=0), weight_table[...])
-    first, share, panel = spread, rolled(spread, plan.ct * plan.width), panel_lanes[...]
+    spread = dot_full(plan.inst_rows(), rows_ref[...])
+    spread = pick(jnp.concatenate([spread[:, at(n)] for n in range(len(tiles))], axis=0), plan.weight_lanes())
+    first, share, panel = spread, rolled(spread, plan.ct * plan.width), plan.panel_lanes()
     lower = (jnp.abs(first - panel) < 0.5).astype(jnp.float32)
     upper = (jnp.abs(first + 1.0 - panel) < 0.5).astype(jnp.float32)
     weights = share * lower + (1.0 - share) * upper
     for n in range(len(tiles)):
         panels = panels_ref[:, at(n)]
         terms_ref[n * pad : (n + 1) * pad, :] = panels + rolled(panels, plan.width)
-    seams = pick(terms_ref[...] * weights, sum_table[...])
+    seams = pick(terms_ref[...] * weights, plan.window_lanes())
 
     even = parity() == 0
     is_first = span == 0
@@ -522,15 +525,15 @@
     write_edges(plan, x_ref, side_out, (c0_ref, c1_ref))
 
 
-def inner(plan, w_ref, m_ref, f_ref, x_ref, c_low, c_high, g_ref, far_ref, p0_ref, p1_ref):
-    far_ref[...] = x_ref[:, plan.slab :] + 0.0 * (c_low[0, 0:1, 0:1] + c_high[0, 0:1, 0:1])
+def inner(plan, w_ref, m_ref, f_ref, x_ref, side_ref, g_ref, far_ref, p0_ref, p1_ref):
+    far_ref[...] = x_ref[:, plan.slab :] + 0.0 * side_ref[0, 0:1, 0:1]
     inner_rows(plan, w_ref, (p0_ref, p1_ref), two_layers(plan, x_ref, m_ref), two_layers(plan, f_ref, m_ref), g_ref)
 
 
 def middle(
     plan, w_ref, m_ref, f_ref, x_ref, g_ref, low_ref, high_ref, side_ref, c_low, c_high,
-    low_first, high_first, side_first, seams_ref, weight_ref, spread_table,
-    h_ref, n0_ref, n1_ref, send_ref, p0_ref, p1_ref, y_ref, inlet_ref,
+    low_first, high_first, side_first, seams_ref, weight_ref,
+    send_ref, n0_ref, h0_ref, x1_ref, rates_ref, p0_ref, p1_ref, y_ref, inlet_ref, h_ref, n1_ref,
 ):
     pad = plan.pad
     own, force = two_layers(plan, x_ref, m_ref), two_layers(plan, f_ref, m_ref)
@@ -548,6 +551,8 @@
     def put(a, r, value):
         cell = a * plan.rows + r
         inlet_ref[...] = jnp.where(lane == cell * WINDOW, rolled(value, cell * WINDOW), inlet_ref[...])
+        if a == 1:
+            x1_ref[:, at(r)] = value
 
     def far_inlet(c):
         tile = low_ref[:, plan.slab :]
@@ -557,26 +562,34 @@
     outer_rows(plan, w_ref, own, near, (far_inlet, Layer(plan, high_ref).chunk), n_refs, h_ref, put)
     inlet = inlet_ref[...]
     inlet = jnp.where(parity() == 0, inlet, rolled(inlet, LANES // 2))
-    back = pick(inlet, spread_table[...]) * weight_ref[...]
+    back = pick(inlet, plan.window_spread()) * weight_ref[...]
     back = back + rolled(back, -plan.width)
     me = lax.axis_index("sector")
     send_ref[...] = jnp.zeros_like(send_ref)
     for t in range(plan.insts):
         to = lax.rem(me + plan.shift[t], plan.sectors)
         send_ref[to, : plan.fields, : plan.width] = back[t * plan.fields : (t + 1) * plan.fields, : plan.width]
-
-
-def outer(plan, w_ref, m_ref, low_first, high_first, n0_ref, n1_ref, h_ref, low_ref, high_ref, out_ref):
+    h0_ref[...] = h_ref[:, : plan.slab]
+    for r in range(plan.rows):
+        rest = jnp.zeros((RATES - 2, LANES), jnp.float32)
+        rates_ref[:, at(r)] = jnp.concatenate([near[0].rate(C_AZ, r), own[0].rate(C_AZ, r), rest], axis=0)
+
+
+def outer(plan, w_ref, rates_ref, n0_ref, h0_ref, x1_ref, far_ref, out_ref):
     mirror = parity()
-    own = two_layers(plan, m_ref)
-    near = Layer(plan, low_first), Layer(plan, high_first, plan.slab)
 
     def put(a, r, value):
         there = jnp.where(mirror == 0, a, plan.ct - 1 - a) * plan.rows + r
         out_ref[pl.ds(there, plan.tf, stride=plan.cells), :] = value[: plan.tf]
 
-    far = Layer(plan, low_ref).chunk, Layer(plan, high_ref).chunk
-    outer_rows(plan, w_ref, own, near, far, (n0_ref, n1_ref), h_ref, put)
+    for r in range(plan.rows):
+        put(1, r, x1_ref[:, at(r)])
+
+    def near_chunk(c):
+        lanes = slice(c * CHUNK, (c + 1) * CHUNK)
+        return n0_ref[:, lanes] - rates_ref[0:1, lanes] * dot3(w_ref[...], far_ref[:, lanes])
+
+    azimuthal(plan, w_ref, 0, near_chunk, lambda r, terms: put(0, r, h0_ref[:, at(r)] - rates_ref[1:2, at(r)] * terms))
 
 
 def collect_panels(plan, got_ref, out_ref, panels_ref):
@@ -632,28 +645,32 @@
 
     stator = jnp.transpose(stator_adj, (1, 2, 3, 0)).reshape(fields, plan.width, insts)
     sent = call(bind(send_panels, plan), f32(sectors * spans, 2 * RATES, LANES), (vmem(insts * RATES, LANES),))(
-        stator, owner.reshape(insts, cells), first_panel_share.reshape(insts, cells)
+        stator,
+        jnp.concatenate([
+            lax.rem(owner, plan.panels).astype(jnp.float32).reshape(insts, cells), first_panel_share.reshape(insts, cells),
+        ], axis=1),
     )
     got = lax.all_to_all(sent, AXES, 0, 0, tiled=True)
     m, side, c0, c1 = call(bind(prepare, plan), (f32(pad + RATES, plan.ct * slab),) + edges(pad + RATES))(
-        rhs.reshape(plan.tf * cells, LANES), diag_coef.reshape(cells, LANES), face_coef.reshape(3, cells, LANES),
-        time_coef.reshape(cells, LANES), wall_mask.reshape(cells, LANES),
+        rhs.reshape(plan.tf * cells, LANES),
+        jnp.concatenate([
+            wall_mask.astype(jnp.float32).reshape(cells, LANES), diag_coef.reshape(cells, LANES),
+            time_coef.reshape(cells, LANES), face_coef.reshape(3 * cells, LANES),
+        ]),
     )
     low_first, high_first = swap(m, next_chip), swap(m, next_core)
     side_first = beside(plan, side, alone)
     c_low, c_high = beside(plan, c0, next_chip), beside(plan, c1, next_core)
-    matrices = call(
-        bind(stack_matrices, plan), jax.ShapeDtypeStruct((7 * pad, 3 * pad), jnp.bfloat16)
+    matrices, down = call(
+        bind(stack_matrices, plan),
+        [jax.ShapeDtypeStruct((count * pad, 3 * pad), jnp.bfloat16) for count in (7, 1)],
     )(jac_up, jac_down, plan.spectral(), plan.field_rows(), plan.field_lanes(), plan.block_diagonal())
     tiles = len(plan.tiles)
     seams, weight, force, g = call(
         bind(begin, plan), (f32(3, 1 + ends, pad, LANES), f32(pad, LANES), whole, whole),
         (vmem(pad, tiles * LANES), vmem(tiles * pad, LANES), vmem(16, tiles * LANES)) + products,
         flops=2_000_000_000,
-    )(
-        matrices, m, got, plan.inst_rows(), plan.twice(plan.weight_lanes()), plan.panel_lanes(),
-        plan.twice(plan.window_lanes()),
-    )
+    )(matrices, m, got)
     x, near, side, c0, c1 = call(
         bind(first_half, plan), (whole, f32(pad, slab + LANES)) + edges(pad),
         products + (vmem(pad, 2 * slab), vmem(pad, 2 * slab), vmem(pad, slab), vmem(pad, slab)), flops=4_000_000_000,
@@ -663,21 +680,18 @@
     side = beside(plan, side, alone)
     c_low, c_high = beside(plan, c0, next_chip), beside(plan, c1, next_core)
     g, far = call(bind(inner, plan), (whole, half), products, flops=2_000_000_000)(
-        matrices, m, force, x, c_low, c_high
+        matrices, m, force, x, side
     )
     far_low = swap(far, next_chip)
-    h, n0, n1, back = call(
-        bind(middle, plan), (whole, half, half, f32(sectors, RATES, LANES)),
-        products + (vmem(pad, 2 * slab), vmem(pad, LANES)), flops=4_000_000_000,
+    back, n0, h0, x1, rates = call(
+        bind(middle, plan), (f32(sectors, RATES, LANES), half, half, half, f32(RATES, slab)),
+        products + (vmem(pad, 2 * slab), vmem(pad, LANES), vmem(pad, 2 * slab), vmem(pad, slab)), flops=4_000_000_000,
     )(
-        matrices, m, force, x, g, low, high, side, c_low, c_high, low_first, high_first, side_first, seams, weight,
-        plan.twice(plan.window_lanes().T),
+        matrices, m, force, x, g, low, high, side, c_low, c_high, low_first, high_first, side_first, seams, weight
     )
     returned = lax.all_to_all(back, "sector", 0, 0, tiled=True)
     sens = call(bind(collect_panels, plan), f32(fields, plan.width, insts), (vmem(insts * RATES, LANES),))(returned)
-    out = call(bind(outer, plan), f32(plan.tf * cells, LANES))(
-        matrices, m, low_first, high_first, n0, n1, h, far_low, high
-    )
+    out = call(bind(outer, plan), f32(plan.tf * cells, LANES))(down, rates, n0, h0, x1, far_low)
     sens = jnp.transpose(sens.reshape(fields, plan.panels, plan.rows, insts), (3, 0, 1, 2))
     return out.reshape(rhs.shape), sens
 

time: 69.8 us -> 61.7 us (0.88)
  local copies, waits for them, and re-layouts: 12.2 us -> 1.91 us
  waiting for transfers between devices: 14.2 us -> 17.9 us
  starting transfers between devices: 28.5 us -> 25.4 us
  other arithmetic: 0 us -> 1.54 us
    unnamed x56 -> x32, local copies, waits for them, and re-layouts: 12 us -> 1.75 us
    ppermute x5, starting transfers between devices: 14.8 us -> 10.9 us  [swap(): return lax.ppermute(array, 'sector', list(enumerate(partner)))]
    all_to_all x1, waiting for transfers between devices: 2.36 us -> 5.58 us  [on_device(): returned = lax.all_to_all(back, 'sector', 0, 0, tiled=True)]
    all_to_all x1, starting transfers between devices: 3.5 us -> 4.36 us  [on_device(): returned = lax.all_to_all(back, 'sector', 0, 0, tiled=True)]
    pallas_call x2, Pallas kernels: 3.98 us -> 4.81 us  [the longest x1 3.69 us: on_device(): call(bind(middle, plan), (f32(sectors, RATES, LANES), half, half, half, f...]
    concatenate x0 -> x2, other arithmetic: none -> 0.82 us  [the longest x1 0.74 us: on_device(): jnp.concatenate([wall_mask.astype(jnp.float32).reshape(cells, LANES), dia...]
    reshape x0 -> x2, other arithmetic: none -> 0.72 us  [the longest x1 0.71 us: on_device(): wall_mask.astype(jnp.float32).reshape(cells, LANES)]
  transfers between devices with their start and end apart: 13 -> 13, of which waited for: 3 -> 4; matrix products, arithmetic and copies ran while one was open for 0% -> 0% of each run, Pallas kernels for 14% -> 16%
where the time goes in v2:
time: 61.7 us; the launch traced here: 61.2 us
  starting transfers between devices  25.4 us (41%)
  waiting for transfers between devices  17.9 us (29%)
  Pallas kernels  13.6 us (22%)
  local copies, waits for them, and re-layouts  1.91 us (3%)
  other arithmetic  1.54 us (2%)
  between operations  0.88 us (1%)
    ppermute x5, starting transfers between devices, swap(): return lax.ppermute(array, 'sector', list(enumerate(partner)))  10.9 us
    ppermute x6, starting transfers between devices, beside(): return lax.ppermute(array, AXES, pairs(0))  7.37 us
    ppermute x6, waiting for transfers between devices, beside(): return lax.ppermute(array, AXES, pairs(0))  6.22 us
    all_to_all x1, waiting for transfers between devices, on_device(): got = lax.all_to_all(sent, AXES, 0, 0, tiled=True)  6.11 us
    all_to_all x1, waiting for transfers between devices, on_device(): returned = lax.all_to_all(back, 'sector', 0, 0, tiled=True)  5.58 us
    all_to_all x1, starting transfers between devices, on_device(): returned = lax.all_to_all(back, 'sector', 0, 0, tiled=True)  4.36 us
    pallas_call x1, Pallas kernels, on_device(): call(bind(middle, plan), (f32(sectors, RATES, LANES), half, half, half, f...  3.69 us
    pallas_call x1, Pallas kernels, on_device(): call(bind(first_half, plan), (whole, f32(pad, slab + LANES)) + edges(pad)...  3.02 us
  transfers between devices with their start and end apart: 13, of which 4 were waited for; matrix products, arithmetic and copies ran while one was open for 0% of the time, Pallas kernels for 16%

profile of v2, /device:TPU:0, one launch (start us, length us, event | category | flops | bytes accessed | tf_op | source)
XLA Modules:
  0.0 61.2 jit_solution(8960685745971487755)
XLA Ops:
  0.7 0.7 %convert_bitcast_fusion = f32[16,128]{1,0:T(8,128)S(1)} fusion(s32[2,8,128]{2,1,0:T(8,128)} %param.20), kind=kLoop, calls=%fused_computation.7 | loop fusion | flops 2048 | bytes 16384 | tf_op jit(solution)/shard_map/reshape | solution.py:657
  1.4 0.7 %pad_maximum_fusion.coef_ref = f32[96,128]{1,0:T(8,128)S(1)} fusion(f32[48,128]{1,0:T(8,128)} %bitcast.20, f32[16,128]{1,0:T(8,128)S(1)} %bitcast.21, f32[16,128]{1,0:T(8,128)S(1)} %bitcast.22, f32[16,128]{1,0:T(8,128)S(1)} %convert_bitcast_fusion), kind=kLoop, calls=%fused_computation | loop fusion | flops 36864 | bytes 98304 | tf_op jit(solution)/shard_map/concatenate | solution.py:656
  2.1 1.1 %copy-done = f32[11,7,2,8,128]{4,3,2,1,0:T(8,128)S(1)} copy-done((f32[11,7,2,8,128]{4,3,2,1,0:T(8,128)S(1)}, f32[11,7,2,8,128]{4,3,2,1,0:T(8,128)}, u32[]{:S(2)}) %copy-start) | copy-done | bytes 630808
  3.5 0.5 collective-permute-start.1
  4.0 5.7 %collective-permute-start = (f32[88,2048]{1,0:T(8,128)S(1)}, f32[88,2048]{1,0:T(8,128)S(1)}, u32[]{:S(2)}, u32[]{:S(2)}) collective-permute-start(f32[88,2048]{1,0:T(8,128)S(1)} %get-tuple-element.26.m_ref), channel_id=1, source_target_pairs={{0,30},{2,4},{4,2},{6,8},{8,6},{10,12},{12,10},{14,16},{16,14},{18... | collective-permute-start | bytes 2162696 | tf_op jit(solution)/shard_map/ppermute | solution.py:614
  9.8 0.6 copy-done.15
  10.5 0.9 %shard_map.151 = f32[32,16,128]{2,1,0:T(8,128)} custom-call(f32[7,32,11]{2,1,0:T(8,128)S(1)} %bitcast.17, f32[11,32]{1,0:T(8,128)S(1)} %pad_maximum_fusion.1.both_ref), custom_call_target="tpu_custom_call" | custom-call | flops 2000000 | bytes 1000000 | tf_op jit(solution)/shard_map/pallas_call | solution.py:647
  11.5 2.7 %all-to-all-start = ((f32[32,16,128]{2,1,0:T(8,128)}), f32[32,16,128]{2,1,0:T(8,128)S(1)}, u32[]{:S(2)}, u32[]{:S(2)}) async-start(f32[32,16,128]{2,1,0:T(8,128)} %shard_map.151), calls=%async_computation | async-start | bytes 524288 | tf_op jit(solution)/shard_map/all_to_all | solution.py:653
  14.2 5.3 %collective-permute-start.3 = (f32[1,88,128]{2,1,0:T(8,128)S(1)}, f32[1,88,128]{2,1,0:T(8,128)S(1)}, u32[]{:S(2)}, u32[]{:S(2)}) collective-permute-start(f32[1,88,128]{2,1,0:T(8,128)S(1)} %get-tuple-element.30), channel_id=1, source_target_pairs={{0,31},{1,30},{2,5},{3,4},{4,3},{5,2},{6,9},{7,8},{8,7},{9,6},{10,... | collective-permute-start | bytes 135176 | tf_op jit(solution)/shard_map/ppermute | solution.py:628
  19.5 0.6 collective-permute-start.2
  20.1 1.1 %shard_map.149 = (bf16[560,240]{1,0:T(8,128)(2,1)S(1)}, bf16[80,240]{1,0:T(8,128)(2,1)S(1)}) custom-call(f32[3,7,7]{2,1,0:T(8,128)S(1)} %copy-done.5, f32[3,7,7]{2,1,0:T(8,128)S(1)} %copy-done.6, bf16[80,240]{1,0:T(8,128)(2,1)S(1)} %copy-done.4, f32[80,7]{1,0:T(8,128)S(1)} %copy-done.3, f32[7,240]{1,0:T(8,128)S(1)} %copy-done.7, f32[80,240]{1,0:T(8,128)S(1)} %copy-done.2), custom_call_target="tpu_custom_call" | custom-call | flops 2000000 | bytes 1000000 | tf_op jit(solution)/shard_map/pallas_call | solution.py:664
  21.2 6.1 %all-to-all-done.got_ref = f32[32,16,128]{2,1,0:T(8,128)S(1)} async-done(((f32[32,16,128]{2,1,0:T(8,128)}), f32[32,16,128]{2,1,0:T(8,128)S(1)}, u32[]{:S(2)}, u32[]{:S(2)}) %all-to-all-start) | async-done | bytes 262176 | tf_op jit(solution)/shard_map/all_to_all | solution.py:653
  27.3 1.7 %shard_map.152 = (f32[3,2,80,128]{3,2,1,0:T(8,128)S(1)}, f32[80,128]{1,0:T(8,128)S(1)}, f32[80,2048]{1,0:T(8,128)S(1)}, f32[80,2048]{1,0:T(8,128)S(1)}) custom-call(bf16[560,240]{1,0:T(8,128)(2,1)S(1)} %get-tuple-element.25.w_ref, f32[88,2048]{1,0:T(8,128)S(1)} %get-tuple-element.26.m_ref, f32[32,16,128]{2,1,0:T(8,128)S(1)} %all-to-all-done.got_ref), custom_call_target="tpu_custom_call" | custom-call | flops 2000000000 | bytes 1000000 | tf_op jit(solution)/shard_map/pallas_call | solution.py:669
  29.2 3.0 %shard_map.153 = (f32[80,2048]{1,0:T(8,128)S(1)}, f32[80,1152]{1,0:T(8,128)S(1)}, f32[1,80,512]{2,1,0:T(8,128)S(1)}, f32[1,80,128]{2,1,0:T(8,128)S(1)}, f32[1,80,128]{2,1,0:T(8,128)S(1)}) custom-call(bf16[560,240]{1,0:T(8,128)(2,1)S(1)} %get-tuple-element.25.w_ref, f32[88,2048]{1,0:T(8,128)S(1)} %get-tuple-element.26.m_ref, ...), custom_call_target="tpu_custom_call" | custom-call | flops 4000000000 | bytes 1000000 | tf_op jit(solution)/shard_map/pallas_call | solution.py:674
  32.3 4.6 %collective-permute-start.6 = (f32[80,1152]{1,0:T(8,128)S(1)}, f32[80,1152]{1,0:T(8,128)S(1)}, u32[]{:S(2)}, u32[]{:S(2)}) collective-permute-start(f32[80,1152]{1,0:T(8,128)S(1)} %get-tuple-element.36), channel_id=1, source_target_pairs={{0,30},{2,4},{4,2},{6,8},{8,6},{10,12},{12,10},{14,16},{16,14},{18... | collective-permute-start | bytes 1105928 | tf_op jit(solution)/shard_map/ppermute | solution.py:614
  36.9 1.5 %collective-permute-start.5 = (f32[1,80,512]{2,1,0:T(8,128)S(1)}, f32[1,80,512]{2,1,0:T(8,128)S(1)}, u32[]{:S(2)}, u32[]{:S(2)}) collective-permute-start(f32[1,80,512]{2,1,0:T(8,128)S(1)} %get-tuple-element.34), channel_id=1, source_target_pairs={{0,1},{1,0},{2,3},{3,2},{4,5},{5,4},{6,7},{7,6},{8,9},{9,8},{10,11... | collective-permute-start | bytes 491528 | tf_op jit(solution)/shard_map/ppermute | solution.py:628
  38.4 4.7 %collective-permute-done.5.side_ref = f32[1,80,512]{2,1,0:T(8,128)S(1)} collective-permute-done((f32[1,80,512]{2,1,0:T(8,128)S(1)}, f32[1,80,512]{2,1,0:T(8,128)S(1)}, u32[]{:S(2)}, u32[]{:S(2)}) %collective-permute-start.5) | collective-permute-done | bytes 163872 | tf_op jit(solution)/shard_map/ppermute | solution.py:628
  43.1 0.8 %shard_map.154 = (f32[80,2048]{1,0:T(8,128)S(1)}, f32[80,1024]{1,0:T(8,128)S(1)}) custom-call(bf16[560,240]{1,0:T(8,128)(2,1)S(1)} %get-tuple-element.25.w_ref, f32[88,2048]{1,0:T(8,128)S(1)} %get-tuple-element.26.m_ref, f32[80,2048]{1,0:T(8,128)S(1)} %get-tuple-element.27.f_ref, f32[80,2048]{1,0:T(8,128)S(1)} %get-tuple-element.33.x_ref, ...), custom_call_target="tpu_custom_call" | custom-call | flops 2000000000 | bytes 1000000 | tf_op jit(solution)/shard_map/pallas_call | solution.py:682
  44.0 1.5 %collective-permute-done.8.c_low = f32[1,80,128]{2,1,0:T(8,128)S(1)} collective-permute-done((f32[1,80,128]{2,1,0:T(8,128)S(1)}, f32[1,80,128]{2,1,0:T(8,128)S(1)}, u32[]{:S(2)}, u32[]{:S(2)}) %collective-permute-start.8) | collective-permute-done | bytes 40992 | tf_op jit(solution)/shard_map/ppermute | solution.py:628
  45.5 3.7 %shard_map.155 = (f32[16,8,128]{2,1,0:T(8,128)}, f32[80,1024]{1,0:T(8,128)S(1)}, f32[80,1024]{1,0:T(8,128)S(1)}, f32[80,1024]{1,0:T(8,128)S(1)}, f32[8,1024]{1,0:T(8,128)S(1)}) custom-call(bf16[560,240]{1,0:T(8,128)(2,1)S(1)} %get-tuple-element.25.w_ref, f32[88,2048]{1,0:T(8,128)S(1)} %get-tuple-element.26.m_ref, f32[80,2048]{1,0:T(8,128)S(1)} %get-tuple-element.27.f_ref, ...), custom_call_target="tpu_custom_call" | custom-call | flops 4000000000 | bytes 1000000 | tf_op jit(solution)/shard_map/pallas_call | solution.py:686
  49.2 4.4 %all-to-all-start.1 = ((f32[16,8,128]{2,1,0:T(8,128)}), f32[16,8,128]{2,1,0:T(8,128)S(1)}, u32[]{:S(2)}, u32[]{:S(2)}) async-start(f32[16,8,128]{2,1,0:T(8,128)} %get-tuple-element.45), calls=%async_computation.1 | async-start | bytes 131072 | tf_op jit(solution)/shard_map/all_to_all | solution.py:692
  53.6 1.3 %shard_map.156 = f32[1232,128]{1,0:T(8,128)} custom-call(bf16[80,240]{1,0:T(8,128)(2,1)S(1)} %get-tuple-element.24.w_ref, f32[8,1024]{1,0:T(8,128)S(1)} %get-tuple-element.40.rates_ref, f32[80,1024]{1,0:T(8,128)S(1)} %get-tuple-element.41.n0_ref, f32[80,1024]{1,0:T(8,128)S(1)} %get-tuple-element.42.h0_ref, f32[80,1024]{1,0:T(8,128)S(1)} %get-tuple-element.43.x1_ref, ...), custom_call_target="tpu_custom_call" | custom-call | flops 2000000 | bytes 1000000 | tf_op jit(solution)/shard_map/pallas_call | solution.py:694
  54.9 5.6 %all-to-all-done.1.got_ref = f32[16,8,128]{2,1,0:T(8,128)S(1)} async-done(((f32[16,8,128]{2,1,0:T(8,128)}), f32[16,8,128]{2,1,0:T(8,128)S(1)}, u32[]{:S(2)}, u32[]{:S(2)}) %all-to-all-start.1) | async-done | bytes 65568 | tf_op jit(solution)/shard_map/all_to_all | solution.py:692
  60.5 0.8 %shard_map.157 = f32[7,32,11]{2,1,0:T(8,128)} custom-call(f32[16,8,128]{2,1,0:T(8,128)S(1)} %all-to-all-done.1.got_ref), custom_call_target="tpu_custom_call" | custom-call | flops 2000000 | bytes 1000000 | tf_op jit(solution)/shard_map/pallas_call | solution.py:693
  (49 shorter events, 0.8 us)
Async XLA Ops:
  3.2 6.5 %copy-start.14 = (s32[11,2,8]{0,2,1:T(8,128)S(1)}, s32[11,2,8]{0,2,1:T(8,128)}, u32[]{:S(2)}) copy-start(s32[11,2,8]{0,2,1:T(8,128)} %param.22) | copy-start | bytes 2116
  3.2 7.3 %copy-start.1 = (f32[11,7,4,8]{0,3,2,1:T(8,128)S(1)}, f32[11,7,4,8]{0,3,2,1:T(8,128)}, u32[]{:S(2)}) copy-start(f32[11,7,4,8]{0,3,2,1:T(8,128)} %param.21) | copy-start | bytes 29572
  3.5 25.7 %collective-permute-start.1 = (f32[88,2048]{1,0:T(8,128)S(1)}, f32[88,2048]{1,0:T(8,128)S(1)}, u32[]{:S(2)}, u32[]{:S(2)}) collective-permute-start(f32[88,2048]{1,0:T(8,128)S(1)} %get-tuple-element.26.m_ref), channel_id=1, source_target_pairs={{0,2},{2,0},{4,6},{6,4},{8,10},{10,8},{12,14},{14,12},{16,18},{18,... | collective-permute-start | bytes 2162696 | tf_op jit(solution)/shard_map/ppermute | solution.py:614
  4.0 25.2 %collective-permute-start = (f32[88,2048]{1,0:T(8,128)S(1)}, f32[88,2048]{1,0:T(8,128)S(1)}, u32[]{:S(2)}, u32[]{:S(2)}) collective-permute-start(f32[88,2048]{1,0:T(8,128)S(1)} %get-tuple-element.26.m_ref), channel_id=1, source_target_pairs={{0,30},{2,4},{4,2},{6,8},{8,6},{10,12},{12,10},{14,16},{16,14},{18... | collective-permute-start | bytes 2162696 | tf_op jit(solution)/shard_map/ppermute | solution.py:614
  11.4 8.6 %copy-start.2 = (f32[80,240]{1,0:T(8,128)S(1)}, f32[80,240]{1,0:T(8,128)}, u32[]{:S(2)}) copy-start(f32[80,240]{1,0:T(8,128)} %constant.16.clone.diagonal_ref) | copy-start | bytes 230404
  11.4 8.6 %copy-start.3 = (f32[80,7]{1,0:T(8,128)S(1)}, f32[80,7]{1,0:T(8,128)}, u32[]{:S(2)}) copy-start(f32[80,7]{1,0:T(8,128)} %constant.14.clone.rows_ref) | copy-start | bytes 6724
  11.4 8.7 %copy-start.4 = (bf16[80,240]{1,0:T(8,128)(2,1)S(1)}, bf16[80,240]{1,0:T(8,128)(2,1)}, u32[]{:S(2)}) copy-start(bf16[80,240]{1,0:T(8,128)(2,1)} %constant.13.clone.spectral_ref) | copy-start | bytes 115204
  11.4 8.7 %copy-start.5 = (f32[3,7,7]{2,1,0:T(8,128)S(1)}, f32[3,7,7]{2,1,0:T(8,128)}, u32[]{:S(2)}) copy-start(f32[3,7,7]{2,1,0:T(8,128)} %up_ref.1) | copy-start | bytes 1768
  11.4 8.7 %copy-start.6 = (f32[3,7,7]{2,1,0:T(8,128)S(1)}, f32[3,7,7]{2,1,0:T(8,128)}, u32[]{:S(2)}) copy-start(f32[3,7,7]{2,1,0:T(8,128)} %down_ref.1) | copy-start | bytes 1768
  11.4 8.6 %copy-start.7 = (f32[7,240]{1,0:T(8,128)S(1)}, f32[7,240]{1,0:T(8,128)}, u32[]{:S(2)}) copy-start(f32[7,240]{1,0:T(8,128)} %constant.15.clone.lanes_ref) | copy-start | bytes 20164
  11.5 15.9 %all-to-all-start = ((f32[32,16,128]{2,1,0:T(8,128)}), f32[32,16,128]{2,1,0:T(8,128)S(1)}, u32[]{:S(2)}, u32[]{:S(2)}) async-start(f32[32,16,128]{2,1,0:T(8,128)} %shard_map.151), calls=%async_computation | async-start | bytes 524288 | tf_op jit(solution)/shard_map/all_to_all | solution.py:653
  14.2 14.9 %collective-permute-start.3 = (f32[1,88,128]{2,1,0:T(8,128)S(1)}, f32[1,88,128]{2,1,0:T(8,128)S(1)}, u32[]{:S(2)}, u32[]{:S(2)}) collective-permute-start(f32[1,88,128]{2,1,0:T(8,128)S(1)} %get-tuple-element.30), channel_id=1, source_target_pairs={{0,31},{1,30},{2,5},{3,4},{4,3},{5,2},{6,9},{7,8},{8,7},{9,6},{10,... | collective-permute-start | bytes 135176 | tf_op jit(solution)/shard_map/ppermute | solution.py:628
  19.5 9.6 %collective-permute-start.4 = (f32[1,88,128]{2,1,0:T(8,128)S(1)}, f32[1,88,128]{2,1,0:T(8,128)S(1)}, u32[]{:S(2)}, u32[]{:S(2)}) collective-permute-start(f32[1,88,128]{2,1,0:T(8,128)S(1)} %get-tuple-element.31), channel_id=1, source_target_pairs={{0,3},{1,2},{2,1},{3,0},{4,7},{5,6},{6,5},{7,4},{8,11},{9,10},{10,... | collective-permute-start | bytes 135176 | tf_op jit(solution)/shard_map/ppermute | solution.py:628
  19.5 9.6 %collective-permute-start.2 = (f32[1,88,512]{2,1,0:T(8,128)S(1)}, f32[1,88,512]{2,1,0:T(8,128)S(1)}, u32[]{:S(2)}, u32[]{:S(2)}) collective-permute-start(f32[1,88,512]{2,1,0:T(8,128)S(1)} %get-tuple-element.29), channel_id=1, source_target_pairs={{0,1},{1,0},{2,3},{3,2},{4,5},{5,4},{6,7},{7,6},{8,9},{9,8},{10,11... | collective-permute-start | bytes 540680 | tf_op jit(solution)/shard_map/ppermute | solution.py:628
  29.1 3.1 %copy-start.10 = (f32[1,88,512]{2,1,0:T(8,128)}, f32[1,88,512]{2,1,0:T(8,128)S(1)}, u32[]{:S(2)}) copy-start(f32[1,88,512]{2,1,0:T(8,128)S(1)} %collective-permute-done.2.side_ref.side_first) | copy-start | bytes 540676
  32.2 13.3 %collective-permute-start.7 = (f32[80,2048]{1,0:T(8,128)S(1)}, f32[80,2048]{1,0:T(8,128)S(1)}, u32[]{:S(2)}, u32[]{:S(2)}) collective-permute-start(f32[80,2048]{1,0:T(8,128)S(1)} %get-tuple-element.33.x_ref), channel_id=1, source_target_pairs={{0,2},{2,0},{4,6},{6,4},{8,10},{10,8},{12,14},{14,12},{16,18},{18,... | collective-permute-start | bytes 1966088 | tf_op jit(solution)/shard_map/ppermute | solution.py:614
  32.3 13.2 %collective-permute-start.6 = (f32[80,1152]{1,0:T(8,128)S(1)}, f32[80,1152]{1,0:T(8,128)S(1)}, u32[]{:S(2)}, u32[]{:S(2)}) collective-permute-start(f32[80,1152]{1,0:T(8,128)S(1)} %get-tuple-element.36), channel_id=1, source_target_pairs={{0,30},{2,4},{4,2},{6,8},{8,6},{10,12},{12,10},{14,16},{16,14},{18... | collective-permute-start | bytes 1105928 | tf_op jit(solution)/shard_map/ppermute | solution.py:614
  36.9 6.2 %collective-permute-start.5 = (f32[1,80,512]{2,1,0:T(8,128)S(1)}, f32[1,80,512]{2,1,0:T(8,128)S(1)}, u32[]{:S(2)}, u32[]{:S(2)}) collective-permute-start(f32[1,80,512]{2,1,0:T(8,128)S(1)} %get-tuple-element.34), channel_id=1, source_target_pairs={{0,1},{1,0},{2,3},{3,2},{4,5},{5,4},{6,7},{7,6},{8,9},{9,8},{10,11... | collective-permute-start | bytes 491528 | tf_op jit(solution)/shard_map/ppermute | solution.py:628
  38.4 7.1 %collective-permute-start.8 = (f32[1,80,128]{2,1,0:T(8,128)S(1)}, f32[1,80,128]{2,1,0:T(8,128)S(1)}, u32[]{:S(2)}, u32[]{:S(2)}) collective-permute-start(f32[1,80,128]{2,1,0:T(8,128)S(1)} %get-tuple-element.37), channel_id=1, source_target_pairs={{0,31},{1,30},{2,5},{3,4},{4,3},{5,2},{6,9},{7,8},{8,7},{9,6},{10,... | collective-permute-start | bytes 122888 | tf_op jit(solution)/shard_map/ppermute | solution.py:628
  38.4 7.1 %copy-start.9 = (f32[88,2048]{1,0:T(8,128)S(1)}, f32[88,2048]{1,0:T(8,128)}, u32[]{:S(2)}) copy-start(f32[88,2048]{1,0:T(8,128)} %copy-done.8) | copy-start | bytes 2162692
  38.4 7.2 %copy-start.11 = (f32[1,88,512]{2,1,0:T(8,128)S(1)}, f32[1,88,512]{2,1,0:T(8,128)}, u32[]{:S(2)}) copy-start(f32[1,88,512]{2,1,0:T(8,128)} %copy-done.10) | copy-start | bytes 540676
  38.4 7.1 %collective-permute-start.9 = (f32[1,80,128]{2,1,0:T(8,128)S(1)}, f32[1,80,128]{2,1,0:T(8,128)S(1)}, u32[]{:S(2)}, u32[]{:S(2)}) collective-permute-start(f32[1,80,128]{2,1,0:T(8,128)S(1)} %get-tuple-element.38), channel_id=1, source_target_pairs={{0,3},{1,2},{2,1},{3,0},{4,7},{5,6},{6,5},{7,4},{8,11},{9,10},{10,... | collective-permute-start | bytes 122888 | tf_op jit(solution)/shard_map/ppermute | solution.py:628
  43.9 9.7 %collective-permute-start.10 = (f32[80,1024]{1,0:T(8,128)S(1)}, f32[80,1024]{1,0:T(8,128)S(1)}, u32[]{:S(2)}, u32[]{:S(2)}) collective-permute-start(f32[80,1024]{1,0:T(8,128)S(1)} %get-tuple-element.44), channel_id=1, source_target_pairs={{0,30},{2,4},{4,2},{6,8},{8,6},{10,12},{12,10},{14,16},{16,14},{18... | collective-permute-start | bytes 983048 | tf_op jit(solution)/shard_map/ppermute | solution.py:614
  49.2 11.3 %all-to-all-start.1 = ((f32[16,8,128]{2,1,0:T(8,128)}), f32[16,8,128]{2,1,0:T(8,128)S(1)}, u32[]{:S(2)}, u32[]{:S(2)}) async-start(f32[16,8,128]{2,1,0:T(8,128)} %get-tuple-element.45), calls=%async_computation.1 | async-start | bytes 131072 | tf_op jit(solution)/shard_map/all_to_all | solution.py:692
  (5 other events, 6.3 us)

commit v3 on v2

--- a/solution.py
+++ b/solution.py
@@ -16,7 +16,7 @@
 WINDOW = 8
 HIGHEST = lax.Precision.HIGHEST
 DOWN_AZ, SPECTRAL, UP_SP, DOWN_SP, UP_AX, DOWN_AX, UP_AZ = range(7)
-C_TIME, C_AZ, C_SP, C_UP, C_DOWN, C_MASK = range(6)
+C_TIME, C_AZ, C_SP, C_UP, C_DOWN, C_MASK, C_OTHER = range(7)
 RATES = 8
 GROUP = 3
 AXES = ("sector", "span")
@@ -167,8 +167,8 @@
 
 
 class Layer:
-    def __init__(self, plan, ref, start=0, rates=None, seam=None, layer=0):
-        self.plan, self.ref, self.start, self.seam, self.layer = plan, ref, start, seam, layer
+    def __init__(self, plan, ref, start=0, rates=None, seam=None, layer=0, scale=C_MASK):
+        self.plan, self.ref, self.start, self.seam, self.layer, self.scale = plan, ref, start, seam, layer, scale
         self.rates = rates or (ref, start)
 
     def rate(self, which, r, count=1):
@@ -180,7 +180,7 @@
         value = self.ref[: self.plan.pad, at(r, 1, self.start)]
         if self.seam is None:
             return value
-        return value + placed(self.seam, self.layer * self.plan.rows + r) * self.rate(C_MASK, r)
+        return value + placed(self.seam, self.layer * self.plan.rows + r) * self.rate(self.scale, r)
 
     def chunk(self, c):
         count = CHUNK // LANES
@@ -363,25 +363,34 @@
     return corner
 
 
-def prepare(plan, rhs_ref, coef_ref, m_ref, side_ref, c0_ref, c1_ref):
+def prepare(plan, rhs_ref, coef_ref, m_ref, near_ref, side_ref, c0_ref, c1_ref):
     pad = plan.pad
     lane = lane_index(1)
     tail = jnp.zeros((pad - plan.tf, LANES), jnp.float32)
     mirror = parity()
-    for cell in range(plan.cells):
-        a, r = divmod(cell, plan.rows)
+
+    def coefs(a, r):
         there = jnp.where(mirror == 0, a, plan.ct - 1 - a) * plan.rows + r
-        mask, diag, time, *face = [coef_ref[pl.ds(there + plan.cells * i, 1), :] for i in range(6)]
-        scale = mask / diag
-        axial = scale * face[2]
-        rates = [
-            scale * time, scale * face[0], scale * face[1],
-            jnp.where(lane < LANES - 1, axial, 0.0), jnp.where(lane > 0, axial, 0.0), scale,
-            jnp.zeros((RATES - 6, LANES), jnp.float32),
-        ]
-        field = jnp.concatenate([rhs_ref[pl.ds(there, plan.tf, stride=plan.cells), :], tail], axis=0) * scale
-        m_ref[:pad, at(cell)] = field
-        m_ref[pad:, at(cell)] = jnp.concatenate(rates, axis=0)
+        mask, diag, *rest = [coef_ref[pl.ds(there + plan.cells * i, 1), :] for i in range(6)]
+        return there, mask / diag, rest
+
+    for r in range(plan.rows):
+        scales = [coefs(a, r)[1] for a in range(plan.ct)]
+        for a in range(plan.ct):
+            there, scale, (time, *face) = coefs(a, r)
+            axial = scale * face[2]
+            rates = jnp.concatenate([
+                scale * time, scale * face[0], scale * face[1],
+                jnp.where(lane < LANES - 1, axial, 0.0), jnp.where(lane > 0, axial, 0.0), scale, scales[1 - a],
+                jnp.zeros((RATES - 7, LANES), jnp.float32),
+            ], axis=0)
+            field = jnp.concatenate([rhs_ref[pl.ds(there, plan.tf, stride=plan.cells), :], tail], axis=0) * scale
+            lanes = at(a * plan.rows + r)
+            m_ref[:pad, lanes] = field
+            m_ref[pad:, lanes] = rates
+            if a == 0:
+                near_ref[:pad, lanes] = field
+                near_ref[pad:, lanes] = rates
     write_edges(plan, m_ref, side_ref, (c0_ref, c1_ref))
 
 
@@ -397,8 +406,9 @@
                     c_refs[a][n] = end
 
 
-def stack_matrices(plan, up_ref, down_ref, spectral_ref, rows_ref, lanes_ref, diagonal_ref, out_ref, down_out):
+def stack_matrices(plan, m_ref, high_ref, up_ref, down_ref, spectral_ref, rows_ref, lanes_ref, diagonal_ref, out_ref, down_out, far_ref):
     pad = plan.pad
+    far_ref[...] = m_ref[:pad, plan.slab :] + 0.0 * high_ref[0:1, 0:1]
     lane = lax.broadcasted_iota(jnp.int32, (pad, 3 * pad), 1)
     second = (lane >= pad) & (lane < 2 * pad)
     out_ref[SPECTRAL * pad : (SPECTRAL + 1) * pad, :] = spectral_ref[...]
@@ -497,19 +507,28 @@
     inner_rows(plan, w_ref, (p0_ref, p1_ref), layers, layers, g_ref)
 
 
-def first_half(
+def middle_first(
     plan, w_ref, m_ref, f_ref, g_ref, low_ref, high_ref, side_ref, c_low, c_high, seams_ref,
-    x_ref, near_ref, side_out, c0_ref, c1_ref, p0_ref, p1_ref, y_ref, h_ref, n0_ref, n1_ref,
+    h_ref, n0_ref, n1_ref, p0_ref, p1_ref, y_ref,
 ):
     own = two_layers(plan, f_ref, m_ref)
-    low = two_layers(plan, low_ref, seam=seams_ref[0, 0])
-    high = two_layers(plan, high_ref, seam=seams_ref[2, 0])
-    near = low[0], high[1]
-    n_refs = n0_ref, n1_ref
+    near = (
+        Layer(plan, low_ref, 0, None, seams_ref[0, 0], 0), Layer(plan, high_ref, plan.slab, None, seams_ref[2, 0], 1),
+    )
     middle_rows(
         plan, w_ref, (p0_ref, p1_ref), own, own, g_ref, near, near, sides_of(plan, side_ref, side_ref, seams_ref),
-        corners_of(plan, (c_low, c_high), seams_ref), y_ref, h_ref, n_refs,
-    )
+        corners_of(plan, (c_low, c_high), seams_ref), y_ref, h_ref, (n0_ref, n1_ref),
+    )
+
+
+def outer_first(
+    plan, w_ref, m_ref, low_first, high_first, n0_ref, n1_ref, h_ref, far_ref, seams_ref,
+    x_ref, near_ref, side_out, c0_ref, c1_ref,
+):
+    own = two_layers(plan, m_ref)
+    near = Layer(plan, low_first), Layer(plan, high_first, plan.slab)
+    far_low = Layer(plan, far_ref, 0, (low_first, 0), seams_ref[0, 0], 1, C_OTHER)
+    far_high = Layer(plan, high_first, 0, None, seams_ref[2, 0], 0)
     lane = lane_index(plan.pad)
     near_ref[:, plan.slab :] = jnp.zeros((plan.pad, LANES), jnp.float32)
 
@@ -521,7 +540,7 @@
             here = rolled(value, r * WINDOW)
             near_ref[:, plan.slab :] = jnp.where(lane == r * WINDOW, here, near_ref[:, plan.slab :])
 
-    outer_rows(plan, w_ref, own, near, (low[1].chunk, high[0].chunk), n_refs, h_ref, put)
+    outer_rows(plan, w_ref, own, near, (far_low.chunk, far_high.chunk), (n0_ref, n1_ref), h_ref, put)
     write_edges(plan, x_ref, side_out, (c0_ref, c1_ref))
 
 
@@ -651,30 +670,34 @@
         ], axis=1),
     )
     got = lax.all_to_all(sent, AXES, 0, 0, tiled=True)
-    m, side, c0, c1 = call(bind(prepare, plan), (f32(pad + RATES, plan.ct * slab),) + edges(pad + RATES))(
+    m, near, side, c0, c1 = call(
+        bind(prepare, plan), (f32(pad + RATES, plan.ct * slab), f32(pad + RATES, slab)) + edges(pad + RATES)
+    )(
         rhs.reshape(plan.tf * cells, LANES),
         jnp.concatenate([
             wall_mask.astype(jnp.float32).reshape(cells, LANES), diag_coef.reshape(cells, LANES),
             time_coef.reshape(cells, LANES), face_coef.reshape(3 * cells, LANES),
         ]),
     )
-    low_first, high_first = swap(m, next_chip), swap(m, next_core)
+    low_first, high_first = swap(near, next_chip), swap(m, next_core)
     side_first = beside(plan, side, alone)
     c_low, c_high = beside(plan, c0, next_chip), beside(plan, c1, next_core)
-    matrices, down = call(
+    matrices, down, far = call(
         bind(stack_matrices, plan),
-        [jax.ShapeDtypeStruct((count * pad, 3 * pad), jnp.bfloat16) for count in (7, 1)],
-    )(jac_up, jac_down, plan.spectral(), plan.field_rows(), plan.field_lanes(), plan.block_diagonal())
+        [jax.ShapeDtypeStruct((count * pad, 3 * pad), jnp.bfloat16) for count in (7, 1)] + [half],
+    )(m, high_first, jac_up, jac_down, plan.spectral(), plan.field_rows(), plan.field_lanes(), plan.block_diagonal())
+    far_low = swap(far, next_chip)
     tiles = len(plan.tiles)
     seams, weight, force, g = call(
         bind(begin, plan), (f32(3, 1 + ends, pad, LANES), f32(pad, LANES), whole, whole),
         (vmem(pad, tiles * LANES), vmem(tiles * pad, LANES), vmem(16, tiles * LANES)) + products,
-        flops=2_000_000_000,
     )(matrices, m, got)
-    x, near, side, c0, c1 = call(
-        bind(first_half, plan), (whole, f32(pad, slab + LANES)) + edges(pad),
-        products + (vmem(pad, 2 * slab), vmem(pad, 2 * slab), vmem(pad, slab), vmem(pad, slab)), flops=4_000_000_000,
-    )(matrices, m, force, g, low_first, high_first, side_first, c_low, c_high, seams)
+    h, n0, n1 = call(bind(middle_first, plan), (whole, half, half), products + (vmem(pad, 2 * slab),))(
+        matrices, m, force, g, low_first, high_first, side_first, c_low, c_high, seams
+    )
+    x, near, side, c0, c1 = call(bind(outer_first, plan), (whole, f32(pad, slab + LANES)) + edges(pad))(
+        matrices, m, low_first, high_first, n0, n1, h, far_low, seams
+    )
 
     low, high = swap(near, next_chip), swap(x, next_core)
     side = beside(plan, side, alone)

time: 61.7 us -> 66.5 us (1.078)
  starting transfers between devices: 25.4 us -> 33.4 us
  waiting for transfers between devices: 17.9 us -> 13.2 us
  Pallas kernels: 13.6 us -> 15.2 us
    all_to_all x1, waiting for transfers between devices: 6.11 us -> 0.01 us  [on_device(): got = lax.all_to_all(sent, AXES, 0, 0, tiled=True)]
    all_to_all x1, starting transfers between devices: 2.73 us -> 6.97 us  [on_device(): got = lax.all_to_all(sent, AXES, 0, 0, tiled=True)]
    ppermute x6, starting transfers between devices: 7.37 us -> 9.18 us  [beside(): return lax.ppermute(array, AXES, pairs(0))]
    all_to_all x1, starting transfers between devices: 4.36 us -> 5.83 us  [on_device(): returned = lax.all_to_all(back, 'sector', 0, 0, tiled=True)]
    ppermute x6, waiting for transfers between devices: 6.22 us -> 7.63 us  [beside(): return lax.ppermute(array, AXES, pairs(0))]
    pallas_call x2 -> x3, Pallas kernels: 3.28 us -> 4.22 us  [the longest x1 2.47 us: on_device(): call(bind(middle_first, plan), (whole, half, half), products + (vmem(pad,...]
    pallas_call x1, Pallas kernels: 1.12 us -> 1.8 us  [on_device(): call(bind(stack_matrices, plan), [jax.ShapeDtypeStruct((count * pad, 3 *...]
    ppermute x5 -> x6, starting transfers between devices: 10.9 us -> 11.4 us  [swap(): return lax.ppermute(array, 'sector', list(enumerate(partner)))]
  transfers between devices with their start and end apart: 13 -> 14, of which waited for: 4 -> 3; matrix products, arithmetic and copies ran while one was open for 0% -> 0% of each run, Pallas kernels for 16% -> 19%
where the time goes in v3:
time: 66.5 us; the launch traced here: 66 us
  starting transfers between devices  33.4 us (50%)
  Pallas kernels  15.2 us (23%)
  waiting for transfers between devices  13.2 us (20%)
  local copies, waits for them, and re-layouts  1.9 us (3%)
  other arithmetic  1.54 us (2%)
  between operations  0.82 us (1%)
    ppermute x6, starting transfers between devices, swap(): return lax.ppermute(array, 'sector', list(enumerate(partner)))  11.4 us
    ppermute x6, starting transfers between devices, beside(): return lax.ppermute(array, AXES, pairs(0))  9.18 us
    ppermute x6, waiting for transfers between devices, beside(): return lax.ppermute(array, AXES, pairs(0))  7.63 us
    all_to_all x1, starting transfers between devices, on_device(): got = lax.all_to_all(sent, AXES, 0, 0, tiled=True)  6.97 us
    all_to_all x1, starting transfers between devices, on_device(): returned = lax.all_to_all(back, 'sector', 0, 0, tiled=True)  5.83 us
    all_to_all x1, waiting for transfers between devices, on_device(): returned = lax.all_to_all(back, 'sector', 0, 0, tiled=True)  5.58 us
    pallas_call x1, Pallas kernels, on_device(): call(bind(middle, plan), (f32(sectors, RATES, LANES), half, half, half, f...  3.56 us
    pallas_call x1, Pallas kernels, on_device(): call(bind(middle_first, plan), (whole, half, half), products + (vmem(pad,...  2.47 us
  transfers between devices with their start and end apart: 14, of which 3 were waited for; matrix products, arithmetic and copies ran while one was open for 0% of the time, Pallas kernels for 19%

profile of v3, /device:TPU:0, one launch (start us, length us, event | category | flops | bytes accessed | tf_op | source)
XLA Modules:
  0.0 66.0 jit_solution(2120689362403114725)
XLA Ops:
  2.1 1.1 %copy-done = f32[11,7,2,8,128]{4,3,2,1,0:T(8,128)S(1)} copy-done((f32[11,7,2,8,128]{4,3,2,1,0:T(8,128)S(1)}, f32[11,7,2,8,128]{4,3,2,1,0:T(8,128)}, u32[]{:S(2)}) %copy-start) | copy-done | bytes 630808
  3.2 1.0 %shard_map.149 = (f32[88,2048]{1,0:T(8,128)S(1)}, f32[88,1024]{1,0:T(8,128)S(1)}, f32[1,88,512]{2,1,0:T(8,128)}, f32[1,88,128]{2,1,0:T(8,128)S(1)}, f32[1,88,128]{2,1,0:T(8,128)S(1)}) custom-call(f32[1232,128]{1,0:T(8,128)S(1)} %bitcast.16, f32[96,128]{1,0:T(8,128)S(1)} %pad_maximum_fusion.coef_ref), custom_call_target="tpu_custom_call" | custom-call | flops 2000000 | bytes 1000000 | tf_op jit(solution)/shard_map/pallas_call | solution.py:673
  5.5 0.9 %shard_map.151 = f32[32,16,128]{2,1,0:T(8,128)} custom-call(f32[7,32,11]{2,1,0:T(8,128)S(1)} %bitcast.17, f32[11,32]{1,0:T(8,128)S(1)} %pad_maximum_fusion.1.both_ref), custom_call_target="tpu_custom_call" | custom-call | flops 2000000 | bytes 1000000 | tf_op jit(solution)/shard_map/pallas_call | solution.py:666
  6.4 7.0 %all-to-all-start = ((f32[32,16,128]{2,1,0:T(8,128)}), f32[32,16,128]{2,1,0:T(8,128)S(1)}, u32[]{:S(2)}, u32[]{:S(2)}) async-start(f32[32,16,128]{2,1,0:T(8,128)} %shard_map.151), calls=%async_computation | async-start | bytes 524288 | tf_op jit(solution)/shard_map/all_to_all | solution.py:672
  13.4 4.4 %collective-permute-start.1 = (f32[88,1024]{1,0:T(8,128)S(1)}, f32[88,1024]{1,0:T(8,128)S(1)}, u32[]{:S(2)}, u32[]{:S(2)}) collective-permute-start(f32[88,1024]{1,0:T(8,128)S(1)} %get-tuple-element.33), channel_id=1, source_target_pairs={{0,30},{2,4},{4,2},{6,8},{8,6},{10,12},{12,10},{14,16},{16,14},{18... | collective-permute-start | bytes 1081352 | tf_op jit(solution)/shard_map/ppermute | solution.py:633
  17.8 1.8 %shard_map.150 = (bf16[560,240]{1,0:T(8,128)(2,1)S(1)}, bf16[80,240]{1,0:T(8,128)(2,1)S(1)}, f32[80,1024]{1,0:T(8,128)}) custom-call(f32[88,2048]{1,0:T(8,128)S(1)} %get-tuple-element.29.m_ref, f32[88,2048]{1,0:T(8,128)S(1)} %collective-permute-done.high_ref.high_first, f32[3,7,7]{2,1,0:T(8,128)S(1)} %copy-done.7, f32[3,7,7]{2,1,0:T(8,128)S(1)} %copy-done.8, ...), custom_call_target="tpu_custom_call" | custom-call | flops 2000000 | bytes 1000000 | tf_op jit(solution)/shard_map/pallas_call | solution.py:685
  19.8 1.8 %collective-permute-start.2 = (f32[1,88,512]{2,1,0:T(8,128)}, f32[1,88,512]{2,1,0:T(8,128)S(1)}, u32[]{:S(2)}, u32[]{:S(2)}) collective-permute-start(f32[1,88,512]{2,1,0:T(8,128)} %get-tuple-element.35), channel_id=1, source_target_pairs={{0,1},{1,0},{2,3},{3,2},{4,5},{5,4},{6,7},{7,6},{8,9},{9,8},{10,11... | collective-permute-start | bytes 540680 | tf_op jit(solution)/shard_map/ppermute | solution.py:647
  21.6 3.7 %collective-permute-start.3 = (f32[1,88,128]{2,1,0:T(8,128)S(1)}, f32[1,88,128]{2,1,0:T(8,128)S(1)}, u32[]{:S(2)}, u32[]{:S(2)}) collective-permute-start(f32[1,88,128]{2,1,0:T(8,128)S(1)} %get-tuple-element.36), channel_id=1, source_target_pairs={{0,31},{1,30},{2,5},{3,4},{4,3},{5,2},{6,9},{7,8},{8,7},{9,6},{10,... | collective-permute-start | bytes 135176 | tf_op jit(solution)/shard_map/ppermute | solution.py:647
  25.3 1.7 %shard_map.152 = (f32[3,2,80,128]{3,2,1,0:T(8,128)S(1)}, f32[80,128]{1,0:T(8,128)S(1)}, f32[80,2048]{1,0:T(8,128)S(1)}, f32[80,2048]{1,0:T(8,128)S(1)}) custom-call(bf16[560,240]{1,0:T(8,128)(2,1)S(1)} %get-tuple-element.31.w_ref, f32[88,2048]{1,0:T(8,128)S(1)} %get-tuple-element.29.m_ref, f32[32,16,128]{2,1,0:T(8,128)S(1)} %all-to-all-done.got_ref), custom_call_target="tpu_custom_call" | custom-call | flops 2000000 | bytes 1000000 | tf_op jit(solution)/shard_map/pallas_call | solution.py:691
  27.0 5.7 %collective-permute-done.3.c_low = f32[1,88,128]{2,1,0:T(8,128)S(1)} collective-permute-done((f32[1,88,128]{2,1,0:T(8,128)S(1)}, f32[1,88,128]{2,1,0:T(8,128)S(1)}, u32[]{:S(2)}, u32[]{:S(2)}) %collective-permute-start.3) | collective-permute-done | bytes 45088 | tf_op jit(solution)/shard_map/ppermute | solution.py:647
  32.7 2.5 %shard_map.153 = (f32[80,2048]{1,0:T(8,128)S(1)}, f32[80,1024]{1,0:T(8,128)S(1)}, f32[80,1024]{1,0:T(8,128)S(1)}) custom-call(bf16[560,240]{1,0:T(8,128)(2,1)S(1)} %get-tuple-element.31.w_ref, f32[88,2048]{1,0:T(8,128)S(1)} %get-tuple-element.29.m_ref, f32[80,2048]{1,0:T(8,128)S(1)} %get-tuple-element.32.f_ref, f32[80,2048]{1,0:T(8,128)S(1)} %get-tuple-element.34.g_ref, ...), custom_call_target="tpu_custom_call" | custom-call | flops 2000000 | bytes 1000000 | tf_op jit(solution)/shard_map/pallas_call | solution.py:695
  35.2 0.7 %shard_map.154 = (f32[80,2048]{1,0:T(8,128)S(1)}, f32[80,1152]{1,0:T(8,128)S(1)}, f32[1,80,512]{2,1,0:T(8,128)S(1)}, f32[1,80,128]{2,1,0:T(8,128)S(1)}, f32[1,80,128]{2,1,0:T(8,128)S(1)}) custom-call(bf16[560,240]{1,0:T(8,128)(2,1)S(1)} %get-tuple-element.31.w_ref, f32[88,2048]{1,0:T(8,128)S(1)} %get-tuple-element.29.m_ref, ...), custom_call_target="tpu_custom_call" | custom-call | flops 2000000 | bytes 1000000 | tf_op jit(solution)/shard_map/pallas_call | solution.py:698
  35.9 1.7 %collective-permute-start.8 = (f32[80,2048]{1,0:T(8,128)S(1)}, f32[80,2048]{1,0:T(8,128)S(1)}, u32[]{:S(2)}, u32[]{:S(2)}) collective-permute-start(f32[80,2048]{1,0:T(8,128)S(1)} %get-tuple-element.43.x_ref), channel_id=1, source_target_pairs={{0,2},{2,0},{4,6},{6,4},{8,10},{10,8},{12,14},{14,12},{16,18},{18,... | collective-permute-start | bytes 1966088 | tf_op jit(solution)/shard_map/ppermute | solution.py:633
  37.6 1.9 %collective-permute-start.7 = (f32[80,1152]{1,0:T(8,128)S(1)}, f32[80,1152]{1,0:T(8,128)S(1)}, u32[]{:S(2)}, u32[]{:S(2)}) collective-permute-start(f32[80,1152]{1,0:T(8,128)S(1)} %get-tuple-element.46), channel_id=1, source_target_pairs={{0,30},{2,4},{4,2},{6,8},{8,6},{10,12},{12,10},{14,16},{16,14},{18... | collective-permute-start | bytes 1105928 | tf_op jit(solution)/shard_map/ppermute | solution.py:633
  39.5 1.1 %collective-permute-start.6 = (f32[1,80,512]{2,1,0:T(8,128)S(1)}, f32[1,80,512]{2,1,0:T(8,128)S(1)}, u32[]{:S(2)}, u32[]{:S(2)}) collective-permute-start(f32[1,80,512]{2,1,0:T(8,128)S(1)} %get-tuple-element.44), channel_id=1, source_target_pairs={{0,1},{1,0},{2,3},{3,2},{4,5},{5,4},{6,7},{7,6},{8,9},{9,8},{10,11... | collective-permute-start | bytes 491528 | tf_op jit(solution)/shard_map/ppermute | solution.py:647
  40.7 2.6 %collective-permute-start.9 = (f32[1,80,128]{2,1,0:T(8,128)S(1)}, f32[1,80,128]{2,1,0:T(8,128)S(1)}, u32[]{:S(2)}, u32[]{:S(2)}) collective-permute-start(f32[1,80,128]{2,1,0:T(8,128)S(1)} %get-tuple-element.47), channel_id=1, source_target_pairs={{0,31},{1,30},{2,5},{3,4},{4,3},{5,2},{6,9},{7,8},{8,7},{9,6},{10,... | collective-permute-start | bytes 122888 | tf_op jit(solution)/shard_map/ppermute | solution.py:647
  43.2 1.9 %collective-permute-done.6.side_ref = f32[1,80,512]{2,1,0:T(8,128)S(1)} collective-permute-done((f32[1,80,512]{2,1,0:T(8,128)S(1)}, f32[1,80,512]{2,1,0:T(8,128)S(1)}, u32[]{:S(2)}, u32[]{:S(2)}) %collective-permute-start.6) | collective-permute-done | bytes 163872 | tf_op jit(solution)/shard_map/ppermute | solution.py:647
  45.2 1.0 %shard_map.155 = (f32[80,2048]{1,0:T(8,128)S(1)}, f32[80,1024]{1,0:T(8,128)}) custom-call(bf16[560,240]{1,0:T(8,128)(2,1)S(1)} %get-tuple-element.31.w_ref, f32[88,2048]{1,0:T(8,128)S(1)} %get-tuple-element.29.m_ref, f32[80,2048]{1,0:T(8,128)S(1)} %get-tuple-element.32.f_ref, f32[80,2048]{1,0:T(8,128)S(1)} %get-tuple-element.43.x_ref, ...), custom_call_target="tpu_custom_call" | custom-call | flops 2000000000 | bytes 1000000 | tf_op jit(solution)/shard_map/pallas_call | solution.py:705
  46.1 2.8 %collective-permute-start.11 = (f32[80,1024]{1,0:T(8,128)}, f32[80,1024]{1,0:T(8,128)S(1)}, u32[]{:S(2)}, u32[]{:S(2)}) collective-permute-start(f32[80,1024]{1,0:T(8,128)} %get-tuple-element.54), channel_id=1, source_target_pairs={{0,30},{2,4},{4,2},{6,8},{8,6},{10,12},{12,10},{14,16},{16,14},{18... | collective-permute-start | bytes 983048 | tf_op jit(solution)/shard_map/ppermute | solution.py:633
  49.0 3.6 %shard_map.156 = (f32[16,8,128]{2,1,0:T(8,128)}, f32[80,1024]{1,0:T(8,128)S(1)}, f32[80,1024]{1,0:T(8,128)S(1)}, f32[80,1024]{1,0:T(8,128)S(1)}, f32[8,1024]{1,0:T(8,128)S(1)}) custom-call(bf16[560,240]{1,0:T(8,128)(2,1)S(1)} %get-tuple-element.31.w_ref, f32[88,2048]{1,0:T(8,128)S(1)} %get-tuple-element.29.m_ref, f32[80,2048]{1,0:T(8,128)S(1)} %get-tuple-element.32.f_ref, ...), custom_call_target="tpu_custom_call" | custom-call | flops 4000000000 | bytes 1000000 | tf_op jit(solution)/shard_map/pallas_call | solution.py:709
  52.5 5.8 %all-to-all-start.1 = ((f32[16,8,128]{2,1,0:T(8,128)}), f32[16,8,128]{2,1,0:T(8,128)S(1)}, u32[]{:S(2)}, u32[]{:S(2)}) async-start(f32[16,8,128]{2,1,0:T(8,128)} %get-tuple-element.55), calls=%async_computation.1 | async-start | bytes 131072 | tf_op jit(solution)/shard_map/all_to_all | solution.py:715
  58.4 1.3 %shard_map.157 = f32[1232,128]{1,0:T(8,128)} custom-call(bf16[80,240]{1,0:T(8,128)(2,1)S(1)} %get-tuple-element.30.w_ref, f32[8,1024]{1,0:T(8,128)S(1)} %get-tuple-element.50.rates_ref, f32[80,1024]{1,0:T(8,128)S(1)} %get-tuple-element.51.n0_ref, f32[80,1024]{1,0:T(8,128)S(1)} %get-tuple-element.52.h0_ref, f32[80,1024]{1,0:T(8,128)S(1)} %get-tuple-element.53.x1_ref, ...), custom_call_target="tpu_custom_call" | custom-call | flops 2000000 | bytes 1000000 | tf_op jit(solution)/shard_map/pallas_call | solution.py:717
  59.7 5.6 %all-to-all-done.1.got_ref = f32[16,8,128]{2,1,0:T(8,128)S(1)} async-done(((f32[16,8,128]{2,1,0:T(8,128)}), f32[16,8,128]{2,1,0:T(8,128)S(1)}, u32[]{:S(2)}, u32[]{:S(2)}) %all-to-all-start.1) | async-done | bytes 65568 | tf_op jit(solution)/shard_map/all_to_all | solution.py:715
  65.3 0.8 %shard_map.158 = f32[7,32,11]{2,1,0:T(8,128)} custom-call(f32[16,8,128]{2,1,0:T(8,128)S(1)} %all-to-all-done.1.got_ref), custom_call_target="tpu_custom_call" | custom-call | flops 2000000 | bytes 1000000 | tf_op jit(solution)/shard_map/pallas_call | solution.py:716
  (48 shorter events, 3.0 us)
Async XLA Ops:
  3.2 1.5 %copy-start.12 = (s32[11,2,8]{0,2,1:T(8,128)S(1)}, s32[11,2,8]{0,2,1:T(8,128)}, u32[]{:S(2)}) copy-start(s32[11,2,8]{0,2,1:T(8,128)} %param.22) | copy-start | bytes 2116
  3.2 2.3 %copy-start.3 = (f32[11,7,4,8]{0,3,2,1:T(8,128)S(1)}, f32[11,7,4,8]{0,3,2,1:T(8,128)}, u32[]{:S(2)}) copy-start(f32[11,7,4,8]{0,3,2,1:T(8,128)} %param.21) | copy-start | bytes 29572
  4.2 13.6 %collective-permute-start = (f32[88,2048]{1,0:T(8,128)S(1)}, f32[88,2048]{1,0:T(8,128)S(1)}, u32[]{:S(2)}, u32[]{:S(2)}) collective-permute-start(f32[88,2048]{1,0:T(8,128)S(1)} %get-tuple-element.29.m_ref), channel_id=1, source_target_pairs={{0,2},{2,0},{4,6},{6,4},{8,10},{10,8},{12,14},{14,12},{16,18},{18,... | collective-permute-start | bytes 2162696 | tf_op jit(solution)/shard_map/ppermute | solution.py:633
  6.4 11.4 %copy-start.4 = (f32[80,240]{1,0:T(8,128)S(1)}, f32[80,240]{1,0:T(8,128)}, u32[]{:S(2)}) copy-start(f32[80,240]{1,0:T(8,128)} %constant.16.clone.diagonal_ref) | copy-start | bytes 230404
  6.4 11.4 %copy-start.5 = (f32[80,7]{1,0:T(8,128)S(1)}, f32[80,7]{1,0:T(8,128)}, u32[]{:S(2)}) copy-start(f32[80,7]{1,0:T(8,128)} %constant.14.clone.rows_ref) | copy-start | bytes 6724
  6.4 11.4 %copy-start.6 = (bf16[80,240]{1,0:T(8,128)(2,1)S(1)}, bf16[80,240]{1,0:T(8,128)(2,1)}, u32[]{:S(2)}) copy-start(bf16[80,240]{1,0:T(8,128)(2,1)} %constant.13.clone.spectral_ref) | copy-start | bytes 115204
  6.4 11.4 %copy-start.7 = (f32[3,7,7]{2,1,0:T(8,128)S(1)}, f32[3,7,7]{2,1,0:T(8,128)}, u32[]{:S(2)}) copy-start(f32[3,7,7]{2,1,0:T(8,128)} %up_ref.1) | copy-start | bytes 1768
  6.4 11.4 %copy-start.8 = (f32[3,7,7]{2,1,0:T(8,128)S(1)}, f32[3,7,7]{2,1,0:T(8,128)}, u32[]{:S(2)}) copy-start(f32[3,7,7]{2,1,0:T(8,128)} %down_ref.1) | copy-start | bytes 1768
  6.4 11.4 %copy-start.9 = (f32[7,240]{1,0:T(8,128)S(1)}, f32[7,240]{1,0:T(8,128)}, u32[]{:S(2)}) copy-start(f32[7,240]{1,0:T(8,128)} %constant.15.clone.lanes_ref) | copy-start | bytes 20164
  6.4 18.8 %all-to-all-start = ((f32[32,16,128]{2,1,0:T(8,128)}), f32[32,16,128]{2,1,0:T(8,128)S(1)}, u32[]{:S(2)}, u32[]{:S(2)}) async-start(f32[32,16,128]{2,1,0:T(8,128)} %shard_map.151), calls=%async_computation | async-start | bytes 524288 | tf_op jit(solution)/shard_map/all_to_all | solution.py:672
  13.4 19.2 %collective-permute-start.1 = (f32[88,1024]{1,0:T(8,128)S(1)}, f32[88,1024]{1,0:T(8,128)S(1)}, u32[]{:S(2)}, u32[]{:S(2)}) collective-permute-start(f32[88,1024]{1,0:T(8,128)S(1)} %get-tuple-element.33), channel_id=1, source_target_pairs={{0,30},{2,4},{4,2},{6,8},{8,6},{10,12},{12,10},{14,16},{16,14},{18... | collective-permute-start | bytes 1081352 | tf_op jit(solution)/shard_map/ppermute | solution.py:633
  19.6 15.5 %collective-permute-start.5 = (f32[80,1024]{1,0:T(8,128)}, f32[80,1024]{1,0:T(8,128)S(1)}, u32[]{:S(2)}, u32[]{:S(2)}) collective-permute-start(f32[80,1024]{1,0:T(8,128)} %get-tuple-element.42), channel_id=1, source_target_pairs={{0,30},{2,4},{4,2},{6,8},{8,6},{10,12},{12,10},{14,16},{16,14},{18... | collective-permute-start | bytes 983048 | tf_op jit(solution)/shard_map/ppermute | solution.py:633
  19.8 12.9 %collective-permute-start.2 = (f32[1,88,512]{2,1,0:T(8,128)}, f32[1,88,512]{2,1,0:T(8,128)S(1)}, u32[]{:S(2)}, u32[]{:S(2)}) collective-permute-start(f32[1,88,512]{2,1,0:T(8,128)} %get-tuple-element.35), channel_id=1, source_target_pairs={{0,1},{1,0},{2,3},{3,2},{4,5},{5,4},{6,7},{7,6},{8,9},{9,8},{10,11... | collective-permute-start | bytes 540680 | tf_op jit(solution)/shard_map/ppermute | solution.py:647
  21.6 11.1 %collective-permute-start.3 = (f32[1,88,128]{2,1,0:T(8,128)S(1)}, f32[1,88,128]{2,1,0:T(8,128)S(1)}, u32[]{:S(2)}, u32[]{:S(2)}) collective-permute-start(f32[1,88,128]{2,1,0:T(8,128)S(1)} %get-tuple-element.36), channel_id=1, source_target_pairs={{0,31},{1,30},{2,5},{3,4},{4,3},{5,2},{6,9},{7,8},{8,7},{9,6},{10,... | collective-permute-start | bytes 135176 | tf_op jit(solution)/shard_map/ppermute | solution.py:647
  25.3 7.4 %collective-permute-start.4 = (f32[1,88,128]{2,1,0:T(8,128)S(1)}, f32[1,88,128]{2,1,0:T(8,128)S(1)}, u32[]{:S(2)}, u32[]{:S(2)}) collective-permute-start(f32[1,88,128]{2,1,0:T(8,128)S(1)} %get-tuple-element.37), channel_id=1, source_target_pairs={{0,3},{1,2},{2,1},{3,0},{4,7},{5,6},{6,5},{7,4},{8,11},{9,10},{10,... | collective-permute-start | bytes 135176 | tf_op jit(solution)/shard_map/ppermute | solution.py:647
  32.6 2.5 %copy-start.1 = (f32[1,88,512]{2,1,0:T(8,128)}, f32[1,88,512]{2,1,0:T(8,128)S(1)}, u32[]{:S(2)}) copy-start(f32[1,88,512]{2,1,0:T(8,128)S(1)} %collective-permute-done.2.side_ref.side_first) | copy-start | bytes 540676
  35.9 13.0 %collective-permute-start.8 = (f32[80,2048]{1,0:T(8,128)S(1)}, f32[80,2048]{1,0:T(8,128)S(1)}, u32[]{:S(2)}, u32[]{:S(2)}) collective-permute-start(f32[80,2048]{1,0:T(8,128)S(1)} %get-tuple-element.43.x_ref), channel_id=1, source_target_pairs={{0,2},{2,0},{4,6},{6,4},{8,10},{10,8},{12,14},{14,12},{16,18},{18,... | collective-permute-start | bytes 1966088 | tf_op jit(solution)/shard_map/ppermute | solution.py:633
  37.6 11.4 %collective-permute-start.7 = (f32[80,1152]{1,0:T(8,128)S(1)}, f32[80,1152]{1,0:T(8,128)S(1)}, u32[]{:S(2)}, u32[]{:S(2)}) collective-permute-start(f32[80,1152]{1,0:T(8,128)S(1)} %get-tuple-element.46), channel_id=1, source_target_pairs={{0,30},{2,4},{4,2},{6,8},{8,6},{10,12},{12,10},{14,16},{16,14},{18... | collective-permute-start | bytes 1105928 | tf_op jit(solution)/shard_map/ppermute | solution.py:633
  39.5 5.6 %collective-permute-start.6 = (f32[1,80,512]{2,1,0:T(8,128)S(1)}, f32[1,80,512]{2,1,0:T(8,128)S(1)}, u32[]{:S(2)}, u32[]{:S(2)}) collective-permute-start(f32[1,80,512]{2,1,0:T(8,128)S(1)} %get-tuple-element.44), channel_id=1, source_target_pairs={{0,1},{1,0},{2,3},{3,2},{4,5},{5,4},{6,7},{7,6},{8,9},{9,8},{10,11... | collective-permute-start | bytes 491528 | tf_op jit(solution)/shard_map/ppermute | solution.py:647
  40.7 8.3 %collective-permute-start.9 = (f32[1,80,128]{2,1,0:T(8,128)S(1)}, f32[1,80,128]{2,1,0:T(8,128)S(1)}, u32[]{:S(2)}, u32[]{:S(2)}) collective-permute-start(f32[1,80,128]{2,1,0:T(8,128)S(1)} %get-tuple-element.47), channel_id=1, source_target_pairs={{0,31},{1,30},{2,5},{3,4},{4,3},{5,2},{6,9},{7,8},{8,7},{9,6},{10,... | collective-permute-start | bytes 122888 | tf_op jit(solution)/shard_map/ppermute | solution.py:647
  43.2 5.7 %copy-start.2 = (f32[1,88,512]{2,1,0:T(8,128)S(1)}, f32[1,88,512]{2,1,0:T(8,128)}, u32[]{:S(2)}) copy-start(f32[1,88,512]{2,1,0:T(8,128)} %copy-done.1) | copy-start | bytes 540676
  43.2 5.7 %collective-permute-start.10 = (f32[1,80,128]{2,1,0:T(8,128)S(1)}, f32[1,80,128]{2,1,0:T(8,128)S(1)}, u32[]{:S(2)}, u32[]{:S(2)}) collective-permute-start(f32[1,80,128]{2,1,0:T(8,128)S(1)} %get-tuple-element.48), channel_id=1, source_target_pairs={{0,3},{1,2},{2,1},{3,0},{4,7},{5,6},{6,5},{7,4},{8,11},{9,10},{10,... | collective-permute-start | bytes 122888 | tf_op jit(solution)/shard_map/ppermute | solution.py:647
  46.1 12.2 %collective-permute-start.11 = (f32[80,1024]{1,0:T(8,128)}, f32[80,1024]{1,0:T(8,128)S(1)}, u32[]{:S(2)}, u32[]{:S(2)}) collective-permute-start(f32[80,1024]{1,0:T(8,128)} %get-tuple-element.54), channel_id=1, source_target_pairs={{0,30},{2,4},{4,2},{6,8},{8,6},{10,12},{12,10},{14,16},{16,14},{18... | collective-permute-start | bytes 983048 | tf_op jit(solution)/shard_map/ppermute | solution.py:633
  52.5 12.7 %all-to-all-start.1 = ((f32[16,8,128]{2,1,0:T(8,128)}), f32[16,8,128]{2,1,0:T(8,128)S(1)}, u32[]{:S(2)}, u32[]{:S(2)}) async-start(f32[16,8,128]{2,1,0:T(8,128)} %get-tuple-element.55), calls=%async_computation.1 | async-start | bytes 131072 | tf_op jit(solution)/shard_map/all_to_all | solution.py:715
  (4 other events, 3.2 us)

commit v4 on v3

--- a/solution.py
+++ b/solution.py
@@ -406,9 +406,8 @@
                     c_refs[a][n] = end
 
 
-def stack_matrices(plan, m_ref, high_ref, up_ref, down_ref, spectral_ref, rows_ref, lanes_ref, diagonal_ref, out_ref, down_out, far_ref):
+def stack_matrices(plan, up_ref, down_ref, spectral_ref, rows_ref, lanes_ref, diagonal_ref, out_ref, down_out):
     pad = plan.pad
-    far_ref[...] = m_ref[:pad, plan.slab :] + 0.0 * high_ref[0:1, 0:1]
     lane = lax.broadcasted_iota(jnp.int32, (pad, 3 * pad), 1)
     second = (lane >= pad) & (lane < 2 * pad)
     out_ref[SPECTRAL * pad : (SPECTRAL + 1) * pad, :] = spectral_ref[...]
@@ -421,6 +420,10 @@
         hi = full.astype(jnp.bfloat16).astype(jnp.float32)
         out_ref[block * pad : (block + 1) * pad, :] = jnp.where(second, full - hi, hi).astype(jnp.bfloat16)
     down_out[...] = matrix(plan, out_ref, DOWN_AZ)
+
+
+def hold_far(plan, m_ref, low_ref, high_ref, far_ref):
+    far_ref[...] = m_ref[: plan.pad, plan.slab :] + 0.0 * (low_ref[0:1, 0:1] + high_ref[0:1, 0:1])
 
 
 def send_panels(plan, stator_ref, both_ref, out_ref, panels_ref):
@@ -682,11 +685,11 @@
     low_first, high_first = swap(near, next_chip), swap(m, next_core)
     side_first = beside(plan, side, alone)
     c_low, c_high = beside(plan, c0, next_chip), beside(plan, c1, next_core)
-    matrices, down, far = call(
+    far_low = swap(call(bind(hold_far, plan), half)(m, low_first, high_first), next_chip)
+    matrices, down = call(
         bind(stack_matrices, plan),
-        [jax.ShapeDtypeStruct((count * pad, 3 * pad), jnp.bfloat16) for count in (7, 1)] + [half],
-    )(m, high_first, jac_up, jac_down, plan.spectral(), plan.field_rows(), plan.field_lanes(), plan.block_diagonal())
-    far_low = swap(far, next_chip)
+        [jax.ShapeDtypeStruct((count * pad, 3 * pad), jnp.bfloat16) for count in (7, 1)],
+    )(jac_up, jac_down, plan.spectral(), plan.field_rows(), plan.field_lanes(), plan.block_diagonal())
     tiles = len(plan.tiles)
     seams, weight, force, g = call(
         bind(begin, plan), (f32(3, 1 + ends, pad, LANES), f32(pad, LANES), whole, whole),

time: 66.5 us -> 63.8 us (0.959)
  starting transfers between devices: 33.4 us -> 30.8 us
    all_to_all x1, starting transfers between devices: 6.97 us -> 2.59 us  [on_device(): got = lax.all_to_all(sent, AXES, 0, 0, tiled=True)]
    ppermute x6, starting transfers between devices: 11.4 us -> 14.8 us  [swap(): return lax.ppermute(array, 'sector', list(enumerate(partner)))]
    ppermute x6, waiting for transfers between devices: 7.63 us -> 4.23 us  [beside(): return lax.ppermute(array, AXES, pairs(0))]
    all_to_all x1, waiting for transfers between devices: 0.01 us -> 3.06 us  [on_device(): got = lax.all_to_all(sent, AXES, 0, 0, tiled=True)]
    ppermute x6, starting transfers between devices: 9.18 us -> 7.13 us  [beside(): return lax.ppermute(array, AXES, pairs(0))]
    ppermute x6, waiting for transfers between devices: 0.02 us -> 0.83 us  [swap(): return lax.ppermute(array, 'sector', list(enumerate(partner)))]
    pallas_call x1, Pallas kernels: 1.8 us -> 1.12 us  [on_device(): call(bind(stack_matrices, plan), [jax.ShapeDtypeStruct((count * pad, 3 *...]
  transfers between devices with their start and end apart: 14 -> 14, of which waited for: 3 -> 6; matrix products, arithmetic and copies ran while one was open for 0% -> 0% of each run, Pallas kernels for 19% -> 19%
where the time goes in v4:
time: 63.8 us; the launch traced here: 63.4 us
  starting transfers between devices  30.8 us (48%)
  Pallas kernels  14.6 us (23%)
  waiting for transfers between devices  13.7 us (21%)
  local copies, waits for them, and re-layouts  1.91 us (3%)
  other arithmetic  1.54 us (2%)
  between operations  0.83 us (1%)
    ppermute x6, starting transfers between devices, swap(): return lax.ppermute(array, 'sector', list(enumerate(partner)))  14.8 us
    ppermute x6, starting transfers between devices, beside(): return lax.ppermute(array, AXES, pairs(0))  7.13 us
    all_to_all x1, starting transfers between devices, on_device(): returned = lax.all_to_all(back, 'sector', 0, 0, tiled=True)  6.33 us
    all_to_all x1, waiting for transfers between devices, on_device(): returned = lax.all_to_all(back, 'sector', 0, 0, tiled=True)  5.58 us
    ppermute x6, waiting for transfers between devices, beside(): return lax.ppermute(array, AXES, pairs(0))  4.23 us
    pallas_call x1, Pallas kernels, on_device(): call(bind(middle, plan), (f32(sectors, RATES, LANES), half, half, half, f...  3.52 us
    all_to_all x1, waiting for transfers between devices, on_device(): got = lax.all_to_all(sent, AXES, 0, 0, tiled=True)  3.06 us
    all_to_all x1, starting transfers between devices, on_device(): got = lax.all_to_all(sent, AXES, 0, 0, tiled=True)  2.59 us
  transfers between devices with their start and end apart: 14, of which 6 were waited for; matrix products, arithmetic and copies ran while one was open for 0% of the time, Pallas kernels for 19%

profile of v4, /device:TPU:0, one launch (start us, length us, event | category | flops | bytes accessed | tf_op | source)
XLA Modules:
  0.0 63.4 jit_solution(17525530478624215555)
XLA Ops:
  2.1 1.1 %copy-done = f32[11,7,2,8,128]{4,3,2,1,0:T(8,128)S(1)} copy-done((f32[11,7,2,8,128]{4,3,2,1,0:T(8,128)S(1)}, f32[11,7,2,8,128]{4,3,2,1,0:T(8,128)}, u32[]{:S(2)}) %copy-start) | copy-done | bytes 630808
  3.2 1.0 %shard_map.150 = (f32[88,2048]{1,0:T(8,128)S(1)}, f32[88,1024]{1,0:T(8,128)S(1)}, f32[1,88,512]{2,1,0:T(8,128)}, f32[1,88,128]{2,1,0:T(8,128)S(1)}, f32[1,88,128]{2,1,0:T(8,128)S(1)}) custom-call(f32[1232,128]{1,0:T(8,128)S(1)} %bitcast.16, f32[96,128]{1,0:T(8,128)S(1)} %pad_maximum_fusion.coef_ref), custom_call_target="tpu_custom_call" | custom-call | flops 2000000 | bytes 1000000 | tf_op jit(solution)/shard_map/pallas_call | solution.py:676
  4.6 5.7 %collective-permute-start = (f32[88,1024]{1,0:T(8,128)S(1)}, f32[88,1024]{1,0:T(8,128)S(1)}, u32[]{:S(2)}, u32[]{:S(2)}) collective-permute-start(f32[88,1024]{1,0:T(8,128)S(1)} %get-tuple-element.32), channel_id=1, source_target_pairs={{0,30},{2,4},{4,2},{6,8},{8,6},{10,12},{12,10},{14,16},{16,14},{18... | collective-permute-start | bytes 1081352 | tf_op jit(solution)/shard_map/ppermute | solution.py:636
  11.2 0.9 %shard_map.151 = f32[32,16,128]{2,1,0:T(8,128)} custom-call(f32[7,32,11]{2,1,0:T(8,128)S(1)} %bitcast.17, f32[11,32]{1,0:T(8,128)S(1)} %pad_maximum_fusion.1.both_ref), custom_call_target="tpu_custom_call" | custom-call | flops 2000000 | bytes 1000000 | tf_op jit(solution)/shard_map/pallas_call | solution.py:669
  12.1 2.6 %all-to-all-start = ((f32[32,16,128]{2,1,0:T(8,128)}), f32[32,16,128]{2,1,0:T(8,128)S(1)}, u32[]{:S(2)}, u32[]{:S(2)}) async-start(f32[32,16,128]{2,1,0:T(8,128)} %shard_map.151), calls=%async_computation | async-start | bytes 524288 | tf_op jit(solution)/shard_map/all_to_all | solution.py:675
  14.7 0.8 %collective-permute-done.low_ref.low_first = f32[88,1024]{1,0:T(8,128)S(1)} collective-permute-done((f32[88,1024]{1,0:T(8,128)S(1)}, f32[88,1024]{1,0:T(8,128)S(1)}, u32[]{:S(2)}, u32[]{:S(2)}) %collective-permute-start) | collective-permute-done | bytes 360480 | tf_op jit(solution)/shard_map/ppermute | solution.py:636
  15.6 4.5 %collective-permute-start.5 = (f32[80,1024]{1,0:T(8,128)S(1)}, f32[80,1024]{1,0:T(8,128)S(1)}, u32[]{:S(2)}, u32[]{:S(2)}) collective-permute-start(f32[80,1024]{1,0:T(8,128)S(1)} %shard_map.154), channel_id=1, source_target_pairs={{0,30},{2,4},{4,2},{6,8},{8,6},{10,12},{12,10},{14,16},{16,14},{18... | collective-permute-start | bytes 983048 | tf_op jit(solution)/shard_map/ppermute | solution.py:636
  20.1 1.5 %collective-permute-start.2 = (f32[1,88,512]{2,1,0:T(8,128)}, f32[1,88,512]{2,1,0:T(8,128)S(1)}, u32[]{:S(2)}, u32[]{:S(2)}) collective-permute-start(f32[1,88,512]{2,1,0:T(8,128)} %get-tuple-element.34), channel_id=1, source_target_pairs={{0,1},{1,0},{2,3},{3,2},{4,5},{5,4},{6,7},{7,6},{8,9},{9,8},{10,11... | collective-permute-start | bytes 540680 | tf_op jit(solution)/shard_map/ppermute | solution.py:650
  21.7 1.1 %shard_map.149 = (bf16[560,240]{1,0:T(8,128)(2,1)S(1)}, bf16[80,240]{1,0:T(8,128)(2,1)S(1)}) custom-call(f32[3,7,7]{2,1,0:T(8,128)S(1)} %copy-done.7, f32[3,7,7]{2,1,0:T(8,128)S(1)} %copy-done.8, bf16[80,240]{1,0:T(8,128)(2,1)S(1)} %copy-done.6, f32[80,7]{1,0:T(8,128)S(1)} %copy-done.5, f32[7,240]{1,0:T(8,128)S(1)} %copy-done.9, f32[80,240]{1,0:T(8,128)S(1)} %copy-done.4), custom_call_target="tpu_custom_call" | custom-call | flops 2000000 | bytes 1000000 | tf_op jit(solution)/shard_map/pallas_call | solution.py:689
  22.8 3.1 %all-to-all-done.got_ref = f32[32,16,128]{2,1,0:T(8,128)S(1)} async-done(((f32[32,16,128]{2,1,0:T(8,128)}), f32[32,16,128]{2,1,0:T(8,128)S(1)}, u32[]{:S(2)}, u32[]{:S(2)}) %all-to-all-start) | async-done | bytes 262176 | tf_op jit(solution)/shard_map/all_to_all | solution.py:675
  25.9 1.7 %shard_map.152 = (f32[3,2,80,128]{3,2,1,0:T(8,128)S(1)}, f32[80,128]{1,0:T(8,128)S(1)}, f32[80,2048]{1,0:T(8,128)S(1)}, f32[80,2048]{1,0:T(8,128)S(1)}) custom-call(bf16[560,240]{1,0:T(8,128)(2,1)S(1)} %get-tuple-element.29.w_ref, f32[88,2048]{1,0:T(8,128)S(1)} %get-tuple-element.30.m_ref, f32[32,16,128]{2,1,0:T(8,128)S(1)} %all-to-all-done.got_ref), custom_call_target="tpu_custom_call" | custom-call | flops 2000000 | bytes 1000000 | tf_op jit(solution)/shard_map/pallas_call | solution.py:694
  27.6 2.4 %collective-permute-done.3.c_low = f32[1,88,128]{2,1,0:T(8,128)S(1)} collective-permute-done((f32[1,88,128]{2,1,0:T(8,128)S(1)}, f32[1,88,128]{2,1,0:T(8,128)S(1)}, u32[]{:S(2)}, u32[]{:S(2)}) %collective-permute-start.3) | collective-permute-done | bytes 45088 | tf_op jit(solution)/shard_map/ppermute | solution.py:650
  29.9 2.5 %shard_map.153 = (f32[80,2048]{1,0:T(8,128)S(1)}, f32[80,1024]{1,0:T(8,128)S(1)}, f32[80,1024]{1,0:T(8,128)S(1)}) custom-call(bf16[560,240]{1,0:T(8,128)(2,1)S(1)} %get-tuple-element.29.w_ref, f32[88,2048]{1,0:T(8,128)S(1)} %get-tuple-element.30.m_ref, f32[80,2048]{1,0:T(8,128)S(1)} %get-tuple-element.31.f_ref, f32[80,2048]{1,0:T(8,128)S(1)} %get-tuple-element.33.g_ref, ...), custom_call_target="tpu_custom_call" | custom-call | flops 2000000 | bytes 1000000 | tf_op jit(solution)/shard_map/pallas_call | solution.py:698
  33.2 1.8 %collective-permute-start.8 = (f32[80,2048]{1,0:T(8,128)S(1)}, f32[80,2048]{1,0:T(8,128)S(1)}, u32[]{:S(2)}, u32[]{:S(2)}) collective-permute-start(f32[80,2048]{1,0:T(8,128)S(1)} %get-tuple-element.41.x_ref), channel_id=1, source_target_pairs={{0,2},{2,0},{4,6},{6,4},{8,10},{10,8},{12,14},{14,12},{16,18},{18,... | collective-permute-start | bytes 1966088 | tf_op jit(solution)/shard_map/ppermute | solution.py:636
  34.9 1.0 %collective-permute-start.6 = (f32[1,80,512]{2,1,0:T(8,128)S(1)}, f32[1,80,512]{2,1,0:T(8,128)S(1)}, u32[]{:S(2)}, u32[]{:S(2)}) collective-permute-start(f32[1,80,512]{2,1,0:T(8,128)S(1)} %get-tuple-element.42), channel_id=1, source_target_pairs={{0,1},{1,0},{2,3},{3,2},{4,5},{5,4},{6,7},{7,6},{8,9},{9,8},{10,11... | collective-permute-start | bytes 491528 | tf_op jit(solution)/shard_map/ppermute | solution.py:650
  35.9 4.6 %collective-permute-start.9 = (f32[1,80,128]{2,1,0:T(8,128)S(1)}, f32[1,80,128]{2,1,0:T(8,128)S(1)}, u32[]{:S(2)}, u32[]{:S(2)}) collective-permute-start(f32[1,80,128]{2,1,0:T(8,128)S(1)} %get-tuple-element.45), channel_id=1, source_target_pairs={{0,31},{1,30},{2,5},{3,4},{4,3},{5,2},{6,9},{7,8},{8,7},{9,6},{10,... | collective-permute-start | bytes 122888 | tf_op jit(solution)/shard_map/ppermute | solution.py:650
  40.6 1.2 %collective-permute-done.6.side_ref = f32[1,80,512]{2,1,0:T(8,128)S(1)} collective-permute-done((f32[1,80,512]{2,1,0:T(8,128)S(1)}, f32[1,80,512]{2,1,0:T(8,128)S(1)}, u32[]{:S(2)}, u32[]{:S(2)}) %collective-permute-start.6) | collective-permute-done | bytes 163872 | tf_op jit(solution)/shard_map/ppermute | solution.py:650
  41.8 1.0 %shard_map.156 = (f32[80,2048]{1,0:T(8,128)S(1)}, f32[80,1024]{1,0:T(8,128)}) custom-call(bf16[560,240]{1,0:T(8,128)(2,1)S(1)} %get-tuple-element.29.w_ref, f32[88,2048]{1,0:T(8,128)S(1)} %get-tuple-element.30.m_ref, f32[80,2048]{1,0:T(8,128)S(1)} %get-tuple-element.31.f_ref, f32[80,2048]{1,0:T(8,128)S(1)} %get-tuple-element.41.x_ref, ...), custom_call_target="tpu_custom_call" | custom-call | flops 2000000000 | bytes 1000000 | tf_op jit(solution)/shard_map/pallas_call | solution.py:708
  42.8 2.4 %collective-permute-start.11 = (f32[80,1024]{1,0:T(8,128)}, f32[80,1024]{1,0:T(8,128)S(1)}, u32[]{:S(2)}, u32[]{:S(2)}) collective-permute-start(f32[80,1024]{1,0:T(8,128)} %get-tuple-element.52), channel_id=1, source_target_pairs={{0,30},{2,4},{4,2},{6,8},{8,6},{10,12},{12,10},{14,16},{16,14},{18... | collective-permute-start | bytes 983048 | tf_op jit(solution)/shard_map/ppermute | solution.py:636
  45.8 3.5 %shard_map.157 = (f32[16,8,128]{2,1,0:T(8,128)}, f32[80,1024]{1,0:T(8,128)S(1)}, f32[80,1024]{1,0:T(8,128)S(1)}, f32[80,1024]{1,0:T(8,128)S(1)}, f32[8,1024]{1,0:T(8,128)S(1)}) custom-call(bf16[560,240]{1,0:T(8,128)(2,1)S(1)} %get-tuple-element.29.w_ref, f32[88,2048]{1,0:T(8,128)S(1)} %get-tuple-element.30.m_ref, f32[80,2048]{1,0:T(8,128)S(1)} %get-tuple-element.31.f_ref, ...), custom_call_target="tpu_custom_call" | custom-call | flops 4000000000 | bytes 1000000 | tf_op jit(solution)/shard_map/pallas_call | solution.py:712
  49.3 6.3 %all-to-all-start.1 = ((f32[16,8,128]{2,1,0:T(8,128)}), f32[16,8,128]{2,1,0:T(8,128)S(1)}, u32[]{:S(2)}, u32[]{:S(2)}) async-start(f32[16,8,128]{2,1,0:T(8,128)} %get-tuple-element.53), calls=%async_computation.1 | async-start | bytes 131072 | tf_op jit(solution)/shard_map/all_to_all | solution.py:718
  55.7 1.3 %shard_map.158 = f32[1232,128]{1,0:T(8,128)} custom-call(bf16[80,240]{1,0:T(8,128)(2,1)S(1)} %get-tuple-element.28.w_ref, f32[8,1024]{1,0:T(8,128)S(1)} %get-tuple-element.48.rates_ref, f32[80,1024]{1,0:T(8,128)S(1)} %get-tuple-element.49.n0_ref, f32[80,1024]{1,0:T(8,128)S(1)} %get-tuple-element.50.h0_ref, f32[80,1024]{1,0:T(8,128)S(1)} %get-tuple-element.51.x1_ref, ...), custom_call_target="tpu_custom_call" | custom-call | flops 2000000 | bytes 1000000 | tf_op jit(solution)/shard_map/pallas_call | solution.py:720
  57.0 5.6 %all-to-all-done.1.got_ref = f32[16,8,128]{2,1,0:T(8,128)S(1)} async-done(((f32[16,8,128]{2,1,0:T(8,128)}), f32[16,8,128]{2,1,0:T(8,128)S(1)}, u32[]{:S(2)}, u32[]{:S(2)}) %all-to-all-start.1) | async-done | bytes 65568 | tf_op jit(solution)/shard_map/all_to_all | solution.py:718
  62.6 0.8 %shard_map.159 = f32[7,32,11]{2,1,0:T(8,128)} custom-call(f32[16,8,128]{2,1,0:T(8,128)S(1)} %all-to-all-done.1.got_ref), custom_call_target="tpu_custom_call" | custom-call | flops 2000000 | bytes 1000000 | tf_op jit(solution)/shard_map/pallas_call | solution.py:719
  (49 shorter events, 4.3 us)
Async XLA Ops:
  3.2 7.1 %copy-start.12 = (s32[11,2,8]{0,2,1:T(8,128)S(1)}, s32[11,2,8]{0,2,1:T(8,128)}, u32[]{:S(2)}) copy-start(s32[11,2,8]{0,2,1:T(8,128)} %param.22) | copy-start | bytes 2116
  3.2 8.0 %copy-start.3 = (f32[11,7,4,8]{0,3,2,1:T(8,128)S(1)}, f32[11,7,4,8]{0,3,2,1:T(8,128)}, u32[]{:S(2)}) copy-start(f32[11,7,4,8]{0,3,2,1:T(8,128)} %param.21) | copy-start | bytes 29572
  4.2 11.3 %collective-permute-start.1 = (f32[88,2048]{1,0:T(8,128)S(1)}, f32[88,2048]{1,0:T(8,128)S(1)}, u32[]{:S(2)}, u32[]{:S(2)}) collective-permute-start(f32[88,2048]{1,0:T(8,128)S(1)} %get-tuple-element.30.m_ref), channel_id=1, source_target_pairs={{0,2},{2,0},{4,6},{6,4},{8,10},{10,8},{12,14},{14,12},{16,18},{18,... | collective-permute-start | bytes 2162696 | tf_op jit(solution)/shard_map/ppermute | solution.py:636
  4.6 10.9 %collective-permute-start = (f32[88,1024]{1,0:T(8,128)S(1)}, f32[88,1024]{1,0:T(8,128)S(1)}, u32[]{:S(2)}, u32[]{:S(2)}) collective-permute-start(f32[88,1024]{1,0:T(8,128)S(1)} %get-tuple-element.32), channel_id=1, source_target_pairs={{0,30},{2,4},{4,2},{6,8},{8,6},{10,12},{12,10},{14,16},{16,14},{18... | collective-permute-start | bytes 1081352 | tf_op jit(solution)/shard_map/ppermute | solution.py:636
  12.1 13.8 %all-to-all-start = ((f32[32,16,128]{2,1,0:T(8,128)}), f32[32,16,128]{2,1,0:T(8,128)S(1)}, u32[]{:S(2)}, u32[]{:S(2)}) async-start(f32[32,16,128]{2,1,0:T(8,128)} %shard_map.151), calls=%async_computation | async-start | bytes 524288 | tf_op jit(solution)/shard_map/all_to_all | solution.py:675
  14.7 7.0 %copy-start.4 = (f32[80,240]{1,0:T(8,128)S(1)}, f32[80,240]{1,0:T(8,128)}, u32[]{:S(2)}) copy-start(f32[80,240]{1,0:T(8,128)} %constant.16.clone.diagonal_ref) | copy-start | bytes 230404
  14.7 7.0 %copy-start.5 = (f32[80,7]{1,0:T(8,128)S(1)}, f32[80,7]{1,0:T(8,128)}, u32[]{:S(2)}) copy-start(f32[80,7]{1,0:T(8,128)} %constant.14.clone.rows_ref) | copy-start | bytes 6724
  14.7 7.0 %copy-start.6 = (bf16[80,240]{1,0:T(8,128)(2,1)S(1)}, bf16[80,240]{1,0:T(8,128)(2,1)}, u32[]{:S(2)}) copy-start(bf16[80,240]{1,0:T(8,128)(2,1)} %constant.13.clone.spectral_ref) | copy-start | bytes 115204
  15.5 6.2 %copy-start.7 = (f32[3,7,7]{2,1,0:T(8,128)S(1)}, f32[3,7,7]{2,1,0:T(8,128)}, u32[]{:S(2)}) copy-start(f32[3,7,7]{2,1,0:T(8,128)} %up_ref.1) | copy-start | bytes 1768
  15.5 6.2 %copy-start.8 = (f32[3,7,7]{2,1,0:T(8,128)S(1)}, f32[3,7,7]{2,1,0:T(8,128)}, u32[]{:S(2)}) copy-start(f32[3,7,7]{2,1,0:T(8,128)} %down_ref.1) | copy-start | bytes 1768
  15.5 6.2 %copy-start.9 = (f32[7,240]{1,0:T(8,128)S(1)}, f32[7,240]{1,0:T(8,128)}, u32[]{:S(2)}) copy-start(f32[7,240]{1,0:T(8,128)} %constant.15.clone.lanes_ref) | copy-start | bytes 20164
  15.6 16.8 %collective-permute-start.5 = (f32[80,1024]{1,0:T(8,128)S(1)}, f32[80,1024]{1,0:T(8,128)S(1)}, u32[]{:S(2)}, u32[]{:S(2)}) collective-permute-start(f32[80,1024]{1,0:T(8,128)S(1)} %shard_map.154), channel_id=1, source_target_pairs={{0,30},{2,4},{4,2},{6,8},{8,6},{10,12},{12,10},{14,16},{16,14},{18... | collective-permute-start | bytes 983048 | tf_op jit(solution)/shard_map/ppermute | solution.py:636
  20.1 9.8 %collective-permute-start.2 = (f32[1,88,512]{2,1,0:T(8,128)}, f32[1,88,512]{2,1,0:T(8,128)S(1)}, u32[]{:S(2)}, u32[]{:S(2)}) collective-permute-start(f32[1,88,512]{2,1,0:T(8,128)} %get-tuple-element.34), channel_id=1, source_target_pairs={{0,1},{1,0},{2,3},{3,2},{4,5},{5,4},{6,7},{7,6},{8,9},{9,8},{10,11... | collective-permute-start | bytes 540680 | tf_op jit(solution)/shard_map/ppermute | solution.py:650
  21.6 8.3 %collective-permute-start.3 = (f32[1,88,128]{2,1,0:T(8,128)S(1)}, f32[1,88,128]{2,1,0:T(8,128)S(1)}, u32[]{:S(2)}, u32[]{:S(2)}) collective-permute-start(f32[1,88,128]{2,1,0:T(8,128)S(1)} %get-tuple-element.35), channel_id=1, source_target_pairs={{0,31},{1,30},{2,5},{3,4},{4,3},{5,2},{6,9},{7,8},{8,7},{9,6},{10,... | collective-permute-start | bytes 135176 | tf_op jit(solution)/shard_map/ppermute | solution.py:650
  21.6 8.3 %collective-permute-start.4 = (f32[1,88,128]{2,1,0:T(8,128)S(1)}, f32[1,88,128]{2,1,0:T(8,128)S(1)}, u32[]{:S(2)}, u32[]{:S(2)}) collective-permute-start(f32[1,88,128]{2,1,0:T(8,128)S(1)} %get-tuple-element.36), channel_id=1, source_target_pairs={{0,3},{1,2},{2,1},{3,0},{4,7},{5,6},{6,5},{7,4},{8,11},{9,10},{10,... | collective-permute-start | bytes 135176 | tf_op jit(solution)/shard_map/ppermute | solution.py:650
  29.9 2.5 %copy-start.1 = (f32[1,88,512]{2,1,0:T(8,128)}, f32[1,88,512]{2,1,0:T(8,128)S(1)}, u32[]{:S(2)}) copy-start(f32[1,88,512]{2,1,0:T(8,128)S(1)} %collective-permute-done.2.side_ref.side_first) | copy-start | bytes 540676
  33.2 12.7 %collective-permute-start.8 = (f32[80,2048]{1,0:T(8,128)S(1)}, f32[80,2048]{1,0:T(8,128)S(1)}, u32[]{:S(2)}, u32[]{:S(2)}) collective-permute-start(f32[80,2048]{1,0:T(8,128)S(1)} %get-tuple-element.41.x_ref), channel_id=1, source_target_pairs={{0,2},{2,0},{4,6},{6,4},{8,10},{10,8},{12,14},{14,12},{16,18},{18,... | collective-permute-start | bytes 1966088 | tf_op jit(solution)/shard_map/ppermute | solution.py:636
  34.9 10.9 %collective-permute-start.7 = (f32[80,1152]{1,0:T(8,128)S(1)}, f32[80,1152]{1,0:T(8,128)S(1)}, u32[]{:S(2)}, u32[]{:S(2)}) collective-permute-start(f32[80,1152]{1,0:T(8,128)S(1)} %get-tuple-element.44), channel_id=1, source_target_pairs={{0,30},{2,4},{4,2},{6,8},{8,6},{10,12},{12,10},{14,16},{16,14},{18... | collective-permute-start | bytes 1105928 | tf_op jit(solution)/shard_map/ppermute | solution.py:636
  34.9 6.9 %collective-permute-start.6 = (f32[1,80,512]{2,1,0:T(8,128)S(1)}, f32[1,80,512]{2,1,0:T(8,128)S(1)}, u32[]{:S(2)}, u32[]{:S(2)}) collective-permute-start(f32[1,80,512]{2,1,0:T(8,128)S(1)} %get-tuple-element.42), channel_id=1, source_target_pairs={{0,1},{1,0},{2,3},{3,2},{4,5},{5,4},{6,7},{7,6},{8,9},{9,8},{10,11... | collective-permute-start | bytes 491528 | tf_op jit(solution)/shard_map/ppermute | solution.py:650
  35.9 9.9 %collective-permute-start.9 = (f32[1,80,128]{2,1,0:T(8,128)S(1)}, f32[1,80,128]{2,1,0:T(8,128)S(1)}, u32[]{:S(2)}, u32[]{:S(2)}) collective-permute-start(f32[1,80,128]{2,1,0:T(8,128)S(1)} %get-tuple-element.45), channel_id=1, source_target_pairs={{0,31},{1,30},{2,5},{3,4},{4,3},{5,2},{6,9},{7,8},{8,7},{9,6},{10,... | collective-permute-start | bytes 122888 | tf_op jit(solution)/shard_map/ppermute | solution.py:650
  40.6 5.3 %copy-start.2 = (f32[1,88,512]{2,1,0:T(8,128)S(1)}, f32[1,88,512]{2,1,0:T(8,128)}, u32[]{:S(2)}) copy-start(f32[1,88,512]{2,1,0:T(8,128)} %copy-done.1) | copy-start | bytes 540676
  40.6 5.2 %collective-permute-start.10 = (f32[1,80,128]{2,1,0:T(8,128)S(1)}, f32[1,80,128]{2,1,0:T(8,128)S(1)}, u32[]{:S(2)}, u32[]{:S(2)}) collective-permute-start(f32[1,80,128]{2,1,0:T(8,128)S(1)} %get-tuple-element.46), channel_id=1, source_target_pairs={{0,3},{1,2},{2,1},{3,0},{4,7},{5,6},{6,5},{7,4},{8,11},{9,10},{10,... | collective-permute-start | bytes 122888 | tf_op jit(solution)/shard_map/ppermute | solution.py:650
  42.8 12.9 %collective-permute-start.11 = (f32[80,1024]{1,0:T(8,128)}, f32[80,1024]{1,0:T(8,128)S(1)}, u32[]{:S(2)}, u32[]{:S(2)}) collective-permute-start(f32[80,1024]{1,0:T(8,128)} %get-tuple-element.52), channel_id=1, source_target_pairs={{0,30},{2,4},{4,2},{6,8},{8,6},{10,12},{12,10},{14,16},{16,14},{18... | collective-permute-start | bytes 983048 | tf_op jit(solution)/shard_map/ppermute | solution.py:636
  49.3 13.2 %all-to-all-start.1 = ((f32[16,8,128]{2,1,0:T(8,128)}), f32[16,8,128]{2,1,0:T(8,128)S(1)}, u32[]{:S(2)}, u32[]{:S(2)}) async-start(f32[16,8,128]{2,1,0:T(8,128)} %get-tuple-element.53), calls=%async_computation.1 | async-start | bytes 131072 | tf_op jit(solution)/shard_map/all_to_all | solution.py:718
  (4 other events, 3.2 us)

commit v5 on v4

--- a/solution.py
+++ b/solution.py
@@ -16,9 +16,8 @@
 WINDOW = 8
 HIGHEST = lax.Precision.HIGHEST
 DOWN_AZ, SPECTRAL, UP_SP, DOWN_SP, UP_AX, DOWN_AX, UP_AZ = range(7)
-C_TIME, C_AZ, C_SP, C_UP, C_DOWN, C_MASK, C_OTHER = range(7)
+C_TIME, C_AZ, C_SP, C_UP, C_DOWN, C_MASK, C_OTHER, C_OWNER = range(8)
 RATES = 8
-GROUP = 3
 AXES = ("sector", "span")
 
 
@@ -224,9 +223,10 @@
     return w_ref[block * plan.pad : (block + count) * plan.pad, :]
 
 
-def two_layers(plan, ref, rates=None, seam=None):
+def two_layers(plan, refs, rates, seam=None):
+    split = isinstance(refs, tuple)
     return [
-        Layer(plan, ref, a * plan.slab, (rates, a * plan.slab) if rates is not None else None, seam, a)
+        Layer(plan, refs[a] if split else refs, 0 if split else a * plan.slab, (rates[a], 0), seam, a)
         for a in range(plan.ct)
     ]
 
@@ -363,42 +363,55 @@
     return corner
 
 
-def prepare(plan, rhs_ref, coef_ref, m_ref, near_ref, side_ref, c0_ref, c1_ref):
-    pad = plan.pad
-    lane = lane_index(1)
+def prepare(plan, rhs_ref, coef_ref, both_ref, m0_ref, m1_ref, side_ref, c0_ref, c1_ref, rates_ref):
+    pad, cells = plan.pad, plan.cells
+    mask, diag, time, *face = [coef_ref[cells * i : cells * (i + 1), :] for i in range(6)]
+    scale = mask / diag
+    lane = lane_index(cells)
+    axial = scale * face[2]
+    rates = (
+        scale * time, scale * face[0], scale * face[1],
+        jnp.where(lane < LANES - 1, axial, 0.0), jnp.where(lane > 0, axial, 0.0), scale,
+    )
+    for i, rate in enumerate(rates):
+        rates_ref[i] = rate
     tail = jnp.zeros((pad - plan.tf, LANES), jnp.float32)
     mirror = parity()
-
-    def coefs(a, r):
+    m_refs = m0_ref, m1_ref
+
+    def rate_of(i, a, r):
         there = jnp.where(mirror == 0, a, plan.ct - 1 - a) * plan.rows + r
-        mask, diag, *rest = [coef_ref[pl.ds(there + plan.cells * i, 1), :] for i in range(6)]
-        return there, mask / diag, rest
-
-    for r in range(plan.rows):
-        scales = [coefs(a, r)[1] for a in range(plan.ct)]
-        for a in range(plan.ct):
-            there, scale, (time, *face) = coefs(a, r)
-            axial = scale * face[2]
-            rates = jnp.concatenate([
-                scale * time, scale * face[0], scale * face[1],
-                jnp.where(lane < LANES - 1, axial, 0.0), jnp.where(lane > 0, axial, 0.0), scale, scales[1 - a],
-                jnp.zeros((RATES - 7, LANES), jnp.float32),
-            ], axis=0)
-            field = jnp.concatenate([rhs_ref[pl.ds(there, plan.tf, stride=plan.cells), :], tail], axis=0) * scale
-            lanes = at(a * plan.rows + r)
-            m_ref[:pad, lanes] = field
-            m_ref[pad:, lanes] = rates
-            if a == 0:
-                near_ref[:pad, lanes] = field
-                near_ref[pad:, lanes] = rates
-    write_edges(plan, m_ref, side_ref, (c0_ref, c1_ref))
-
-
-def write_edges(plan, x_ref, side_ref, c_refs):
+        return rates_ref[i, pl.ds(there, 1), :]
+
+    for a, m_ref in enumerate(m_refs):
+        for r in range(plan.rows):
+            there = jnp.where(mirror == 0, a, plan.ct - 1 - a) * plan.rows + r
+            table = [rate_of(i, a, r) for i in range(6)]
+            field = jnp.concatenate([rhs_ref[pl.ds(there, plan.tf, stride=cells), :], tail], axis=0)
+            m_ref[:pad, at(r)] = field * table[C_MASK]
+            m_ref[pad:, at(r)] = jnp.concatenate(
+                table + [rate_of(C_MASK, 1 - a, r), jnp.zeros((1, LANES), jnp.float32)], axis=0
+            )
+    write_edges(plan, [m_ref[...] for m_ref in m_refs], side_ref, (c0_ref, c1_ref))
+    wide = 2 * cells
+    row = slice(pad + C_OWNER, pad + C_OWNER + 1)
+    for t in range(plan.insts):
+        both = both_ref[t : t + 1, :]
+        lanes = slice(t * wide, (t + 1) * wide)
+        for ref in m_refs:
+            ref[row, lanes] = both
+        group, part = divmod(t, LANES // wide)
+        for n in range(plan.ends):
+            side_ref[n, row, lanes] = both
+            for ref in (c0_ref, c1_ref):
+                ref[n, pad + group : pad + group + 1, part * wide : (part + 1) * wide] = both
+
+
+def write_edges(plan, layers, side_ref, c_refs):
     first = lax.axis_index("span") == 0
     for a in range(plan.ct):
         for e in range(DEPTH):
-            low, high = x_ref[:, at(a * plan.rows + e)], x_ref[:, at((a + 1) * plan.rows - 1 - e)]
+            low, high = layers[a][:, at(e)], layers[a][:, at(plan.rows - 1 - e)]
             ends = [jnp.where(first, high, low)] if plan.ends == 1 else [low, high]
             for n, end in enumerate(ends):
                 side_ref[n, :, at(e * plan.ct + a)] = end
@@ -406,7 +419,7 @@
                     c_refs[a][n] = end
 
 
-def stack_matrices(plan, up_ref, down_ref, spectral_ref, rows_ref, lanes_ref, diagonal_ref, out_ref, down_out):
+def stack_matrices(plan, up_ref, down_ref, spectral_ref, rows_ref, lanes_ref, diagonal_ref, out_ref, down_out, up_out):
     pad = plan.pad
     lane = lax.broadcasted_iota(jnp.int32, (pad, 3 * pad), 1)
     second = (lane >= pad) & (lane < 2 * pad)
@@ -420,23 +433,20 @@
         hi = full.astype(jnp.bfloat16).astype(jnp.float32)
         out_ref[block * pad : (block + 1) * pad, :] = jnp.where(second, full - hi, hi).astype(jnp.bfloat16)
     down_out[...] = matrix(plan, out_ref, DOWN_AZ)
-
-
-def hold_far(plan, m_ref, low_ref, high_ref, far_ref):
-    far_ref[...] = m_ref[: plan.pad, plan.slab :] + 0.0 * (low_ref[0:1, 0:1] + high_ref[0:1, 0:1])
-
-
-def send_panels(plan, stator_ref, both_ref, out_ref, panels_ref):
+    up_out[...] = matrix(plan, out_ref, UP_AZ)
+
+
+def hold_far(plan, m0_ref, m1_ref, low_ref, high_ref, side_ref, c_low, c_high, far0_ref, far1_ref):
+    come = 0.0 * (low_ref[0:1, 0:1] + high_ref[0:1, 0:1] + side_ref[0, 0:1, 0:1] + c_low[0, 0:1, 0:1] + c_high[0, 0:1, 0:1])
+    far0_ref[...] = m0_ref[: plan.pad, :] + come
+    far1_ref[...] = m1_ref[: plan.pad, :] + come
+
+
+def send_panels(plan, stator_ref, out_ref, panels_ref):
     me = lax.axis_index("sector")
     for f in range(plan.fields):
         panels_ref[pl.ds(f, plan.insts, stride=RATES), : plan.width] = jnp.transpose(stator_ref[f])
     out_ref[...] = jnp.zeros_like(out_ref)
-    both = both_ref[...]
-    for t in range(plan.insts):
-        group, row = divmod(t, GROUP)
-        lanes = slice(group * 2 * plan.cells, (group + 1) * 2 * plan.cells)
-        row += RATES
-        out_ref[:, row : row + 1, lanes] = jnp.broadcast_to(both[t : t + 1][None], (out_ref.shape[0], 1, 2 * plan.cells))
     for o, slots in enumerate(plan.slots):
         to = lax.rem(me + (plan.sectors - o), plan.sectors) * plan.spans
         for slot, t in enumerate(slots):
@@ -447,27 +457,51 @@
 
 
 def begin(
-    plan, w_ref, m_ref, got_ref,
+    plan, w_ref, m0_ref, m1_ref, got_ref, low_ref, high_ref, side_ref, c_low, c_high,
     seams_ref, weight_ref, x_ref, g_ref, panels_ref, terms_ref, rows_ref, p0_ref, p1_ref,
 ):
     pad, insts, fields = plan.pad, plan.insts, plan.fields
     me, span = lax.axis_index("sector"), lax.axis_index("span")
+    even, is_first = parity() == 0, span == 0
     tiles = plan.tiles
     panels_ref[...] = jnp.zeros_like(panels_ref)
-    rows_ref[...] = jnp.zeros_like(rows_ref)
-    wide = 2 * plan.cells
     for n, (k, x) in enumerate(tiles):
         at_span = x if plan.spans == 2 else jnp.clip(span + x, 0, plan.spans - 1)
         for t in range(insts):
             o = (k + plan.shift[t]) % plan.sectors
             source = lax.rem(me + o, plan.sectors) * plan.spans + at_span
-            tile = rolled(got_ref[source, :RATES], -plan.slots[o].index(t) * plan.width)
+            tile = rolled(got_ref[source], -plan.slots[o].index(t) * plan.width)
             panels_ref[t * fields : (t + 1) * fields, n * LANES : n * LANES + plan.width] = tile[:fields, : plan.width]
-        source = lax.rem(me + k + plan.sectors, plan.sectors) * plan.spans + at_span
-        table = got_ref[source, RATES:]
-        for group in range(-(-insts // GROUP)):
-            shifted = rolled(table, -group * wide)
-            rows_ref[group * GROUP : (group + 1) * GROUP, n * LANES : n * LANES + wide] = shifted[:GROUP, :wide]
+
+    wide = 2 * plan.cells
+    row = slice(pad + C_OWNER, pad + C_OWNER + 1)
+    zeros = jnp.zeros((16 - insts, LANES), jnp.float32)
+
+    def table(read, packed):
+        out = []
+        for t in range(insts):
+            group, part = divmod(t, LANES // wide)
+            lanes = at(0 if packed else group)
+            out.append(rolled(read(pad + group if packed else row.start, lanes), -part * wide))
+        return jnp.concatenate(out + [zeros], axis=0)
+
+    own = [table(lambda i, lanes: m0_ref[i : i + 1, lanes], False)]
+    low = [table(lambda i, lanes: low_ref[i : i + 1, lanes], False)]
+    high = [table(lambda i, lanes: high_ref[i : i + 1, lanes], False)]
+    for n in range(plan.ends):
+        own.append(table(lambda i, lanes: side_ref[n, i : i + 1, lanes], False))
+        low.append(table(lambda i, lanes: c_low[n, i : i + 1, lanes], True))
+        high.append(table(lambda i, lanes: c_high[n, i : i + 1, lanes], True))
+    for n, (k, x) in enumerate(tiles):
+        if k == 0:
+            block = own
+        else:
+            block = [jnp.where(even, *pair) for pair in (zip(low, high) if k < 0 else zip(high, low))]
+        if plan.spans == 2:
+            value = jnp.where(is_first, block[x], block[1 - x])
+        else:
+            value = block[(0, 1, 2)[x]]
+        rows_ref[:, at(n)] = value
     spread = dot_full(plan.inst_rows(), rows_ref[...])
     spread = pick(jnp.concatenate([spread[:, at(n)] for n in range(len(tiles))], axis=0), plan.weight_lanes())
     first, share, panel = spread, rolled(spread, plan.ct * plan.width), plan.panel_lanes()
@@ -479,9 +513,6 @@
         terms_ref[n * pad : (n + 1) * pad, :] = panels + rolled(panels, plan.width)
     seams = pick(terms_ref[...] * weights, plan.window_lanes())
 
-    even = parity() == 0
-    is_first = span == 0
-
     def tile(values, k, x):
         n = tiles.index((k, x))
         return values[n * pad : (n + 1) * pad]
@@ -503,21 +534,20 @@
         seams_ref[2, i] = jnp.where(even, mirrored(ahead[i]), behind[i])
     weight_ref[...] = around(weights, 0)[0]
 
-    for layer in two_layers(plan, m_ref, seam=seams_ref[1, 0]):
+    rates = m0_ref, m1_ref
+    for a, layer in enumerate(two_layers(plan, rates, rates, seams_ref[1, 0])):
         for r in range(plan.rows):
-            x_ref[:, at(r, 1, layer.start)] = layer.row(r)
-    layers = two_layers(plan, x_ref, m_ref)
+            x_ref[:, at(r, 1, a * plan.slab)] = layer.row(r)
+    layers = two_layers(plan, x_ref, rates)
     inner_rows(plan, w_ref, (p0_ref, p1_ref), layers, layers, g_ref)
 
 
 def middle_first(
-    plan, w_ref, m_ref, f_ref, g_ref, low_ref, high_ref, side_ref, c_low, c_high, seams_ref,
+    plan, w_ref, m0_ref, m1_ref, f_ref, g_ref, low_ref, high_ref, side_ref, c_low, c_high, seams_ref,
     h_ref, n0_ref, n1_ref, p0_ref, p1_ref, y_ref,
 ):
-    own = two_layers(plan, f_ref, m_ref)
-    near = (
-        Layer(plan, low_ref, 0, None, seams_ref[0, 0], 0), Layer(plan, high_ref, plan.slab, None, seams_ref[2, 0], 1),
-    )
+    own = two_layers(plan, f_ref, (m0_ref, m1_ref))
+    near = Layer(plan, low_ref, 0, None, seams_ref[0, 0], 0), Layer(plan, high_ref, 0, None, seams_ref[2, 0], 1)
     middle_rows(
         plan, w_ref, (p0_ref, p1_ref), own, own, g_ref, near, near, sides_of(plan, side_ref, side_ref, seams_ref),
         corners_of(plan, (c_low, c_high), seams_ref), y_ref, h_ref, (n0_ref, n1_ref),
@@ -525,46 +555,56 @@
 
 
 def outer_first(
-    plan, w_ref, m_ref, low_first, high_first, n0_ref, n1_ref, h_ref, far_ref, seams_ref,
-    x_ref, near_ref, side_out, c0_ref, c1_ref,
-):
-    own = two_layers(plan, m_ref)
-    near = Layer(plan, low_first), Layer(plan, high_first, plan.slab)
-    far_low = Layer(plan, far_ref, 0, (low_first, 0), seams_ref[0, 0], 1, C_OTHER)
-    far_high = Layer(plan, high_first, 0, None, seams_ref[2, 0], 0)
-    lane = lane_index(plan.pad)
-    near_ref[:, plan.slab :] = jnp.zeros((plan.pad, LANES), jnp.float32)
-
-    def put(a, r, value):
-        x_ref[:, at(r, 1, a * plan.slab)] = value
-        if a == 0:
-            near_ref[:, at(r)] = value
-        else:
-            here = rolled(value, r * WINDOW)
-            near_ref[:, plan.slab :] = jnp.where(lane == r * WINDOW, here, near_ref[:, plan.slab :])
-
-    outer_rows(plan, w_ref, own, near, (far_low.chunk, far_high.chunk), (n0_ref, n1_ref), h_ref, put)
-    write_edges(plan, x_ref, side_out, (c0_ref, c1_ref))
-
-
-def inner(plan, w_ref, m_ref, f_ref, x_ref, side_ref, g_ref, far_ref, p0_ref, p1_ref):
-    far_ref[...] = x_ref[:, plan.slab :] + 0.0 * side_ref[0, 0:1, 0:1]
-    inner_rows(plan, w_ref, (p0_ref, p1_ref), two_layers(plan, x_ref, m_ref), two_layers(plan, f_ref, m_ref), g_ref)
-
-
-def middle(
-    plan, w_ref, m_ref, f_ref, x_ref, g_ref, low_ref, high_ref, side_ref, c_low, c_high,
-    low_first, high_first, side_first, seams_ref, weight_ref,
-    send_ref, n0_ref, h0_ref, x1_ref, rates_ref, p0_ref, p1_ref, y_ref, inlet_ref, h_ref, n1_ref,
+    plan, w_ref, m0_ref, m1_ref, low_first, high_first, n0_ref, n1_ref, h_ref, far_low, far_high, seams_ref,
+    x0_ref, x1_ref, side_out, c0_ref, c1_ref,
 ):
     pad = plan.pad
-    own, force = two_layers(plan, x_ref, m_ref), two_layers(plan, f_ref, m_ref)
-    low_force = Layer(plan, low_first, 0, None, seams_ref[0, 0], 0)
-    high_force = Layer(plan, high_first, plan.slab, None, seams_ref[2, 0], 1)
-    near = Layer(plan, low_ref, 0, low_force.rates), Layer(plan, high_ref, plan.slab, high_force.rates)
+    rates = m0_ref, m1_ref
+    own = two_layers(plan, rates, rates)
+    near = Layer(plan, low_first), Layer(plan, high_first)
+    far = (
+        Layer(plan, far_low, 0, (low_first, 0), seams_ref[0, 0], 1, C_OTHER),
+        Layer(plan, far_high, 0, (high_first, 0), seams_ref[2, 0], 0, C_OTHER),
+    )
+    lane = lane_index(pad)
+    x_refs = x0_ref, x1_ref
+    for ref in x_refs:
+        ref[:, plan.slab :] = jnp.zeros((pad, LANES), jnp.float32)
+
+    def put(a, r, value):
+        x_refs[a][:, at(r)] = value
+        inlet = x_refs[1 - a].at[:, plan.slab :]
+        inlet[...] = jnp.where(lane == r * WINDOW, rolled(value, r * WINDOW), inlet[...])
+
+    outer_rows(plan, w_ref, own, near, [layer.chunk for layer in far], (n0_ref, n1_ref), h_ref, put)
+    write_edges(plan, x_refs, side_out, (c0_ref, c1_ref))
+
+
+def inner(plan, w_ref, m0_ref, m1_ref, f_ref, x0_ref, x1_ref, side_ref, g_ref, far0_ref, far1_ref, p0_ref, p1_ref):
+    come = 0.0 * side_ref[0, 0:1, 0:1]
+    far0_ref[...] = x0_ref[:, : plan.slab] + come
+    far1_ref[...] = x1_ref[:, : plan.slab] + come
+    rates = m0_ref, m1_ref
+    inner_rows(
+        plan, w_ref, (p0_ref, p1_ref), two_layers(plan, (x0_ref, x1_ref), rates), two_layers(plan, f_ref, rates), g_ref
+    )
+
+
+def middle(
+    plan, w_ref, m0_ref, m1_ref, f_ref, x0_ref, x1_ref, g_ref, low_ref, high_ref, side_ref, c_low, c_high,
+    low_first, high_first, side_first, seams_ref, weight_ref,
+    send_ref, n0_ref, n1_ref, h_ref, rates_ref, p0_ref, p1_ref, y_ref, inlet_ref,
+):
+    pad = plan.pad
+    rates = m0_ref, m1_ref
+    own, force = two_layers(plan, (x0_ref, x1_ref), rates), two_layers(plan, f_ref, rates)
+    near_force = (
+        Layer(plan, low_first, 0, None, seams_ref[0, 0], 0), Layer(plan, high_first, 0, None, seams_ref[2, 0], 1),
+    )
+    near = Layer(plan, low_ref, 0, (low_first, 0)), Layer(plan, high_ref, 0, (high_first, 0))
     n_refs = n0_ref, n1_ref
     middle_rows(
-        plan, w_ref, (p0_ref, p1_ref), own, force, g_ref, near, (low_force, high_force),
+        plan, w_ref, (p0_ref, p1_ref), own, force, g_ref, near, near_force,
         sides_of(plan, side_ref, side_first, seams_ref), corners_of(plan, (c_low, c_high), None), y_ref, h_ref, n_refs,
     )
     lane = lane_index(pad)
@@ -573,15 +613,16 @@
     def put(a, r, value):
         cell = a * plan.rows + r
         inlet_ref[...] = jnp.where(lane == cell * WINDOW, rolled(value, cell * WINDOW), inlet_ref[...])
-        if a == 1:
-            x1_ref[:, at(r)] = value
-
-    def far_inlet(c):
-        tile = low_ref[:, plan.slab :]
-        count = CHUNK // LANES
-        return jnp.concatenate([placed(tile, c * count + part) for part in range(count)], axis=1)
-
-    outer_rows(plan, w_ref, own, near, (far_inlet, Layer(plan, high_ref).chunk), n_refs, h_ref, put)
+
+    def far_inlet(ref):
+        def chunk(c):
+            tile = ref[:, plan.slab :]
+            count = CHUNK // LANES
+            return jnp.concatenate([placed(tile, c * count + part) for part in range(count)], axis=1)
+
+        return chunk
+
+    outer_rows(plan, w_ref, own, near, (far_inlet(low_ref), far_inlet(high_ref)), n_refs, h_ref, put)
     inlet = inlet_ref[...]
     inlet = jnp.where(parity() == 0, inlet, rolled(inlet, LANES // 2))
     back = pick(inlet, plan.window_spread()) * weight_ref[...]
@@ -591,27 +632,25 @@
     for t in range(plan.insts):
         to = lax.rem(me + plan.shift[t], plan.sectors)
         send_ref[to, : plan.fields, : plan.width] = back[t * plan.fields : (t + 1) * plan.fields, : plan.width]
-    h0_ref[...] = h_ref[:, : plan.slab]
     for r in range(plan.rows):
-        rest = jnp.zeros((RATES - 2, LANES), jnp.float32)
-        rates_ref[:, at(r)] = jnp.concatenate([near[0].rate(C_AZ, r), own[0].rate(C_AZ, r), rest], axis=0)
-
-
-def outer(plan, w_ref, rates_ref, n0_ref, h0_ref, x1_ref, far_ref, out_ref):
+        last = [layer.rate(C_AZ, r) for layer in near + tuple(own)]
+        rates_ref[:, at(r)] = jnp.concatenate(last + [jnp.zeros((RATES - 4, LANES), jnp.float32)], axis=0)
+
+
+def outer(plan, down_ref, up_ref, rates_ref, n0_ref, n1_ref, h_ref, low_ref, high_ref, out_ref):
     mirror = parity()
-
-    def put(a, r, value):
-        there = jnp.where(mirror == 0, a, plan.ct - 1 - a) * plan.rows + r
-        out_ref[pl.ds(there, plan.tf, stride=plan.cells), :] = value[: plan.tf]
-
-    for r in range(plan.rows):
-        put(1, r, x1_ref[:, at(r)])
-
-    def near_chunk(c):
-        lanes = slice(c * CHUNK, (c + 1) * CHUNK)
-        return n0_ref[:, lanes] - rates_ref[0:1, lanes] * dot3(w_ref[...], far_ref[:, lanes])
-
-    azimuthal(plan, w_ref, 0, near_chunk, lambda r, terms: put(0, r, h0_ref[:, at(r)] - rates_ref[1:2, at(r)] * terms))
+    for a, (w_ref, n_ref, far_ref) in enumerate(((down_ref, n0_ref, low_ref), (up_ref, n1_ref, high_ref))):
+
+        def near_chunk(c):
+            lanes = slice(c * CHUNK, (c + 1) * CHUNK)
+            return n_ref[:, lanes] - rates_ref[a : a + 1, lanes] * dot3(w_ref[...], far_ref[:, lanes])
+
+        def take(r, terms):
+            value = h_ref[:, at(r, 1, a * plan.slab)] - rates_ref[2 + a : 3 + a, at(r)] * terms
+            there = jnp.where(mirror == 0, a, plan.ct - 1 - a) * plan.rows + r
+            out_ref[pl.ds(there, plan.tf, stride=plan.cells), :] = value[: plan.tf]
+
+        azimuthal(plan, w_ref, 0, near_chunk, take)
 
 
 def collect_panels(plan, got_ref, out_ref, panels_ref):
@@ -666,58 +705,59 @@
         return f32(ends, rows, DEPTH * plan.ct * LANES), f32(ends, rows, LANES), f32(ends, rows, LANES)
 
     stator = jnp.transpose(stator_adj, (1, 2, 3, 0)).reshape(fields, plan.width, insts)
-    sent = call(bind(send_panels, plan), f32(sectors * spans, 2 * RATES, LANES), (vmem(insts * RATES, LANES),))(
-        stator,
-        jnp.concatenate([
-            lax.rem(owner, plan.panels).astype(jnp.float32).reshape(insts, cells), first_panel_share.reshape(insts, cells),
-        ], axis=1),
-    )
+    sent = call(bind(send_panels, plan), f32(sectors * spans, RATES, LANES), (vmem(insts * RATES, LANES),))(stator)
     got = lax.all_to_all(sent, AXES, 0, 0, tiled=True)
-    m, near, side, c0, c1 = call(
-        bind(prepare, plan), (f32(pad + RATES, plan.ct * slab), f32(pad + RATES, slab)) + edges(pad + RATES)
+    m0, m1, side, c0, c1 = call(
+        bind(prepare, plan), (f32(pad + RATES, slab),) * 2 + edges(pad + RATES), (vmem(6, cells, LANES),)
     )(
         rhs.reshape(plan.tf * cells, LANES),
         jnp.concatenate([
             wall_mask.astype(jnp.float32).reshape(cells, LANES), diag_coef.reshape(cells, LANES),
             time_coef.reshape(cells, LANES), face_coef.reshape(3 * cells, LANES),
         ]),
-    )
-    low_first, high_first = swap(near, next_chip), swap(m, next_core)
+        jnp.concatenate([
+            lax.rem(owner, plan.panels).astype(jnp.float32).reshape(insts, cells), first_panel_share.reshape(insts, cells),
+        ], axis=1),
+    )
+    low_first, high_first = swap(m0, next_chip), swap(m1, next_core)
     side_first = beside(plan, side, alone)
     c_low, c_high = beside(plan, c0, next_chip), beside(plan, c1, next_core)
-    far_low = swap(call(bind(hold_far, plan), half)(m, low_first, high_first), next_chip)
-    matrices, down = call(
+    far0, far1 = call(bind(hold_far, plan), (half, half))(m0, m1, low_first, high_first, side_first, c_low, c_high)
+    far_low, far_high = swap(far1, next_chip), swap(far0, next_core)
+    matrices, down, up = call(
         bind(stack_matrices, plan),
-        [jax.ShapeDtypeStruct((count * pad, 3 * pad), jnp.bfloat16) for count in (7, 1)],
+        [jax.ShapeDtypeStruct((count * pad, 3 * pad), jnp.bfloat16) for count in (7, 1, 1)],
     )(jac_up, jac_down, plan.spectral(), plan.field_rows(), plan.field_lanes(), plan.block_diagonal())
     tiles = len(plan.tiles)
     seams, weight, force, g = call(
         bind(begin, plan), (f32(3, 1 + ends, pad, LANES), f32(pad, LANES), whole, whole),
         (vmem(pad, tiles * LANES), vmem(tiles * pad, LANES), vmem(16, tiles * LANES)) + products,
-    )(matrices, m, got)
+    )(matrices, m0, m1, got, low_first, high_first, side_first, c_low, c_high)
     h, n0, n1 = call(bind(middle_first, plan), (whole, half, half), products + (vmem(pad, 2 * slab),))(
-        matrices, m, force, g, low_first, high_first, side_first, c_low, c_high, seams
-    )
-    x, near, side, c0, c1 = call(bind(outer_first, plan), (whole, f32(pad, slab + LANES)) + edges(pad))(
-        matrices, m, low_first, high_first, n0, n1, h, far_low, seams
-    )
-
-    low, high = swap(near, next_chip), swap(x, next_core)
+        matrices, m0, m1, force, g, low_first, high_first, side_first, c_low, c_high, seams
+    )
+    with_inlet = f32(pad, slab + LANES)
+    x0, x1, side, c0, c1 = call(bind(outer_first, plan), (with_inlet, with_inlet) + edges(pad))(
+        matrices, m0, m1, low_first, high_first, n0, n1, h, far_low, far_high, seams
+    )
+
+    low, high = swap(x0, next_chip), swap(x1, next_core)
     side = beside(plan, side, alone)
     c_low, c_high = beside(plan, c0, next_chip), beside(plan, c1, next_core)
-    g, far = call(bind(inner, plan), (whole, half), products, flops=2_000_000_000)(
-        matrices, m, force, x, side
-    )
-    far_low = swap(far, next_chip)
-    back, n0, h0, x1, rates = call(
-        bind(middle, plan), (f32(sectors, RATES, LANES), half, half, half, f32(RATES, slab)),
-        products + (vmem(pad, 2 * slab), vmem(pad, LANES), vmem(pad, 2 * slab), vmem(pad, slab)), flops=4_000_000_000,
+    g, far0, far1 = call(bind(inner, plan), (whole, half, half), products, flops=2_000_000_000)(
+        matrices, m0, m1, force, x0, x1, side
+    )
+    far_low, far_high = swap(far1, next_chip), swap(far0, next_core)
+    back, n0, n1, h, rates = call(
+        bind(middle, plan), (f32(sectors, RATES, LANES), half, half, whole, f32(RATES, slab)),
+        products + (vmem(pad, 2 * slab), vmem(pad, LANES)), flops=4_000_000_000,
     )(
-        matrices, m, force, x, g, low, high, side, c_low, c_high, low_first, high_first, side_first, seams, weight
+        matrices, m0, m1, force, x0, x1, g, low, high, side, c_low, c_high, low_first, high_first, side_first, seams,
+        weight,
     )
     returned = lax.all_to_all(back, "sector", 0, 0, tiled=True)
     sens = call(bind(collect_panels, plan), f32(fields, plan.width, insts), (vmem(insts * RATES, LANES),))(returned)
-    out = call(bind(outer, plan), f32(plan.tf * cells, LANES))(down, rates, n0, h0, x1, far_low)
+    out = call(bind(outer, plan), f32(plan.tf * cells, LANES))(down, up, rates, n0, n1, h, far_low, far_high)
     sens = jnp.transpose(sens.reshape(fields, plan.panels, plan.rows, insts), (3, 0, 1, 2))
     return out.reshape(rhs.shape), sens
 

time: 63.8 us -> 69.5 us (1.089)
  blocking collectives: 0 us -> 12.8 us
  starting transfers between devices: 30.8 us -> 21.5 us
  waiting for transfers between devices: 13.7 us -> 16.8 us
  Pallas kernels: 14.6 us -> 13.8 us
  other arithmetic: 1.54 us -> 0.79 us
    all_to_all x0 -> x1, blocking collectives: none -> 12.8 us  [on_device(): returned = lax.all_to_all(back, 'sector', 0, 0, tiled=True)]
    all_to_all x1 -> x0, starting transfers between devices: 6.33 us -> none  [on_device(): returned = lax.all_to_all(back, 'sector', 0, 0, tiled=True)]
    all_to_all x1 -> x0, waiting for transfers between devices: 5.58 us -> none  [on_device(): returned = lax.all_to_all(back, 'sector', 0, 0, tiled=True)]
    ppermute x6, waiting for transfers between devices: 4.23 us -> 9.34 us  [beside(): return lax.ppermute(array, AXES, pairs(0))]
    all_to_all x1, waiting for transfers between devices: 3.06 us -> 7.45 us  [on_device(): got = lax.all_to_all(sent, AXES, 0, 0, tiled=True)]
    ppermute x6 -> x8, starting transfers between devices: 14.8 us -> 11 us  [swap(): return lax.ppermute(array, 'sector', list(enumerate(partner)))]
    pallas_call x6, Pallas kernels: 7.23 us -> 6.38 us  [the longest x1 2.85 us: on_device(): call(bind(middle, plan), (f32(sectors, RATES, LANES), half, half, whole,...]
    all_to_all x1, starting transfers between devices: 2.59 us -> 3.43 us  [on_device(): got = lax.all_to_all(sent, AXES, 0, 0, tiled=True)]
  transfers between devices with their start and end apart: 14 -> 15, of which waited for: 6 -> 4; matrix products, arithmetic and copies ran while one was open for 0% -> 0% of each run, Pallas kernels for 19% -> 15%
where the time goes in v5:
time: 69.5 us; the launch traced here: 69 us
  starting transfers between devices  21.5 us (31%)
  waiting for transfers between devices  16.8 us (24%)
  Pallas kernels  13.8 us (20%)
  blocking collectives  12.8 us (18%)
  local copies, waits for them, and re-layouts  2.52 us (4%)
  between operations  0.83 us (1%)
  other arithmetic  0.79 us (1%)
    all_to_all x1, blocking collectives, on_device(): returned = lax.all_to_all(back, 'sector', 0, 0, tiled=True)  12.8 us
    ppermute x8, starting transfers between devices, swap(): return lax.ppermute(array, 'sector', list(enumerate(partner)))  11 us
    ppermute x6, waiting for transfers between devices, beside(): return lax.ppermute(array, AXES, pairs(0))  9.34 us
    all_to_all x1, waiting for transfers between devices, on_device(): got = lax.all_to_all(sent, AXES, 0, 0, tiled=True)  7.45 us
    ppermute x6, starting transfers between devices, beside(): return lax.ppermute(array, AXES, pairs(0))  7 us
    all_to_all x1, starting transfers between devices, on_device(): got = lax.all_to_all(sent, AXES, 0, 0, tiled=True)  3.43 us
    pallas_call x1, Pallas kernels, on_device(): call(bind(middle, plan), (f32(sectors, RATES, LANES), half, half, whole,...  2.85 us
    pallas_call x1, Pallas kernels, on_device(): call(bind(middle_first, plan), (whole, half, half), products + (vmem(pad,...  2.47 us
  transfers between devices with their start and end apart: 15, of which 4 were waited for; matrix products, arithmetic and copies ran while one was open for 0% of the time, Pallas kernels for 15%

profile of v5, /device:TPU:0, one launch (start us, length us, event | category | flops | bytes accessed | tf_op | source)
XLA Modules:
  0.0 69.0 jit_solution(2662493891278958671)
XLA Ops:
  0.6 0.7 %convert_bitcast_fusion = f32[16,128]{1,0:T(8,128)S(1)} fusion(s32[2,8,128]{2,1,0:T(8,128)} %param.20), kind=kLoop, calls=%fused_computation.7 | loop fusion | flops 2048 | bytes 16384 | tf_op jit(solution)/shard_map/reshape | solution.py:715
  2.9 1.1 %copy-done = f32[11,7,2,8,128]{4,3,2,1,0:T(8,128)S(1)} copy-done((f32[11,7,2,8,128]{4,3,2,1,0:T(8,128)S(1)}, f32[11,7,2,8,128]{4,3,2,1,0:T(8,128)}, u32[]{:S(2)}) %copy-start) | copy-done | bytes 630808
  4.2 5.5 %collective-permute-start = (f32[88,1024]{1,0:T(8,128)S(1)}, f32[88,1024]{1,0:T(8,128)S(1)}, u32[]{:S(2)}, u32[]{:S(2)}) collective-permute-start(f32[88,1024]{1,0:T(8,128)S(1)} %get-tuple-element.35.m0_ref), channel_id=1, source_target_pairs={{0,30},{2,4},{4,2},{6,8},{8,6},{10,12},{12,10},{14,16},{16,14},{18... | collective-permute-start | bytes 1081352 | tf_op jit(solution)/shard_map/ppermute | solution.py:675
  9.8 1.5 %collective-permute-start.2 = (f32[1,88,512]{2,1,0:T(8,128)S(1)}, f32[1,88,512]{2,1,0:T(8,128)S(1)}, u32[]{:S(2)}, u32[]{:S(2)}) collective-permute-start(f32[1,88,512]{2,1,0:T(8,128)S(1)} %get-tuple-element.37), channel_id=1, source_target_pairs={{0,1},{1,0},{2,3},{3,2},{4,5},{5,4},{6,7},{7,6},{8,9},{9,8},{10,11... | collective-permute-start | bytes 540680 | tf_op jit(solution)/shard_map/ppermute | solution.py:689
  11.7 6.6 %collective-permute-done.3.c_low = f32[1,88,128]{2,1,0:T(8,128)S(1)} collective-permute-done((f32[1,88,128]{2,1,0:T(8,128)S(1)}, f32[1,88,128]{2,1,0:T(8,128)S(1)}, u32[]{:S(2)}, u32[]{:S(2)}) %collective-permute-start.3) | collective-permute-done | bytes 45088 | tf_op jit(solution)/shard_map/ppermute | solution.py:689
  18.7 0.8 %shard_map.154 = (f32[80,1024]{1,0:T(8,128)S(1)}, f32[80,1024]{1,0:T(8,128)}) custom-call(f32[88,1024]{1,0:T(8,128)S(1)} %get-tuple-element.35.m0_ref, f32[88,1024]{1,0:T(8,128)S(1)} %get-tuple-element.36.m1_ref, f32[88,1024]{1,0:T(8,128)S(1)} %collective-permute-done.low_ref.low_first, f32[88,1024]{1,0:T(8,128)S(1)} %collective-permute-done.1.high_ref.high_first, ...), custom_call_target="tpu_custom_call" | custom-call | flops 2000000 | bytes 1000000 | tf_op jit(solution)/shard_map/pallas_call | solution.py:725
  19.5 2.7 %collective-permute-start.5 = (f32[80,1024]{1,0:T(8,128)}, f32[80,1024]{1,0:T(8,128)S(1)}, u32[]{:S(2)}, u32[]{:S(2)}) collective-permute-start(f32[80,1024]{1,0:T(8,128)} %get-tuple-element.46), channel_id=1, source_target_pairs={{0,30},{2,4},{4,2},{6,8},{8,6},{10,12},{12,10},{14,16},{16,14},{18... | collective-permute-start | bytes 983048 | tf_op jit(solution)/shard_map/ppermute | solution.py:675
  22.2 0.8 %shard_map.151 = f32[32,8,128]{2,1,0:T(8,128)} custom-call(f32[7,32,11]{2,1,0:T(8,128)S(1)} %bitcast.17), custom_call_target="tpu_custom_call" | custom-call | flops 2000000 | bytes 1000000 | tf_op jit(solution)/shard_map/pallas_call | solution.py:708
  23.1 3.4 %all-to-all-start = ((f32[32,8,128]{2,1,0:T(8,128)}), f32[32,8,128]{2,1,0:T(8,128)S(1)}, u32[]{:S(2)}, u32[]{:S(2)}) async-start(f32[32,8,128]{2,1,0:T(8,128)} %shard_map.151), calls=%async_computation | async-start | bytes 262144 | tf_op jit(solution)/shard_map/all_to_all | solution.py:709
  26.6 1.1 %shard_map.149 = (bf16[560,240]{1,0:T(8,128)(2,1)S(1)}, bf16[80,240]{1,0:T(8,128)(2,1)S(1)}, bf16[80,240]{1,0:T(8,128)(2,1)S(1)}) custom-call(f32[3,7,7]{2,1,0:T(8,128)S(1)} %copy-done.5, f32[3,7,7]{2,1,0:T(8,128)S(1)} %copy-done.6, bf16[80,240]{1,0:T(8,128)(2,1)S(1)} %copy-done.4, f32[80,7]{1,0:T(8,128)S(1)} %copy-done.3, f32[7,240]{1,0:T(8,128)S(1)} %copy-done.7, ...), custom_call_target="tpu_custom_call" | custom-call | flops 2000000 | bytes 1000000 | tf_op jit(solution)/shard_map/pallas_call | solution.py:727
  27.7 7.4 %all-to-all-done.got_ref = f32[32,8,128]{2,1,0:T(8,128)S(1)} async-done(((f32[32,8,128]{2,1,0:T(8,128)}), f32[32,8,128]{2,1,0:T(8,128)S(1)}, u32[]{:S(2)}, u32[]{:S(2)}) %all-to-all-start) | async-done | bytes 131104 | tf_op jit(solution)/shard_map/all_to_all | solution.py:709
  35.1 1.7 %shard_map.152 = (f32[3,2,80,128]{3,2,1,0:T(8,128)S(1)}, f32[80,128]{1,0:T(8,128)S(1)}, f32[80,2048]{1,0:T(8,128)S(1)}, f32[80,2048]{1,0:T(8,128)S(1)}) custom-call(bf16[560,240]{1,0:T(8,128)(2,1)S(1)} %get-tuple-element.34.w_ref, f32[88,1024]{1,0:T(8,128)S(1)} %get-tuple-element.35.m0_ref, f32[88,1024]{1,0:T(8,128)S(1)} %get-tuple-element.36.m1_ref, ...), custom_call_target="tpu_custom_call" | custom-call | flops 2000000 | bytes 1000000 | tf_op jit(solution)/shard_map/pallas_call | solution.py:732
  36.8 2.5 %shard_map.153 = (f32[80,2048]{1,0:T(8,128)S(1)}, f32[80,1024]{1,0:T(8,128)S(1)}, f32[80,1024]{1,0:T(8,128)S(1)}) custom-call(bf16[560,240]{1,0:T(8,128)(2,1)S(1)} %get-tuple-element.34.w_ref, f32[88,1024]{1,0:T(8,128)S(1)} %get-tuple-element.35.m0_ref, f32[88,1024]{1,0:T(8,128)S(1)} %get-tuple-element.36.m1_ref, f32[80,2048]{1,0:T(8,128)S(1)} %get-tuple-element.40.f_ref, ...), custom_call_target="tpu_custom_call" | custom-call | flops 2000000 | bytes 1000000 | tf_op jit(solution)/shard_map/pallas_call | solution.py:736
  39.3 0.8 %shard_map.155 = (f32[80,1152]{1,0:T(8,128)S(1)}, f32[80,1152]{1,0:T(8,128)S(1)}, f32[1,80,512]{2,1,0:T(8,128)S(1)}, f32[1,80,128]{2,1,0:T(8,128)S(1)}, f32[1,80,128]{2,1,0:T(8,128)S(1)}) custom-call(bf16[560,240]{1,0:T(8,128)(2,1)S(1)} %get-tuple-element.34.w_ref, f32[88,1024]{1,0:T(8,128)S(1)} %get-tuple-element.35.m0_ref, ...), custom_call_target="tpu_custom_call" | custom-call | flops 2000000 | bytes 1000000 | tf_op jit(solution)/shard_map/pallas_call | solution.py:740
  40.1 0.7 collective-permute-start.8
  40.7 0.7 %collective-permute-start.7 = (f32[1,80,512]{2,1,0:T(8,128)S(1)}, f32[1,80,512]{2,1,0:T(8,128)S(1)}, u32[]{:S(2)}, u32[]{:S(2)}) collective-permute-start(f32[1,80,512]{2,1,0:T(8,128)S(1)} %get-tuple-element.50), channel_id=1, source_target_pairs={{0,1},{1,0},{2,3},{3,2},{4,5},{5,4},{6,7},{7,6},{8,9},{9,8},{10,11... | collective-permute-start | bytes 491528 | tf_op jit(solution)/shard_map/ppermute | solution.py:689
  41.4 4.3 %collective-permute-start.10 = (f32[1,80,128]{2,1,0:T(8,128)S(1)}, f32[1,80,128]{2,1,0:T(8,128)S(1)}, u32[]{:S(2)}, u32[]{:S(2)}) collective-permute-start(f32[1,80,128]{2,1,0:T(8,128)S(1)} %get-tuple-element.52), channel_id=1, source_target_pairs={{0,31},{1,30},{2,5},{3,4},{4,3},{5,2},{6,9},{7,8},{8,7},{9,6},{10,... | collective-permute-start | bytes 122888 | tf_op jit(solution)/shard_map/ppermute | solution.py:689
  45.8 2.4 %collective-permute-done.7.side_ref = f32[1,80,512]{2,1,0:T(8,128)S(1)} collective-permute-done((f32[1,80,512]{2,1,0:T(8,128)S(1)}, f32[1,80,512]{2,1,0:T(8,128)S(1)}, u32[]{:S(2)}, u32[]{:S(2)}) %collective-permute-start.7) | collective-permute-done | bytes 163872 | tf_op jit(solution)/shard_map/ppermute | solution.py:689
  48.2 0.8 %shard_map.156 = (f32[80,2048]{1,0:T(8,128)S(1)}, f32[80,1024]{1,0:T(8,128)S(1)}, f32[80,1024]{1,0:T(8,128)S(1)}) custom-call(bf16[560,240]{1,0:T(8,128)(2,1)S(1)} %get-tuple-element.34.w_ref, f32[88,1024]{1,0:T(8,128)S(1)} %get-tuple-element.35.m0_ref, f32[88,1024]{1,0:T(8,128)S(1)} %get-tuple-element.36.m1_ref, f32[80,2048]{1,0:T(8,128)S(1)} %get-tuple-element.40.f_ref, ...), custom_call_target="tpu_custom_call" | custom-call | flops 2000000000 | bytes 1000000 | tf_op jit(solution)/shard_map/pallas_call | solution.py:747
  49.0 2.2 %collective-permute-start.12 = (f32[80,1024]{1,0:T(8,128)S(1)}, f32[80,1024]{1,0:T(8,128)S(1)}, u32[]{:S(2)}, u32[]{:S(2)}) collective-permute-start(f32[80,1024]{1,0:T(8,128)S(1)} %get-tuple-element.59), channel_id=1, source_target_pairs={{0,30},{2,4},{4,2},{6,8},{8,6},{10,12},{12,10},{14,16},{16,14},{18... | collective-permute-start | bytes 983048 | tf_op jit(solution)/shard_map/ppermute | solution.py:675
  51.2 2.9 %shard_map.157 = (f32[16,8,128]{2,1,0:T(8,128)S(1)}, f32[80,1024]{1,0:T(8,128)S(1)}, f32[80,1024]{1,0:T(8,128)S(1)}, f32[80,2048]{1,0:T(8,128)S(1)}, f32[8,1024]{1,0:T(8,128)S(1)}) custom-call(bf16[560,240]{1,0:T(8,128)(2,1)S(1)} %get-tuple-element.34.w_ref, f32[88,1024]{1,0:T(8,128)S(1)} %get-tuple-element.35.m0_ref, ...), custom_call_target="tpu_custom_call" | custom-call | flops 4000000000 | bytes 1000000 | tf_op jit(solution)/shard_map/pallas_call | solution.py:751
  54.0 12.8 %all_to_all.10.got_ref = f32[16,8,128]{2,1,0:T(8,128)S(1)} all-to-all(f32[16,8,128]{2,1,0:T(8,128)S(1)} %get-tuple-element.61), channel_id=1, replica_groups=mesh['sector'=16,'span'=2] {'sector'}, dimensions={0} | all-to-all | bytes 131072 | tf_op jit(solution)/shard_map/all_to_all | solution.py:758
  66.8 0.8 %shard_map.159 = f32[7,32,11]{2,1,0:T(8,128)} custom-call(f32[16,8,128]{2,1,0:T(8,128)S(1)} %all_to_all.10.got_ref), custom_call_target="tpu_custom_call" | custom-call | flops 2000000 | bytes 1000000 | tf_op jit(solution)/shard_map/pallas_call | solution.py:759
  67.6 1.4 %shard_map.158 = f32[1232,128]{1,0:T(8,128)} custom-call(bf16[80,240]{1,0:T(8,128)(2,1)S(1)} %get-tuple-element.32.down_ref, bf16[80,240]{1,0:T(8,128)(2,1)S(1)} %get-tuple-element.33.up_ref, f32[8,1024]{1,0:T(8,128)S(1)} %get-tuple-element.55.rates_ref, f32[80,1024]{1,0:T(8,128)S(1)} %get-tuple-element.56.n0_ref, f32[80,1024]{1,0:T(8,128)S(1)} %get-tuple-element.57.n1_ref, ...), custom_call_target="tpu_custom_call" | custom-call | flops 2000000 | bytes 1000000 | tf_op jit(solution)/shard_map/pallas_call | solution.py:760
  (50 shorter events, 2.7 us)
Async XLA Ops:
  1.4 0.8 %copy-start.8 = (f32[3,2,8,128]{3,2,1,0:T(8,128)S(1)}, f32[3,2,8,128]{3,2,1,0:T(8,128)}, u32[]{:S(2)}) copy-start(f32[3,2,8,128]{3,2,1,0:T(8,128)} %param.16) | copy-start | bytes 73732
  2.9 1.1 %copy-start = (f32[11,7,2,8,128]{4,3,2,1,0:T(8,128)S(1)}, f32[11,7,2,8,128]{4,3,2,1,0:T(8,128)}, u32[]{:S(2)}) copy-start(f32[11,7,2,8,128]{4,3,2,1,0:T(8,128)} %param.14) | copy-start | bytes 1892356
  4.2 14.4 %collective-permute-start = (f32[88,1024]{1,0:T(8,128)S(1)}, f32[88,1024]{1,0:T(8,128)S(1)}, u32[]{:S(2)}, u32[]{:S(2)}) collective-permute-start(f32[88,1024]{1,0:T(8,128)S(1)} %get-tuple-element.35.m0_ref), channel_id=1, source_target_pairs={{0,30},{2,4},{4,2},{6,8},{8,6},{10,12},{12,10},{14,16},{16,14},{18... | collective-permute-start | bytes 1081352 | tf_op jit(solution)/shard_map/ppermute | solution.py:675
  9.7 8.9 %collective-permute-start.1 = (f32[88,1024]{1,0:T(8,128)S(1)}, f32[88,1024]{1,0:T(8,128)S(1)}, u32[]{:S(2)}, u32[]{:S(2)}) collective-permute-start(f32[88,1024]{1,0:T(8,128)S(1)} %get-tuple-element.36.m1_ref), channel_id=1, source_target_pairs={{0,2},{2,0},{4,6},{6,4},{8,10},{10,8},{12,14},{14,12},{16,18},{18,... | collective-permute-start | bytes 1081352 | tf_op jit(solution)/shard_map/ppermute | solution.py:675
  9.8 8.9 %collective-permute-start.2 = (f32[1,88,512]{2,1,0:T(8,128)S(1)}, f32[1,88,512]{2,1,0:T(8,128)S(1)}, u32[]{:S(2)}, u32[]{:S(2)}) collective-permute-start(f32[1,88,512]{2,1,0:T(8,128)S(1)} %get-tuple-element.37), channel_id=1, source_target_pairs={{0,1},{1,0},{2,3},{3,2},{4,5},{5,4},{6,7},{7,6},{8,9},{9,8},{10,11... | collective-permute-start | bytes 540680 | tf_op jit(solution)/shard_map/ppermute | solution.py:689
  11.2 7.1 %collective-permute-start.3 = (f32[1,88,128]{2,1,0:T(8,128)S(1)}, f32[1,88,128]{2,1,0:T(8,128)S(1)}, u32[]{:S(2)}, u32[]{:S(2)}) collective-permute-start(f32[1,88,128]{2,1,0:T(8,128)S(1)} %get-tuple-element.38), channel_id=1, source_target_pairs={{0,31},{1,30},{2,5},{3,4},{4,3},{5,2},{6,9},{7,8},{8,7},{9,6},{10,... | collective-permute-start | bytes 135176 | tf_op jit(solution)/shard_map/ppermute | solution.py:689
  11.7 10.5 %copy-start.1 = (f32[11,7,4,8]{0,3,2,1:T(8,128)S(1)}, f32[11,7,4,8]{0,3,2,1:T(8,128)}, u32[]{:S(2)}) copy-start(f32[11,7,4,8]{0,3,2,1:T(8,128)} %param.21) | copy-start | bytes 29572
  11.7 6.9 %collective-permute-start.4 = (f32[1,88,128]{2,1,0:T(8,128)S(1)}, f32[1,88,128]{2,1,0:T(8,128)S(1)}, u32[]{:S(2)}, u32[]{:S(2)}) collective-permute-start(f32[1,88,128]{2,1,0:T(8,128)S(1)} %get-tuple-element.39), channel_id=1, source_target_pairs={{0,3},{1,2},{2,1},{3,0},{4,7},{5,6},{6,5},{7,4},{8,11},{9,10},{10,... | collective-permute-start | bytes 135176 | tf_op jit(solution)/shard_map/ppermute | solution.py:689
  19.5 19.8 %collective-permute-start.5 = (f32[80,1024]{1,0:T(8,128)}, f32[80,1024]{1,0:T(8,128)S(1)}, u32[]{:S(2)}, u32[]{:S(2)}) collective-permute-start(f32[80,1024]{1,0:T(8,128)} %get-tuple-element.46), channel_id=1, source_target_pairs={{0,30},{2,4},{4,2},{6,8},{8,6},{10,12},{12,10},{14,16},{16,14},{18... | collective-permute-start | bytes 983048 | tf_op jit(solution)/shard_map/ppermute | solution.py:675
  22.2 17.1 %collective-permute-start.6 = (f32[80,1024]{1,0:T(8,128)S(1)}, f32[80,1024]{1,0:T(8,128)S(1)}, u32[]{:S(2)}, u32[]{:S(2)}) collective-permute-start(f32[80,1024]{1,0:T(8,128)S(1)} %get-tuple-element.47), channel_id=1, source_target_pairs={{0,2},{2,0},{4,6},{6,4},{8,10},{10,8},{12,14},{14,12},{16,18},{18,... | collective-permute-start | bytes 983048 | tf_op jit(solution)/shard_map/ppermute | solution.py:675
  23.0 3.5 %copy-start.2 = (f32[80,240]{1,0:T(8,128)S(1)}, f32[80,240]{1,0:T(8,128)}, u32[]{:S(2)}) copy-start(f32[80,240]{1,0:T(8,128)} %constant.16.clone.diagonal_ref) | copy-start | bytes 230404
  23.0 3.5 %copy-start.3 = (f32[80,7]{1,0:T(8,128)S(1)}, f32[80,7]{1,0:T(8,128)}, u32[]{:S(2)}) copy-start(f32[80,7]{1,0:T(8,128)} %constant.14.clone.rows_ref) | copy-start | bytes 6724
  23.0 3.5 %copy-start.4 = (bf16[80,240]{1,0:T(8,128)(2,1)S(1)}, bf16[80,240]{1,0:T(8,128)(2,1)}, u32[]{:S(2)}) copy-start(bf16[80,240]{1,0:T(8,128)(2,1)} %constant.13.clone.spectral_ref) | copy-start | bytes 115204
  23.0 3.5 %copy-start.5 = (f32[3,7,7]{2,1,0:T(8,128)S(1)}, f32[3,7,7]{2,1,0:T(8,128)}, u32[]{:S(2)}) copy-start(f32[3,7,7]{2,1,0:T(8,128)} %up_ref.1) | copy-start | bytes 1768
  23.0 3.5 %copy-start.6 = (f32[3,7,7]{2,1,0:T(8,128)S(1)}, f32[3,7,7]{2,1,0:T(8,128)}, u32[]{:S(2)}) copy-start(f32[3,7,7]{2,1,0:T(8,128)} %down_ref.1) | copy-start | bytes 1768
  23.0 3.5 %copy-start.7 = (f32[7,240]{1,0:T(8,128)S(1)}, f32[7,240]{1,0:T(8,128)}, u32[]{:S(2)}) copy-start(f32[7,240]{1,0:T(8,128)} %constant.15.clone.lanes_ref) | copy-start | bytes 20164
  23.1 12.1 %all-to-all-start = ((f32[32,8,128]{2,1,0:T(8,128)}), f32[32,8,128]{2,1,0:T(8,128)S(1)}, u32[]{:S(2)}, u32[]{:S(2)}) async-start(f32[32,8,128]{2,1,0:T(8,128)} %shard_map.151), calls=%async_computation | async-start | bytes 262144 | tf_op jit(solution)/shard_map/all_to_all | solution.py:709
  40.1 11.1 %collective-permute-start.8 = (f32[80,1152]{1,0:T(8,128)S(1)}, f32[80,1152]{1,0:T(8,128)S(1)}, u32[]{:S(2)}, u32[]{:S(2)}) collective-permute-start(f32[80,1152]{1,0:T(8,128)S(1)} %get-tuple-element.48.x0_ref), channel_id=1, source_target_pairs={{0,30},{2,4},{4,2},{6,8},{8,6},{10,12},{12,10},{14,16},{16,14},{18... | collective-permute-start | bytes 1105928 | tf_op jit(solution)/shard_map/ppermute | solution.py:675
  40.7 10.5 %collective-permute-start.9 = (f32[80,1152]{1,0:T(8,128)S(1)}, f32[80,1152]{1,0:T(8,128)S(1)}, u32[]{:S(2)}, u32[]{:S(2)}) collective-permute-start(f32[80,1152]{1,0:T(8,128)S(1)} %get-tuple-element.49.x1_ref), channel_id=1, source_target_pairs={{0,2},{2,0},{4,6},{6,4},{8,10},{10,8},{12,14},{14,12},{16,18},{18,... | collective-permute-start | bytes 1105928 | tf_op jit(solution)/shard_map/ppermute | solution.py:675
  40.7 7.4 %collective-permute-start.7 = (f32[1,80,512]{2,1,0:T(8,128)S(1)}, f32[1,80,512]{2,1,0:T(8,128)S(1)}, u32[]{:S(2)}, u32[]{:S(2)}) collective-permute-start(f32[1,80,512]{2,1,0:T(8,128)S(1)} %get-tuple-element.50), channel_id=1, source_target_pairs={{0,1},{1,0},{2,3},{3,2},{4,5},{5,4},{6,7},{7,6},{8,9},{9,8},{10,11... | collective-permute-start | bytes 491528 | tf_op jit(solution)/shard_map/ppermute | solution.py:689
  41.4 9.7 %collective-permute-start.10 = (f32[1,80,128]{2,1,0:T(8,128)S(1)}, f32[1,80,128]{2,1,0:T(8,128)S(1)}, u32[]{:S(2)}, u32[]{:S(2)}) collective-permute-start(f32[1,80,128]{2,1,0:T(8,128)S(1)} %get-tuple-element.52), channel_id=1, source_target_pairs={{0,31},{1,30},{2,5},{3,4},{4,3},{5,2},{6,9},{7,8},{8,7},{9,6},{10,... | collective-permute-start | bytes 122888 | tf_op jit(solution)/shard_map/ppermute | solution.py:689
  45.8 5.4 %collective-permute-start.11 = (f32[1,80,128]{2,1,0:T(8,128)S(1)}, f32[1,80,128]{2,1,0:T(8,128)S(1)}, u32[]{:S(2)}, u32[]{:S(2)}) collective-permute-start(f32[1,80,128]{2,1,0:T(8,128)S(1)} %get-tuple-element.53), channel_id=1, source_target_pairs={{0,3},{1,2},{2,1},{3,0},{4,7},{5,6},{6,5},{7,4},{8,11},{9,10},{10,... | collective-permute-start | bytes 122888 | tf_op jit(solution)/shard_map/ppermute | solution.py:689
  49.0 18.6 %collective-permute-start.12 = (f32[80,1024]{1,0:T(8,128)S(1)}, f32[80,1024]{1,0:T(8,128)S(1)}, u32[]{:S(2)}, u32[]{:S(2)}) collective-permute-start(f32[80,1024]{1,0:T(8,128)S(1)} %get-tuple-element.59), channel_id=1, source_target_pairs={{0,30},{2,4},{4,2},{6,8},{8,6},{10,12},{12,10},{14,16},{16,14},{18... | collective-permute-start | bytes 983048 | tf_op jit(solution)/shard_map/ppermute | solution.py:675
  51.2 16.4 %collective-permute-start.13 = (f32[80,1024]{1,0:T(8,128)S(1)}, f32[80,1024]{1,0:T(8,128)S(1)}, u32[]{:S(2)}, u32[]{:S(2)}) collective-permute-start(f32[80,1024]{1,0:T(8,128)S(1)} %get-tuple-element.60), channel_id=1, source_target_pairs={{0,2},{2,0},{4,6},{6,4},{8,10},{10,8},{12,14},{14,12},{16,18},{18,... | collective-permute-start | bytes 983048 | tf_op jit(solution)/shard_map/ppermute | solution.py:675
  (4 other events, 2.8 us)

commit v6 on v5

--- a/solution.py
+++ b/solution.py
@@ -436,8 +436,9 @@
     up_out[...] = matrix(plan, out_ref, UP_AZ)
 
 
-def hold_far(plan, m0_ref, m1_ref, low_ref, high_ref, side_ref, c_low, c_high, far0_ref, far1_ref):
+def hold_far(plan, m0_ref, m1_ref, low_ref, high_ref, side_ref, c_low, c_high, w_ref, far0_ref, far1_ref):
     come = 0.0 * (low_ref[0:1, 0:1] + high_ref[0:1, 0:1] + side_ref[0, 0:1, 0:1] + c_low[0, 0:1, 0:1] + c_high[0, 0:1, 0:1])
+    come = come + 0.0 * w_ref[:16, :LANES].astype(jnp.float32)[0:1, 0:1]
     far0_ref[...] = m0_ref[: plan.pad, :] + come
     far1_ref[...] = m1_ref[: plan.pad, :] + come
 
@@ -722,12 +723,12 @@
     low_first, high_first = swap(m0, next_chip), swap(m1, next_core)
     side_first = beside(plan, side, alone)
     c_low, c_high = beside(plan, c0, next_chip), beside(plan, c1, next_core)
-    far0, far1 = call(bind(hold_far, plan), (half, half))(m0, m1, low_first, high_first, side_first, c_low, c_high)
-    far_low, far_high = swap(far1, next_chip), swap(far0, next_core)
     matrices, down, up = call(
         bind(stack_matrices, plan),
         [jax.ShapeDtypeStruct((count * pad, 3 * pad), jnp.bfloat16) for count in (7, 1, 1)],
     )(jac_up, jac_down, plan.spectral(), plan.field_rows(), plan.field_lanes(), plan.block_diagonal())
+    far0, far1 = call(bind(hold_far, plan), (half, half))(m0, m1, low_first, high_first, side_first, c_low, c_high, down)
+    far_low, far_high = swap(far1, next_chip), swap(far0, next_core)
     tiles = len(plan.tiles)
     seams, weight, force, g = call(
         bind(begin, plan), (f32(3, 1 + ends, pad, LANES), f32(pad, LANES), whole, whole),

time: 69.5 us -> 68.2 us (0.981)
  blocking collectives: 12.8 us -> 24.6 us
  waiting for transfers between devices: 16.8 us -> 8.19 us
  starting transfers between devices: 21.5 us -> 18.1 us
  Pallas kernels: 13.8 us -> 12.7 us
    all_to_all x0 -> x1, blocking collectives: none -> 11.9 us  [on_device(): got = lax.all_to_all(sent, AXES, 0, 0, tiled=True)]
    all_to_all x1 -> x0, waiting for transfers between devices: 7.45 us -> none  [on_device(): got = lax.all_to_all(sent, AXES, 0, 0, tiled=True)]
    all_to_all x1 -> x0, starting transfers between devices: 3.43 us -> none  [on_device(): got = lax.all_to_all(sent, AXES, 0, 0, tiled=True)]
    ppermute x6, waiting for transfers between devices: 9.34 us -> 8.17 us  [beside(): return lax.ppermute(array, AXES, pairs(0))]
    pallas_call x1, Pallas kernels: 0.81 us -> 0.09 us  [on_device(): call(bind(hold_far, plan), (half, half))]
  transfers between devices with their start and end apart: 15 -> 14, of which waited for: 4 -> 3; matrix products, arithmetic and copies ran while one was open for 0% -> 0% of each run, Pallas kernels for 15% -> 15%
where the time goes in v6:
time: 68.2 us; the launch traced here: 67.7 us
  blocking collectives  24.6 us (36%)
  starting transfers between devices  18.1 us (27%)
  Pallas kernels  12.7 us (19%)
  waiting for transfers between devices  8.19 us (12%)
  local copies, waits for them, and re-layouts  2.53 us (4%)
  between operations  0.83 us (1%)
  other arithmetic  0.79 us (1%)
    all_to_all x1, blocking collectives, on_device(): returned = lax.all_to_all(back, 'sector', 0, 0, tiled=True)  12.8 us
    all_to_all x1, blocking collectives, on_device(): got = lax.all_to_all(sent, AXES, 0, 0, tiled=True)  11.9 us
    ppermute x8, starting transfers between devices, swap(): return lax.ppermute(array, 'sector', list(enumerate(partner)))  11.1 us
    ppermute x6, waiting for transfers between devices, beside(): return lax.ppermute(array, AXES, pairs(0))  8.17 us
    ppermute x6, starting transfers between devices, beside(): return lax.ppermute(array, AXES, pairs(0))  7 us
    pallas_call x1, Pallas kernels, on_device(): call(bind(middle, plan), (f32(sectors, RATES, LANES), half, half, whole,...  2.94 us
    pallas_call x1, Pallas kernels, on_device(): call(bind(middle_first, plan), (whole, half, half), products + (vmem(pad,...  2.53 us
    unnamed x26, local copies, waits for them, and re-layouts  2.36 us
  transfers between devices with their start and end apart: 14, of which 3 were waited for; matrix products, arithmetic and copies ran while one was open for 0% of the time, Pallas kernels for 15%

profile of v6, /device:TPU:0, one launch (start us, length us, event | category | flops | bytes accessed | tf_op | source)
XLA Modules:
  0.0 67.7 jit_solution(18181468365566090700)
XLA Ops:
  0.6 0.7 %convert_bitcast_fusion = f32[16,128]{1,0:T(8,128)S(1)} fusion(s32[2,8,128]{2,1,0:T(8,128)} %param.20), kind=kLoop, calls=%fused_computation.7 | loop fusion | flops 2048 | bytes 16384 | tf_op jit(solution)/shard_map/reshape | solution.py:716
  1.5 0.6 copy-done.12
  2.2 0.6 copy-done.9
  2.9 1.1 %copy-done = f32[11,7,2,8,128]{4,3,2,1,0:T(8,128)S(1)} copy-done((f32[11,7,2,8,128]{4,3,2,1,0:T(8,128)S(1)}, f32[11,7,2,8,128]{4,3,2,1,0:T(8,128)}, u32[]{:S(2)}) %copy-start) | copy-done | bytes 630808
  4.3 5.5 %collective-permute-start = (f32[88,1024]{1,0:T(8,128)S(1)}, f32[88,1024]{1,0:T(8,128)S(1)}, u32[]{:S(2)}, u32[]{:S(2)}) collective-permute-start(f32[88,1024]{1,0:T(8,128)S(1)} %get-tuple-element.35.m0_ref), channel_id=1, source_target_pairs={{0,30},{2,4},{4,2},{6,8},{8,6},{10,12},{12,10},{14,16},{16,14},{18... | collective-permute-start | bytes 1081352 | tf_op jit(solution)/shard_map/ppermute | solution.py:676
  9.8 1.5 %collective-permute-start.2 = (f32[1,88,512]{2,1,0:T(8,128)S(1)}, f32[1,88,512]{2,1,0:T(8,128)S(1)}, u32[]{:S(2)}, u32[]{:S(2)}) collective-permute-start(f32[1,88,512]{2,1,0:T(8,128)S(1)} %get-tuple-element.37), channel_id=1, source_target_pairs={{0,1},{1,0},{2,3},{3,2},{4,5},{5,4},{6,7},{7,6},{8,9},{9,8},{10,11... | collective-permute-start | bytes 540680 | tf_op jit(solution)/shard_map/ppermute | solution.py:690
  11.3 0.5 collective-permute-start.3
  11.8 1.1 %shard_map.149 = (bf16[560,240]{1,0:T(8,128)(2,1)S(1)}, bf16[80,240]{1,0:T(8,128)(2,1)S(1)}, bf16[80,240]{1,0:T(8,128)(2,1)S(1)}) custom-call(f32[3,7,7]{2,1,0:T(8,128)S(1)} %copy-done.5, f32[3,7,7]{2,1,0:T(8,128)S(1)} %copy-done.6, bf16[80,240]{1,0:T(8,128)(2,1)S(1)} %copy-done.4, f32[80,7]{1,0:T(8,128)S(1)} %copy-done.3, f32[7,240]{1,0:T(8,128)S(1)} %copy-done.7, ...), custom_call_target="tpu_custom_call" | custom-call | flops 2000000 | bytes 1000000 | tf_op jit(solution)/shard_map/pallas_call | solution.py:726
  12.9 5.4 %collective-permute-done.3.c_low = f32[1,88,128]{2,1,0:T(8,128)S(1)} collective-permute-done((f32[1,88,128]{2,1,0:T(8,128)S(1)}, f32[1,88,128]{2,1,0:T(8,128)S(1)}, u32[]{:S(2)}, u32[]{:S(2)}) %collective-permute-start.3) | collective-permute-done | bytes 45088 | tf_op jit(solution)/shard_map/ppermute | solution.py:690
  18.8 2.8 %collective-permute-start.5 = (f32[80,1024]{1,0:T(8,128)S(1)}, f32[80,1024]{1,0:T(8,128)S(1)}, u32[]{:S(2)}, u32[]{:S(2)}) collective-permute-start(f32[80,1024]{1,0:T(8,128)S(1)} %get-tuple-element.46), channel_id=1, source_target_pairs={{0,30},{2,4},{4,2},{6,8},{8,6},{10,12},{12,10},{14,16},{16,14},{18... | collective-permute-start | bytes 983048 | tf_op jit(solution)/shard_map/ppermute | solution.py:676
  21.8 11.9 %all_to_all.10.got_ref = f32[32,8,128]{2,1,0:T(8,128)S(1)} all-to-all(f32[32,8,128]{2,1,0:T(8,128)S(1)} %shard_map.151), channel_id=1, replica_groups=mesh['sector'=16,'span'=2] {'sector','span'}, dimensions={0} | all-to-all | bytes 262144 | tf_op jit(solution)/shard_map/all_to_all | solution.py:710
  33.6 1.7 %shard_map.152 = (f32[3,2,80,128]{3,2,1,0:T(8,128)S(1)}, f32[80,128]{1,0:T(8,128)S(1)}, f32[80,2048]{1,0:T(8,128)S(1)}, f32[80,2048]{1,0:T(8,128)S(1)}) custom-call(bf16[560,240]{1,0:T(8,128)(2,1)S(1)} %get-tuple-element.34.w_ref, f32[88,1024]{1,0:T(8,128)S(1)} %get-tuple-element.35.m0_ref, f32[88,1024]{1,0:T(8,128)S(1)} %get-tuple-element.36.m1_ref, ...), custom_call_target="tpu_custom_call" | custom-call | flops 2000000 | bytes 1000000 | tf_op jit(solution)/shard_map/pallas_call | solution.py:733
  35.3 2.5 %shard_map.153 = (f32[80,2048]{1,0:T(8,128)S(1)}, f32[80,1024]{1,0:T(8,128)S(1)}, f32[80,1024]{1,0:T(8,128)S(1)}) custom-call(bf16[560,240]{1,0:T(8,128)(2,1)S(1)} %get-tuple-element.34.w_ref, f32[88,1024]{1,0:T(8,128)S(1)} %get-tuple-element.35.m0_ref, f32[88,1024]{1,0:T(8,128)S(1)} %get-tuple-element.36.m1_ref, f32[80,2048]{1,0:T(8,128)S(1)} %get-tuple-element.40.f_ref, ...), custom_call_target="tpu_custom_call" | custom-call | flops 2000000 | bytes 1000000 | tf_op jit(solution)/shard_map/pallas_call | solution.py:737
  37.9 0.8 %shard_map.155 = (f32[80,1152]{1,0:T(8,128)S(1)}, f32[80,1152]{1,0:T(8,128)S(1)}, f32[1,80,512]{2,1,0:T(8,128)S(1)}, f32[1,80,128]{2,1,0:T(8,128)S(1)}, f32[1,80,128]{2,1,0:T(8,128)S(1)}) custom-call(bf16[560,240]{1,0:T(8,128)(2,1)S(1)} %get-tuple-element.34.w_ref, f32[88,1024]{1,0:T(8,128)S(1)} %get-tuple-element.35.m0_ref, ...), custom_call_target="tpu_custom_call" | custom-call | flops 2000000 | bytes 1000000 | tf_op jit(solution)/shard_map/pallas_call | solution.py:741
  38.7 0.7 collective-permute-start.8
  39.3 0.7 %collective-permute-start.7 = (f32[1,80,512]{2,1,0:T(8,128)S(1)}, f32[1,80,512]{2,1,0:T(8,128)S(1)}, u32[]{:S(2)}, u32[]{:S(2)}) collective-permute-start(f32[1,80,512]{2,1,0:T(8,128)S(1)} %get-tuple-element.50), channel_id=1, source_target_pairs={{0,1},{1,0},{2,3},{3,2},{4,5},{5,4},{6,7},{7,6},{8,9},{9,8},{10,11... | collective-permute-start | bytes 491528 | tf_op jit(solution)/shard_map/ppermute | solution.py:690
  40.0 4.3 %collective-permute-start.10 = (f32[1,80,128]{2,1,0:T(8,128)S(1)}, f32[1,80,128]{2,1,0:T(8,128)S(1)}, u32[]{:S(2)}, u32[]{:S(2)}) collective-permute-start(f32[1,80,128]{2,1,0:T(8,128)S(1)} %get-tuple-element.52), channel_id=1, source_target_pairs={{0,31},{1,30},{2,5},{3,4},{4,3},{5,2},{6,9},{7,8},{8,7},{9,6},{10,... | collective-permute-start | bytes 122888 | tf_op jit(solution)/shard_map/ppermute | solution.py:690
  44.4 2.4 %collective-permute-done.7.side_ref = f32[1,80,512]{2,1,0:T(8,128)S(1)} collective-permute-done((f32[1,80,512]{2,1,0:T(8,128)S(1)}, f32[1,80,512]{2,1,0:T(8,128)S(1)}, u32[]{:S(2)}, u32[]{:S(2)}) %collective-permute-start.7) | collective-permute-done | bytes 163872 | tf_op jit(solution)/shard_map/ppermute | solution.py:690
  46.8 0.8 %shard_map.156 = (f32[80,2048]{1,0:T(8,128)S(1)}, f32[80,1024]{1,0:T(8,128)S(1)}, f32[80,1024]{1,0:T(8,128)S(1)}) custom-call(bf16[560,240]{1,0:T(8,128)(2,1)S(1)} %get-tuple-element.34.w_ref, f32[88,1024]{1,0:T(8,128)S(1)} %get-tuple-element.35.m0_ref, f32[88,1024]{1,0:T(8,128)S(1)} %get-tuple-element.36.m1_ref, f32[80,2048]{1,0:T(8,128)S(1)} %get-tuple-element.40.f_ref, ...), custom_call_target="tpu_custom_call" | custom-call | flops 2000000000 | bytes 1000000 | tf_op jit(solution)/shard_map/pallas_call | solution.py:748
  47.6 2.2 %collective-permute-start.12 = (f32[80,1024]{1,0:T(8,128)S(1)}, f32[80,1024]{1,0:T(8,128)S(1)}, u32[]{:S(2)}, u32[]{:S(2)}) collective-permute-start(f32[80,1024]{1,0:T(8,128)S(1)} %get-tuple-element.59), channel_id=1, source_target_pairs={{0,30},{2,4},{4,2},{6,8},{8,6},{10,12},{12,10},{14,16},{16,14},{18... | collective-permute-start | bytes 983048 | tf_op jit(solution)/shard_map/ppermute | solution.py:676
  49.8 2.9 %shard_map.157 = (f32[16,8,128]{2,1,0:T(8,128)S(1)}, f32[80,1024]{1,0:T(8,128)S(1)}, f32[80,1024]{1,0:T(8,128)S(1)}, f32[80,2048]{1,0:T(8,128)S(1)}, f32[8,1024]{1,0:T(8,128)S(1)}) custom-call(bf16[560,240]{1,0:T(8,128)(2,1)S(1)} %get-tuple-element.34.w_ref, f32[88,1024]{1,0:T(8,128)S(1)} %get-tuple-element.35.m0_ref, ...), custom_call_target="tpu_custom_call" | custom-call | flops 4000000000 | bytes 1000000 | tf_op jit(solution)/shard_map/pallas_call | solution.py:752
  52.8 12.8 %all_to_all.11.got_ref = f32[16,8,128]{2,1,0:T(8,128)S(1)} all-to-all(f32[16,8,128]{2,1,0:T(8,128)S(1)} %get-tuple-element.61), channel_id=1, replica_groups=mesh['sector'=16,'span'=2] {'sector'}, dimensions={0} | all-to-all | bytes 131072 | tf_op jit(solution)/shard_map/all_to_all | solution.py:759
  65.5 0.8 %shard_map.159 = f32[7,32,11]{2,1,0:T(8,128)} custom-call(f32[16,8,128]{2,1,0:T(8,128)S(1)} %all_to_all.11.got_ref), custom_call_target="tpu_custom_call" | custom-call | flops 2000000 | bytes 1000000 | tf_op jit(solution)/shard_map/pallas_call | solution.py:760
  66.3 1.4 %shard_map.158 = f32[1232,128]{1,0:T(8,128)} custom-call(bf16[80,240]{1,0:T(8,128)(2,1)S(1)} %get-tuple-element.32.w_ref.down_ref, bf16[80,240]{1,0:T(8,128)(2,1)S(1)} %get-tuple-element.33.up_ref, f32[8,1024]{1,0:T(8,128)S(1)} %get-tuple-element.55.rates_ref, f32[80,1024]{1,0:T(8,128)S(1)} %get-tuple-element.56.n0_ref, ...), custom_call_target="tpu_custom_call" | custom-call | flops 2000000 | bytes 1000000 | tf_op jit(solution)/shard_map/pallas_call | solution.py:761
  (49 shorter events, 1.3 us)
Async XLA Ops:
  0.6 0.7 %copy-start.11 = (s32[11,2,8]{0,2,1:T(8,128)S(1)}, s32[11,2,8]{0,2,1:T(8,128)}, u32[]{:S(2)}) copy-start(s32[11,2,8]{0,2,1:T(8,128)} %param.22) | copy-start | bytes 2116
  1.4 0.8 %copy-start.8 = (f32[3,2,8,128]{3,2,1,0:T(8,128)S(1)}, f32[3,2,8,128]{3,2,1,0:T(8,128)}, u32[]{:S(2)}) copy-start(f32[3,2,8,128]{3,2,1,0:T(8,128)} %param.16) | copy-start | bytes 73732
  2.9 1.1 %copy-start = (f32[11,7,2,8,128]{4,3,2,1,0:T(8,128)S(1)}, f32[11,7,2,8,128]{4,3,2,1,0:T(8,128)}, u32[]{:S(2)}) copy-start(f32[11,7,2,8,128]{4,3,2,1,0:T(8,128)} %param.14) | copy-start | bytes 1892356
  3.9 7.8 %copy-start.2 = (f32[80,240]{1,0:T(8,128)S(1)}, f32[80,240]{1,0:T(8,128)}, u32[]{:S(2)}) copy-start(f32[80,240]{1,0:T(8,128)} %constant.16.clone.diagonal_ref) | copy-start | bytes 230404
  3.9 7.8 %copy-start.3 = (f32[80,7]{1,0:T(8,128)S(1)}, f32[80,7]{1,0:T(8,128)}, u32[]{:S(2)}) copy-start(f32[80,7]{1,0:T(8,128)} %constant.14.clone.rows_ref) | copy-start | bytes 6724
  3.9 7.8 %copy-start.4 = (bf16[80,240]{1,0:T(8,128)(2,1)S(1)}, bf16[80,240]{1,0:T(8,128)(2,1)}, u32[]{:S(2)}) copy-start(bf16[80,240]{1,0:T(8,128)(2,1)} %constant.13.clone.spectral_ref) | copy-start | bytes 115204
  3.9 7.8 %copy-start.5 = (f32[3,7,7]{2,1,0:T(8,128)S(1)}, f32[3,7,7]{2,1,0:T(8,128)}, u32[]{:S(2)}) copy-start(f32[3,7,7]{2,1,0:T(8,128)} %up_ref.1) | copy-start | bytes 1768
  3.9 7.8 %copy-start.6 = (f32[3,7,7]{2,1,0:T(8,128)S(1)}, f32[3,7,7]{2,1,0:T(8,128)}, u32[]{:S(2)}) copy-start(f32[3,7,7]{2,1,0:T(8,128)} %down_ref.1) | copy-start | bytes 1768
  4.3 7.5 %copy-start.7 = (f32[7,240]{1,0:T(8,128)S(1)}, f32[7,240]{1,0:T(8,128)}, u32[]{:S(2)}) copy-start(f32[7,240]{1,0:T(8,128)} %constant.15.clone.lanes_ref) | copy-start | bytes 20164
  4.3 14.4 %collective-permute-start = (f32[88,1024]{1,0:T(8,128)S(1)}, f32[88,1024]{1,0:T(8,128)S(1)}, u32[]{:S(2)}, u32[]{:S(2)}) collective-permute-start(f32[88,1024]{1,0:T(8,128)S(1)} %get-tuple-element.35.m0_ref), channel_id=1, source_target_pairs={{0,30},{2,4},{4,2},{6,8},{8,6},{10,12},{12,10},{14,16},{16,14},{18... | collective-permute-start | bytes 1081352 | tf_op jit(solution)/shard_map/ppermute | solution.py:676
  9.8 8.9 %collective-permute-start.1 = (f32[88,1024]{1,0:T(8,128)S(1)}, f32[88,1024]{1,0:T(8,128)S(1)}, u32[]{:S(2)}, u32[]{:S(2)}) collective-permute-start(f32[88,1024]{1,0:T(8,128)S(1)} %get-tuple-element.36.m1_ref), channel_id=1, source_target_pairs={{0,2},{2,0},{4,6},{6,4},{8,10},{10,8},{12,14},{14,12},{16,18},{18,... | collective-permute-start | bytes 1081352 | tf_op jit(solution)/shard_map/ppermute | solution.py:676
  9.8 8.9 %collective-permute-start.2 = (f32[1,88,512]{2,1,0:T(8,128)S(1)}, f32[1,88,512]{2,1,0:T(8,128)S(1)}, u32[]{:S(2)}, u32[]{:S(2)}) collective-permute-start(f32[1,88,512]{2,1,0:T(8,128)S(1)} %get-tuple-element.37), channel_id=1, source_target_pairs={{0,1},{1,0},{2,3},{3,2},{4,5},{5,4},{6,7},{7,6},{8,9},{9,8},{10,11... | collective-permute-start | bytes 540680 | tf_op jit(solution)/shard_map/ppermute | solution.py:690
  11.3 7.1 %collective-permute-start.3 = (f32[1,88,128]{2,1,0:T(8,128)S(1)}, f32[1,88,128]{2,1,0:T(8,128)S(1)}, u32[]{:S(2)}, u32[]{:S(2)}) collective-permute-start(f32[1,88,128]{2,1,0:T(8,128)S(1)} %get-tuple-element.38), channel_id=1, source_target_pairs={{0,31},{1,30},{2,5},{3,4},{4,3},{5,2},{6,9},{7,8},{8,7},{9,6},{10,... | collective-permute-start | bytes 135176 | tf_op jit(solution)/shard_map/ppermute | solution.py:690
  11.8 6.9 %collective-permute-start.4 = (f32[1,88,128]{2,1,0:T(8,128)S(1)}, f32[1,88,128]{2,1,0:T(8,128)S(1)}, u32[]{:S(2)}, u32[]{:S(2)}) collective-permute-start(f32[1,88,128]{2,1,0:T(8,128)S(1)} %get-tuple-element.39), channel_id=1, source_target_pairs={{0,3},{1,2},{2,1},{3,0},{4,7},{5,6},{6,5},{7,4},{8,11},{9,10},{10,... | collective-permute-start | bytes 135176 | tf_op jit(solution)/shard_map/ppermute | solution.py:690
  18.7 2.9 %copy-start.1 = (f32[11,7,4,8]{0,3,2,1:T(8,128)S(1)}, f32[11,7,4,8]{0,3,2,1:T(8,128)}, u32[]{:S(2)}) copy-start(f32[11,7,4,8]{0,3,2,1:T(8,128)} %param.21) | copy-start | bytes 29572
  18.8 19.1 %collective-permute-start.5 = (f32[80,1024]{1,0:T(8,128)S(1)}, f32[80,1024]{1,0:T(8,128)S(1)}, u32[]{:S(2)}, u32[]{:S(2)}) collective-permute-start(f32[80,1024]{1,0:T(8,128)S(1)} %get-tuple-element.46), channel_id=1, source_target_pairs={{0,30},{2,4},{4,2},{6,8},{8,6},{10,12},{12,10},{14,16},{16,14},{18... | collective-permute-start | bytes 983048 | tf_op jit(solution)/shard_map/ppermute | solution.py:676
  21.6 16.3 %collective-permute-start.6 = (f32[80,1024]{1,0:T(8,128)S(1)}, f32[80,1024]{1,0:T(8,128)S(1)}, u32[]{:S(2)}, u32[]{:S(2)}) collective-permute-start(f32[80,1024]{1,0:T(8,128)S(1)} %get-tuple-element.47), channel_id=1, source_target_pairs={{0,2},{2,0},{4,6},{6,4},{8,10},{10,8},{12,14},{14,12},{16,18},{18,... | collective-permute-start | bytes 983048 | tf_op jit(solution)/shard_map/ppermute | solution.py:676
  38.7 11.1 %collective-permute-start.8 = (f32[80,1152]{1,0:T(8,128)S(1)}, f32[80,1152]{1,0:T(8,128)S(1)}, u32[]{:S(2)}, u32[]{:S(2)}) collective-permute-start(f32[80,1152]{1,0:T(8,128)S(1)} %get-tuple-element.48.x0_ref), channel_id=1, source_target_pairs={{0,30},{2,4},{4,2},{6,8},{8,6},{10,12},{12,10},{14,16},{16,14},{18... | collective-permute-start | bytes 1105928 | tf_op jit(solution)/shard_map/ppermute | solution.py:676
  39.3 10.5 %collective-permute-start.9 = (f32[80,1152]{1,0:T(8,128)S(1)}, f32[80,1152]{1,0:T(8,128)S(1)}, u32[]{:S(2)}, u32[]{:S(2)}) collective-permute-start(f32[80,1152]{1,0:T(8,128)S(1)} %get-tuple-element.49.x1_ref), channel_id=1, source_target_pairs={{0,2},{2,0},{4,6},{6,4},{8,10},{10,8},{12,14},{14,12},{16,18},{18,... | collective-permute-start | bytes 1105928 | tf_op jit(solution)/shard_map/ppermute | solution.py:676
  39.3 7.4 %collective-permute-start.7 = (f32[1,80,512]{2,1,0:T(8,128)S(1)}, f32[1,80,512]{2,1,0:T(8,128)S(1)}, u32[]{:S(2)}, u32[]{:S(2)}) collective-permute-start(f32[1,80,512]{2,1,0:T(8,128)S(1)} %get-tuple-element.50), channel_id=1, source_target_pairs={{0,1},{1,0},{2,3},{3,2},{4,5},{5,4},{6,7},{7,6},{8,9},{9,8},{10,11... | collective-permute-start | bytes 491528 | tf_op jit(solution)/shard_map/ppermute | solution.py:690
  40.0 9.7 %collective-permute-start.10 = (f32[1,80,128]{2,1,0:T(8,128)S(1)}, f32[1,80,128]{2,1,0:T(8,128)S(1)}, u32[]{:S(2)}, u32[]{:S(2)}) collective-permute-start(f32[1,80,128]{2,1,0:T(8,128)S(1)} %get-tuple-element.52), channel_id=1, source_target_pairs={{0,31},{1,30},{2,5},{3,4},{4,3},{5,2},{6,9},{7,8},{8,7},{9,6},{10,... | collective-permute-start | bytes 122888 | tf_op jit(solution)/shard_map/ppermute | solution.py:690
  44.4 5.4 %collective-permute-start.11 = (f32[1,80,128]{2,1,0:T(8,128)S(1)}, f32[1,80,128]{2,1,0:T(8,128)S(1)}, u32[]{:S(2)}, u32[]{:S(2)}) collective-permute-start(f32[1,80,128]{2,1,0:T(8,128)S(1)} %get-tuple-element.53), channel_id=1, source_target_pairs={{0,3},{1,2},{2,1},{3,0},{4,7},{5,6},{6,5},{7,4},{8,11},{9,10},{10,... | collective-permute-start | bytes 122888 | tf_op jit(solution)/shard_map/ppermute | solution.py:690
  47.6 18.7 %collective-permute-start.12 = (f32[80,1024]{1,0:T(8,128)S(1)}, f32[80,1024]{1,0:T(8,128)S(1)}, u32[]{:S(2)}, u32[]{:S(2)}) collective-permute-start(f32[80,1024]{1,0:T(8,128)S(1)} %get-tuple-element.59), channel_id=1, source_target_pairs={{0,30},{2,4},{4,2},{6,8},{8,6},{10,12},{12,10},{14,16},{16,14},{18... | collective-permute-start | bytes 983048 | tf_op jit(solution)/shard_map/ppermute | solution.py:676
  49.8 16.5 %collective-permute-start.13 = (f32[80,1024]{1,0:T(8,128)S(1)}, f32[80,1024]{1,0:T(8,128)S(1)}, u32[]{:S(2)}, u32[]{:S(2)}) collective-permute-start(f32[80,1024]{1,0:T(8,128)S(1)} %get-tuple-element.60), channel_id=1, source_target_pairs={{0,2},{2,0},{4,6},{6,4},{8,10},{10,8},{12,14},{14,12},{16,18},{18,... | collective-permute-start | bytes 983048 | tf_op jit(solution)/shard_map/ppermute | solution.py:676
  (3 other events, 2.1 us)

commit v7 on v2

--- a/solution.py
+++ b/solution.py
@@ -16,9 +16,8 @@
 WINDOW = 8
 HIGHEST = lax.Precision.HIGHEST
 DOWN_AZ, SPECTRAL, UP_SP, DOWN_SP, UP_AX, DOWN_AX, UP_AZ = range(7)
-C_TIME, C_AZ, C_SP, C_UP, C_DOWN, C_MASK = range(6)
+C_TIME, C_AZ, C_SP, C_UP, C_DOWN, C_MASK, C_OWNER = range(7)
 RATES = 8
-GROUP = 3
 AXES = ("sector", "span")
 
 
@@ -363,26 +362,40 @@
     return corner
 
 
-def prepare(plan, rhs_ref, coef_ref, m_ref, side_ref, c0_ref, c1_ref):
-    pad = plan.pad
-    lane = lane_index(1)
+def prepare(plan, rhs_ref, coef_ref, both_ref, m_ref, side_ref, c0_ref, c1_ref, rates_ref):
+    pad, cells = plan.pad, plan.cells
+    mask, diag, time, *face = [coef_ref[cells * i : cells * (i + 1), :] for i in range(6)]
+    scale = mask / diag
+    lane = lane_index(cells)
+    axial = scale * face[2]
+    rates = (
+        scale * time, scale * face[0], scale * face[1],
+        jnp.where(lane < LANES - 1, axial, 0.0), jnp.where(lane > 0, axial, 0.0), scale,
+    )
+    for i, rate in enumerate(rates):
+        rates_ref[i] = rate
     tail = jnp.zeros((pad - plan.tf, LANES), jnp.float32)
+    rest = jnp.zeros((RATES - 6, LANES), jnp.float32)
     mirror = parity()
-    for cell in range(plan.cells):
+    for cell in range(cells):
         a, r = divmod(cell, plan.rows)
         there = jnp.where(mirror == 0, a, plan.ct - 1 - a) * plan.rows + r
-        mask, diag, time, *face = [coef_ref[pl.ds(there + plan.cells * i, 1), :] for i in range(6)]
-        scale = mask / diag
-        axial = scale * face[2]
-        rates = [
-            scale * time, scale * face[0], scale * face[1],
-            jnp.where(lane < LANES - 1, axial, 0.0), jnp.where(lane > 0, axial, 0.0), scale,
-            jnp.zeros((RATES - 6, LANES), jnp.float32),
-        ]
-        field = jnp.concatenate([rhs_ref[pl.ds(there, plan.tf, stride=plan.cells), :], tail], axis=0) * scale
-        m_ref[:pad, at(cell)] = field
-        m_ref[pad:, at(cell)] = jnp.concatenate(rates, axis=0)
+        table = [rates_ref[i, pl.ds(there, 1), :] for i in range(6)]
+        field = jnp.concatenate([rhs_ref[pl.ds(there, plan.tf, stride=cells), :], tail], axis=0)
+        m_ref[:pad, at(cell)] = field * table[C_MASK]
+        m_ref[pad:, at(cell)] = jnp.concatenate(table + [rest], axis=0)
     write_edges(plan, m_ref, side_ref, (c0_ref, c1_ref))
+    wide = 2 * cells
+    row = slice(pad + C_OWNER, pad + C_OWNER + 1)
+    for t in range(plan.insts):
+        both = both_ref[t : t + 1, :]
+        lanes = slice(t * wide, (t + 1) * wide)
+        m_ref[row, lanes] = both
+        group, part = divmod(t, LANES // wide)
+        for n in range(plan.ends):
+            side_ref[n, row, lanes] = both
+            for ref in (c0_ref, c1_ref):
+                ref[n, pad + group : pad + group + 1, part * wide : (part + 1) * wide] = both
 
 
 def write_edges(plan, x_ref, side_ref, c_refs):
@@ -413,17 +426,11 @@
     down_out[...] = matrix(plan, out_ref, DOWN_AZ)
 
 
-def send_panels(plan, stator_ref, both_ref, out_ref, panels_ref):
+def send_panels(plan, stator_ref, out_ref, panels_ref):
     me = lax.axis_index("sector")
     for f in range(plan.fields):
         panels_ref[pl.ds(f, plan.insts, stride=RATES), : plan.width] = jnp.transpose(stator_ref[f])
     out_ref[...] = jnp.zeros_like(out_ref)
-    both = both_ref[...]
-    for t in range(plan.insts):
-        group, row = divmod(t, GROUP)
-        lanes = slice(group * 2 * plan.cells, (group + 1) * 2 * plan.cells)
-        row += RATES
-        out_ref[:, row : row + 1, lanes] = jnp.broadcast_to(both[t : t + 1][None], (out_ref.shape[0], 1, 2 * plan.cells))
     for o, slots in enumerate(plan.slots):
         to = lax.rem(me + (plan.sectors - o), plan.sectors) * plan.spans
         for slot, t in enumerate(slots):
@@ -434,27 +441,51 @@
 
 
 def begin(
-    plan, w_ref, m_ref, got_ref,
+    plan, w_ref, m_ref, got_ref, low_ref, high_ref, side_ref, c_low, c_high,
     seams_ref, weight_ref, x_ref, g_ref, panels_ref, terms_ref, rows_ref, p0_ref, p1_ref,
 ):
     pad, insts, fields = plan.pad, plan.insts, plan.fields
     me, span = lax.axis_index("sector"), lax.axis_index("span")
+    even, is_first = parity() == 0, span == 0
     tiles = plan.tiles
     panels_ref[...] = jnp.zeros_like(panels_ref)
-    rows_ref[...] = jnp.zeros_like(rows_ref)
-    wide = 2 * plan.cells
     for n, (k, x) in enumerate(tiles):
         at_span = x if plan.spans == 2 else jnp.clip(span + x, 0, plan.spans - 1)
         for t in range(insts):
             o = (k + plan.shift[t]) % plan.sectors
             source = lax.rem(me + o, plan.sectors) * plan.spans + at_span
-            tile = rolled(got_ref[source, :RATES], -plan.slots[o].index(t) * plan.width)
+            tile = rolled(got_ref[source], -plan.slots[o].index(t) * plan.width)
             panels_ref[t * fields : (t + 1) * fields, n * LANES : n * LANES + plan.width] = tile[:fields, : plan.width]
-        source = lax.rem(me + k + plan.sectors, plan.sectors) * plan.spans + at_span
-        table = got_ref[source, RATES:]
-        for group in range(-(-insts // GROUP)):
-            shifted = rolled(table, -group * wide)
-            rows_ref[group * GROUP : (group + 1) * GROUP, n * LANES : n * LANES + wide] = shifted[:GROUP, :wide]
+
+    wide = 2 * plan.cells
+    row = slice(pad + C_OWNER, pad + C_OWNER + 1)
+    zeros = jnp.zeros((16 - insts, LANES), jnp.float32)
+
+    def table(read, packed):
+        out = []
+        for t in range(insts):
+            group, part = divmod(t, LANES // wide)
+            lanes = at(0 if packed else group)
+            out.append(rolled(read(pad + group if packed else row.start, lanes), -part * wide))
+        return jnp.concatenate(out + [zeros], axis=0)
+
+    own = [table(lambda i, lanes: m_ref[i : i + 1, lanes], False)]
+    low = [table(lambda i, lanes: low_ref[i : i + 1, lanes], False)]
+    high = [table(lambda i, lanes: high_ref[i : i + 1, lanes], False)]
+    for n in range(plan.ends):
+        own.append(table(lambda i, lanes: side_ref[n, i : i + 1, lanes], False))
+        low.append(table(lambda i, lanes: c_low[n, i : i + 1, lanes], True))
+        high.append(table(lambda i, lanes: c_high[n, i : i + 1, lanes], True))
+    for n, (k, x) in enumerate(tiles):
+        if k == 0:
+            block = own
+        else:
+            block = [jnp.where(even, *pair) for pair in (zip(low, high) if k < 0 else zip(high, low))]
+        if plan.spans == 2:
+            value = jnp.where(is_first, block[x], block[1 - x])
+        else:
+            value = block[(0, 1, 2)[x]]
+        rows_ref[:, at(n)] = value
     spread = dot_full(plan.inst_rows(), rows_ref[...])
     spread = pick(jnp.concatenate([spread[:, at(n)] for n in range(len(tiles))], axis=0), plan.weight_lanes())
     first, share, panel = spread, rolled(spread, plan.ct * plan.width), plan.panel_lanes()
@@ -466,9 +497,6 @@
         terms_ref[n * pad : (n + 1) * pad, :] = panels + rolled(panels, plan.width)
     seams = pick(terms_ref[...] * weights, plan.window_lanes())
 
-    even = parity() == 0
-    is_first = span == 0
-
     def tile(values, k, x):
         n = tiles.index((k, x))
         return values[n * pad : (n + 1) * pad]
@@ -499,7 +527,7 @@
 
 def first_half(
     plan, w_ref, m_ref, f_ref, g_ref, low_ref, high_ref, side_ref, c_low, c_high, seams_ref,
-    x_ref, near_ref, side_out, c0_ref, c1_ref, p0_ref, p1_ref, y_ref, h_ref, n0_ref, n1_ref,
+    x_ref, near_ref, side_out, c0_ref, c1_ref, p0_ref, p1_ref, y_ref, h_ref, n0_ref, n1_ref, inlet_ref,
 ):
     own = two_layers(plan, f_ref, m_ref)
     low = two_layers(plan, low_ref, seam=seams_ref[0, 0])
@@ -511,17 +539,19 @@
         corners_of(plan, (c_low, c_high), seams_ref), y_ref, h_ref, n_refs,
     )
     lane = lane_index(plan.pad)
-    near_ref[:, plan.slab :] = jnp.zeros((plan.pad, LANES), jnp.float32)
+    inlet_ref[...] = jnp.zeros_like(inlet_ref)
 
     def put(a, r, value):
         x_ref[:, at(r, 1, a * plan.slab)] = value
         if a == 0:
             near_ref[:, at(r)] = value
         else:
-            here = rolled(value, r * WINDOW)
-            near_ref[:, plan.slab :] = jnp.where(lane == r * WINDOW, here, near_ref[:, plan.slab :])
+            inlet_ref[: plan.pad, :] = jnp.where(lane == r, rolled(value, r), inlet_ref[: plan.pad, :])
 
     outer_rows(plan, w_ref, own, near, (low[1].chunk, high[0].chunk), n_refs, h_ref, put)
+    turned = jnp.transpose(inlet_ref[...])
+    for r in range(plan.rows):
+        near_ref[plan.tf : plan.tf + 1, at(r)] = turned[r : r + 1, :]
     write_edges(plan, x_ref, side_out, (c0_ref, c1_ref))
 
 
@@ -533,7 +563,7 @@
 def middle(
     plan, w_ref, m_ref, f_ref, x_ref, g_ref, low_ref, high_ref, side_ref, c_low, c_high,
     low_first, high_first, side_first, seams_ref, weight_ref,
-    send_ref, n0_ref, h0_ref, x1_ref, rates_ref, p0_ref, p1_ref, y_ref, inlet_ref, h_ref, n1_ref,
+    send_ref, n0_ref, h0_ref, x1_ref, rates_ref, p0_ref, p1_ref, y_ref, inlet_ref, h_ref, n1_ref, turn_ref,
 ):
     pad = plan.pad
     own, force = two_layers(plan, x_ref, m_ref), two_layers(plan, f_ref, m_ref)
@@ -554,10 +584,15 @@
         if a == 1:
             x1_ref[:, at(r)] = value
 
+    turn_ref[...] = jnp.zeros_like(turn_ref)
+    for r in range(plan.rows):
+        turn_ref[r : r + 1, :] = low_ref[plan.tf : plan.tf + 1, at(r)]
+    far_tile = jnp.transpose(turn_ref[...])[:pad]
+
     def far_inlet(c):
-        tile = low_ref[:, plan.slab :]
         count = CHUNK // LANES
-        return jnp.concatenate([placed(tile, c * count + part) for part in range(count)], axis=1)
+        parts = [rolled(far_tile, -(c * count + part)) for part in range(count)]
+        return jnp.concatenate([jnp.where(lane == 0, part, 0.0) for part in parts], axis=1)
 
     outer_rows(plan, w_ref, own, near, (far_inlet, Layer(plan, high_ref).chunk), n_refs, h_ref, put)
     inlet = inlet_ref[...]
@@ -644,19 +679,19 @@
         return f32(ends, rows, DEPTH * plan.ct * LANES), f32(ends, rows, LANES), f32(ends, rows, LANES)
 
     stator = jnp.transpose(stator_adj, (1, 2, 3, 0)).reshape(fields, plan.width, insts)
-    sent = call(bind(send_panels, plan), f32(sectors * spans, 2 * RATES, LANES), (vmem(insts * RATES, LANES),))(
-        stator,
-        jnp.concatenate([
-            lax.rem(owner, plan.panels).astype(jnp.float32).reshape(insts, cells), first_panel_share.reshape(insts, cells),
-        ], axis=1),
-    )
+    sent = call(bind(send_panels, plan), f32(sectors * spans, RATES, LANES), (vmem(insts * RATES, LANES),))(stator)
     got = lax.all_to_all(sent, AXES, 0, 0, tiled=True)
-    m, side, c0, c1 = call(bind(prepare, plan), (f32(pad + RATES, plan.ct * slab),) + edges(pad + RATES))(
+    m, side, c0, c1 = call(
+        bind(prepare, plan), (f32(pad + RATES, plan.ct * slab),) + edges(pad + RATES), (vmem(6, cells, LANES),)
+    )(
         rhs.reshape(plan.tf * cells, LANES),
         jnp.concatenate([
             wall_mask.astype(jnp.float32).reshape(cells, LANES), diag_coef.reshape(cells, LANES),
             time_coef.reshape(cells, LANES), face_coef.reshape(3 * cells, LANES),
         ]),
+        jnp.concatenate([
+            lax.rem(owner, plan.panels).astype(jnp.float32).reshape(insts, cells), first_panel_share.reshape(insts, cells),
+        ], axis=1),
     )
     low_first, high_first = swap(m, next_chip), swap(m, next_core)
     side_first = beside(plan, side, alone)
@@ -670,10 +705,11 @@
         bind(begin, plan), (f32(3, 1 + ends, pad, LANES), f32(pad, LANES), whole, whole),
         (vmem(pad, tiles * LANES), vmem(tiles * pad, LANES), vmem(16, tiles * LANES)) + products,
         flops=2_000_000_000,
-    )(matrices, m, got)
+    )(matrices, m, got, low_first, high_first, side_first, c_low, c_high)
     x, near, side, c0, c1 = call(
-        bind(first_half, plan), (whole, f32(pad, slab + LANES)) + edges(pad),
-        products + (vmem(pad, 2 * slab), vmem(pad, 2 * slab), vmem(pad, slab), vmem(pad, slab)), flops=4_000_000_000,
+        bind(first_half, plan), (whole, half) + edges(pad),
+        products + (vmem(pad, 2 * slab), vmem(pad, 2 * slab), vmem(pad, slab), vmem(pad, slab), vmem(LANES, LANES)),
+        flops=4_000_000_000,
     )(matrices, m, force, g, low_first, high_first, side_first, c_low, c_high, seams)
 
     low, high = swap(near, next_chip), swap(x, next_core)
@@ -685,7 +721,8 @@
     far_low = swap(far, next_chip)
     back, n0, h0, x1, rates = call(
         bind(middle, plan), (f32(sectors, RATES, LANES), half, half, half, f32(RATES, slab)),
-        products + (vmem(pad, 2 * slab), vmem(pad, LANES), vmem(pad, 2 * slab), vmem(pad, slab)), flops=4_000_000_000,
+        products + (vmem(pad, 2 * slab), vmem(pad, LANES), vmem(pad, 2 * slab), vmem(pad, slab), vmem(LANES, LANES)),
+        flops=4_000_000_000,
     )(
         matrices, m, force, x, g, low, high, side, c_low, c_high, low_first, high_first, side_first, seams, weight
     )

time: 61.7 us -> 64.7 us (1.049)
  starting transfers between devices: 25.4 us -> 32.1 us
  waiting for transfers between devices: 17.9 us -> 14.3 us
  other arithmetic: 1.54 us -> 0.79 us
    all_to_all x1, starting transfers between devices: 4.36 us -> 8.28 us  [on_device(): returned = lax.all_to_all(back, 'sector', 0, 0, tiled=True)]
    all_to_all x1, waiting for transfers between devices: 6.11 us -> 2.82 us  [on_device(): got = lax.all_to_all(sent, AXES, 0, 0, tiled=True)]
    ppermute x5, starting transfers between devices: 10.9 us -> 13.2 us  [swap(): return lax.ppermute(array, 'sector', list(enumerate(partner)))]
    concatenate x1, other arithmetic: 0.74 us -> 0.01 us  [on_device(): jnp.concatenate([wall_mask.astype(jnp.float32).reshape(cells, LANES), dia...]
    unnamed x32 -> x34, local copies, waits for them, and re-layouts: 1.75 us -> 2.38 us
  transfers between devices with their start and end apart: 13 -> 13, of which waited for: 4 -> 6; matrix products, arithmetic and copies ran while one was open for 0% -> 0% of each run, Pallas kernels for 16% -> 12%
where the time goes in v7:
time: 64.7 us; the launch traced here: 64.2 us
  starting transfers between devices  32.1 us (50%)
  waiting for transfers between devices  14.3 us (22%)
  Pallas kernels  13.6 us (21%)
  local copies, waits for them, and re-layouts  2.54 us (4%)
  between operations  0.82 us (1%)
  other arithmetic  0.79 us (1%)
    ppermute x5, starting transfers between devices, swap(): return lax.ppermute(array, 'sector', list(enumerate(partner)))  13.2 us
    all_to_all x1, starting transfers between devices, on_device(): returned = lax.all_to_all(back, 'sector', 0, 0, tiled=True)  8.28 us
    ppermute x6, starting transfers between devices, beside(): return lax.ppermute(array, AXES, pairs(0))  7.89 us
    ppermute x6, waiting for transfers between devices, beside(): return lax.ppermute(array, AXES, pairs(0))  5.91 us
    all_to_all x1, waiting for transfers between devices, on_device(): returned = lax.all_to_all(back, 'sector', 0, 0, tiled=True)  5.58 us
    pallas_call x1, Pallas kernels, on_device(): call(bind(middle, plan), (f32(sectors, RATES, LANES), half, half, half, f...  3.68 us
    pallas_call x1, Pallas kernels, on_device(): call(bind(first_half, plan), (whole, half) + edges(pad), products + (vmem...  3.04 us
    all_to_all x1, waiting for transfers between devices, on_device(): got = lax.all_to_all(sent, AXES, 0, 0, tiled=True)  2.82 us
  transfers between devices with their start and end apart: 13, of which 6 were waited for; matrix products, arithmetic and copies ran while one was open for 0% of the time, Pallas kernels for 12%

profile of v7, /device:TPU:0, one launch (start us, length us, event | category | flops | bytes accessed | tf_op | source)
XLA Modules:
  0.0 64.2 jit_solution(15878982405166374914)
XLA Ops:
  0.6 0.7 %convert_bitcast_fusion = f32[16,128]{1,0:T(8,128)S(1)} fusion(s32[2,8,128]{2,1,0:T(8,128)} %param.20), kind=kLoop, calls=%fused_computation.7 | loop fusion | flops 2048 | bytes 16384 | tf_op jit(solution)/shard_map/reshape | solution.py:689
  2.9 1.1 %copy-done = f32[11,7,2,8,128]{4,3,2,1,0:T(8,128)S(1)} copy-done((f32[11,7,2,8,128]{4,3,2,1,0:T(8,128)S(1)}, f32[11,7,2,8,128]{4,3,2,1,0:T(8,128)}, u32[]{:S(2)}) %copy-start) | copy-done | bytes 630808
  4.8 5.7 %collective-permute-start = (f32[88,2048]{1,0:T(8,128)S(1)}, f32[88,2048]{1,0:T(8,128)S(1)}, u32[]{:S(2)}, u32[]{:S(2)}) collective-permute-start(f32[88,2048]{1,0:T(8,128)S(1)} %get-tuple-element.26.m_ref), channel_id=1, source_target_pairs={{0,30},{2,4},{4,2},{6,8},{8,6},{10,12},{12,10},{14,16},{16,14},{18... | collective-permute-start | bytes 2162696 | tf_op jit(solution)/shard_map/ppermute | solution.py:649
  10.4 0.8 %shard_map.151 = f32[32,8,128]{2,1,0:T(8,128)} custom-call(f32[7,32,11]{2,1,0:T(8,128)S(1)} %bitcast.17), custom_call_target="tpu_custom_call" | custom-call | flops 2000000 | bytes 1000000 | tf_op jit(solution)/shard_map/pallas_call | solution.py:682
  11.3 2.7 %all-to-all-start = ((f32[32,8,128]{2,1,0:T(8,128)}), f32[32,8,128]{2,1,0:T(8,128)S(1)}, u32[]{:S(2)}, u32[]{:S(2)}) async-start(f32[32,8,128]{2,1,0:T(8,128)} %shard_map.151), calls=%async_computation | async-start | bytes 262144 | tf_op jit(solution)/shard_map/all_to_all | solution.py:683
  14.0 1.7 %collective-permute-start.2 = (f32[1,88,512]{2,1,0:T(8,128)S(1)}, f32[1,88,512]{2,1,0:T(8,128)S(1)}, u32[]{:S(2)}, u32[]{:S(2)}) collective-permute-start(f32[1,88,512]{2,1,0:T(8,128)S(1)} %get-tuple-element.27), channel_id=1, source_target_pairs={{0,1},{1,0},{2,3},{3,2},{4,5},{5,4},{6,7},{7,6},{8,9},{9,8},{10,11... | collective-permute-start | bytes 540680 | tf_op jit(solution)/shard_map/ppermute | solution.py:663
  15.7 3.9 %collective-permute-start.3 = (f32[1,88,128]{2,1,0:T(8,128)S(1)}, f32[1,88,128]{2,1,0:T(8,128)S(1)}, u32[]{:S(2)}, u32[]{:S(2)}) collective-permute-start(f32[1,88,128]{2,1,0:T(8,128)S(1)} %get-tuple-element.28), channel_id=1, source_target_pairs={{0,31},{1,30},{2,5},{3,4},{4,3},{5,2},{6,9},{7,8},{8,7},{9,6},{10,... | collective-permute-start | bytes 135176 | tf_op jit(solution)/shard_map/ppermute | solution.py:663
  19.6 1.1 %shard_map.149 = (bf16[560,240]{1,0:T(8,128)(2,1)S(1)}, bf16[80,240]{1,0:T(8,128)(2,1)S(1)}) custom-call(f32[3,7,7]{2,1,0:T(8,128)S(1)} %copy-done.5, f32[3,7,7]{2,1,0:T(8,128)S(1)} %copy-done.6, bf16[80,240]{1,0:T(8,128)(2,1)S(1)} %copy-done.4, f32[80,7]{1,0:T(8,128)S(1)} %copy-done.3, f32[7,240]{1,0:T(8,128)S(1)} %copy-done.7, f32[80,240]{1,0:T(8,128)S(1)} %copy-done.2), custom_call_target="tpu_custom_call" | custom-call | flops 2000000 | bytes 1000000 | tf_op jit(solution)/shard_map/pallas_call | solution.py:699
  20.7 2.4 %collective-permute-done.3.c_low = f32[1,88,128]{2,1,0:T(8,128)S(1)} collective-permute-done((f32[1,88,128]{2,1,0:T(8,128)S(1)}, f32[1,88,128]{2,1,0:T(8,128)S(1)}, u32[]{:S(2)}, u32[]{:S(2)}) %collective-permute-start.3) | collective-permute-done | bytes 45088 | tf_op jit(solution)/shard_map/ppermute | solution.py:663
  23.2 0.7 %collective-permute-done.4.c_high = f32[1,88,128]{2,1,0:T(8,128)S(1)} collective-permute-done((f32[1,88,128]{2,1,0:T(8,128)S(1)}, f32[1,88,128]{2,1,0:T(8,128)S(1)}, u32[]{:S(2)}, u32[]{:S(2)}) %collective-permute-start.4) | collective-permute-done | bytes 45088 | tf_op jit(solution)/shard_map/ppermute | solution.py:663
  23.9 2.8 %all-to-all-done.got_ref = f32[32,8,128]{2,1,0:T(8,128)S(1)} async-done(((f32[32,8,128]{2,1,0:T(8,128)}), f32[32,8,128]{2,1,0:T(8,128)S(1)}, u32[]{:S(2)}, u32[]{:S(2)}) %all-to-all-start) | async-done | bytes 131104 | tf_op jit(solution)/shard_map/all_to_all | solution.py:683
  26.7 1.7 %shard_map.152 = (f32[3,2,80,128]{3,2,1,0:T(8,128)S(1)}, f32[80,128]{1,0:T(8,128)S(1)}, f32[80,2048]{1,0:T(8,128)S(1)}, f32[80,2048]{1,0:T(8,128)S(1)}) custom-call(bf16[560,240]{1,0:T(8,128)(2,1)S(1)} %get-tuple-element.25.w_ref, f32[88,2048]{1,0:T(8,128)S(1)} %get-tuple-element.26.m_ref, f32[32,8,128]{2,1,0:T(8,128)S(1)} %all-to-all-done.got_ref, ...), custom_call_target="tpu_custom_call" | custom-call | flops 2000000000 | bytes 1000000 | tf_op jit(solution)/shard_map/pallas_call | solution.py:704
  28.5 3.0 %shard_map.153 = (f32[80,2048]{1,0:T(8,128)S(1)}, f32[80,1024]{1,0:T(8,128)S(1)}, f32[1,80,512]{2,1,0:T(8,128)S(1)}, f32[1,80,128]{2,1,0:T(8,128)S(1)}, f32[1,80,128]{2,1,0:T(8,128)S(1)}) custom-call(bf16[560,240]{1,0:T(8,128)(2,1)S(1)} %get-tuple-element.25.w_ref, f32[88,2048]{1,0:T(8,128)S(1)} %get-tuple-element.26.m_ref, ...), custom_call_target="tpu_custom_call" | custom-call | flops 4000000000 | bytes 1000000 | tf_op jit(solution)/shard_map/pallas_call | solution.py:709
  31.5 2.1 %collective-permute-start.5 = (f32[1,80,512]{2,1,0:T(8,128)S(1)}, f32[1,80,512]{2,1,0:T(8,128)S(1)}, u32[]{:S(2)}, u32[]{:S(2)}) collective-permute-start(f32[1,80,512]{2,1,0:T(8,128)S(1)} %get-tuple-element.34), channel_id=1, source_target_pairs={{0,1},{1,0},{2,3},{3,2},{4,5},{5,4},{6,7},{7,6},{8,9},{9,8},{10,11... | collective-permute-start | bytes 491528 | tf_op jit(solution)/shard_map/ppermute | solution.py:663
  33.6 3.7 %collective-permute-start.6 = (f32[80,1024]{1,0:T(8,128)S(1)}, f32[80,1024]{1,0:T(8,128)S(1)}, u32[]{:S(2)}, u32[]{:S(2)}) collective-permute-start(f32[80,1024]{1,0:T(8,128)S(1)} %get-tuple-element.36), channel_id=1, source_target_pairs={{0,30},{2,4},{4,2},{6,8},{8,6},{10,12},{12,10},{14,16},{16,14},{18... | collective-permute-start | bytes 983048 | tf_op jit(solution)/shard_map/ppermute | solution.py:649
  37.6 1.1 %collective-permute-done.5.side_ref = f32[1,80,512]{2,1,0:T(8,128)S(1)} collective-permute-done((f32[1,80,512]{2,1,0:T(8,128)S(1)}, f32[1,80,512]{2,1,0:T(8,128)S(1)}, u32[]{:S(2)}, u32[]{:S(2)}) %collective-permute-start.5) | collective-permute-done | bytes 163872 | tf_op jit(solution)/shard_map/ppermute | solution.py:663
  38.7 0.8 %shard_map.154 = (f32[80,2048]{1,0:T(8,128)S(1)}, f32[80,1024]{1,0:T(8,128)S(1)}) custom-call(bf16[560,240]{1,0:T(8,128)(2,1)S(1)} %get-tuple-element.25.w_ref, f32[88,2048]{1,0:T(8,128)S(1)} %get-tuple-element.26.m_ref, f32[80,2048]{1,0:T(8,128)S(1)} %get-tuple-element.30.f_ref, f32[80,2048]{1,0:T(8,128)S(1)} %get-tuple-element.33.x_ref, ...), custom_call_target="tpu_custom_call" | custom-call | flops 2000000000 | bytes 1000000 | tf_op jit(solution)/shard_map/pallas_call | solution.py:718
  39.5 3.3 %collective-permute-start.10 = (f32[80,1024]{1,0:T(8,128)S(1)}, f32[80,1024]{1,0:T(8,128)S(1)}, u32[]{:S(2)}, u32[]{:S(2)}) collective-permute-start(f32[80,1024]{1,0:T(8,128)S(1)} %get-tuple-element.44), channel_id=1, source_target_pairs={{0,30},{2,4},{4,2},{6,8},{8,6},{10,12},{12,10},{14,16},{16,14},{18... | collective-permute-start | bytes 983048 | tf_op jit(solution)/shard_map/ppermute | solution.py:649
  42.8 1.7 %collective-permute-done.8.c_low = f32[1,80,128]{2,1,0:T(8,128)S(1)} collective-permute-done((f32[1,80,128]{2,1,0:T(8,128)S(1)}, f32[1,80,128]{2,1,0:T(8,128)S(1)}, u32[]{:S(2)}, u32[]{:S(2)}) %collective-permute-start.8) | collective-permute-done | bytes 40992 | tf_op jit(solution)/shard_map/ppermute | solution.py:663
  44.5 3.7 %shard_map.155 = (f32[16,8,128]{2,1,0:T(8,128)}, f32[80,1024]{1,0:T(8,128)S(1)}, f32[80,1024]{1,0:T(8,128)S(1)}, f32[80,1024]{1,0:T(8,128)S(1)}, f32[8,1024]{1,0:T(8,128)S(1)}) custom-call(bf16[560,240]{1,0:T(8,128)(2,1)S(1)} %get-tuple-element.25.w_ref, f32[88,2048]{1,0:T(8,128)S(1)} %get-tuple-element.26.m_ref, f32[80,2048]{1,0:T(8,128)S(1)} %get-tuple-element.30.f_ref, ...), custom_call_target="tpu_custom_call" | custom-call | flops 4000000000 | bytes 1000000 | tf_op jit(solution)/shard_map/pallas_call | solution.py:722
  48.2 8.3 %all-to-all-start.1 = ((f32[16,8,128]{2,1,0:T(8,128)}), f32[16,8,128]{2,1,0:T(8,128)S(1)}, u32[]{:S(2)}, u32[]{:S(2)}) async-start(f32[16,8,128]{2,1,0:T(8,128)} %get-tuple-element.45), calls=%async_computation.1 | async-start | bytes 131072 | tf_op jit(solution)/shard_map/all_to_all | solution.py:729
  56.5 1.3 %shard_map.156 = f32[1232,128]{1,0:T(8,128)} custom-call(bf16[80,240]{1,0:T(8,128)(2,1)S(1)} %get-tuple-element.24.w_ref, f32[8,1024]{1,0:T(8,128)S(1)} %get-tuple-element.40.rates_ref, f32[80,1024]{1,0:T(8,128)S(1)} %get-tuple-element.41.n0_ref, f32[80,1024]{1,0:T(8,128)S(1)} %get-tuple-element.42.h0_ref, f32[80,1024]{1,0:T(8,128)S(1)} %get-tuple-element.43.x1_ref, ...), custom_call_target="tpu_custom_call" | custom-call | flops 2000000 | bytes 1000000 | tf_op jit(solution)/shard_map/pallas_call | solution.py:731
  57.8 5.6 %all-to-all-done.1.got_ref = f32[16,8,128]{2,1,0:T(8,128)S(1)} async-done(((f32[16,8,128]{2,1,0:T(8,128)}), f32[16,8,128]{2,1,0:T(8,128)S(1)}, u32[]{:S(2)}, u32[]{:S(2)}) %all-to-all-start.1) | async-done | bytes 65568 | tf_op jit(solution)/shard_map/all_to_all | solution.py:729
  63.4 0.8 %shard_map.157 = f32[7,32,11]{2,1,0:T(8,128)} custom-call(f32[16,8,128]{2,1,0:T(8,128)S(1)} %all-to-all-done.1.got_ref), custom_call_target="tpu_custom_call" | custom-call | flops 2000000 | bytes 1000000 | tf_op jit(solution)/shard_map/pallas_call | solution.py:730
  (51 shorter events, 2.6 us)
Async XLA Ops:
  3.9 6.5 %copy-start.1 = (f32[11,7,4,8]{0,3,2,1:T(8,128)S(1)}, f32[11,7,4,8]{0,3,2,1:T(8,128)}, u32[]{:S(2)}) copy-start(f32[11,7,4,8]{0,3,2,1:T(8,128)} %param.21) | copy-start | bytes 29572
  4.2 22.5 %collective-permute-start.1 = (f32[88,2048]{1,0:T(8,128)S(1)}, f32[88,2048]{1,0:T(8,128)S(1)}, u32[]{:S(2)}, u32[]{:S(2)}) collective-permute-start(f32[88,2048]{1,0:T(8,128)S(1)} %get-tuple-element.26.m_ref), channel_id=1, source_target_pairs={{0,2},{2,0},{4,6},{6,4},{8,10},{10,8},{12,14},{14,12},{16,18},{18,... | collective-permute-start | bytes 2162696 | tf_op jit(solution)/shard_map/ppermute | solution.py:649
  4.8 22.0 %collective-permute-start = (f32[88,2048]{1,0:T(8,128)S(1)}, f32[88,2048]{1,0:T(8,128)S(1)}, u32[]{:S(2)}, u32[]{:S(2)}) collective-permute-start(f32[88,2048]{1,0:T(8,128)S(1)} %get-tuple-element.26.m_ref), channel_id=1, source_target_pairs={{0,30},{2,4},{4,2},{6,8},{8,6},{10,12},{12,10},{14,16},{16,14},{18... | collective-permute-start | bytes 2162696 | tf_op jit(solution)/shard_map/ppermute | solution.py:649
  11.3 8.3 %copy-start.2 = (f32[80,240]{1,0:T(8,128)S(1)}, f32[80,240]{1,0:T(8,128)}, u32[]{:S(2)}) copy-start(f32[80,240]{1,0:T(8,128)} %constant.16.clone.diagonal_ref) | copy-start | bytes 230404
  11.3 8.3 %copy-start.3 = (f32[80,7]{1,0:T(8,128)S(1)}, f32[80,7]{1,0:T(8,128)}, u32[]{:S(2)}) copy-start(f32[80,7]{1,0:T(8,128)} %constant.14.clone.rows_ref) | copy-start | bytes 6724
  11.3 8.3 %copy-start.4 = (bf16[80,240]{1,0:T(8,128)(2,1)S(1)}, bf16[80,240]{1,0:T(8,128)(2,1)}, u32[]{:S(2)}) copy-start(bf16[80,240]{1,0:T(8,128)(2,1)} %constant.13.clone.spectral_ref) | copy-start | bytes 115204
  11.3 8.3 %copy-start.5 = (f32[3,7,7]{2,1,0:T(8,128)S(1)}, f32[3,7,7]{2,1,0:T(8,128)}, u32[]{:S(2)}) copy-start(f32[3,7,7]{2,1,0:T(8,128)} %up_ref.1) | copy-start | bytes 1768
  11.3 8.3 %copy-start.6 = (f32[3,7,7]{2,1,0:T(8,128)S(1)}, f32[3,7,7]{2,1,0:T(8,128)}, u32[]{:S(2)}) copy-start(f32[3,7,7]{2,1,0:T(8,128)} %down_ref.1) | copy-start | bytes 1768
  11.3 8.3 %copy-start.7 = (f32[7,240]{1,0:T(8,128)S(1)}, f32[7,240]{1,0:T(8,128)}, u32[]{:S(2)}) copy-start(f32[7,240]{1,0:T(8,128)} %constant.15.clone.lanes_ref) | copy-start | bytes 20164
  11.3 15.4 %all-to-all-start = ((f32[32,8,128]{2,1,0:T(8,128)}), f32[32,8,128]{2,1,0:T(8,128)S(1)}, u32[]{:S(2)}, u32[]{:S(2)}) async-start(f32[32,8,128]{2,1,0:T(8,128)} %shard_map.151), calls=%async_computation | async-start | bytes 262144 | tf_op jit(solution)/shard_map/all_to_all | solution.py:683
  14.0 9.9 %collective-permute-start.2 = (f32[1,88,512]{2,1,0:T(8,128)S(1)}, f32[1,88,512]{2,1,0:T(8,128)S(1)}, u32[]{:S(2)}, u32[]{:S(2)}) collective-permute-start(f32[1,88,512]{2,1,0:T(8,128)S(1)} %get-tuple-element.27), channel_id=1, source_target_pairs={{0,1},{1,0},{2,3},{3,2},{4,5},{5,4},{6,7},{7,6},{8,9},{9,8},{10,11... | collective-permute-start | bytes 540680 | tf_op jit(solution)/shard_map/ppermute | solution.py:663
  15.7 7.5 %collective-permute-start.3 = (f32[1,88,128]{2,1,0:T(8,128)S(1)}, f32[1,88,128]{2,1,0:T(8,128)S(1)}, u32[]{:S(2)}, u32[]{:S(2)}) collective-permute-start(f32[1,88,128]{2,1,0:T(8,128)S(1)} %get-tuple-element.28), channel_id=1, source_target_pairs={{0,31},{1,30},{2,5},{3,4},{4,3},{5,2},{6,9},{7,8},{8,7},{9,6},{10,... | collective-permute-start | bytes 135176 | tf_op jit(solution)/shard_map/ppermute | solution.py:663
  19.6 4.3 %collective-permute-start.4 = (f32[1,88,128]{2,1,0:T(8,128)S(1)}, f32[1,88,128]{2,1,0:T(8,128)S(1)}, u32[]{:S(2)}, u32[]{:S(2)}) collective-permute-start(f32[1,88,128]{2,1,0:T(8,128)S(1)} %get-tuple-element.29), channel_id=1, source_target_pairs={{0,3},{1,2},{2,1},{3,0},{4,7},{5,6},{6,5},{7,4},{8,11},{9,10},{10,... | collective-permute-start | bytes 135176 | tf_op jit(solution)/shard_map/ppermute | solution.py:663
  23.9 4.6 %copy-start.10 = (f32[1,88,512]{2,1,0:T(8,128)}, f32[1,88,512]{2,1,0:T(8,128)S(1)}, u32[]{:S(2)}) copy-start(f32[1,88,512]{2,1,0:T(8,128)S(1)} %collective-permute-done.2.side_ref.side_first) | copy-start | bytes 540676
  26.7 1.7 %copy-start.8 = (f32[88,2048]{1,0:T(8,128)}, f32[88,2048]{1,0:T(8,128)S(1)}, u32[]{:S(2)}) copy-start(f32[88,2048]{1,0:T(8,128)S(1)} %collective-permute-done.low_ref.low_first) | copy-start | bytes 2162692
  31.5 13.0 %collective-permute-start.7 = (f32[80,2048]{1,0:T(8,128)S(1)}, f32[80,2048]{1,0:T(8,128)S(1)}, u32[]{:S(2)}, u32[]{:S(2)}) collective-permute-start(f32[80,2048]{1,0:T(8,128)S(1)} %get-tuple-element.33.x_ref), channel_id=1, source_target_pairs={{0,2},{2,0},{4,6},{6,4},{8,10},{10,8},{12,14},{14,12},{16,18},{18,... | collective-permute-start | bytes 1966088 | tf_op jit(solution)/shard_map/ppermute | solution.py:649
  31.5 7.1 %collective-permute-start.5 = (f32[1,80,512]{2,1,0:T(8,128)S(1)}, f32[1,80,512]{2,1,0:T(8,128)S(1)}, u32[]{:S(2)}, u32[]{:S(2)}) collective-permute-start(f32[1,80,512]{2,1,0:T(8,128)S(1)} %get-tuple-element.34), channel_id=1, source_target_pairs={{0,1},{1,0},{2,3},{3,2},{4,5},{5,4},{6,7},{7,6},{8,9},{9,8},{10,11... | collective-permute-start | bytes 491528 | tf_op jit(solution)/shard_map/ppermute | solution.py:663
  33.6 10.9 %collective-permute-start.6 = (f32[80,1024]{1,0:T(8,128)S(1)}, f32[80,1024]{1,0:T(8,128)S(1)}, u32[]{:S(2)}, u32[]{:S(2)}) collective-permute-start(f32[80,1024]{1,0:T(8,128)S(1)} %get-tuple-element.36), channel_id=1, source_target_pairs={{0,30},{2,4},{4,2},{6,8},{8,6},{10,12},{12,10},{14,16},{16,14},{18... | collective-permute-start | bytes 983048 | tf_op jit(solution)/shard_map/ppermute | solution.py:649
  37.4 7.1 %collective-permute-start.8 = (f32[1,80,128]{2,1,0:T(8,128)S(1)}, f32[1,80,128]{2,1,0:T(8,128)S(1)}, u32[]{:S(2)}, u32[]{:S(2)}) collective-permute-start(f32[1,80,128]{2,1,0:T(8,128)S(1)} %get-tuple-element.37), channel_id=1, source_target_pairs={{0,31},{1,30},{2,5},{3,4},{4,3},{5,2},{6,9},{7,8},{8,7},{9,6},{10,... | collective-permute-start | bytes 122888 | tf_op jit(solution)/shard_map/ppermute | solution.py:663
  37.6 6.9 %copy-start.9 = (f32[88,2048]{1,0:T(8,128)S(1)}, f32[88,2048]{1,0:T(8,128)}, u32[]{:S(2)}) copy-start(f32[88,2048]{1,0:T(8,128)} %copy-done.8) | copy-start | bytes 2162692
  37.6 6.9 %copy-start.11 = (f32[1,88,512]{2,1,0:T(8,128)S(1)}, f32[1,88,512]{2,1,0:T(8,128)}, u32[]{:S(2)}) copy-start(f32[1,88,512]{2,1,0:T(8,128)} %copy-done.10) | copy-start | bytes 540676
  37.6 6.9 %collective-permute-start.9 = (f32[1,80,128]{2,1,0:T(8,128)S(1)}, f32[1,80,128]{2,1,0:T(8,128)S(1)}, u32[]{:S(2)}, u32[]{:S(2)}) collective-permute-start(f32[1,80,128]{2,1,0:T(8,128)S(1)} %get-tuple-element.38), channel_id=1, source_target_pairs={{0,3},{1,2},{2,1},{3,0},{4,7},{5,6},{6,5},{7,4},{8,11},{9,10},{10,... | collective-permute-start | bytes 122888 | tf_op jit(solution)/shard_map/ppermute | solution.py:663
  39.5 17.0 %collective-permute-start.10 = (f32[80,1024]{1,0:T(8,128)S(1)}, f32[80,1024]{1,0:T(8,128)S(1)}, u32[]{:S(2)}, u32[]{:S(2)}) collective-permute-start(f32[80,1024]{1,0:T(8,128)S(1)} %get-tuple-element.44), channel_id=1, source_target_pairs={{0,30},{2,4},{4,2},{6,8},{8,6},{10,12},{12,10},{14,16},{16,14},{18... | collective-permute-start | bytes 983048 | tf_op jit(solution)/shard_map/ppermute | solution.py:649
  48.2 15.2 %all-to-all-start.1 = ((f32[16,8,128]{2,1,0:T(8,128)}), f32[16,8,128]{2,1,0:T(8,128)S(1)}, u32[]{:S(2)}, u32[]{:S(2)}) async-start(f32[16,8,128]{2,1,0:T(8,128)} %get-tuple-element.45), calls=%async_computation.1 | async-start | bytes 131072 | tf_op jit(solution)/shard_map/all_to_all | solution.py:729
  (6 other events, 4.7 us)

commit v8 on v7

--- a/solution.py
+++ b/solution.py
@@ -237,7 +237,10 @@
         other = second.get(UP_AZ, r), first.get(DOWN_AZ, r)
         for a, products in enumerate((first, second)):
             total = products.own_terms(r) + layers[a].rate(C_AZ, r) * other[a]
-            g_ref[:, at(r, 1, a * plan.slab)] = force[a].row(r) - total
+            if isinstance(g_ref, tuple):
+                g_ref[a][:, at(r)] = force[a].row(r) - total
+            else:
+                g_ref[:, at(r, 1, a * plan.slab)] = force[a].row(r) - total
 
 
 def azimuthal(plan, w_ref, block, chunk_of, take):
@@ -247,7 +250,7 @@
             take(c * (CHUNK // LANES) + part, terms[:, at(part)])
 
 
-def middle_rows(plan, w_ref, p_refs, own, own_force, g_ref, near, near_force, side, corner, y_ref, h_ref, n_refs):
+def middle_rows(plan, w_ref, p_refs, own, own_force, g_ref, near, near_force, side, corner, y_ref, h_refs, n_refs):
     pad, rows, ct = plan.pad, plan.rows, plan.ct
     outward, inward, last = (UP_SP, DOWN_SP), (DOWN_SP, UP_SP), (rows - 1, 0)
     edge_terms, edge_new, corner_terms = [], [], []
@@ -294,14 +297,13 @@
         azimuthal(plan, w_ref, to_near, own[a].chunk, take)
 
     after = [Layer(plan, y_ref, a * plan.slab, own[a].rates) for a in range(ct)]
-    inner_rows(plan, w_ref, p_refs, after, own_force, h_ref)
+    inner_rows(plan, w_ref, p_refs, after, own_force, h_refs)
     for a in range(ct):
         for n in range(2):
-            lanes = at(last[n], 1, a * plan.slab)
-            h_ref[:, lanes] -= own[a].rate(C_SP, last[n]) * edge_new[n][:, at(a)]
-
-
-def outer_rows(plan, w_ref, own, near, far_chunks, n_refs, h_ref, put, layers=(0, 1)):
+            h_refs[a][:, at(last[n])] -= own[a].rate(C_SP, last[n]) * edge_new[n][:, at(a)]
+
+
+def outer_rows(plan, w_ref, own, near, far_chunks, n_refs, h_refs, put, layers=(0, 1)):
     count = CHUNK // LANES
     for a in layers:
         block = (DOWN_AZ, UP_AZ)[a]
@@ -311,7 +313,7 @@
             return n_refs[a][:, at(c * count, count)] - near[a].rate(C_AZ, c * count, count) * terms
 
         def take(r, terms):
-            put(a, r, h_ref[:, at(r, 1, a * plan.slab)] - own[a].rate(C_AZ, r) * terms)
+            put(a, r, h_refs[a][:, at(r)] - own[a].rate(C_AZ, r) * terms)
 
         azimuthal(plan, w_ref, block, near_chunk, take)
 
@@ -527,7 +529,7 @@
 
 def first_half(
     plan, w_ref, m_ref, f_ref, g_ref, low_ref, high_ref, side_ref, c_low, c_high, seams_ref,
-    x_ref, near_ref, side_out, c0_ref, c1_ref, p0_ref, p1_ref, y_ref, h_ref, n0_ref, n1_ref, inlet_ref,
+    x_ref, near_ref, side_out, c0_ref, c1_ref, p0_ref, p1_ref, y_ref, h0_ref, h1_ref, n0_ref, n1_ref, inlet_ref,
 ):
     own = two_layers(plan, f_ref, m_ref)
     low = two_layers(plan, low_ref, seam=seams_ref[0, 0])
@@ -536,7 +538,7 @@
     n_refs = n0_ref, n1_ref
     middle_rows(
         plan, w_ref, (p0_ref, p1_ref), own, own, g_ref, near, near, sides_of(plan, side_ref, side_ref, seams_ref),
-        corners_of(plan, (c_low, c_high), seams_ref), y_ref, h_ref, n_refs,
+        corners_of(plan, (c_low, c_high), seams_ref), y_ref, (h0_ref, h1_ref), n_refs,
     )
     lane = lane_index(plan.pad)
     inlet_ref[...] = jnp.zeros_like(inlet_ref)
@@ -548,22 +550,26 @@
         else:
             inlet_ref[: plan.pad, :] = jnp.where(lane == r, rolled(value, r), inlet_ref[: plan.pad, :])
 
-    outer_rows(plan, w_ref, own, near, (low[1].chunk, high[0].chunk), n_refs, h_ref, put)
+    outer_rows(plan, w_ref, own, near, (low[1].chunk, high[0].chunk), n_refs, (h0_ref, h1_ref), put)
     turned = jnp.transpose(inlet_ref[...])
     for r in range(plan.rows):
         near_ref[plan.tf : plan.tf + 1, at(r)] = turned[r : r + 1, :]
     write_edges(plan, x_ref, side_out, (c0_ref, c1_ref))
 
 
-def inner(plan, w_ref, m_ref, f_ref, x_ref, side_ref, g_ref, far_ref, p0_ref, p1_ref):
-    far_ref[...] = x_ref[:, plan.slab :] + 0.0 * side_ref[0, 0:1, 0:1]
+def hold_far(plan, x_ref, side_ref, c_low, c_high, far_ref):
+    come = side_ref[0, 0:1, 0:1] + c_low[0, 0:1, 0:1] + c_high[0, 0:1, 0:1]
+    far_ref[...] = x_ref[:, plan.slab :] + 0.0 * come
+
+
+def inner(plan, w_ref, m_ref, f_ref, x_ref, g_ref, p0_ref, p1_ref):
     inner_rows(plan, w_ref, (p0_ref, p1_ref), two_layers(plan, x_ref, m_ref), two_layers(plan, f_ref, m_ref), g_ref)
 
 
 def middle(
     plan, w_ref, m_ref, f_ref, x_ref, g_ref, low_ref, high_ref, side_ref, c_low, c_high,
     low_first, high_first, side_first, seams_ref, weight_ref,
-    send_ref, n0_ref, h0_ref, x1_ref, rates_ref, p0_ref, p1_ref, y_ref, inlet_ref, h_ref, n1_ref, turn_ref,
+    send_ref, n0_ref, h0_ref, x1_ref, rates_ref, p0_ref, p1_ref, y_ref, h1_ref, n1_ref, turn_ref,
 ):
     pad = plan.pad
     own, force = two_layers(plan, x_ref, m_ref), two_layers(plan, f_ref, m_ref)
@@ -573,30 +579,39 @@
     n_refs = n0_ref, n1_ref
     middle_rows(
         plan, w_ref, (p0_ref, p1_ref), own, force, g_ref, near, (low_force, high_force),
-        sides_of(plan, side_ref, side_first, seams_ref), corners_of(plan, (c_low, c_high), None), y_ref, h_ref, n_refs,
-    )
-    lane = lane_index(pad)
-    inlet_ref[...] = jnp.zeros_like(inlet_ref)
+        sides_of(plan, side_ref, side_first, seams_ref), corners_of(plan, (c_low, c_high), None), y_ref,
+        (h0_ref, h1_ref), n_refs,
+    )
 
     def put(a, r, value):
-        cell = a * plan.rows + r
-        inlet_ref[...] = jnp.where(lane == cell * WINDOW, rolled(value, cell * WINDOW), inlet_ref[...])
-        if a == 1:
-            x1_ref[:, at(r)] = value
+        x1_ref[:, at(r)] = value
+
+    outer_rows(plan, w_ref, own, near, (None, Layer(plan, high_ref).chunk), n_refs, (h0_ref, h1_ref), put, (1,))
+    for r in range(plan.rows):
+        last = [near[0].rate(C_AZ, r), own[0].rate(C_AZ, r), jnp.zeros((RATES - 2, LANES), jnp.float32)]
+        rates_ref[:, at(r)] = jnp.concatenate(last, axis=0)
 
     turn_ref[...] = jnp.zeros_like(turn_ref)
     for r in range(plan.rows):
         turn_ref[r : r + 1, :] = low_ref[plan.tf : plan.tf + 1, at(r)]
-    far_tile = jnp.transpose(turn_ref[...])[:pad]
-
-    def far_inlet(c):
-        count = CHUNK // LANES
-        parts = [rolled(far_tile, -(c * count + part)) for part in range(count)]
-        return jnp.concatenate([jnp.where(lane == 0, part, 0.0) for part in parts], axis=1)
-
-    outer_rows(plan, w_ref, own, near, (far_inlet, Layer(plan, high_ref).chunk), n_refs, h_ref, put)
-    inlet = inlet_ref[...]
-    inlet = jnp.where(parity() == 0, inlet, rolled(inlet, LANES // 2))
+    far = jnp.transpose(turn_ref[...])[:pad]
+
+    def packed(read, count, first=0, step=1):
+        lane = lane_index(count)
+        out = jnp.zeros((count, LANES), jnp.float32)
+        for r in range(plan.rows):
+            to = first + r * step
+            out = jnp.where(lane == to, rolled(read(r), to), out)
+        return out
+
+    rates = packed(lambda r: rates_ref[:, at(r)], RATES)
+    inlet = packed(lambda r: n0_ref[:, at(r)], pad) - rates[0:1] * dot3(matrix(plan, w_ref, DOWN_AZ), far)
+    inlet = packed(lambda r: h0_ref[:, at(r)], pad) - rates[1:2] * dot3(matrix(plan, w_ref, DOWN_AZ), inlet)
+    lane = lane_index(pad)
+    spread = packed(lambda r: x1_ref[:, at(r)], pad, plan.rows * WINDOW, WINDOW)
+    for r in range(plan.rows):
+        spread = jnp.where(lane == r * WINDOW, rolled(inlet, r * (WINDOW - 1)), spread)
+    inlet = jnp.where(parity() == 0, spread, rolled(spread, LANES // 2))
     back = pick(inlet, plan.window_spread()) * weight_ref[...]
     back = back + rolled(back, -plan.width)
     me = lax.axis_index("sector")
@@ -604,10 +619,6 @@
     for t in range(plan.insts):
         to = lax.rem(me + plan.shift[t], plan.sectors)
         send_ref[to, : plan.fields, : plan.width] = back[t * plan.fields : (t + 1) * plan.fields, : plan.width]
-    h0_ref[...] = h_ref[:, : plan.slab]
-    for r in range(plan.rows):
-        rest = jnp.zeros((RATES - 2, LANES), jnp.float32)
-        rates_ref[:, at(r)] = jnp.concatenate([near[0].rate(C_AZ, r), own[0].rate(C_AZ, r), rest], axis=0)
 
 
 def outer(plan, w_ref, rates_ref, n0_ref, h0_ref, x1_ref, far_ref, out_ref):
@@ -708,20 +719,19 @@
     )(matrices, m, got, low_first, high_first, side_first, c_low, c_high)
     x, near, side, c0, c1 = call(
         bind(first_half, plan), (whole, half) + edges(pad),
-        products + (vmem(pad, 2 * slab), vmem(pad, 2 * slab), vmem(pad, slab), vmem(pad, slab), vmem(LANES, LANES)),
+        products + (vmem(pad, 2 * slab),) + (vmem(pad, slab),) * 4 + (vmem(LANES, LANES),),
         flops=4_000_000_000,
     )(matrices, m, force, g, low_first, high_first, side_first, c_low, c_high, seams)
 
     low, high = swap(near, next_chip), swap(x, next_core)
     side = beside(plan, side, alone)
     c_low, c_high = beside(plan, c0, next_chip), beside(plan, c1, next_core)
-    g, far = call(bind(inner, plan), (whole, half), products, flops=2_000_000_000)(
-        matrices, m, force, x, side
-    )
+    (g,) = call(bind(inner, plan), (whole,), products, flops=2_000_000_000)(matrices, m, force, x)
+    far = call(bind(hold_far, plan), half)(x, side, c_low, c_high)
     far_low = swap(far, next_chip)
     back, n0, h0, x1, rates = call(
         bind(middle, plan), (f32(sectors, RATES, LANES), half, half, half, f32(RATES, slab)),
-        products + (vmem(pad, 2 * slab), vmem(pad, LANES), vmem(pad, 2 * slab), vmem(pad, slab), vmem(LANES, LANES)),
+        products + (vmem(pad, 2 * slab), vmem(pad, slab), vmem(pad, slab), vmem(LANES, LANES)),
         flops=4_000_000_000,
     )(
         matrices, m, force, x, g, low, high, side, c_low, c_high, low_first, high_first, side_first, seams, weight

time: 64.7 us -> 62.5 us (0.966)
  starting transfers between devices: 32.1 us -> 26 us
  waiting for transfers between devices: 14.3 us -> 18.3 us
    all_to_all x1, starting transfers between devices: 8.28 us -> 3.5 us  [on_device(): returned = lax.all_to_all(back, 'sector', 0, 0, tiled=True)]
    ppermute x6, waiting for transfers between devices: 5.91 us -> 9.34 us  [beside(): return lax.ppermute(array, AXES, pairs(0))]
    ppermute x6, starting transfers between devices: 7.89 us -> 7.06 us  [beside(): return lax.ppermute(array, AXES, pairs(0))]
  transfers between devices with their start and end apart: 13 -> 13, of which waited for: 6 -> 5; matrix products, arithmetic and copies ran while one was open for 0% -> 0% of each run, Pallas kernels for 12% -> 12%
where the time goes in v8:
time: 62.5 us; the launch traced here: 62 us
  starting transfers between devices  26 us (42%)
  waiting for transfers between devices  18.3 us (29%)
  Pallas kernels  13.5 us (22%)
  local copies, waits for them, and re-layouts  2.55 us (4%)
  between operations  0.83 us (1%)
  other arithmetic  0.79 us (1%)
    ppermute x5, starting transfers between devices, swap(): return lax.ppermute(array, 'sector', list(enumerate(partner)))  12.7 us
    ppermute x6, waiting for transfers between devices, beside(): return lax.ppermute(array, AXES, pairs(0))  9.34 us
    ppermute x6, starting transfers between devices, beside(): return lax.ppermute(array, AXES, pairs(0))  7.06 us
    all_to_all x1, waiting for transfers between devices, on_device(): returned = lax.all_to_all(back, 'sector', 0, 0, tiled=True)  5.54 us
    pallas_call x1, Pallas kernels, on_device(): call(bind(middle, plan), (f32(sectors, RATES, LANES), half, half, half, f...  3.59 us
    all_to_all x1, starting transfers between devices, on_device(): returned = lax.all_to_all(back, 'sector', 0, 0, tiled=True)  3.5 us
    all_to_all x1, waiting for transfers between devices, on_device(): got = lax.all_to_all(sent, AXES, 0, 0, tiled=True)  3.39 us
    pallas_call x1, Pallas kernels, on_device(): call(bind(first_half, plan), (whole, half) + edges(pad), products + (vmem...  3.04 us
  transfers between devices with their start and end apart: 13, of which 5 were waited for; matrix products, arithmetic and copies ran while one was open for 0% of the time, Pallas kernels for 12%

profile of v8, /device:TPU:0, one launch (start us, length us, event | category | flops | bytes accessed | tf_op | source)
XLA Modules:
  0.0 62.0 jit_solution(8776560090358703050)
XLA Ops:
  0.6 0.7 %convert_bitcast_fusion = f32[16,128]{1,0:T(8,128)S(1)} fusion(s32[2,8,128]{2,1,0:T(8,128)} %param.20), kind=kLoop, calls=%fused_computation.7 | loop fusion | flops 2048 | bytes 16384 | tf_op jit(solution)/shard_map/reshape | solution.py:700
  1.4 0.6 copy-done.16
  2.2 0.6 copy-done.12
  2.9 1.1 %copy-done = f32[11,7,2,8,128]{4,3,2,1,0:T(8,128)S(1)} copy-done((f32[11,7,2,8,128]{4,3,2,1,0:T(8,128)S(1)}, f32[11,7,2,8,128]{4,3,2,1,0:T(8,128)}, u32[]{:S(2)}) %copy-start) | copy-done | bytes 630808
  4.2 5.5 %collective-permute-start = (f32[88,2048]{1,0:T(8,128)S(1)}, f32[88,2048]{1,0:T(8,128)S(1)}, u32[]{:S(2)}, u32[]{:S(2)}) collective-permute-start(f32[88,2048]{1,0:T(8,128)S(1)} %get-tuple-element.24.m_ref), channel_id=1, source_target_pairs={{0,30},{2,4},{4,2},{6,8},{8,6},{10,12},{12,10},{14,16},{16,14},{18... | collective-permute-start | bytes 2162696 | tf_op jit(solution)/shard_map/ppermute | solution.py:660
  9.7 0.8 %shard_map.151 = f32[32,8,128]{2,1,0:T(8,128)} custom-call(f32[7,32,11]{2,1,0:T(8,128)S(1)} %bitcast.17), custom_call_target="tpu_custom_call" | custom-call | flops 2000000 | bytes 1000000 | tf_op jit(solution)/shard_map/pallas_call | solution.py:693
  10.6 2.7 %all-to-all-start = ((f32[32,8,128]{2,1,0:T(8,128)}), f32[32,8,128]{2,1,0:T(8,128)S(1)}, u32[]{:S(2)}, u32[]{:S(2)}) async-start(f32[32,8,128]{2,1,0:T(8,128)} %shard_map.151), calls=%async_computation | async-start | bytes 262144 | tf_op jit(solution)/shard_map/all_to_all | solution.py:694
  13.3 1.7 %collective-permute-start.2 = (f32[1,88,512]{2,1,0:T(8,128)S(1)}, f32[1,88,512]{2,1,0:T(8,128)S(1)}, u32[]{:S(2)}, u32[]{:S(2)}) collective-permute-start(f32[1,88,512]{2,1,0:T(8,128)S(1)} %get-tuple-element.25), channel_id=1, source_target_pairs={{0,1},{1,0},{2,3},{3,2},{4,5},{5,4},{6,7},{7,6},{8,9},{9,8},{10,11... | collective-permute-start | bytes 540680 | tf_op jit(solution)/shard_map/ppermute | solution.py:674
  15.0 3.9 %collective-permute-start.3 = (f32[1,88,128]{2,1,0:T(8,128)S(1)}, f32[1,88,128]{2,1,0:T(8,128)S(1)}, u32[]{:S(2)}, u32[]{:S(2)}) collective-permute-start(f32[1,88,128]{2,1,0:T(8,128)S(1)} %get-tuple-element.26), channel_id=1, source_target_pairs={{0,31},{1,30},{2,5},{3,4},{4,3},{5,2},{6,9},{7,8},{8,7},{9,6},{10,... | collective-permute-start | bytes 135176 | tf_op jit(solution)/shard_map/ppermute | solution.py:674
  18.9 1.1 %shard_map.149 = (bf16[560,240]{1,0:T(8,128)(2,1)S(1)}, bf16[80,240]{1,0:T(8,128)(2,1)S(1)}) custom-call(f32[3,7,7]{2,1,0:T(8,128)S(1)} %copy-done.5, f32[3,7,7]{2,1,0:T(8,128)S(1)} %copy-done.6, bf16[80,240]{1,0:T(8,128)(2,1)S(1)} %copy-done.3, f32[80,7]{1,0:T(8,128)S(1)} %copy-done.4, f32[7,240]{1,0:T(8,128)S(1)} %copy-done.7, f32[80,240]{1,0:T(8,128)S(1)} %copy-done.2), custom_call_target="tpu_custom_call" | custom-call | flops 2000000 | bytes 1000000 | tf_op jit(solution)/shard_map/pallas_call | solution.py:710
  20.1 2.7 %collective-permute-done.3.c_low = f32[1,88,128]{2,1,0:T(8,128)S(1)} collective-permute-done((f32[1,88,128]{2,1,0:T(8,128)S(1)}, f32[1,88,128]{2,1,0:T(8,128)S(1)}, u32[]{:S(2)}, u32[]{:S(2)}) %collective-permute-start.3) | collective-permute-done | bytes 45088 | tf_op jit(solution)/shard_map/ppermute | solution.py:674
  23.2 3.4 %all-to-all-done.got_ref = f32[32,8,128]{2,1,0:T(8,128)S(1)} async-done(((f32[32,8,128]{2,1,0:T(8,128)}), f32[32,8,128]{2,1,0:T(8,128)S(1)}, u32[]{:S(2)}, u32[]{:S(2)}) %all-to-all-start) | async-done | bytes 131104 | tf_op jit(solution)/shard_map/all_to_all | solution.py:694
  26.6 1.7 %shard_map.152 = (f32[3,2,80,128]{3,2,1,0:T(8,128)S(1)}, f32[80,128]{1,0:T(8,128)S(1)}, f32[80,2048]{1,0:T(8,128)S(1)}, f32[80,2048]{1,0:T(8,128)S(1)}) custom-call(bf16[560,240]{1,0:T(8,128)(2,1)S(1)} %get-tuple-element.23.w_ref, f32[88,2048]{1,0:T(8,128)S(1)} %get-tuple-element.24.m_ref, f32[32,8,128]{2,1,0:T(8,128)S(1)} %all-to-all-done.got_ref, ...), custom_call_target="tpu_custom_call" | custom-call | flops 2000000000 | bytes 1000000 | tf_op jit(solution)/shard_map/pallas_call | solution.py:715
  28.4 3.0 %shard_map.153 = (f32[80,2048]{1,0:T(8,128)S(1)}, f32[80,1024]{1,0:T(8,128)S(1)}, f32[1,80,512]{2,1,0:T(8,128)S(1)}, f32[1,80,128]{2,1,0:T(8,128)S(1)}, f32[1,80,128]{2,1,0:T(8,128)S(1)}) custom-call(bf16[560,240]{1,0:T(8,128)(2,1)S(1)} %get-tuple-element.23.w_ref, f32[88,2048]{1,0:T(8,128)S(1)} %get-tuple-element.24.m_ref, ...), custom_call_target="tpu_custom_call" | custom-call | flops 4000000000 | bytes 1000000 | tf_op jit(solution)/shard_map/pallas_call | solution.py:720
  31.5 4.6 %collective-permute-start.5 = (f32[80,1024]{1,0:T(8,128)S(1)}, f32[80,1024]{1,0:T(8,128)S(1)}, u32[]{:S(2)}, u32[]{:S(2)}) collective-permute-start(f32[80,1024]{1,0:T(8,128)S(1)} %get-tuple-element.32), channel_id=1, source_target_pairs={{0,30},{2,4},{4,2},{6,8},{8,6},{10,12},{12,10},{14,16},{16,14},{18... | collective-permute-start | bytes 983048 | tf_op jit(solution)/shard_map/ppermute | solution.py:660
  36.1 1.5 %collective-permute-start.7 = (f32[1,80,512]{2,1,0:T(8,128)S(1)}, f32[1,80,512]{2,1,0:T(8,128)S(1)}, u32[]{:S(2)}, u32[]{:S(2)}) collective-permute-start(f32[1,80,512]{2,1,0:T(8,128)S(1)} %get-tuple-element.33), channel_id=1, source_target_pairs={{0,1},{1,0},{2,3},{3,2},{4,5},{5,4},{6,7},{7,6},{8,9},{9,8},{10,11... | collective-permute-start | bytes 491528 | tf_op jit(solution)/shard_map/ppermute | solution.py:674
  37.6 0.8 %shard_map.154.g_ref = f32[80,2048]{1,0:T(8,128)S(1)} custom-call(bf16[560,240]{1,0:T(8,128)(2,1)S(1)} %get-tuple-element.23.w_ref, f32[88,2048]{1,0:T(8,128)S(1)} %get-tuple-element.24.m_ref, f32[80,2048]{1,0:T(8,128)S(1)} %get-tuple-element.28.f_ref, f32[80,2048]{1,0:T(8,128)S(1)} %get-tuple-element.31.x_ref), custom_call_target="tpu_custom_call" | custom-call | flops 2000000000 | bytes 1000000 | tf_op jit(solution)/shard_map/pallas_call | solution.py:729
  38.4 6.2 %collective-permute-done.8.c_low = f32[1,80,128]{2,1,0:T(8,128)S(1)} collective-permute-done((f32[1,80,128]{2,1,0:T(8,128)S(1)}, f32[1,80,128]{2,1,0:T(8,128)S(1)}, u32[]{:S(2)}, u32[]{:S(2)}) %collective-permute-start.8) | collective-permute-done | bytes 40992 | tf_op jit(solution)/shard_map/ppermute | solution.py:674
  44.7 2.6 %collective-permute-start.10 = (f32[80,1024]{1,0:T(8,128)S(1)}, f32[80,1024]{1,0:T(8,128)S(1)}, u32[]{:S(2)}, u32[]{:S(2)}) collective-permute-start(f32[80,1024]{1,0:T(8,128)S(1)} %shard_map.156), channel_id=1, source_target_pairs={{0,30},{2,4},{4,2},{6,8},{8,6},{10,12},{12,10},{14,16},{16,14},{18... | collective-permute-start | bytes 983048 | tf_op jit(solution)/shard_map/ppermute | solution.py:660
  47.3 3.6 %shard_map.155 = (f32[16,8,128]{2,1,0:T(8,128)}, f32[80,1024]{1,0:T(8,128)S(1)}, f32[80,1024]{1,0:T(8,128)S(1)}, f32[80,1024]{1,0:T(8,128)S(1)}, f32[8,1024]{1,0:T(8,128)S(1)}) custom-call(bf16[560,240]{1,0:T(8,128)(2,1)S(1)} %get-tuple-element.23.w_ref, f32[88,2048]{1,0:T(8,128)S(1)} %get-tuple-element.24.m_ref, f32[80,2048]{1,0:T(8,128)S(1)} %get-tuple-element.28.f_ref, ...), custom_call_target="tpu_custom_call" | custom-call | flops 4000000000 | bytes 1000000 | tf_op jit(solution)/shard_map/pallas_call | solution.py:732
  50.9 3.5 %all-to-all-start.1 = ((f32[16,8,128]{2,1,0:T(8,128)}), f32[16,8,128]{2,1,0:T(8,128)S(1)}, u32[]{:S(2)}, u32[]{:S(2)}) async-start(f32[16,8,128]{2,1,0:T(8,128)} %get-tuple-element.41), calls=%async_computation.1 | async-start | bytes 131072 | tf_op jit(solution)/shard_map/all_to_all | solution.py:739
  54.4 1.3 %shard_map.157 = f32[1232,128]{1,0:T(8,128)} custom-call(bf16[80,240]{1,0:T(8,128)(2,1)S(1)} %get-tuple-element.22.w_ref, f32[8,1024]{1,0:T(8,128)S(1)} %get-tuple-element.37.rates_ref, f32[80,1024]{1,0:T(8,128)S(1)} %get-tuple-element.38.n0_ref, f32[80,1024]{1,0:T(8,128)S(1)} %get-tuple-element.39.h0_ref, f32[80,1024]{1,0:T(8,128)S(1)} %get-tuple-element.40.x1_ref, ...), custom_call_target="tpu_custom_call" | custom-call | flops 2000000 | bytes 1000000 | tf_op jit(solution)/shard_map/pallas_call | solution.py:741
  55.7 5.5 %all-to-all-done.1.got_ref = f32[16,8,128]{2,1,0:T(8,128)S(1)} async-done(((f32[16,8,128]{2,1,0:T(8,128)}), f32[16,8,128]{2,1,0:T(8,128)S(1)}, u32[]{:S(2)}, u32[]{:S(2)}) %all-to-all-start.1) | async-done | bytes 65568 | tf_op jit(solution)/shard_map/all_to_all | solution.py:739
  61.2 0.8 %shard_map.158 = f32[7,32,11]{2,1,0:T(8,128)} custom-call(f32[16,8,128]{2,1,0:T(8,128)S(1)} %all-to-all-done.1.got_ref), custom_call_target="tpu_custom_call" | custom-call | flops 2000000 | bytes 1000000 | tf_op jit(solution)/shard_map/pallas_call | solution.py:740
  (52 shorter events, 1.2 us)
Async XLA Ops:
  3.9 5.8 %copy-start.1 = (f32[11,7,4,8]{0,3,2,1:T(8,128)S(1)}, f32[11,7,4,8]{0,3,2,1:T(8,128)}, u32[]{:S(2)}) copy-start(f32[11,7,4,8]{0,3,2,1:T(8,128)} %param.21) | copy-start | bytes 29572
  4.2 22.4 %collective-permute-start = (f32[88,2048]{1,0:T(8,128)S(1)}, f32[88,2048]{1,0:T(8,128)S(1)}, u32[]{:S(2)}, u32[]{:S(2)}) collective-permute-start(f32[88,2048]{1,0:T(8,128)S(1)} %get-tuple-element.24.m_ref), channel_id=1, source_target_pairs={{0,30},{2,4},{4,2},{6,8},{8,6},{10,12},{12,10},{14,16},{16,14},{18... | collective-permute-start | bytes 2162696 | tf_op jit(solution)/shard_map/ppermute | solution.py:660
  9.7 16.9 %collective-permute-start.1 = (f32[88,2048]{1,0:T(8,128)S(1)}, f32[88,2048]{1,0:T(8,128)S(1)}, u32[]{:S(2)}, u32[]{:S(2)}) collective-permute-start(f32[88,2048]{1,0:T(8,128)S(1)} %get-tuple-element.24.m_ref), channel_id=1, source_target_pairs={{0,2},{2,0},{4,6},{6,4},{8,10},{10,8},{12,14},{14,12},{16,18},{18,... | collective-permute-start | bytes 2162696 | tf_op jit(solution)/shard_map/ppermute | solution.py:660
  10.6 8.3 %copy-start.2 = (f32[80,240]{1,0:T(8,128)S(1)}, f32[80,240]{1,0:T(8,128)}, u32[]{:S(2)}) copy-start(f32[80,240]{1,0:T(8,128)} %constant.16.clone.diagonal_ref) | copy-start | bytes 230404
  10.6 8.3 %copy-start.3 = (bf16[80,240]{1,0:T(8,128)(2,1)S(1)}, bf16[80,240]{1,0:T(8,128)(2,1)}, u32[]{:S(2)}) copy-start(bf16[80,240]{1,0:T(8,128)(2,1)} %constant.13.clone.spectral_ref) | copy-start | bytes 115204
  10.6 8.3 %copy-start.4 = (f32[80,7]{1,0:T(8,128)S(1)}, f32[80,7]{1,0:T(8,128)}, u32[]{:S(2)}) copy-start(f32[80,7]{1,0:T(8,128)} %constant.14.clone.rows_ref) | copy-start | bytes 6724
  10.6 8.3 %copy-start.5 = (f32[3,7,7]{2,1,0:T(8,128)S(1)}, f32[3,7,7]{2,1,0:T(8,128)}, u32[]{:S(2)}) copy-start(f32[3,7,7]{2,1,0:T(8,128)} %up_ref.1) | copy-start | bytes 1768
  10.6 8.3 %copy-start.6 = (f32[3,7,7]{2,1,0:T(8,128)S(1)}, f32[3,7,7]{2,1,0:T(8,128)}, u32[]{:S(2)}) copy-start(f32[3,7,7]{2,1,0:T(8,128)} %down_ref.1) | copy-start | bytes 1768
  10.6 8.3 %copy-start.7 = (f32[7,240]{1,0:T(8,128)S(1)}, f32[7,240]{1,0:T(8,128)}, u32[]{:S(2)}) copy-start(f32[7,240]{1,0:T(8,128)} %constant.15.clone.lanes_ref) | copy-start | bytes 20164
  10.6 16.0 %all-to-all-start = ((f32[32,8,128]{2,1,0:T(8,128)}), f32[32,8,128]{2,1,0:T(8,128)S(1)}, u32[]{:S(2)}, u32[]{:S(2)}) async-start(f32[32,8,128]{2,1,0:T(8,128)} %shard_map.151), calls=%async_computation | async-start | bytes 262144 | tf_op jit(solution)/shard_map/all_to_all | solution.py:694
  13.3 9.9 %collective-permute-start.2 = (f32[1,88,512]{2,1,0:T(8,128)S(1)}, f32[1,88,512]{2,1,0:T(8,128)S(1)}, u32[]{:S(2)}, u32[]{:S(2)}) collective-permute-start(f32[1,88,512]{2,1,0:T(8,128)S(1)} %get-tuple-element.25), channel_id=1, source_target_pairs={{0,1},{1,0},{2,3},{3,2},{4,5},{5,4},{6,7},{7,6},{8,9},{9,8},{10,11... | collective-permute-start | bytes 540680 | tf_op jit(solution)/shard_map/ppermute | solution.py:674
  15.0 7.8 %collective-permute-start.3 = (f32[1,88,128]{2,1,0:T(8,128)S(1)}, f32[1,88,128]{2,1,0:T(8,128)S(1)}, u32[]{:S(2)}, u32[]{:S(2)}) collective-permute-start(f32[1,88,128]{2,1,0:T(8,128)S(1)} %get-tuple-element.26), channel_id=1, source_target_pairs={{0,31},{1,30},{2,5},{3,4},{4,3},{5,2},{6,9},{7,8},{8,7},{9,6},{10,... | collective-permute-start | bytes 135176 | tf_op jit(solution)/shard_map/ppermute | solution.py:674
  18.9 4.3 %collective-permute-start.4 = (f32[1,88,128]{2,1,0:T(8,128)S(1)}, f32[1,88,128]{2,1,0:T(8,128)S(1)}, u32[]{:S(2)}, u32[]{:S(2)}) collective-permute-start(f32[1,88,128]{2,1,0:T(8,128)S(1)} %get-tuple-element.27), channel_id=1, source_target_pairs={{0,3},{1,2},{2,1},{3,0},{4,7},{5,6},{6,5},{7,4},{8,11},{9,10},{10,... | collective-permute-start | bytes 135176 | tf_op jit(solution)/shard_map/ppermute | solution.py:674
  23.2 5.1 %copy-start.10 = (f32[1,88,512]{2,1,0:T(8,128)}, f32[1,88,512]{2,1,0:T(8,128)S(1)}, u32[]{:S(2)}) copy-start(f32[1,88,512]{2,1,0:T(8,128)S(1)} %collective-permute-done.2.side_ref.side_first) | copy-start | bytes 540676
  26.6 1.7 %copy-start.8 = (f32[88,2048]{1,0:T(8,128)}, f32[88,2048]{1,0:T(8,128)S(1)}, u32[]{:S(2)}) copy-start(f32[88,2048]{1,0:T(8,128)S(1)} %collective-permute-done.1.high_ref.high_first) | copy-start | bytes 2162692
  31.4 15.8 %collective-permute-start.6 = (f32[80,2048]{1,0:T(8,128)S(1)}, f32[80,2048]{1,0:T(8,128)S(1)}, u32[]{:S(2)}, u32[]{:S(2)}) collective-permute-start(f32[80,2048]{1,0:T(8,128)S(1)} %get-tuple-element.31.x_ref), channel_id=1, source_target_pairs={{0,2},{2,0},{4,6},{6,4},{8,10},{10,8},{12,14},{14,12},{16,18},{18,... | collective-permute-start | bytes 1966088 | tf_op jit(solution)/shard_map/ppermute | solution.py:660
  31.5 15.8 %collective-permute-start.5 = (f32[80,1024]{1,0:T(8,128)S(1)}, f32[80,1024]{1,0:T(8,128)S(1)}, u32[]{:S(2)}, u32[]{:S(2)}) collective-permute-start(f32[80,1024]{1,0:T(8,128)S(1)} %get-tuple-element.32), channel_id=1, source_target_pairs={{0,30},{2,4},{4,2},{6,8},{8,6},{10,12},{12,10},{14,16},{16,14},{18... | collective-permute-start | bytes 983048 | tf_op jit(solution)/shard_map/ppermute | solution.py:660
  36.1 8.5 %collective-permute-start.7 = (f32[1,80,512]{2,1,0:T(8,128)S(1)}, f32[1,80,512]{2,1,0:T(8,128)S(1)}, u32[]{:S(2)}, u32[]{:S(2)}) collective-permute-start(f32[1,80,512]{2,1,0:T(8,128)S(1)} %get-tuple-element.33), channel_id=1, source_target_pairs={{0,1},{1,0},{2,3},{3,2},{4,5},{5,4},{6,7},{7,6},{8,9},{9,8},{10,11... | collective-permute-start | bytes 491528 | tf_op jit(solution)/shard_map/ppermute | solution.py:674
  37.6 7.0 %collective-permute-start.8 = (f32[1,80,128]{2,1,0:T(8,128)S(1)}, f32[1,80,128]{2,1,0:T(8,128)S(1)}, u32[]{:S(2)}, u32[]{:S(2)}) collective-permute-start(f32[1,80,128]{2,1,0:T(8,128)S(1)} %get-tuple-element.34), channel_id=1, source_target_pairs={{0,31},{1,30},{2,5},{3,4},{4,3},{5,2},{6,9},{7,8},{8,7},{9,6},{10,... | collective-permute-start | bytes 122888 | tf_op jit(solution)/shard_map/ppermute | solution.py:674
  37.6 7.0 %collective-permute-start.9 = (f32[1,80,128]{2,1,0:T(8,128)S(1)}, f32[1,80,128]{2,1,0:T(8,128)S(1)}, u32[]{:S(2)}, u32[]{:S(2)}) collective-permute-start(f32[1,80,128]{2,1,0:T(8,128)S(1)} %get-tuple-element.35), channel_id=1, source_target_pairs={{0,3},{1,2},{2,1},{3,0},{4,7},{5,6},{6,5},{7,4},{8,11},{9,10},{10,... | collective-permute-start | bytes 122888 | tf_op jit(solution)/shard_map/ppermute | solution.py:674
  38.4 8.9 %copy-start.9 = (f32[88,2048]{1,0:T(8,128)S(1)}, f32[88,2048]{1,0:T(8,128)}, u32[]{:S(2)}) copy-start(f32[88,2048]{1,0:T(8,128)} %copy-done.8) | copy-start | bytes 2162692
  38.4 8.9 %copy-start.11 = (f32[1,88,512]{2,1,0:T(8,128)S(1)}, f32[1,88,512]{2,1,0:T(8,128)}, u32[]{:S(2)}) copy-start(f32[1,88,512]{2,1,0:T(8,128)} %copy-done.10) | copy-start | bytes 540676
  44.7 9.7 %collective-permute-start.10 = (f32[80,1024]{1,0:T(8,128)S(1)}, f32[80,1024]{1,0:T(8,128)S(1)}, u32[]{:S(2)}, u32[]{:S(2)}) collective-permute-start(f32[80,1024]{1,0:T(8,128)S(1)} %shard_map.156), channel_id=1, source_target_pairs={{0,30},{2,4},{4,2},{6,8},{8,6},{10,12},{12,10},{14,16},{16,14},{18... | collective-permute-start | bytes 983048 | tf_op jit(solution)/shard_map/ppermute | solution.py:660
  50.9 10.4 %all-to-all-start.1 = ((f32[16,8,128]{2,1,0:T(8,128)}), f32[16,8,128]{2,1,0:T(8,128)S(1)}, u32[]{:S(2)}, u32[]{:S(2)}) async-start(f32[16,8,128]{2,1,0:T(8,128)} %get-tuple-element.41), calls=%async_computation.1 | async-start | bytes 131072 | tf_op jit(solution)/shard_map/all_to_all | solution.py:739
  (6 other events, 4.6 us)

commit v9 on v8

--- a/solution.py
+++ b/solution.py
@@ -16,7 +16,7 @@
 WINDOW = 8
 HIGHEST = lax.Precision.HIGHEST
 DOWN_AZ, SPECTRAL, UP_SP, DOWN_SP, UP_AX, DOWN_AX, UP_AZ = range(7)
-C_TIME, C_AZ, C_SP, C_UP, C_DOWN, C_MASK, C_OWNER = range(7)
+C_TIME, C_AZ, C_SP, C_UP, C_DOWN, C_MASK = range(6)
 RATES = 8
 AXES = ("sector", "span")
 
@@ -46,7 +46,12 @@
             [t for t in range(self.insts) if any((k + self.shift[t]) % sectors == o for k in self.blocks)]
             for o in range(sectors)
         ]
-        assert max(map(len, self.slots)) * self.width <= LANES
+        last = LANES - self.width
+        self.weight_at = [(t, last) for t in range(self.fields)] + [
+            (self.fields, i * self.width) for i in range(self.insts - self.fields)
+        ]
+        assert max(map(len, self.slots)) * self.width <= last and 2 * self.cells == self.width
+        assert self.fields == RATES - 1 and (self.insts - self.fields) * self.width <= LANES
 
     def spectral(self):
         t = np.arange(self.insts)
@@ -364,7 +369,7 @@
     return corner
 
 
-def prepare(plan, rhs_ref, coef_ref, both_ref, m_ref, side_ref, c0_ref, c1_ref, rates_ref):
+def prepare(plan, rhs_ref, coef_ref, m_ref, side_ref, c0_ref, c1_ref, rates_ref):
     pad, cells = plan.pad, plan.cells
     mask, diag, time, *face = [coef_ref[cells * i : cells * (i + 1), :] for i in range(6)]
     scale = mask / diag
@@ -387,17 +392,6 @@
         m_ref[:pad, at(cell)] = field * table[C_MASK]
         m_ref[pad:, at(cell)] = jnp.concatenate(table + [rest], axis=0)
     write_edges(plan, m_ref, side_ref, (c0_ref, c1_ref))
-    wide = 2 * cells
-    row = slice(pad + C_OWNER, pad + C_OWNER + 1)
-    for t in range(plan.insts):
-        both = both_ref[t : t + 1, :]
-        lanes = slice(t * wide, (t + 1) * wide)
-        m_ref[row, lanes] = both
-        group, part = divmod(t, LANES // wide)
-        for n in range(plan.ends):
-            side_ref[n, row, lanes] = both
-            for ref in (c0_ref, c1_ref):
-                ref[n, pad + group : pad + group + 1, part * wide : (part + 1) * wide] = both
 
 
 def write_edges(plan, x_ref, side_ref, c_refs):
@@ -428,11 +422,14 @@
     down_out[...] = matrix(plan, out_ref, DOWN_AZ)
 
 
-def send_panels(plan, stator_ref, out_ref, panels_ref):
+def send_panels(plan, stator_ref, both_ref, out_ref, panels_ref):
     me = lax.axis_index("sector")
     for f in range(plan.fields):
         panels_ref[pl.ds(f, plan.insts, stride=RATES), : plan.width] = jnp.transpose(stator_ref[f])
     out_ref[...] = jnp.zeros_like(out_ref)
+    for t, (row, start) in enumerate(plan.weight_at):
+        both = jnp.broadcast_to(both_ref[t : t + 1, :][None], (out_ref.shape[0], 1, plan.width))
+        out_ref[:, row : row + 1, start : start + plan.width] = both
     for o, slots in enumerate(plan.slots):
         to = lax.rem(me + (plan.sectors - o), plan.sectors) * plan.spans
         for slot, t in enumerate(slots):
@@ -443,7 +440,7 @@
 
 
 def begin(
-    plan, w_ref, m_ref, got_ref, low_ref, high_ref, side_ref, c_low, c_high,
+    plan, w_ref, m_ref, got_ref,
     seams_ref, weight_ref, x_ref, g_ref, panels_ref, terms_ref, rows_ref, p0_ref, p1_ref,
 ):
     pad, insts, fields = plan.pad, plan.insts, plan.fields
@@ -451,6 +448,7 @@
     even, is_first = parity() == 0, span == 0
     tiles = plan.tiles
     panels_ref[...] = jnp.zeros_like(panels_ref)
+    rows_ref[...] = jnp.zeros_like(rows_ref)
     for n, (k, x) in enumerate(tiles):
         at_span = x if plan.spans == 2 else jnp.clip(span + x, 0, plan.spans - 1)
         for t in range(insts):
@@ -458,36 +456,12 @@
             source = lax.rem(me + o, plan.sectors) * plan.spans + at_span
             tile = rolled(got_ref[source], -plan.slots[o].index(t) * plan.width)
             panels_ref[t * fields : (t + 1) * fields, n * LANES : n * LANES + plan.width] = tile[:fields, : plan.width]
-
-    wide = 2 * plan.cells
-    row = slice(pad + C_OWNER, pad + C_OWNER + 1)
-    zeros = jnp.zeros((16 - insts, LANES), jnp.float32)
-
-    def table(read, packed):
-        out = []
-        for t in range(insts):
-            group, part = divmod(t, LANES // wide)
-            lanes = at(0 if packed else group)
-            out.append(rolled(read(pad + group if packed else row.start, lanes), -part * wide))
-        return jnp.concatenate(out + [zeros], axis=0)
-
-    own = [table(lambda i, lanes: m_ref[i : i + 1, lanes], False)]
-    low = [table(lambda i, lanes: low_ref[i : i + 1, lanes], False)]
-    high = [table(lambda i, lanes: high_ref[i : i + 1, lanes], False)]
-    for n in range(plan.ends):
-        own.append(table(lambda i, lanes: side_ref[n, i : i + 1, lanes], False))
-        low.append(table(lambda i, lanes: c_low[n, i : i + 1, lanes], True))
-        high.append(table(lambda i, lanes: c_high[n, i : i + 1, lanes], True))
-    for n, (k, x) in enumerate(tiles):
-        if k == 0:
-            block = own
-        else:
-            block = [jnp.where(even, *pair) for pair in (zip(low, high) if k < 0 else zip(high, low))]
-        if plan.spans == 2:
-            value = jnp.where(is_first, block[x], block[1 - x])
-        else:
-            value = block[(0, 1, 2)[x]]
-        rows_ref[:, at(n)] = value
+        tile = got_ref[lax.rem(me + k + plan.sectors, plan.sectors) * plan.spans + at_span]
+        lanes = slice(n * LANES, n * LANES + plan.width)
+        rows_ref[:fields, lanes] = rolled(tile, -plan.weight_at[0][1])[:fields, : plan.width]
+        for t in range(fields, insts):
+            row, start = plan.weight_at[t]
+            rows_ref[t : t + 1, lanes] = rolled(tile, -start)[row : row + 1, : plan.width]
     spread = dot_full(plan.inst_rows(), rows_ref[...])
     spread = pick(jnp.concatenate([spread[:, at(n)] for n in range(len(tiles))], axis=0), plan.weight_lanes())
     first, share, panel = spread, rolled(spread, plan.ct * plan.width), plan.panel_lanes()
@@ -557,8 +531,8 @@
     write_edges(plan, x_ref, side_out, (c0_ref, c1_ref))
 
 
-def hold_far(plan, x_ref, side_ref, c_low, c_high, far_ref):
-    come = side_ref[0, 0:1, 0:1] + c_low[0, 0:1, 0:1] + c_high[0, 0:1, 0:1]
+def hold_far(plan, x_ref, side_ref, c_high, far_ref):
+    come = side_ref[0, 0:1, 0:1] + c_high[0, 0:1, 0:1]
     far_ref[...] = x_ref[:, plan.slab :] + 0.0 * come
 
 
@@ -690,7 +664,12 @@
         return f32(ends, rows, DEPTH * plan.ct * LANES), f32(ends, rows, LANES), f32(ends, rows, LANES)
 
     stator = jnp.transpose(stator_adj, (1, 2, 3, 0)).reshape(fields, plan.width, insts)
-    sent = call(bind(send_panels, plan), f32(sectors * spans, RATES, LANES), (vmem(insts * RATES, LANES),))(stator)
+    sent = call(bind(send_panels, plan), f32(sectors * spans, RATES, LANES), (vmem(insts * RATES, LANES),))(
+        stator,
+        jnp.concatenate([
+            lax.rem(owner, plan.panels).astype(jnp.float32).reshape(insts, cells), first_panel_share.reshape(insts, cells),
+        ], axis=1),
+    )
     got = lax.all_to_all(sent, AXES, 0, 0, tiled=True)
     m, side, c0, c1 = call(
         bind(prepare, plan), (f32(pad + RATES, plan.ct * slab),) + edges(pad + RATES), (vmem(6, cells, LANES),)
@@ -700,9 +679,6 @@
             wall_mask.astype(jnp.float32).reshape(cells, LANES), diag_coef.reshape(cells, LANES),
             time_coef.reshape(cells, LANES), face_coef.reshape(3 * cells, LANES),
         ]),
-        jnp.concatenate([
-            lax.rem(owner, plan.panels).astype(jnp.float32).reshape(insts, cells), first_panel_share.reshape(insts, cells),
-        ], axis=1),
     )
     low_first, high_first = swap(m, next_chip), swap(m, next_core)
     side_first = beside(plan, side, alone)
@@ -716,7 +692,7 @@
         bind(begin, plan), (f32(3, 1 + ends, pad, LANES), f32(pad, LANES), whole, whole),
         (vmem(pad, tiles * LANES), vmem(tiles * pad, LANES), vmem(16, tiles * LANES)) + products,
         flops=2_000_000_000,
-    )(matrices, m, got, low_first, high_first, side_first, c_low, c_high)
+    )(matrices, m, got)
     x, near, side, c0, c1 = call(
         bind(first_half, plan), (whole, half) + edges(pad),
         products + (vmem(pad, 2 * slab),) + (vmem(pad, slab),) * 4 + (vmem(LANES, LANES),),
@@ -727,7 +703,7 @@
     side = beside(plan, side, alone)
     c_low, c_high = beside(plan, c0, next_chip), beside(plan, c1, next_core)
     (g,) = call(bind(inner, plan), (whole,), products, flops=2_000_000_000)(matrices, m, force, x)
-    far = call(bind(hold_far, plan), half)(x, side, c_low, c_high)
+    far = call(bind(hold_far, plan), half)(x, side, c_high)
     far_low = swap(far, next_chip)
     back, n0, h0, x1, rates = call(
         bind(middle, plan), (f32(sectors, RATES, LANES), half, half, half, f32(RATES, slab)),

time: 62.5 us -> 60.4 us (0.966)
  waiting for transfers between devices: 18.3 us -> 15.1 us
  starting transfers between devices: 26 us -> 26.9 us
  other arithmetic: 0.79 us -> 1.54 us
  local copies, waits for them, and re-layouts: 2.55 us -> 1.92 us
    ppermute x6, waiting for transfers between devices: 9.34 us -> 3.87 us  [beside(): return lax.ppermute(array, AXES, pairs(0))]
    all_to_all x1, waiting for transfers between devices: 3.39 us -> 5.64 us  [on_device(): got = lax.all_to_all(sent, AXES, 0, 0, tiled=True)]
    ppermute x5, starting transfers between devices: 12.7 us -> 13.7 us  [swap(): return lax.ppermute(array, 'sector', list(enumerate(partner)))]
    concatenate x1, other arithmetic: 0.01 us -> 0.74 us  [on_device(): jnp.concatenate([wall_mask.astype(jnp.float32).reshape(cells, LANES), dia...]
    unnamed x34 -> x32, local copies, waits for them, and re-layouts: 2.39 us -> 1.76 us
  transfers between devices with their start and end apart: 13 -> 13, of which waited for: 5 -> 4; matrix products, arithmetic and copies ran while one was open for 0% -> 0% of each run, Pallas kernels for 12% -> 16%
where the time goes in v9:
time: 60.4 us; the launch traced here: 59.9 us
  starting transfers between devices  26.9 us (45%)
  waiting for transfers between devices  15.1 us (25%)
  Pallas kernels  13.6 us (23%)
  local copies, waits for them, and re-layouts  1.92 us (3%)
  other arithmetic  1.54 us (3%)
  between operations  0.88 us (1%)
    ppermute x5, starting transfers between devices, swap(): return lax.ppermute(array, 'sector', list(enumerate(partner)))  13.7 us
    ppermute x6, starting transfers between devices, beside(): return lax.ppermute(array, AXES, pairs(0))  7.05 us
    all_to_all x1, waiting for transfers between devices, on_device(): got = lax.all_to_all(sent, AXES, 0, 0, tiled=True)  5.64 us
    all_to_all x1, waiting for transfers between devices, on_device(): returned = lax.all_to_all(back, 'sector', 0, 0, tiled=True)  5.54 us
    ppermute x6, waiting for transfers between devices, beside(): return lax.ppermute(array, AXES, pairs(0))  3.87 us
    pallas_call x1, Pallas kernels, on_device(): call(bind(middle, plan), (f32(sectors, RATES, LANES), half, half, half, f...  3.6 us
    all_to_all x1, starting transfers between devices, on_device(): returned = lax.all_to_all(back, 'sector', 0, 0, tiled=True)  3.5 us
    pallas_call x1, Pallas kernels, on_device(): call(bind(first_half, plan), (whole, half) + edges(pad), products + (vmem...  3.04 us
  transfers between devices with their start and end apart: 13, of which 4 were waited for; matrix products, arithmetic and copies ran while one was open for 0% of the time, Pallas kernels for 16%

profile of v9, /device:TPU:0, one launch (start us, length us, event | category | flops | bytes accessed | tf_op | source)
XLA Modules:
  0.0 59.9 jit_solution(9266212849036022012)
XLA Ops:
  0.7 0.7 %convert_bitcast_fusion = f32[16,128]{1,0:T(8,128)S(1)} fusion(s32[2,8,128]{2,1,0:T(8,128)} %param.20), kind=kLoop, calls=%fused_computation.7 | loop fusion | flops 2048 | bytes 16384 | tf_op jit(solution)/shard_map/reshape | solution.py:679
  1.4 0.7 %pad_maximum_fusion.coef_ref = f32[96,128]{1,0:T(8,128)S(1)} fusion(f32[48,128]{1,0:T(8,128)} %bitcast.20, f32[16,128]{1,0:T(8,128)S(1)} %bitcast.21, f32[16,128]{1,0:T(8,128)S(1)} %bitcast.22, f32[16,128]{1,0:T(8,128)S(1)} %convert_bitcast_fusion), kind=kLoop, calls=%fused_computation | loop fusion | flops 36864 | bytes 98304 | tf_op jit(solution)/shard_map/concatenate | solution.py:678
  2.1 1.1 %copy-done = f32[11,7,2,8,128]{4,3,2,1,0:T(8,128)S(1)} copy-done((f32[11,7,2,8,128]{4,3,2,1,0:T(8,128)S(1)}, f32[11,7,2,8,128]{4,3,2,1,0:T(8,128)}, u32[]{:S(2)}) %copy-start) | copy-done | bytes 630808
  3.5 5.5 %collective-permute-start = (f32[88,2048]{1,0:T(8,128)S(1)}, f32[88,2048]{1,0:T(8,128)S(1)}, u32[]{:S(2)}, u32[]{:S(2)}) collective-permute-start(f32[88,2048]{1,0:T(8,128)S(1)} %get-tuple-element.24.m_ref), channel_id=1, source_target_pairs={{0,30},{2,4},{4,2},{6,8},{8,6},{10,12},{12,10},{14,16},{16,14},{18... | collective-permute-start | bytes 2162696 | tf_op jit(solution)/shard_map/ppermute | solution.py:634
  9.1 0.6 %copy-done.15 = s32[11,2,8]{0,2,1:T(8,128)S(1)} copy-done((s32[11,2,8]{0,2,1:T(8,128)S(1)}, s32[11,2,8]{0,2,1:T(8,128)}, u32[]{:S(2)}) %copy-start.15) | copy-done | bytes 728
  9.9 0.9 %shard_map.151 = f32[32,8,128]{2,1,0:T(8,128)} custom-call(f32[7,32,11]{2,1,0:T(8,128)S(1)} %bitcast.17, f32[11,32]{1,0:T(8,128)S(1)} %pad_maximum_fusion.1.both_ref), custom_call_target="tpu_custom_call" | custom-call | flops 2000000 | bytes 1000000 | tf_op jit(solution)/shard_map/pallas_call | solution.py:667
  10.8 2.7 %all-to-all-start = ((f32[32,8,128]{2,1,0:T(8,128)}), f32[32,8,128]{2,1,0:T(8,128)S(1)}, u32[]{:S(2)}, u32[]{:S(2)}) async-start(f32[32,8,128]{2,1,0:T(8,128)} %shard_map.151), calls=%async_computation | async-start | bytes 262144 | tf_op jit(solution)/shard_map/all_to_all | solution.py:673
  13.5 1.7 %collective-permute-start.2 = (f32[1,88,512]{2,1,0:T(8,128)S(1)}, f32[1,88,512]{2,1,0:T(8,128)S(1)}, u32[]{:S(2)}, u32[]{:S(2)}) collective-permute-start(f32[1,88,512]{2,1,0:T(8,128)S(1)} %get-tuple-element.27), channel_id=1, source_target_pairs={{0,1},{1,0},{2,3},{3,2},{4,5},{5,4},{6,7},{7,6},{8,9},{9,8},{10,11... | collective-permute-start | bytes 540680 | tf_op jit(solution)/shard_map/ppermute | solution.py:648
  15.2 3.9 %collective-permute-start.3 = (f32[1,88,128]{2,1,0:T(8,128)S(1)}, f32[1,88,128]{2,1,0:T(8,128)S(1)}, u32[]{:S(2)}, u32[]{:S(2)}) collective-permute-start(f32[1,88,128]{2,1,0:T(8,128)S(1)} %get-tuple-element.28), channel_id=1, source_target_pairs={{0,31},{1,30},{2,5},{3,4},{4,3},{5,2},{6,9},{7,8},{8,7},{9,6},{10,... | collective-permute-start | bytes 135176 | tf_op jit(solution)/shard_map/ppermute | solution.py:648
  19.1 1.1 %shard_map.149 = (bf16[560,240]{1,0:T(8,128)(2,1)S(1)}, bf16[80,240]{1,0:T(8,128)(2,1)S(1)}) custom-call(f32[3,7,7]{2,1,0:T(8,128)S(1)} %copy-done.5, f32[3,7,7]{2,1,0:T(8,128)S(1)} %copy-done.6, bf16[80,240]{1,0:T(8,128)(2,1)S(1)} %copy-done.3, f32[80,7]{1,0:T(8,128)S(1)} %copy-done.4, f32[7,240]{1,0:T(8,128)S(1)} %copy-done.7, f32[80,240]{1,0:T(8,128)S(1)} %copy-done.2), custom_call_target="tpu_custom_call" | custom-call | flops 2000000 | bytes 1000000 | tf_op jit(solution)/shard_map/pallas_call | solution.py:686
  20.2 5.6 %all-to-all-done.got_ref = f32[32,8,128]{2,1,0:T(8,128)S(1)} async-done(((f32[32,8,128]{2,1,0:T(8,128)}), f32[32,8,128]{2,1,0:T(8,128)S(1)}, u32[]{:S(2)}, u32[]{:S(2)}) %all-to-all-start) | async-done | bytes 131104 | tf_op jit(solution)/shard_map/all_to_all | solution.py:673
  25.9 1.7 %shard_map.152 = (f32[3,2,80,128]{3,2,1,0:T(8,128)S(1)}, f32[80,128]{1,0:T(8,128)S(1)}, f32[80,2048]{1,0:T(8,128)S(1)}, f32[80,2048]{1,0:T(8,128)S(1)}) custom-call(bf16[560,240]{1,0:T(8,128)(2,1)S(1)} %get-tuple-element.23.w_ref, f32[88,2048]{1,0:T(8,128)S(1)} %get-tuple-element.24.m_ref, f32[32,8,128]{2,1,0:T(8,128)S(1)} %all-to-all-done.got_ref), custom_call_target="tpu_custom_call" | custom-call | flops 2000000000 | bytes 1000000 | tf_op jit(solution)/shard_map/pallas_call | solution.py:691
  27.7 3.0 %shard_map.153 = (f32[80,2048]{1,0:T(8,128)S(1)}, f32[80,1024]{1,0:T(8,128)S(1)}, f32[1,80,512]{2,1,0:T(8,128)S(1)}, f32[1,80,128]{2,1,0:T(8,128)S(1)}, f32[1,80,128]{2,1,0:T(8,128)S(1)}) custom-call(bf16[560,240]{1,0:T(8,128)(2,1)S(1)} %get-tuple-element.23.w_ref, f32[88,2048]{1,0:T(8,128)S(1)} %get-tuple-element.24.m_ref, ...), custom_call_target="tpu_custom_call" | custom-call | flops 4000000000 | bytes 1000000 | tf_op jit(solution)/shard_map/pallas_call | solution.py:696
  30.8 4.6 %collective-permute-start.5 = (f32[80,1024]{1,0:T(8,128)S(1)}, f32[80,1024]{1,0:T(8,128)S(1)}, u32[]{:S(2)}, u32[]{:S(2)}) collective-permute-start(f32[80,1024]{1,0:T(8,128)S(1)} %get-tuple-element.32), channel_id=1, source_target_pairs={{0,30},{2,4},{4,2},{6,8},{8,6},{10,12},{12,10},{14,16},{16,14},{18... | collective-permute-start | bytes 983048 | tf_op jit(solution)/shard_map/ppermute | solution.py:634
  35.4 1.5 %collective-permute-start.7 = (f32[1,80,512]{2,1,0:T(8,128)S(1)}, f32[1,80,512]{2,1,0:T(8,128)S(1)}, u32[]{:S(2)}, u32[]{:S(2)}) collective-permute-start(f32[1,80,512]{2,1,0:T(8,128)S(1)} %get-tuple-element.33), channel_id=1, source_target_pairs={{0,1},{1,0},{2,3},{3,2},{4,5},{5,4},{6,7},{7,6},{8,9},{9,8},{10,11... | collective-permute-start | bytes 491528 | tf_op jit(solution)/shard_map/ppermute | solution.py:648
  36.9 0.8 %shard_map.154.g_ref = f32[80,2048]{1,0:T(8,128)S(1)} custom-call(bf16[560,240]{1,0:T(8,128)(2,1)S(1)} %get-tuple-element.23.w_ref, f32[88,2048]{1,0:T(8,128)S(1)} %get-tuple-element.24.m_ref, f32[80,2048]{1,0:T(8,128)S(1)} %get-tuple-element.25.f_ref, f32[80,2048]{1,0:T(8,128)S(1)} %get-tuple-element.31.x_ref), custom_call_target="tpu_custom_call" | custom-call | flops 2000000000 | bytes 1000000 | tf_op jit(solution)/shard_map/pallas_call | solution.py:705
  37.7 3.4 %collective-permute-done.9.c_high = f32[1,80,128]{2,1,0:T(8,128)S(1)} collective-permute-done((f32[1,80,128]{2,1,0:T(8,128)S(1)}, f32[1,80,128]{2,1,0:T(8,128)S(1)}, u32[]{:S(2)}, u32[]{:S(2)}) %collective-permute-start.9) | collective-permute-done | bytes 40992 | tf_op jit(solution)/shard_map/ppermute | solution.py:648
  41.2 0.4 collective-permute-done.7.side_ref
  41.6 3.5 %collective-permute-start.10 = (f32[80,1024]{1,0:T(8,128)S(1)}, f32[80,1024]{1,0:T(8,128)S(1)}, u32[]{:S(2)}, u32[]{:S(2)}) collective-permute-start(f32[80,1024]{1,0:T(8,128)S(1)} %shard_map.156), channel_id=1, source_target_pairs={{0,30},{2,4},{4,2},{6,8},{8,6},{10,12},{12,10},{14,16},{16,14},{18... | collective-permute-start | bytes 983048 | tf_op jit(solution)/shard_map/ppermute | solution.py:634
  45.2 3.6 %shard_map.155 = (f32[16,8,128]{2,1,0:T(8,128)}, f32[80,1024]{1,0:T(8,128)S(1)}, f32[80,1024]{1,0:T(8,128)S(1)}, f32[80,1024]{1,0:T(8,128)S(1)}, f32[8,1024]{1,0:T(8,128)S(1)}) custom-call(bf16[560,240]{1,0:T(8,128)(2,1)S(1)} %get-tuple-element.23.w_ref, f32[88,2048]{1,0:T(8,128)S(1)} %get-tuple-element.24.m_ref, f32[80,2048]{1,0:T(8,128)S(1)} %get-tuple-element.25.f_ref, ...), custom_call_target="tpu_custom_call" | custom-call | flops 4000000000 | bytes 1000000 | tf_op jit(solution)/shard_map/pallas_call | solution.py:708
  48.8 3.5 %all-to-all-start.1 = ((f32[16,8,128]{2,1,0:T(8,128)}), f32[16,8,128]{2,1,0:T(8,128)S(1)}, u32[]{:S(2)}, u32[]{:S(2)}) async-start(f32[16,8,128]{2,1,0:T(8,128)} %get-tuple-element.41), calls=%async_computation.1 | async-start | bytes 131072 | tf_op jit(solution)/shard_map/all_to_all | solution.py:715
  52.3 1.3 %shard_map.157 = f32[1232,128]{1,0:T(8,128)} custom-call(bf16[80,240]{1,0:T(8,128)(2,1)S(1)} %get-tuple-element.22.w_ref, f32[8,1024]{1,0:T(8,128)S(1)} %get-tuple-element.37.rates_ref, f32[80,1024]{1,0:T(8,128)S(1)} %get-tuple-element.38.n0_ref, f32[80,1024]{1,0:T(8,128)S(1)} %get-tuple-element.39.h0_ref, f32[80,1024]{1,0:T(8,128)S(1)} %get-tuple-element.40.x1_ref, ...), custom_call_target="tpu_custom_call" | custom-call | flops 2000000 | bytes 1000000 | tf_op jit(solution)/shard_map/pallas_call | solution.py:717
  53.6 5.5 %all-to-all-done.1.got_ref = f32[16,8,128]{2,1,0:T(8,128)S(1)} async-done(((f32[16,8,128]{2,1,0:T(8,128)}), f32[16,8,128]{2,1,0:T(8,128)S(1)}, u32[]{:S(2)}, u32[]{:S(2)}) %all-to-all-start.1) | async-done | bytes 65568 | tf_op jit(solution)/shard_map/all_to_all | solution.py:715
  59.1 0.8 %shard_map.158 = f32[7,32,11]{2,1,0:T(8,128)} custom-call(f32[16,8,128]{2,1,0:T(8,128)S(1)} %all-to-all-done.1.got_ref), custom_call_target="tpu_custom_call" | custom-call | flops 2000000 | bytes 1000000 | tf_op jit(solution)/shard_map/pallas_call | solution.py:716
  (50 shorter events, 0.8 us)
Async XLA Ops:
  3.2 5.8 %copy-start.14 = (f32[11,2,8]{0,2,1:T(8,128)S(1)}, f32[11,2,8]{0,2,1:T(8,128)}, u32[]{:S(2)}) copy-start(f32[11,2,8]{0,2,1:T(8,128)} %param.23) | copy-start | bytes 2116
  3.2 6.7 %copy-start.1 = (f32[11,7,4,8]{0,3,2,1:T(8,128)S(1)}, f32[11,7,4,8]{0,3,2,1:T(8,128)}, u32[]{:S(2)}) copy-start(f32[11,7,4,8]{0,3,2,1:T(8,128)} %param.21) | copy-start | bytes 29572
  3.5 24.2 %collective-permute-start = (f32[88,2048]{1,0:T(8,128)S(1)}, f32[88,2048]{1,0:T(8,128)S(1)}, u32[]{:S(2)}, u32[]{:S(2)}) collective-permute-start(f32[88,2048]{1,0:T(8,128)S(1)} %get-tuple-element.24.m_ref), channel_id=1, source_target_pairs={{0,30},{2,4},{4,2},{6,8},{8,6},{10,12},{12,10},{14,16},{16,14},{18... | collective-permute-start | bytes 2162696 | tf_op jit(solution)/shard_map/ppermute | solution.py:634
  9.0 18.7 %collective-permute-start.1 = (f32[88,2048]{1,0:T(8,128)S(1)}, f32[88,2048]{1,0:T(8,128)S(1)}, u32[]{:S(2)}, u32[]{:S(2)}) collective-permute-start(f32[88,2048]{1,0:T(8,128)S(1)} %get-tuple-element.24.m_ref), channel_id=1, source_target_pairs={{0,2},{2,0},{4,6},{6,4},{8,10},{10,8},{12,14},{14,12},{16,18},{18,... | collective-permute-start | bytes 2162696 | tf_op jit(solution)/shard_map/ppermute | solution.py:634
  10.7 8.3 %copy-start.2 = (f32[80,240]{1,0:T(8,128)S(1)}, f32[80,240]{1,0:T(8,128)}, u32[]{:S(2)}) copy-start(f32[80,240]{1,0:T(8,128)} %constant.16.clone.diagonal_ref) | copy-start | bytes 230404
  10.7 8.3 %copy-start.3 = (bf16[80,240]{1,0:T(8,128)(2,1)S(1)}, bf16[80,240]{1,0:T(8,128)(2,1)}, u32[]{:S(2)}) copy-start(bf16[80,240]{1,0:T(8,128)(2,1)} %constant.13.clone.spectral_ref) | copy-start | bytes 115204
  10.7 8.3 %copy-start.4 = (f32[80,7]{1,0:T(8,128)S(1)}, f32[80,7]{1,0:T(8,128)}, u32[]{:S(2)}) copy-start(f32[80,7]{1,0:T(8,128)} %constant.14.clone.rows_ref) | copy-start | bytes 6724
  10.7 8.3 %copy-start.5 = (f32[3,7,7]{2,1,0:T(8,128)S(1)}, f32[3,7,7]{2,1,0:T(8,128)}, u32[]{:S(2)}) copy-start(f32[3,7,7]{2,1,0:T(8,128)} %up_ref.1) | copy-start | bytes 1768
  10.7 8.3 %copy-start.6 = (f32[3,7,7]{2,1,0:T(8,128)S(1)}, f32[3,7,7]{2,1,0:T(8,128)}, u32[]{:S(2)}) copy-start(f32[3,7,7]{2,1,0:T(8,128)} %down_ref.1) | copy-start | bytes 1768
  10.8 8.3 %copy-start.7 = (f32[7,240]{1,0:T(8,128)S(1)}, f32[7,240]{1,0:T(8,128)}, u32[]{:S(2)}) copy-start(f32[7,240]{1,0:T(8,128)} %constant.15.clone.lanes_ref) | copy-start | bytes 20164
  10.8 15.1 %all-to-all-start = ((f32[32,8,128]{2,1,0:T(8,128)}), f32[32,8,128]{2,1,0:T(8,128)S(1)}, u32[]{:S(2)}, u32[]{:S(2)}) async-start(f32[32,8,128]{2,1,0:T(8,128)} %shard_map.151), calls=%async_computation | async-start | bytes 262144 | tf_op jit(solution)/shard_map/all_to_all | solution.py:673
  13.5 14.1 %collective-permute-start.2 = (f32[1,88,512]{2,1,0:T(8,128)S(1)}, f32[1,88,512]{2,1,0:T(8,128)S(1)}, u32[]{:S(2)}, u32[]{:S(2)}) collective-permute-start(f32[1,88,512]{2,1,0:T(8,128)S(1)} %get-tuple-element.27), channel_id=1, source_target_pairs={{0,1},{1,0},{2,3},{3,2},{4,5},{5,4},{6,7},{7,6},{8,9},{9,8},{10,11... | collective-permute-start | bytes 540680 | tf_op jit(solution)/shard_map/ppermute | solution.py:648
  15.2 12.4 %collective-permute-start.3 = (f32[1,88,128]{2,1,0:T(8,128)S(1)}, f32[1,88,128]{2,1,0:T(8,128)S(1)}, u32[]{:S(2)}, u32[]{:S(2)}) collective-permute-start(f32[1,88,128]{2,1,0:T(8,128)S(1)} %get-tuple-element.28), channel_id=1, source_target_pairs={{0,31},{1,30},{2,5},{3,4},{4,3},{5,2},{6,9},{7,8},{8,7},{9,6},{10,... | collective-permute-start | bytes 135176 | tf_op jit(solution)/shard_map/ppermute | solution.py:648
  19.0 8.6 %collective-permute-start.4 = (f32[1,88,128]{2,1,0:T(8,128)S(1)}, f32[1,88,128]{2,1,0:T(8,128)S(1)}, u32[]{:S(2)}, u32[]{:S(2)}) collective-permute-start(f32[1,88,128]{2,1,0:T(8,128)S(1)} %get-tuple-element.29), channel_id=1, source_target_pairs={{0,3},{1,2},{2,1},{3,0},{4,7},{5,6},{6,5},{7,4},{8,11},{9,10},{10,... | collective-permute-start | bytes 135176 | tf_op jit(solution)/shard_map/ppermute | solution.py:648
  27.6 3.1 %copy-start.10 = (f32[1,88,512]{2,1,0:T(8,128)}, f32[1,88,512]{2,1,0:T(8,128)S(1)}, u32[]{:S(2)}) copy-start(f32[1,88,512]{2,1,0:T(8,128)S(1)} %collective-permute-done.2.side_ref.side_first) | copy-start | bytes 540676
  30.7 14.4 %collective-permute-start.6 = (f32[80,2048]{1,0:T(8,128)S(1)}, f32[80,2048]{1,0:T(8,128)S(1)}, u32[]{:S(2)}, u32[]{:S(2)}) collective-permute-start(f32[80,2048]{1,0:T(8,128)S(1)} %get-tuple-element.31.x_ref), channel_id=1, source_target_pairs={{0,2},{2,0},{4,6},{6,4},{8,10},{10,8},{12,14},{14,12},{16,18},{18,... | collective-permute-start | bytes 1966088 | tf_op jit(solution)/shard_map/ppermute | solution.py:634
  30.8 14.4 %collective-permute-start.5 = (f32[80,1024]{1,0:T(8,128)S(1)}, f32[80,1024]{1,0:T(8,128)S(1)}, u32[]{:S(2)}, u32[]{:S(2)}) collective-permute-start(f32[80,1024]{1,0:T(8,128)S(1)} %get-tuple-element.32), channel_id=1, source_target_pairs={{0,30},{2,4},{4,2},{6,8},{8,6},{10,12},{12,10},{14,16},{16,14},{18... | collective-permute-start | bytes 983048 | tf_op jit(solution)/shard_map/ppermute | solution.py:634
  35.4 6.2 %collective-permute-start.7 = (f32[1,80,512]{2,1,0:T(8,128)S(1)}, f32[1,80,512]{2,1,0:T(8,128)S(1)}, u32[]{:S(2)}, u32[]{:S(2)}) collective-permute-start(f32[1,80,512]{2,1,0:T(8,128)S(1)} %get-tuple-element.33), channel_id=1, source_target_pairs={{0,1},{1,0},{2,3},{3,2},{4,5},{5,4},{6,7},{7,6},{8,9},{9,8},{10,11... | collective-permute-start | bytes 491528 | tf_op jit(solution)/shard_map/ppermute | solution.py:648
  36.9 8.3 %collective-permute-start.8 = (f32[1,80,128]{2,1,0:T(8,128)S(1)}, f32[1,80,128]{2,1,0:T(8,128)S(1)}, u32[]{:S(2)}, u32[]{:S(2)}) collective-permute-start(f32[1,80,128]{2,1,0:T(8,128)S(1)} %get-tuple-element.34), channel_id=1, source_target_pairs={{0,31},{1,30},{2,5},{3,4},{4,3},{5,2},{6,9},{7,8},{8,7},{9,6},{10,... | collective-permute-start | bytes 122888 | tf_op jit(solution)/shard_map/ppermute | solution.py:648
  36.9 4.3 %collective-permute-start.9 = (f32[1,80,128]{2,1,0:T(8,128)S(1)}, f32[1,80,128]{2,1,0:T(8,128)S(1)}, u32[]{:S(2)}, u32[]{:S(2)}) collective-permute-start(f32[1,80,128]{2,1,0:T(8,128)S(1)} %get-tuple-element.35), channel_id=1, source_target_pairs={{0,3},{1,2},{2,1},{3,0},{4,7},{5,6},{6,5},{7,4},{8,11},{9,10},{10,... | collective-permute-start | bytes 122888 | tf_op jit(solution)/shard_map/ppermute | solution.py:648
  37.7 7.5 %copy-start.9 = (f32[88,2048]{1,0:T(8,128)S(1)}, f32[88,2048]{1,0:T(8,128)}, u32[]{:S(2)}) copy-start(f32[88,2048]{1,0:T(8,128)} %copy-done.8) | copy-start | bytes 2162692
  37.7 7.5 %copy-start.11 = (f32[1,88,512]{2,1,0:T(8,128)S(1)}, f32[1,88,512]{2,1,0:T(8,128)}, u32[]{:S(2)}) copy-start(f32[1,88,512]{2,1,0:T(8,128)} %copy-done.10) | copy-start | bytes 540676
  41.6 10.6 %collective-permute-start.10 = (f32[80,1024]{1,0:T(8,128)S(1)}, f32[80,1024]{1,0:T(8,128)S(1)}, u32[]{:S(2)}, u32[]{:S(2)}) collective-permute-start(f32[80,1024]{1,0:T(8,128)S(1)} %shard_map.156), channel_id=1, source_target_pairs={{0,30},{2,4},{4,2},{6,8},{8,6},{10,12},{12,10},{14,16},{16,14},{18... | collective-permute-start | bytes 983048 | tf_op jit(solution)/shard_map/ppermute | solution.py:634
  48.8 10.4 %all-to-all-start.1 = ((f32[16,8,128]{2,1,0:T(8,128)}), f32[16,8,128]{2,1,0:T(8,128)S(1)}, u32[]{:S(2)}, u32[]{:S(2)}) async-start(f32[16,8,128]{2,1,0:T(8,128)} %get-tuple-element.41), calls=%async_computation.1 | async-start | bytes 131072 | tf_op jit(solution)/shard_map/all_to_all | solution.py:715
  (5 other events, 6.3 us)

commit v10 on v9

--- a/solution.py
+++ b/solution.py
@@ -37,7 +37,7 @@
         assert self.ct == 2 and self.nax == LANES and SWEEPS % DEPTH == 0 and spans > 1
         assert len(set(self.shift)) == self.insts and self.cells * WINDOW == LANES and self.rows >= SWEEPS
         assert self.slab % CHUNK == 0 and 3 * self.pad <= 256 and 2 * self.ct * self.width == LANES
-        assert sectors % 2 == 0
+        assert sectors % 2 == 0 and self.pad - self.tf == 3
         self.ends = 1 if spans == 2 else 2
         self.blocks = [-1, 0, 1]
         self.halves = [0, 1] if spans == 2 else [-1, 0, 1]
@@ -176,6 +176,8 @@
         self.rates = rates or (ref, start)
 
     def rate(self, which, r, count=1):
+        if isinstance(self.rates, Layer):
+            return self.rates.rate(which, r, count)
         ref, start = self.rates
         row = self.plan.pad + which
         return ref[row : row + 1, at(r, count, start)]
@@ -191,6 +193,18 @@
         if self.seam is None:
             return self.ref[: self.plan.pad, at(c * count, count, self.start)]
         return jnp.concatenate([self.row(c * count + part) for part in range(count)], axis=1)
+
+
+class Packed(Layer):
+    def rate(self, which, r, count=1):
+        where = {C_AZ: (0, 0), C_SP: (1, 0), C_UP: (2, 0), C_DOWN: (2, 0), C_TIME: (0, 1), C_MASK: (1, 1)}
+        row, layer = where[which] if self.layer == 0 else (2, 1)
+        row += self.plan.tf
+        value = self.ref[row : row + 1, at(r, count, layer * self.plan.slab)]
+        if which in (C_UP, C_DOWN):
+            end = LANES - 1 if which == C_UP else 0
+            value = jnp.where(lane_index(1) == end, 0.0, value)
+        return value
 
 
 def placed(tile, cell):
@@ -369,27 +383,36 @@
     return corner
 
 
-def prepare(plan, rhs_ref, coef_ref, m_ref, side_ref, c0_ref, c1_ref, rates_ref):
+def prepare(plan, rhs_ref, coef_ref, m_ref, out_ref, side_ref, c0_ref, c1_ref, rates_ref):
     pad, cells = plan.pad, plan.cells
-    mask, diag, time, *face = [coef_ref[cells * i : cells * (i + 1), :] for i in range(6)]
+    mask, diag, time, *face = [coef_ref[i] for i in range(6)]
     scale = mask / diag
     lane = lane_index(cells)
     axial = scale * face[2]
     rates = (
         scale * time, scale * face[0], scale * face[1],
-        jnp.where(lane < LANES - 1, axial, 0.0), jnp.where(lane > 0, axial, 0.0), scale,
+        jnp.where(lane < LANES - 1, axial, 0.0), jnp.where(lane > 0, axial, 0.0), scale, axial,
     )
     for i, rate in enumerate(rates):
         rates_ref[i] = rate
-    tail = jnp.zeros((pad - plan.tf, LANES), jnp.float32)
     rest = jnp.zeros((RATES - 6, LANES), jnp.float32)
     mirror = parity()
+
+    def rate(i, a, r):
+        return rates_ref[i, pl.ds(jnp.where(mirror == 0, a, plan.ct - 1 - a) * plan.rows + r, 1), :]
+
     for cell in range(cells):
         a, r = divmod(cell, plan.rows)
         there = jnp.where(mirror == 0, a, plan.ct - 1 - a) * plan.rows + r
-        table = [rates_ref[i, pl.ds(there, 1), :] for i in range(6)]
-        field = jnp.concatenate([rhs_ref[pl.ds(there, plan.tf, stride=cells), :], tail], axis=0)
-        m_ref[:pad, at(cell)] = field * table[C_MASK]
+        table = [rate(i, a, r) for i in range(6)]
+        if a == 0:
+            spare = [table[C_AZ], table[C_SP], rate(6, 0, r)]
+        else:
+            spare = [rate(C_TIME, 0, r), rate(C_MASK, 0, r), table[C_MASK]]
+        field = rhs_ref[pl.ds(there, plan.tf, stride=cells), :] * table[C_MASK]
+        field = jnp.concatenate([field] + spare, axis=0)
+        m_ref[:pad, at(cell)] = field
+        out_ref[:, at(cell)] = field
         m_ref[pad:, at(cell)] = jnp.concatenate(table + [rest], axis=0)
     write_edges(plan, m_ref, side_ref, (c0_ref, c1_ref))
 
@@ -506,7 +529,7 @@
     x_ref, near_ref, side_out, c0_ref, c1_ref, p0_ref, p1_ref, y_ref, h0_ref, h1_ref, n0_ref, n1_ref, inlet_ref,
 ):
     own = two_layers(plan, f_ref, m_ref)
-    low = two_layers(plan, low_ref, seam=seams_ref[0, 0])
+    low = [Packed(plan, low_ref, a * plan.slab, None, seams_ref[0, 0], a) for a in range(plan.ct)]
     high = two_layers(plan, high_ref, seam=seams_ref[2, 0])
     near = low[0], high[1]
     n_refs = n0_ref, n1_ref
@@ -547,9 +570,9 @@
 ):
     pad = plan.pad
     own, force = two_layers(plan, x_ref, m_ref), two_layers(plan, f_ref, m_ref)
-    low_force = Layer(plan, low_first, 0, None, seams_ref[0, 0], 0)
+    low_force = Packed(plan, low_first, 0, None, seams_ref[0, 0], 0)
     high_force = Layer(plan, high_first, plan.slab, None, seams_ref[2, 0], 1)
-    near = Layer(plan, low_ref, 0, low_force.rates), Layer(plan, high_ref, plan.slab, high_force.rates)
+    near = Layer(plan, low_ref, 0, low_force), Layer(plan, high_ref, plan.slab, high_force.rates)
     n_refs = n0_ref, n1_ref
     middle_rows(
         plan, w_ref, (p0_ref, p1_ref), own, force, g_ref, near, (low_force, high_force),
@@ -671,16 +694,14 @@
         ], axis=1),
     )
     got = lax.all_to_all(sent, AXES, 0, 0, tiled=True)
-    m, side, c0, c1 = call(
-        bind(prepare, plan), (f32(pad + RATES, plan.ct * slab),) + edges(pad + RATES), (vmem(6, cells, LANES),)
-    )(
-        rhs.reshape(plan.tf * cells, LANES),
-        jnp.concatenate([
-            wall_mask.astype(jnp.float32).reshape(cells, LANES), diag_coef.reshape(cells, LANES),
-            time_coef.reshape(cells, LANES), face_coef.reshape(3 * cells, LANES),
-        ]),
-    )
-    low_first, high_first = swap(m, next_chip), swap(m, next_core)
+    which = lax.broadcasted_iota(jnp.int32, (6, cells, LANES), 0)
+    coefs = jnp.pad(face_coef.reshape(3, cells, LANES), ((3, 0), (0, 0), (0, 0)))
+    for i, value in enumerate((wall_mask.astype(jnp.float32), diag_coef, time_coef)):
+        coefs = jnp.where(which == i, value.reshape(1, cells, LANES), coefs)
+    m, to_next, side, c0, c1 = call(
+        bind(prepare, plan), (f32(pad + RATES, plan.ct * slab), whole) + edges(pad + RATES), (vmem(7, cells, LANES),)
+    )(rhs.reshape(plan.tf * cells, LANES), coefs)
+    low_first, high_first = swap(to_next, next_chip), swap(m, next_core)
     side_first = beside(plan, side, alone)
     c_low, c_high = beside(plan, c0, next_chip), beside(plan, c1, next_core)
     matrices, down = call(

time: 60.4 us -> 61.8 us (1.023)
  Pallas kernels: 13.6 us -> 16.4 us
  waiting for transfers between devices: 15.1 us -> 13.6 us
    all_to_all x1, waiting for transfers between devices: 5.64 us -> 4.17 us  [on_device(): got = lax.all_to_all(sent, AXES, 0, 0, tiled=True)]
    pallas_call x1, Pallas kernels: 3.04 us -> 4.22 us  [on_device(): call(bind(first_half, plan), (whole, half) + edges(pad), products + (vmem...]
    pallas_call x1, Pallas kernels: 3.6 us -> 4.53 us  [on_device(): call(bind(middle, plan), (f32(sectors, RATES, LANES), half, half, half, f...]
    select_n x0 -> x1, other arithmetic: none -> 0.8 us  [on_device(): coefs = jnp.where(which == i, value.reshape(1, cells, LANES), coefs)]
    concatenate x1 -> x0, other arithmetic: 0.74 us -> none  [on_device(): jnp.concatenate([wall_mask.astype(jnp.float32).reshape(cells, LANES), dia...]
    pallas_call x1, Pallas kernels: 0.28 us -> 0.99 us  [on_device(): call(bind(prepare, plan), (f32(pad + RATES, plan.ct * slab), whole) + edg...]
    reshape x1 -> x0, other arithmetic: 0.71 us -> none  [on_device(): wall_mask.astype(jnp.float32).reshape(cells, LANES)]
    broadcast_in_dim x0 -> x1, other arithmetic: none -> 0.7 us  [on_device(): coefs = jnp.where(which == i, value.reshape(1, cells, LANES), coefs)]
  transfers between devices with their start and end apart: 13 -> 13, of which waited for: 4 -> 4; matrix products, arithmetic and copies ran while one was open for 0% -> 0% of each run, Pallas kernels for 16% -> 17%
where the time goes in v10:
time: 61.8 us; the launch traced here: 61.3 us
  starting transfers between devices  26.8 us (43%)
  Pallas kernels  16.4 us (27%)
  waiting for transfers between devices  13.6 us (22%)
  local copies, waits for them, and re-layouts  1.97 us (3%)
  other arithmetic  1.59 us (3%)
  between operations  0.87 us (1%)
    ppermute x5, starting transfers between devices, swap(): return lax.ppermute(array, 'sector', list(enumerate(partner)))  13.6 us
    ppermute x6, starting transfers between devices, beside(): return lax.ppermute(array, AXES, pairs(0))  7.05 us
    all_to_all x1, waiting for transfers between devices, on_device(): returned = lax.all_to_all(back, 'sector', 0, 0, tiled=True)  5.54 us
    pallas_call x1, Pallas kernels, on_device(): call(bind(middle, plan), (f32(sectors, RATES, LANES), half, half, half, f...  4.53 us
    pallas_call x1, Pallas kernels, on_device(): call(bind(first_half, plan), (whole, half) + edges(pad), products + (vmem...  4.22 us
    all_to_all x1, waiting for transfers between devices, on_device(): got = lax.all_to_all(sent, AXES, 0, 0, tiled=True)  4.17 us
    ppermute x6, waiting for transfers between devices, beside(): return lax.ppermute(array, AXES, pairs(0))  3.89 us
    all_to_all x1, starting transfers between devices, on_device(): returned = lax.all_to_all(back, 'sector', 0, 0, tiled=True)  3.5 us
  transfers between devices with their start and end apart: 13, of which 4 were waited for; matrix products, arithmetic and copies ran while one was open for 0% of the time, Pallas kernels for 17%

profile of v10, /device:TPU:0, one launch (start us, length us, event | category | flops | bytes accessed | tf_op | source)
XLA Modules:
  0.0 61.3 jit_solution(11152816904413229386)
XLA Ops:
  0.7 0.7 %convert_bitcast_fusion = f32[16,128]{1,0:T(8,128)S(1)} fusion(s32[2,8,128]{2,1,0:T(8,128)} %param.20), kind=kLoop, calls=%fused_computation.7 | loop fusion | flops 2048 | bytes 16384 | tf_op jit(solution)/shard_map/jit(_where)/broadcast_in_dim | solution.py:700
  1.4 0.8 %select_select_fusion.coef_ref = f32[6,16,128]{2,1,0:T(8,128)S(1)} fusion(f32[3,16,128]{2,1,0:T(8,128)S(1)} %bitcast.20, f32[16,128]{1,0:T(8,128)S(1)} %convert_bitcast_fusion, f32[16,128]{1,0:T(8,128)} %bitcast.21, f32[16,128]{1,0:T(8,128)} %bitcast.22, pred[6]{0:T(512)(128)(4,1)S(1)} %get-tuple-element.44, pred[6]{0:T(512)(128)(4,1)S(1)} %get-tuple-element.45, ...), kind=kLoop, calls=%fused_computation | loop fusion | flops 36864 | bytes 98322 | tf_op jit(solution)/shard_map/jit(_where)/select_n | solution.py:700
  2.2 1.1 %copy-done = f32[11,7,2,8,128]{4,3,2,1,0:T(8,128)S(1)} copy-done((f32[11,7,2,8,128]{4,3,2,1,0:T(8,128)S(1)}, f32[11,7,2,8,128]{4,3,2,1,0:T(8,128)}, u32[]{:S(2)}) %copy-start) | copy-done | bytes 630808
  3.3 1.0 %shard_map.150 = (f32[88,2048]{1,0:T(8,128)S(1)}, f32[80,2048]{1,0:T(8,128)S(1)}, f32[1,88,512]{2,1,0:T(8,128)}, f32[1,88,128]{2,1,0:T(8,128)S(1)}, f32[1,88,128]{2,1,0:T(8,128)S(1)}) custom-call(f32[1232,128]{1,0:T(8,128)S(1)} %bitcast.16, f32[6,16,128]{2,1,0:T(8,128)S(1)} %select_select_fusion.coef_ref), custom_call_target="tpu_custom_call" | custom-call | flops 2000000 | bytes 1000000 | tf_op jit(solution)/shard_map/pallas_call | solution.py:701
  4.3 5.4 %collective-permute-start = (f32[80,2048]{1,0:T(8,128)S(1)}, f32[80,2048]{1,0:T(8,128)S(1)}, u32[]{:S(2)}, u32[]{:S(2)}) collective-permute-start(f32[80,2048]{1,0:T(8,128)S(1)} %get-tuple-element.28), channel_id=1, source_target_pairs={{0,30},{2,4},{4,2},{6,8},{8,6},{10,12},{12,10},{14,16},{16,14},{18... | collective-permute-start | bytes 1966088 | tf_op jit(solution)/shard_map/ppermute | solution.py:657
  9.7 0.7 %copy-done.12 = f32[11,2,8]{0,2,1:T(8,128)S(1)} copy-done((f32[11,2,8]{0,2,1:T(8,128)S(1)}, f32[11,2,8]{0,2,1:T(8,128)}, u32[]{:S(2)}) %copy-start.12) | copy-done | bytes 728
  10.6 0.9 %shard_map.151 = f32[32,8,128]{2,1,0:T(8,128)} custom-call(f32[7,32,11]{2,1,0:T(8,128)S(1)} %bitcast.17, f32[11,32]{1,0:T(8,128)S(1)} %pad_maximum_fusion.both_ref), custom_call_target="tpu_custom_call" | custom-call | flops 2000000 | bytes 1000000 | tf_op jit(solution)/shard_map/pallas_call | solution.py:690
  11.5 2.7 %all-to-all-start = ((f32[32,8,128]{2,1,0:T(8,128)}), f32[32,8,128]{2,1,0:T(8,128)S(1)}, u32[]{:S(2)}, u32[]{:S(2)}) async-start(f32[32,8,128]{2,1,0:T(8,128)} %shard_map.151), calls=%async_computation | async-start | bytes 262144 | tf_op jit(solution)/shard_map/all_to_all | solution.py:696
  14.3 1.7 %collective-permute-start.2 = (f32[1,88,512]{2,1,0:T(8,128)}, f32[1,88,512]{2,1,0:T(8,128)}, u32[]{:S(2)}, u32[]{:S(2)}) collective-permute-start(f32[1,88,512]{2,1,0:T(8,128)} %get-tuple-element.29), channel_id=1, source_target_pairs={{0,1},{1,0},{2,3},{3,2},{4,5},{5,4},{6,7},{7,6},{8,9},{9,8},{10,11... | collective-permute-start | bytes 540680 | tf_op jit(solution)/shard_map/ppermute | solution.py:671
  16.0 3.9 %collective-permute-start.3 = (f32[1,88,128]{2,1,0:T(8,128)S(1)}, f32[1,88,128]{2,1,0:T(8,128)}, u32[]{:S(2)}, u32[]{:S(2)}) collective-permute-start(f32[1,88,128]{2,1,0:T(8,128)S(1)} %get-tuple-element.30), channel_id=1, source_target_pairs={{0,31},{1,30},{2,5},{3,4},{4,3},{5,2},{6,9},{7,8},{8,7},{9,6},{10,... | collective-permute-start | bytes 135176 | tf_op jit(solution)/shard_map/ppermute | solution.py:671
  19.9 1.1 %shard_map.149 = (bf16[560,240]{1,0:T(8,128)(2,1)S(1)}, bf16[80,240]{1,0:T(8,128)(2,1)S(1)}) custom-call(f32[3,7,7]{2,1,0:T(8,128)S(1)} %copy-done.5, f32[3,7,7]{2,1,0:T(8,128)S(1)} %copy-done.6, bf16[80,240]{1,0:T(8,128)(2,1)S(1)} %copy-done.3, f32[80,7]{1,0:T(8,128)S(1)} %copy-done.4, f32[7,240]{1,0:T(8,128)S(1)} %copy-done.7, f32[80,240]{1,0:T(8,128)S(1)} %copy-done.2), custom_call_target="tpu_custom_call" | custom-call | flops 2000000 | bytes 1000000 | tf_op jit(solution)/shard_map/pallas_call | solution.py:707
  21.0 4.2 %all-to-all-done.got_ref = f32[32,8,128]{2,1,0:T(8,128)S(1)} async-done(((f32[32,8,128]{2,1,0:T(8,128)}), f32[32,8,128]{2,1,0:T(8,128)S(1)}, u32[]{:S(2)}, u32[]{:S(2)}) %all-to-all-start) | async-done | bytes 131104 | tf_op jit(solution)/shard_map/all_to_all | solution.py:696
  25.2 1.7 %shard_map.152 = (f32[3,2,80,128]{3,2,1,0:T(8,128)S(1)}, f32[80,128]{1,0:T(8,128)S(1)}, f32[80,2048]{1,0:T(8,128)S(1)}, f32[80,2048]{1,0:T(8,128)S(1)}) custom-call(bf16[560,240]{1,0:T(8,128)(2,1)S(1)} %get-tuple-element.24.w_ref, f32[88,2048]{1,0:T(8,128)S(1)} %get-tuple-element.25.m_ref, f32[32,8,128]{2,1,0:T(8,128)S(1)} %all-to-all-done.got_ref), custom_call_target="tpu_custom_call" | custom-call | flops 2000000000 | bytes 1000000 | tf_op jit(solution)/shard_map/pallas_call | solution.py:712
  27.0 4.2 %shard_map.153 = (f32[80,2048]{1,0:T(8,128)S(1)}, f32[80,1024]{1,0:T(8,128)S(1)}, f32[1,80,512]{2,1,0:T(8,128)S(1)}, f32[1,80,128]{2,1,0:T(8,128)S(1)}, f32[1,80,128]{2,1,0:T(8,128)S(1)}) custom-call(bf16[560,240]{1,0:T(8,128)(2,1)S(1)} %get-tuple-element.24.w_ref, f32[88,2048]{1,0:T(8,128)S(1)} %get-tuple-element.25.m_ref, ...), custom_call_target="tpu_custom_call" | custom-call | flops 4000000000 | bytes 1000000 | tf_op jit(solution)/shard_map/pallas_call | solution.py:717
  31.2 4.6 %collective-permute-start.5 = (f32[80,1024]{1,0:T(8,128)S(1)}, f32[80,1024]{1,0:T(8,128)S(1)}, u32[]{:S(2)}, u32[]{:S(2)}) collective-permute-start(f32[80,1024]{1,0:T(8,128)S(1)} %get-tuple-element.34), channel_id=1, source_target_pairs={{0,30},{2,4},{4,2},{6,8},{8,6},{10,12},{12,10},{14,16},{16,14},{18... | collective-permute-start | bytes 983048 | tf_op jit(solution)/shard_map/ppermute | solution.py:657
  35.8 1.5 %collective-permute-start.7 = (f32[1,80,512]{2,1,0:T(8,128)S(1)}, f32[1,80,512]{2,1,0:T(8,128)S(1)}, u32[]{:S(2)}, u32[]{:S(2)}) collective-permute-start(f32[1,80,512]{2,1,0:T(8,128)S(1)} %get-tuple-element.35), channel_id=1, source_target_pairs={{0,1},{1,0},{2,3},{3,2},{4,5},{5,4},{6,7},{7,6},{8,9},{9,8},{10,11... | collective-permute-start | bytes 491528 | tf_op jit(solution)/shard_map/ppermute | solution.py:671
  37.3 0.8 %shard_map.154.g_ref = f32[80,2048]{1,0:T(8,128)S(1)} custom-call(bf16[560,240]{1,0:T(8,128)(2,1)S(1)} %get-tuple-element.24.w_ref, f32[88,2048]{1,0:T(8,128)S(1)} %get-tuple-element.25.m_ref, f32[80,2048]{1,0:T(8,128)S(1)} %get-tuple-element.26.f_ref, f32[80,2048]{1,0:T(8,128)S(1)} %get-tuple-element.33.x_ref), custom_call_target="tpu_custom_call" | custom-call | flops 2000000000 | bytes 1000000 | tf_op jit(solution)/shard_map/pallas_call | solution.py:726
  38.1 3.5 %collective-permute-done.9.c_high = f32[1,80,128]{2,1,0:T(8,128)S(1)} collective-permute-done((f32[1,80,128]{2,1,0:T(8,128)S(1)}, f32[1,80,128]{2,1,0:T(8,128)S(1)}, u32[]{:S(2)}, u32[]{:S(2)}) %collective-permute-start.9) | collective-permute-done | bytes 40992 | tf_op jit(solution)/shard_map/ppermute | solution.py:671
  42.1 3.5 %collective-permute-start.10 = (f32[80,1024]{1,0:T(8,128)S(1)}, f32[80,1024]{1,0:T(8,128)S(1)}, u32[]{:S(2)}, u32[]{:S(2)}) collective-permute-start(f32[80,1024]{1,0:T(8,128)S(1)} %shard_map.156), channel_id=1, source_target_pairs={{0,30},{2,4},{4,2},{6,8},{8,6},{10,12},{12,10},{14,16},{16,14},{18... | collective-permute-start | bytes 983048 | tf_op jit(solution)/shard_map/ppermute | solution.py:657
  45.6 4.5 %shard_map.155 = (f32[16,8,128]{2,1,0:T(8,128)}, f32[80,1024]{1,0:T(8,128)S(1)}, f32[80,1024]{1,0:T(8,128)S(1)}, f32[80,1024]{1,0:T(8,128)S(1)}, f32[8,1024]{1,0:T(8,128)S(1)}) custom-call(bf16[560,240]{1,0:T(8,128)(2,1)S(1)} %get-tuple-element.24.w_ref, f32[88,2048]{1,0:T(8,128)S(1)} %get-tuple-element.25.m_ref, f32[80,2048]{1,0:T(8,128)S(1)} %get-tuple-element.26.f_ref, ...), custom_call_target="tpu_custom_call" | custom-call | flops 4000000000 | bytes 1000000 | tf_op jit(solution)/shard_map/pallas_call | solution.py:729
  50.1 3.5 %all-to-all-start.1 = ((f32[16,8,128]{2,1,0:T(8,128)}), f32[16,8,128]{2,1,0:T(8,128)S(1)}, u32[]{:S(2)}, u32[]{:S(2)}) async-start(f32[16,8,128]{2,1,0:T(8,128)} %get-tuple-element.43), calls=%async_computation.1 | async-start | bytes 131072 | tf_op jit(solution)/shard_map/all_to_all | solution.py:736
  53.7 1.3 %shard_map.157 = f32[1232,128]{1,0:T(8,128)} custom-call(bf16[80,240]{1,0:T(8,128)(2,1)S(1)} %get-tuple-element.23.w_ref, f32[8,1024]{1,0:T(8,128)S(1)} %get-tuple-element.39.rates_ref, f32[80,1024]{1,0:T(8,128)S(1)} %get-tuple-element.40.n0_ref, f32[80,1024]{1,0:T(8,128)S(1)} %get-tuple-element.41.h0_ref, f32[80,1024]{1,0:T(8,128)S(1)} %get-tuple-element.42.x1_ref, ...), custom_call_target="tpu_custom_call" | custom-call | flops 2000000 | bytes 1000000 | tf_op jit(solution)/shard_map/pallas_call | solution.py:738
  55.0 5.5 %all-to-all-done.1.got_ref = f32[16,8,128]{2,1,0:T(8,128)S(1)} async-done(((f32[16,8,128]{2,1,0:T(8,128)}), f32[16,8,128]{2,1,0:T(8,128)S(1)}, u32[]{:S(2)}, u32[]{:S(2)}) %all-to-all-start.1) | async-done | bytes 65568 | tf_op jit(solution)/shard_map/all_to_all | solution.py:736
  60.5 0.8 %shard_map.158 = f32[7,32,11]{2,1,0:T(8,128)} custom-call(f32[16,8,128]{2,1,0:T(8,128)S(1)} %all-to-all-done.1.got_ref), custom_call_target="tpu_custom_call" | custom-call | flops 2000000 | bytes 1000000 | tf_op jit(solution)/shard_map/pallas_call | solution.py:737
  (46 shorter events, 0.9 us)
Async XLA Ops:
  2.2 1.1 %copy-start = (f32[11,7,2,8,128]{4,3,2,1,0:T(8,128)S(1)}, f32[11,7,2,8,128]{4,3,2,1,0:T(8,128)}, u32[]{:S(2)}) copy-start(f32[11,7,2,8,128]{4,3,2,1,0:T(8,128)} %param.14) | copy-start | bytes 1892356
  3.3 6.4 %copy-start.11 = (s32[11,2,8]{0,2,1:T(8,128)S(1)}, s32[11,2,8]{0,2,1:T(8,128)}, u32[]{:S(2)}) copy-start(s32[11,2,8]{0,2,1:T(8,128)} %param.22) | copy-start | bytes 2116
  3.3 7.4 %copy-start.1 = (f32[11,7,4,8]{0,3,2,1:T(8,128)S(1)}, f32[11,7,4,8]{0,3,2,1:T(8,128)}, u32[]{:S(2)}) copy-start(f32[11,7,4,8]{0,3,2,1:T(8,128)} %param.21) | copy-start | bytes 29572
  4.3 22.7 %collective-permute-start = (f32[80,2048]{1,0:T(8,128)S(1)}, f32[80,2048]{1,0:T(8,128)S(1)}, u32[]{:S(2)}, u32[]{:S(2)}) collective-permute-start(f32[80,2048]{1,0:T(8,128)S(1)} %get-tuple-element.28), channel_id=1, source_target_pairs={{0,30},{2,4},{4,2},{6,8},{8,6},{10,12},{12,10},{14,16},{16,14},{18... | collective-permute-start | bytes 1966088 | tf_op jit(solution)/shard_map/ppermute | solution.py:657
  9.7 17.3 %collective-permute-start.1 = (f32[88,2048]{1,0:T(8,128)S(1)}, f32[88,2048]{1,0:T(8,128)S(1)}, u32[]{:S(2)}, u32[]{:S(2)}) collective-permute-start(f32[88,2048]{1,0:T(8,128)S(1)} %get-tuple-element.25.m_ref), channel_id=1, source_target_pairs={{0,2},{2,0},{4,6},{6,4},{8,10},{10,8},{12,14},{14,12},{16,18},{18,... | collective-permute-start | bytes 2162696 | tf_op jit(solution)/shard_map/ppermute | solution.py:657
  11.5 8.3 %copy-start.2 = (f32[80,240]{1,0:T(8,128)S(1)}, f32[80,240]{1,0:T(8,128)}, u32[]{:S(2)}) copy-start(f32[80,240]{1,0:T(8,128)} %constant.24.clone.diagonal_ref) | copy-start | bytes 230404
  11.5 8.3 %copy-start.3 = (bf16[80,240]{1,0:T(8,128)(2,1)S(1)}, bf16[80,240]{1,0:T(8,128)(2,1)}, u32[]{:S(2)}) copy-start(bf16[80,240]{1,0:T(8,128)(2,1)} %constant.21.clone.spectral_ref) | copy-start | bytes 115204
  11.5 8.3 %copy-start.4 = (f32[80,7]{1,0:T(8,128)S(1)}, f32[80,7]{1,0:T(8,128)}, u32[]{:S(2)}) copy-start(f32[80,7]{1,0:T(8,128)} %constant.22.clone.rows_ref) | copy-start | bytes 6724
  11.5 8.3 %copy-start.5 = (f32[3,7,7]{2,1,0:T(8,128)S(1)}, f32[3,7,7]{2,1,0:T(8,128)}, u32[]{:S(2)}) copy-start(f32[3,7,7]{2,1,0:T(8,128)} %up_ref.1) | copy-start | bytes 1768
  11.5 8.3 %copy-start.6 = (f32[3,7,7]{2,1,0:T(8,128)S(1)}, f32[3,7,7]{2,1,0:T(8,128)}, u32[]{:S(2)}) copy-start(f32[3,7,7]{2,1,0:T(8,128)} %down_ref.1) | copy-start | bytes 1768
  11.5 8.3 %copy-start.7 = (f32[7,240]{1,0:T(8,128)S(1)}, f32[7,240]{1,0:T(8,128)}, u32[]{:S(2)}) copy-start(f32[7,240]{1,0:T(8,128)} %constant.23.clone.lanes_ref) | copy-start | bytes 20164
  11.5 13.6 %all-to-all-start = ((f32[32,8,128]{2,1,0:T(8,128)}), f32[32,8,128]{2,1,0:T(8,128)S(1)}, u32[]{:S(2)}, u32[]{:S(2)}) async-start(f32[32,8,128]{2,1,0:T(8,128)} %shard_map.151), calls=%async_computation | async-start | bytes 262144 | tf_op jit(solution)/shard_map/all_to_all | solution.py:696
  14.3 12.7 %collective-permute-start.2 = (f32[1,88,512]{2,1,0:T(8,128)}, f32[1,88,512]{2,1,0:T(8,128)}, u32[]{:S(2)}, u32[]{:S(2)}) collective-permute-start(f32[1,88,512]{2,1,0:T(8,128)} %get-tuple-element.29), channel_id=1, source_target_pairs={{0,1},{1,0},{2,3},{3,2},{4,5},{5,4},{6,7},{7,6},{8,9},{9,8},{10,11... | collective-permute-start | bytes 540680 | tf_op jit(solution)/shard_map/ppermute | solution.py:671
  16.0 10.9 %collective-permute-start.3 = (f32[1,88,128]{2,1,0:T(8,128)S(1)}, f32[1,88,128]{2,1,0:T(8,128)}, u32[]{:S(2)}, u32[]{:S(2)}) collective-permute-start(f32[1,88,128]{2,1,0:T(8,128)S(1)} %get-tuple-element.30), channel_id=1, source_target_pairs={{0,31},{1,30},{2,5},{3,4},{4,3},{5,2},{6,9},{7,8},{8,7},{9,6},{10,... | collective-permute-start | bytes 135176 | tf_op jit(solution)/shard_map/ppermute | solution.py:671
  19.8 7.1 %collective-permute-start.4 = (f32[1,88,128]{2,1,0:T(8,128)S(1)}, f32[1,88,128]{2,1,0:T(8,128)}, u32[]{:S(2)}, u32[]{:S(2)}) collective-permute-start(f32[1,88,128]{2,1,0:T(8,128)S(1)} %get-tuple-element.31), channel_id=1, source_target_pairs={{0,3},{1,2},{2,1},{3,0},{4,7},{5,6},{6,5},{7,4},{8,11},{9,10},{10,... | collective-permute-start | bytes 135176 | tf_op jit(solution)/shard_map/ppermute | solution.py:671
  26.9 4.2 %copy-start.8 = (f32[80,2048]{1,0:T(8,128)}, f32[80,2048]{1,0:T(8,128)S(1)}, u32[]{:S(2)}) copy-start(f32[80,2048]{1,0:T(8,128)S(1)} %collective-permute-done.low_ref.low_first) | copy-start | bytes 1966084
  31.2 14.4 %collective-permute-start.6 = (f32[80,2048]{1,0:T(8,128)S(1)}, f32[80,2048]{1,0:T(8,128)S(1)}, u32[]{:S(2)}, u32[]{:S(2)}) collective-permute-start(f32[80,2048]{1,0:T(8,128)S(1)} %get-tuple-element.33.x_ref), channel_id=1, source_target_pairs={{0,2},{2,0},{4,6},{6,4},{8,10},{10,8},{12,14},{14,12},{16,18},{18,... | collective-permute-start | bytes 1966088 | tf_op jit(solution)/shard_map/ppermute | solution.py:657
  31.2 14.4 %collective-permute-start.5 = (f32[80,1024]{1,0:T(8,128)S(1)}, f32[80,1024]{1,0:T(8,128)S(1)}, u32[]{:S(2)}, u32[]{:S(2)}) collective-permute-start(f32[80,1024]{1,0:T(8,128)S(1)} %get-tuple-element.34), channel_id=1, source_target_pairs={{0,30},{2,4},{4,2},{6,8},{8,6},{10,12},{12,10},{14,16},{16,14},{18... | collective-permute-start | bytes 983048 | tf_op jit(solution)/shard_map/ppermute | solution.py:657
  35.8 6.2 %collective-permute-start.7 = (f32[1,80,512]{2,1,0:T(8,128)S(1)}, f32[1,80,512]{2,1,0:T(8,128)S(1)}, u32[]{:S(2)}, u32[]{:S(2)}) collective-permute-start(f32[1,80,512]{2,1,0:T(8,128)S(1)} %get-tuple-element.35), channel_id=1, source_target_pairs={{0,1},{1,0},{2,3},{3,2},{4,5},{5,4},{6,7},{7,6},{8,9},{9,8},{10,11... | collective-permute-start | bytes 491528 | tf_op jit(solution)/shard_map/ppermute | solution.py:671
  37.3 8.3 %collective-permute-start.8 = (f32[1,80,128]{2,1,0:T(8,128)S(1)}, f32[1,80,128]{2,1,0:T(8,128)S(1)}, u32[]{:S(2)}, u32[]{:S(2)}) collective-permute-start(f32[1,80,128]{2,1,0:T(8,128)S(1)} %get-tuple-element.36), channel_id=1, source_target_pairs={{0,31},{1,30},{2,5},{3,4},{4,3},{5,2},{6,9},{7,8},{8,7},{9,6},{10,... | collective-permute-start | bytes 122888 | tf_op jit(solution)/shard_map/ppermute | solution.py:671
  37.3 4.3 %collective-permute-start.9 = (f32[1,80,128]{2,1,0:T(8,128)S(1)}, f32[1,80,128]{2,1,0:T(8,128)S(1)}, u32[]{:S(2)}, u32[]{:S(2)}) collective-permute-start(f32[1,80,128]{2,1,0:T(8,128)S(1)} %get-tuple-element.37), channel_id=1, source_target_pairs={{0,3},{1,2},{2,1},{3,0},{4,7},{5,6},{6,5},{7,4},{8,11},{9,10},{10,... | collective-permute-start | bytes 122888 | tf_op jit(solution)/shard_map/ppermute | solution.py:671
  38.1 7.5 %copy-start.9 = (f32[80,2048]{1,0:T(8,128)S(1)}, f32[80,2048]{1,0:T(8,128)}, u32[]{:S(2)}) copy-start(f32[80,2048]{1,0:T(8,128)} %copy-done.8) | copy-start | bytes 1966084
  42.1 11.6 %collective-permute-start.10 = (f32[80,1024]{1,0:T(8,128)S(1)}, f32[80,1024]{1,0:T(8,128)S(1)}, u32[]{:S(2)}, u32[]{:S(2)}) collective-permute-start(f32[80,1024]{1,0:T(8,128)S(1)} %shard_map.156), channel_id=1, source_target_pairs={{0,30},{2,4},{4,2},{6,8},{8,6},{10,12},{12,10},{14,16},{16,14},{18... | collective-permute-start | bytes 983048 | tf_op jit(solution)/shard_map/ppermute | solution.py:657
  50.1 10.4 %all-to-all-start.1 = ((f32[16,8,128]{2,1,0:T(8,128)}), f32[16,8,128]{2,1,0:T(8,128)S(1)}, u32[]{:S(2)}, u32[]{:S(2)}) async-start(f32[16,8,128]{2,1,0:T(8,128)} %get-tuple-element.43), calls=%async_computation.1 | async-start | bytes 131072 | tf_op jit(solution)/shard_map/all_to_all | solution.py:736
  (2 other events, 1.4 us)

commit v11 on v9

--- a/solution.py
+++ b/solution.py
@@ -10,6 +10,7 @@
 from jax.sharding import PartitionSpec as P
 
 SWEEPS = 4
+GROUP = 4
 DEPTH = 2
 LANES = 128
 CHUNK = 256
@@ -38,6 +39,8 @@
         assert len(set(self.shift)) == self.insts and self.cells * WINDOW == LANES and self.rows >= SWEEPS
         assert self.slab % CHUNK == 0 and 3 * self.pad <= 256 and 2 * self.ct * self.width == LANES
         assert sectors % 2 == 0
+        self.groups = sectors // GROUP
+        assert sectors % GROUP == 0 and self.groups & (self.groups - 1) == 0
         self.ends = 1 if spans == 2 else 2
         self.blocks = [-1, 0, 1]
         self.halves = [0, 1] if spans == 2 else [-1, 0, 1]
@@ -543,9 +546,11 @@
 def middle(
     plan, w_ref, m_ref, f_ref, x_ref, g_ref, low_ref, high_ref, side_ref, c_low, c_high,
     low_first, high_first, side_first, seams_ref, weight_ref,
-    send_ref, n0_ref, h0_ref, x1_ref, rates_ref, p0_ref, p1_ref, y_ref, h1_ref, n1_ref, turn_ref,
+    *refs,
 ):
     pad = plan.pad
+    send_refs = refs[: plan.groups]
+    n0_ref, h0_ref, x1_ref, rates_ref, p0_ref, p1_ref, y_ref, h1_ref, n1_ref, turn_ref, send_ref = refs[plan.groups :]
     own, force = two_layers(plan, x_ref, m_ref), two_layers(plan, f_ref, m_ref)
     low_force = Layer(plan, low_first, 0, None, seams_ref[0, 0], 0)
     high_force = Layer(plan, high_first, plan.slab, None, seams_ref[2, 0], 1)
@@ -592,7 +597,10 @@
     send_ref[...] = jnp.zeros_like(send_ref)
     for t in range(plan.insts):
         to = lax.rem(me + plan.shift[t], plan.sectors)
-        send_ref[to, : plan.fields, : plan.width] = back[t * plan.fields : (t + 1) * plan.fields, : plan.width]
+        place = (lax.div(to, GROUP) ^ lax.div(me, GROUP)) * GROUP + lax.rem(to, GROUP)
+        send_ref[place, : plan.fields, : plan.width] = back[t * plan.fields : (t + 1) * plan.fields, : plan.width]
+    for i, ref in enumerate(send_refs):
+        ref[...] = send_ref[i * GROUP : (i + 1) * GROUP]
 
 
 def outer(plan, w_ref, rates_ref, n0_ref, h0_ref, x1_ref, far_ref, out_ref):
@@ -612,11 +620,23 @@
     azimuthal(plan, w_ref, 0, near_chunk, lambda r, terms: put(0, r, h0_ref[:, at(r)] - rates_ref[1:2, at(r)] * terms))
 
 
-def collect_panels(plan, got_ref, out_ref, panels_ref):
+def turn_panels(plan, *refs):
+    place = lax.rem(lax.axis_index("sector"), GROUP)
+    for j, out_ref in enumerate(refs[plan.groups :]):
+        for i, ref in enumerate(refs[: plan.groups]):
+            out_ref[i] = ref[place ^ j]
+
+
+def collect_panels(plan, *refs):
+    out_ref, tiles_ref, panels_ref = refs[GROUP:]
+    for j, ref in enumerate(refs[:GROUP]):
+        tiles_ref[j * plan.groups : (j + 1) * plan.groups] = ref[...]
     me = lax.axis_index("sector")
     for t in range(plan.insts):
         source = lax.rem(me + (plan.sectors - plan.shift[t]), plan.sectors)
-        panels_ref[t * RATES : (t + 1) * RATES, :] = got_ref[source]
+        j = lax.rem(source, GROUP) ^ lax.rem(me, GROUP)
+        i = lax.div(source, GROUP) ^ lax.div(me, GROUP)
+        panels_ref[t * RATES : (t + 1) * RATES, :] = tiles_ref[j * plan.groups + i]
     for f in range(plan.fields):
         tile = panels_ref[pl.ds(f, plan.insts, stride=RATES), : plan.width]
         out_ref[f] = jnp.transpose(tile)
@@ -705,15 +725,25 @@
     (g,) = call(bind(inner, plan), (whole,), products, flops=2_000_000_000)(matrices, m, force, x)
     far = call(bind(hold_far, plan), half)(x, side, c_high)
     far_low = swap(far, next_chip)
-    back, n0, h0, x1, rates = call(
-        bind(middle, plan), (f32(sectors, RATES, LANES), half, half, half, f32(RATES, slab)),
-        products + (vmem(pad, 2 * slab), vmem(pad, slab), vmem(pad, slab), vmem(LANES, LANES)),
+    tiles = f32(GROUP, RATES, LANES)
+    *back, n0, h0, x1, rates = call(
+        bind(middle, plan), (tiles,) * plan.groups + (half, half, half, f32(RATES, slab)),
+        products + (
+            vmem(pad, 2 * slab), vmem(pad, slab), vmem(pad, slab), vmem(LANES, LANES), vmem(sectors, RATES, LANES),
+        ),
         flops=4_000_000_000,
     )(
         matrices, m, force, x, g, low, high, side, c_low, c_high, low_first, high_first, side_first, seams, weight
     )
-    returned = lax.all_to_all(back, "sector", 0, 0, tiled=True)
-    sens = call(bind(collect_panels, plan), f32(fields, plan.width, insts), (vmem(insts * RATES, LANES),))(returned)
+    for i in range(1, plan.groups):
+        back[i] = swap(back[i], [(s // GROUP ^ i) * GROUP + s % GROUP for s in range(sectors)])
+    back = list(call(bind(turn_panels, plan), (f32(plan.groups, RATES, LANES),) * GROUP)(*back))
+    for j in range(1, GROUP):
+        back[j] = swap(back[j], [s ^ j for s in range(sectors)])
+    sens = call(
+        bind(collect_panels, plan), f32(fields, plan.width, insts),
+        (vmem(sectors, RATES, LANES), vmem(insts * RATES, LANES)),
+    )(*back)
     out = call(bind(outer, plan), f32(plan.tf * cells, LANES))(down, rates, n0, h0, x1, far_low)
     sens = jnp.transpose(sens.reshape(fields, plan.panels, plan.rows, insts), (3, 0, 1, 2))
     return out.reshape(rhs.shape), sens

time: 60.4 us -> 59.9 us (level)
  starting transfers between devices: 26.9 us -> 29.8 us
  waiting for transfers between devices: 15.1 us -> 12.5 us
    ppermute x5 -> x11, starting transfers between devices: 13.7 us -> 20 us  [swap(): return lax.ppermute(array, 'sector', list(enumerate(partner)))]
    all_to_all x1 -> x0, waiting for transfers between devices: 5.54 us -> none  [on_device(): returned = lax.all_to_all(back, 'sector', 0, 0, tiled=True)]
    all_to_all x1 -> x0, starting transfers between devices: 3.5 us -> none  [on_device(): returned = lax.all_to_all(back, 'sector', 0, 0, tiled=True)]
    ppermute x5 -> x11, waiting for transfers between devices: 0.01 us -> 2.98 us  [swap(): return lax.ppermute(array, 'sector', list(enumerate(partner)))]
    pallas_call x2 -> x3, Pallas kernels: 4.37 us -> 3.78 us  [the longest x1 2.97 us: on_device(): call(bind(middle, plan), (tiles,) * plan.groups + (half, half, half, f32(...]
    unnamed x32 -> x24, local copies, waits for them, and re-layouts: 1.76 us -> 1.74 us
  transfers between devices with their start and end apart: 13 -> 18, of which waited for: 4 -> 7; matrix products, arithmetic and copies ran while one was open for 0% -> 0% of each run, Pallas kernels for 16% -> 15%
where the time goes in v11:
time: 59.9 us; the launch traced here: 59.6 us
  starting transfers between devices  29.8 us (50%)
  Pallas kernels  13 us (22%)
  waiting for transfers between devices  12.5 us (21%)
  local copies, waits for them, and re-layouts  1.9 us (3%)
  other arithmetic  1.54 us (3%)
  between operations  0.84 us (1%)
    ppermute x11, starting transfers between devices, swap(): return lax.ppermute(array, 'sector', list(enumerate(partner)))  20 us
    ppermute x6, starting transfers between devices, beside(): return lax.ppermute(array, AXES, pairs(0))  7.06 us
    all_to_all x1, waiting for transfers between devices, on_device(): got = lax.all_to_all(sent, AXES, 0, 0, tiled=True)  5.64 us
    ppermute x6, waiting for transfers between devices, beside(): return lax.ppermute(array, AXES, pairs(0))  3.89 us
    pallas_call x1, Pallas kernels, on_device(): call(bind(first_half, plan), (whole, half) + edges(pad), products + (vmem...  3.06 us
    ppermute x11, waiting for transfers between devices, swap(): return lax.ppermute(array, 'sector', list(enumerate(partner)))  2.98 us
    pallas_call x1, Pallas kernels, on_device(): call(bind(middle, plan), (tiles,) * plan.groups + (half, half, half, f32(...  2.97 us
    all_to_all x1, starting transfers between devices, on_device(): got = lax.all_to_all(sent, AXES, 0, 0, tiled=True)  2.72 us
  transfers between devices with their start and end apart: 18, of which 7 were waited for; matrix products, arithmetic and copies ran while one was open for 0% of the time, Pallas kernels for 15%

profile of v11, /device:TPU:0, one launch (start us, length us, event | category | flops | bytes accessed | tf_op | source)
XLA Modules:
  0.0 59.6 jit_solution(8992736316027704166)
XLA Ops:
  0.7 0.7 %convert_bitcast_fusion = f32[16,128]{1,0:T(8,128)S(1)} fusion(s32[2,8,128]{2,1,0:T(8,128)} %param.20), kind=kLoop, calls=%fused_computation.7 | loop fusion | flops 2048 | bytes 16384 | tf_op jit(solution)/shard_map/reshape | solution.py:699
  1.4 0.7 %pad_maximum_fusion.coef_ref = f32[96,128]{1,0:T(8,128)S(1)} fusion(f32[48,128]{1,0:T(8,128)} %bitcast.20, f32[16,128]{1,0:T(8,128)S(1)} %bitcast.21, f32[16,128]{1,0:T(8,128)S(1)} %bitcast.22, f32[16,128]{1,0:T(8,128)S(1)} %convert_bitcast_fusion), kind=kLoop, calls=%fused_computation | loop fusion | flops 36864 | bytes 98304 | tf_op jit(solution)/shard_map/concatenate | solution.py:698
  2.1 1.1 %copy-done = f32[11,7,2,8,128]{4,3,2,1,0:T(8,128)S(1)} copy-done((f32[11,7,2,8,128]{4,3,2,1,0:T(8,128)S(1)}, f32[11,7,2,8,128]{4,3,2,1,0:T(8,128)}, u32[]{:S(2)}) %copy-start) | copy-done | bytes 630808
  3.5 5.5 %collective-permute-start = (f32[88,2048]{1,0:T(8,128)S(1)}, f32[88,2048]{1,0:T(8,128)S(1)}, u32[]{:S(2)}, u32[]{:S(2)}) collective-permute-start(f32[88,2048]{1,0:T(8,128)S(1)} %get-tuple-element.31.m_ref), channel_id=1, source_target_pairs={{0,30},{2,4},{4,2},{6,8},{8,6},{10,12},{12,10},{14,16},{16,14},{18... | collective-permute-start | bytes 2162696 | tf_op jit(solution)/shard_map/ppermute | solution.py:654
  9.9 0.9 %shard_map.151 = f32[32,8,128]{2,1,0:T(8,128)} custom-call(f32[7,32,11]{2,1,0:T(8,128)S(1)} %bitcast.17, f32[11,32]{1,0:T(8,128)S(1)} %pad_maximum_fusion.1.both_ref), custom_call_target="tpu_custom_call" | custom-call | flops 2000000 | bytes 1000000 | tf_op jit(solution)/shard_map/pallas_call | solution.py:687
  10.8 2.7 %all-to-all-start = ((f32[32,8,128]{2,1,0:T(8,128)}), f32[32,8,128]{2,1,0:T(8,128)S(1)}, u32[]{:S(2)}, u32[]{:S(2)}) async-start(f32[32,8,128]{2,1,0:T(8,128)} %shard_map.151), calls=%async_computation | async-start | bytes 262144 | tf_op jit(solution)/shard_map/all_to_all | solution.py:693
  13.5 1.7 %collective-permute-start.2 = (f32[1,88,512]{2,1,0:T(8,128)S(1)}, f32[1,88,512]{2,1,0:T(8,128)S(1)}, u32[]{:S(2)}, u32[]{:S(2)}) collective-permute-start(f32[1,88,512]{2,1,0:T(8,128)S(1)} %get-tuple-element.34), channel_id=1, source_target_pairs={{0,1},{1,0},{2,3},{3,2},{4,5},{5,4},{6,7},{7,6},{8,9},{9,8},{10,11... | collective-permute-start | bytes 540680 | tf_op jit(solution)/shard_map/ppermute | solution.py:668
  15.2 3.9 %collective-permute-start.3 = (f32[1,88,128]{2,1,0:T(8,128)S(1)}, f32[1,88,128]{2,1,0:T(8,128)S(1)}, u32[]{:S(2)}, u32[]{:S(2)}) collective-permute-start(f32[1,88,128]{2,1,0:T(8,128)S(1)} %get-tuple-element.35), channel_id=1, source_target_pairs={{0,31},{1,30},{2,5},{3,4},{4,3},{5,2},{6,9},{7,8},{8,7},{9,6},{10,... | collective-permute-start | bytes 135176 | tf_op jit(solution)/shard_map/ppermute | solution.py:668
  19.1 1.1 %shard_map.149 = (bf16[560,240]{1,0:T(8,128)(2,1)S(1)}, bf16[80,240]{1,0:T(8,128)(2,1)S(1)}) custom-call(f32[3,7,7]{2,1,0:T(8,128)S(1)} %copy-done.5, f32[3,7,7]{2,1,0:T(8,128)S(1)} %copy-done.6, bf16[80,240]{1,0:T(8,128)(2,1)S(1)} %copy-done.3, f32[80,7]{1,0:T(8,128)S(1)} %copy-done.4, f32[7,240]{1,0:T(8,128)S(1)} %copy-done.7, f32[80,240]{1,0:T(8,128)S(1)} %copy-done.2), custom_call_target="tpu_custom_call" | custom-call | flops 2000000 | bytes 1000000 | tf_op jit(solution)/shard_map/pallas_call | solution.py:706
  20.2 5.6 %all-to-all-done.got_ref = f32[32,8,128]{2,1,0:T(8,128)S(1)} async-done(((f32[32,8,128]{2,1,0:T(8,128)}), f32[32,8,128]{2,1,0:T(8,128)S(1)}, u32[]{:S(2)}, u32[]{:S(2)}) %all-to-all-start) | async-done | bytes 131104 | tf_op jit(solution)/shard_map/all_to_all | solution.py:693
  25.9 1.7 %shard_map.152 = (f32[3,2,80,128]{3,2,1,0:T(8,128)S(1)}, f32[80,128]{1,0:T(8,128)S(1)}, f32[80,2048]{1,0:T(8,128)S(1)}, f32[80,2048]{1,0:T(8,128)S(1)}) custom-call(bf16[560,240]{1,0:T(8,128)(2,1)S(1)} %get-tuple-element.30.w_ref, f32[88,2048]{1,0:T(8,128)S(1)} %get-tuple-element.31.m_ref, f32[32,8,128]{2,1,0:T(8,128)S(1)} %all-to-all-done.got_ref), custom_call_target="tpu_custom_call" | custom-call | flops 2000000000 | bytes 1000000 | tf_op jit(solution)/shard_map/pallas_call | solution.py:711
  27.6 3.1 %shard_map.153 = (f32[80,2048]{1,0:T(8,128)S(1)}, f32[80,1024]{1,0:T(8,128)S(1)}, f32[1,80,512]{2,1,0:T(8,128)S(1)}, f32[1,80,128]{2,1,0:T(8,128)S(1)}, f32[1,80,128]{2,1,0:T(8,128)S(1)}) custom-call(bf16[560,240]{1,0:T(8,128)(2,1)S(1)} %get-tuple-element.30.w_ref, f32[88,2048]{1,0:T(8,128)S(1)} %get-tuple-element.31.m_ref, ...), custom_call_target="tpu_custom_call" | custom-call | flops 4000000000 | bytes 1000000 | tf_op jit(solution)/shard_map/pallas_call | solution.py:716
  30.7 4.6 %collective-permute-start.5 = (f32[80,1024]{1,0:T(8,128)S(1)}, f32[80,1024]{1,0:T(8,128)S(1)}, u32[]{:S(2)}, u32[]{:S(2)}) collective-permute-start(f32[80,1024]{1,0:T(8,128)S(1)} %get-tuple-element.39), channel_id=1, source_target_pairs={{0,30},{2,4},{4,2},{6,8},{8,6},{10,12},{12,10},{14,16},{16,14},{18... | collective-permute-start | bytes 983048 | tf_op jit(solution)/shard_map/ppermute | solution.py:654
  35.3 1.5 %collective-permute-start.7 = (f32[1,80,512]{2,1,0:T(8,128)S(1)}, f32[1,80,512]{2,1,0:T(8,128)S(1)}, u32[]{:S(2)}, u32[]{:S(2)}) collective-permute-start(f32[1,80,512]{2,1,0:T(8,128)S(1)} %get-tuple-element.40), channel_id=1, source_target_pairs={{0,1},{1,0},{2,3},{3,2},{4,5},{5,4},{6,7},{7,6},{8,9},{9,8},{10,11... | collective-permute-start | bytes 491528 | tf_op jit(solution)/shard_map/ppermute | solution.py:668
  36.8 0.8 %shard_map.154.g_ref = f32[80,2048]{1,0:T(8,128)S(1)} custom-call(bf16[560,240]{1,0:T(8,128)(2,1)S(1)} %get-tuple-element.30.w_ref, f32[88,2048]{1,0:T(8,128)S(1)} %get-tuple-element.31.m_ref, f32[80,2048]{1,0:T(8,128)S(1)} %get-tuple-element.32.f_ref, f32[80,2048]{1,0:T(8,128)S(1)} %get-tuple-element.38.x_ref), custom_call_target="tpu_custom_call" | custom-call | flops 2000000000 | bytes 1000000 | tf_op jit(solution)/shard_map/pallas_call | solution.py:725
  37.6 3.5 %collective-permute-done.9.c_high = f32[1,80,128]{2,1,0:T(8,128)S(1)} collective-permute-done((f32[1,80,128]{2,1,0:T(8,128)S(1)}, f32[1,80,128]{2,1,0:T(8,128)S(1)}, u32[]{:S(2)}, u32[]{:S(2)}) %collective-permute-start.9) | collective-permute-done | bytes 40992 | tf_op jit(solution)/shard_map/ppermute | solution.py:668
  41.6 3.5 %collective-permute-start.10 = (f32[80,1024]{1,0:T(8,128)S(1)}, f32[80,1024]{1,0:T(8,128)S(1)}, u32[]{:S(2)}, u32[]{:S(2)}) collective-permute-start(f32[80,1024]{1,0:T(8,128)S(1)} %shard_map.156), channel_id=1, source_target_pairs={{0,30},{2,4},{4,2},{6,8},{8,6},{10,12},{12,10},{14,16},{16,14},{18... | collective-permute-start | bytes 983048 | tf_op jit(solution)/shard_map/ppermute | solution.py:654
  45.1 3.0 %shard_map.155 = (f32[4,8,128]{2,1,0:T(8,128)S(1)}, f32[4,8,128]{2,1,0:T(8,128)S(1)}, f32[4,8,128]{2,1,0:T(8,128)S(1)}, f32[4,8,128]{2,1,0:T(8,128)S(1)}, f32[80...) custom-call(bf16[560,240]{1,0:T(8,128)(2,1)S(1)} %get-tuple-element.30.w_ref, ...), custom_call_target="tpu_custom_call" | custom-call | flops 4000000000 | bytes 1000000 | tf_op jit(solution)/shard_map/pallas_call | solution.py:729
  48.7 3.8 %collective-permute-start.13 = (f32[4,8,128]{2,1,0:T(8,128)S(1)}, f32[4,8,128]{2,1,0:T(8,128)S(1)}, u32[]{:S(2)}, u32[]{:S(2)}) collective-permute-start(f32[4,8,128]{2,1,0:T(8,128)S(1)} %get-tuple-element.51), channel_id=1, source_target_pairs={{0,24},{2,26},{4,28},{6,30},{8,16},{10,18},{12,20},{14,22},{16,8},... | collective-permute-start | bytes 49160 | tf_op jit(solution)/shard_map/ppermute | solution.py:654
  52.8 1.6 %collective-permute-done.13.refs_3_ = f32[4,8,128]{2,1,0:T(8,128)S(1)} collective-permute-done((f32[4,8,128]{2,1,0:T(8,128)S(1)}, f32[4,8,128]{2,1,0:T(8,128)S(1)}, u32[]{:S(2)}, u32[]{:S(2)}) %collective-permute-start.13) | collective-permute-done | bytes 16416 | tf_op jit(solution)/shard_map/ppermute | solution.py:654
  54.5 1.1 %collective-permute-start.15 = (f32[4,8,128]{2,1,0:T(8,128)S(1)}, f32[4,8,128]{2,1,0:T(8,128)S(1)}, u32[]{:S(2)}, u32[]{:S(2)}) collective-permute-start(f32[4,8,128]{2,1,0:T(8,128)S(1)} %get-tuple-element.54), channel_id=1, source_target_pairs={{0,4},{2,6},{4,0},{6,2},{8,12},{10,14},{12,8},{14,10},{16,20},{18,... | collective-permute-start | bytes 49160 | tf_op jit(solution)/shard_map/ppermute | solution.py:654
  55.6 0.8 %collective-permute-start.16 = (f32[4,8,128]{2,1,0:T(8,128)S(1)}, f32[4,8,128]{2,1,0:T(8,128)S(1)}, u32[]{:S(2)}, u32[]{:S(2)}) collective-permute-start(f32[4,8,128]{2,1,0:T(8,128)S(1)} %get-tuple-element.55), channel_id=1, source_target_pairs={{0,6},{2,4},{4,2},{6,0},{8,14},{10,12},{12,10},{14,8},{16,22},{18,... | collective-permute-start | bytes 49160 | tf_op jit(solution)/shard_map/ppermute | solution.py:654
  56.4 1.3 %shard_map.157 = f32[1232,128]{1,0:T(8,128)} custom-call(bf16[80,240]{1,0:T(8,128)(2,1)S(1)} %get-tuple-element.29.w_ref, f32[8,1024]{1,0:T(8,128)S(1)} %get-tuple-element.44.rates_ref, f32[80,1024]{1,0:T(8,128)S(1)} %get-tuple-element.45.n0_ref, f32[80,1024]{1,0:T(8,128)S(1)} %get-tuple-element.46.h0_ref, f32[80,1024]{1,0:T(8,128)S(1)} %get-tuple-element.47.x1_ref, ...), custom_call_target="tpu_custom_call" | custom-call | flops 2000000 | bytes 1000000 | tf_op jit(solution)/shard_map/pallas_call | solution.py:747
  58.7 0.8 %shard_map.159 = f32[7,32,11]{2,1,0:T(8,128)} custom-call(f32[4,8,128]{2,1,0:T(8,128)S(1)} %get-tuple-element.52.refs_0_, f32[4,8,128]{2,1,0:T(8,128)S(1)} %collective-permute-done.14.refs_1_, f32[4,8,128]{2,1,0:T(8,128)S(1)} %collective-permute-done.15.refs_2_, f32[4,8,128]{2,1,0:T(8,128)S(1)} %collective-permute-done.16.refs_3_), custom_call_target="tpu_custom_call" | custom-call | flops 2000000 | bytes 1000000 | tf_op jit(solution)/shard_map/pallas_call | solution.py:743
  (53 shorter events, 3.8 us)
Async XLA Ops:
  3.5 24.1 %collective-permute-start = (f32[88,2048]{1,0:T(8,128)S(1)}, f32[88,2048]{1,0:T(8,128)S(1)}, u32[]{:S(2)}, u32[]{:S(2)}) collective-permute-start(f32[88,2048]{1,0:T(8,128)S(1)} %get-tuple-element.31.m_ref), channel_id=1, source_target_pairs={{0,30},{2,4},{4,2},{6,8},{8,6},{10,12},{12,10},{14,16},{16,14},{18... | collective-permute-start | bytes 2162696 | tf_op jit(solution)/shard_map/ppermute | solution.py:654
  9.0 18.7 %collective-permute-start.1 = (f32[88,2048]{1,0:T(8,128)S(1)}, f32[88,2048]{1,0:T(8,128)S(1)}, u32[]{:S(2)}, u32[]{:S(2)}) collective-permute-start(f32[88,2048]{1,0:T(8,128)S(1)} %get-tuple-element.31.m_ref), channel_id=1, source_target_pairs={{0,2},{2,0},{4,6},{6,4},{8,10},{10,8},{12,14},{14,12},{16,18},{18,... | collective-permute-start | bytes 2162696 | tf_op jit(solution)/shard_map/ppermute | solution.py:654
  10.7 8.3 %copy-start.2 = (f32[80,240]{1,0:T(8,128)S(1)}, f32[80,240]{1,0:T(8,128)}, u32[]{:S(2)}) copy-start(f32[80,240]{1,0:T(8,128)} %constant.16.clone.diagonal_ref) | copy-start | bytes 230404
  10.7 8.3 %copy-start.3 = (bf16[80,240]{1,0:T(8,128)(2,1)S(1)}, bf16[80,240]{1,0:T(8,128)(2,1)}, u32[]{:S(2)}) copy-start(bf16[80,240]{1,0:T(8,128)(2,1)} %constant.13.clone.spectral_ref) | copy-start | bytes 115204
  10.7 8.3 %copy-start.4 = (f32[80,7]{1,0:T(8,128)S(1)}, f32[80,7]{1,0:T(8,128)}, u32[]{:S(2)}) copy-start(f32[80,7]{1,0:T(8,128)} %constant.14.clone.rows_ref) | copy-start | bytes 6724
  10.7 8.3 %copy-start.5 = (f32[3,7,7]{2,1,0:T(8,128)S(1)}, f32[3,7,7]{2,1,0:T(8,128)}, u32[]{:S(2)}) copy-start(f32[3,7,7]{2,1,0:T(8,128)} %up_ref.1) | copy-start | bytes 1768
  10.7 8.3 %copy-start.6 = (f32[3,7,7]{2,1,0:T(8,128)S(1)}, f32[3,7,7]{2,1,0:T(8,128)}, u32[]{:S(2)}) copy-start(f32[3,7,7]{2,1,0:T(8,128)} %down_ref.1) | copy-start | bytes 1768
  10.8 8.3 %copy-start.7 = (f32[7,240]{1,0:T(8,128)S(1)}, f32[7,240]{1,0:T(8,128)}, u32[]{:S(2)}) copy-start(f32[7,240]{1,0:T(8,128)} %constant.15.clone.lanes_ref) | copy-start | bytes 20164
  10.8 15.1 %all-to-all-start = ((f32[32,8,128]{2,1,0:T(8,128)}), f32[32,8,128]{2,1,0:T(8,128)S(1)}, u32[]{:S(2)}, u32[]{:S(2)}) async-start(f32[32,8,128]{2,1,0:T(8,128)} %shard_map.151), calls=%async_computation | async-start | bytes 262144 | tf_op jit(solution)/shard_map/all_to_all | solution.py:693
  13.5 14.1 %collective-permute-start.2 = (f32[1,88,512]{2,1,0:T(8,128)S(1)}, f32[1,88,512]{2,1,0:T(8,128)S(1)}, u32[]{:S(2)}, u32[]{:S(2)}) collective-permute-start(f32[1,88,512]{2,1,0:T(8,128)S(1)} %get-tuple-element.34), channel_id=1, source_target_pairs={{0,1},{1,0},{2,3},{3,2},{4,5},{5,4},{6,7},{7,6},{8,9},{9,8},{10,11... | collective-permute-start | bytes 540680 | tf_op jit(solution)/shard_map/ppermute | solution.py:668
  15.2 12.4 %collective-permute-start.3 = (f32[1,88,128]{2,1,0:T(8,128)S(1)}, f32[1,88,128]{2,1,0:T(8,128)S(1)}, u32[]{:S(2)}, u32[]{:S(2)}) collective-permute-start(f32[1,88,128]{2,1,0:T(8,128)S(1)} %get-tuple-element.35), channel_id=1, source_target_pairs={{0,31},{1,30},{2,5},{3,4},{4,3},{5,2},{6,9},{7,8},{8,7},{9,6},{10,... | collective-permute-start | bytes 135176 | tf_op jit(solution)/shard_map/ppermute | solution.py:668
  19.0 8.6 %collective-permute-start.4 = (f32[1,88,128]{2,1,0:T(8,128)S(1)}, f32[1,88,128]{2,1,0:T(8,128)S(1)}, u32[]{:S(2)}, u32[]{:S(2)}) collective-permute-start(f32[1,88,128]{2,1,0:T(8,128)S(1)} %get-tuple-element.36), channel_id=1, source_target_pairs={{0,3},{1,2},{2,1},{3,0},{4,7},{5,6},{6,5},{7,4},{8,11},{9,10},{10,... | collective-permute-start | bytes 135176 | tf_op jit(solution)/shard_map/ppermute | solution.py:668
  30.7 14.4 %collective-permute-start.6 = (f32[80,2048]{1,0:T(8,128)S(1)}, f32[80,2048]{1,0:T(8,128)S(1)}, u32[]{:S(2)}, u32[]{:S(2)}) collective-permute-start(f32[80,2048]{1,0:T(8,128)S(1)} %get-tuple-element.38.x_ref), channel_id=1, source_target_pairs={{0,2},{2,0},{4,6},{6,4},{8,10},{10,8},{12,14},{14,12},{16,18},{18,... | collective-permute-start | bytes 1966088 | tf_op jit(solution)/shard_map/ppermute | solution.py:654
  30.7 14.4 %collective-permute-start.5 = (f32[80,1024]{1,0:T(8,128)S(1)}, f32[80,1024]{1,0:T(8,128)S(1)}, u32[]{:S(2)}, u32[]{:S(2)}) collective-permute-start(f32[80,1024]{1,0:T(8,128)S(1)} %get-tuple-element.39), channel_id=1, source_target_pairs={{0,30},{2,4},{4,2},{6,8},{8,6},{10,12},{12,10},{14,16},{16,14},{18... | collective-permute-start | bytes 983048 | tf_op jit(solution)/shard_map/ppermute | solution.py:654
  35.3 6.2 %collective-permute-start.7 = (f32[1,80,512]{2,1,0:T(8,128)S(1)}, f32[1,80,512]{2,1,0:T(8,128)S(1)}, u32[]{:S(2)}, u32[]{:S(2)}) collective-permute-start(f32[1,80,512]{2,1,0:T(8,128)S(1)} %get-tuple-element.40), channel_id=1, source_target_pairs={{0,1},{1,0},{2,3},{3,2},{4,5},{5,4},{6,7},{7,6},{8,9},{9,8},{10,11... | collective-permute-start | bytes 491528 | tf_op jit(solution)/shard_map/ppermute | solution.py:668
  36.8 8.3 %collective-permute-start.8 = (f32[1,80,128]{2,1,0:T(8,128)S(1)}, f32[1,80,128]{2,1,0:T(8,128)S(1)}, u32[]{:S(2)}, u32[]{:S(2)}) collective-permute-start(f32[1,80,128]{2,1,0:T(8,128)S(1)} %get-tuple-element.41), channel_id=1, source_target_pairs={{0,31},{1,30},{2,5},{3,4},{4,3},{5,2},{6,9},{7,8},{8,7},{9,6},{10,... | collective-permute-start | bytes 122888 | tf_op jit(solution)/shard_map/ppermute | solution.py:668
  36.8 4.3 %collective-permute-start.9 = (f32[1,80,128]{2,1,0:T(8,128)S(1)}, f32[1,80,128]{2,1,0:T(8,128)S(1)}, u32[]{:S(2)}, u32[]{:S(2)}) collective-permute-start(f32[1,80,128]{2,1,0:T(8,128)S(1)} %get-tuple-element.42), channel_id=1, source_target_pairs={{0,3},{1,2},{2,1},{3,0},{4,7},{5,6},{6,5},{7,4},{8,11},{9,10},{10,... | collective-permute-start | bytes 122888 | tf_op jit(solution)/shard_map/ppermute | solution.py:668
  41.6 14.8 %collective-permute-start.10 = (f32[80,1024]{1,0:T(8,128)S(1)}, f32[80,1024]{1,0:T(8,128)S(1)}, u32[]{:S(2)}, u32[]{:S(2)}) collective-permute-start(f32[80,1024]{1,0:T(8,128)S(1)} %shard_map.156), channel_id=1, source_target_pairs={{0,30},{2,4},{4,2},{6,8},{8,6},{10,12},{12,10},{14,16},{16,14},{18... | collective-permute-start | bytes 983048 | tf_op jit(solution)/shard_map/ppermute | solution.py:654
  48.1 4.5 %collective-permute-start.11 = (f32[4,8,128]{2,1,0:T(8,128)S(1)}, f32[4,8,128]{2,1,0:T(8,128)S(1)}, u32[]{:S(2)}, u32[]{:S(2)}) collective-permute-start(f32[4,8,128]{2,1,0:T(8,128)S(1)} %get-tuple-element.49), channel_id=1, source_target_pairs={{0,8},{2,10},{4,12},{6,14},{8,0},{10,2},{12,4},{14,6},{16,24},{18,... | collective-permute-start | bytes 49160 | tf_op jit(solution)/shard_map/ppermute | solution.py:654
  48.1 4.7 %collective-permute-start.12 = (f32[4,8,128]{2,1,0:T(8,128)S(1)}, f32[4,8,128]{2,1,0:T(8,128)S(1)}, u32[]{:S(2)}, u32[]{:S(2)}) collective-permute-start(f32[4,8,128]{2,1,0:T(8,128)S(1)} %get-tuple-element.50), channel_id=1, source_target_pairs={{0,16},{2,18},{4,20},{6,22},{8,24},{10,26},{12,28},{14,30},{16,0},... | collective-permute-start | bytes 49160 | tf_op jit(solution)/shard_map/ppermute | solution.py:654
  48.7 5.7 %collective-permute-start.13 = (f32[4,8,128]{2,1,0:T(8,128)S(1)}, f32[4,8,128]{2,1,0:T(8,128)S(1)}, u32[]{:S(2)}, u32[]{:S(2)}) collective-permute-start(f32[4,8,128]{2,1,0:T(8,128)S(1)} %get-tuple-element.51), channel_id=1, source_target_pairs={{0,24},{2,26},{4,28},{6,30},{8,16},{10,18},{12,20},{14,22},{16,8},... | collective-permute-start | bytes 49160 | tf_op jit(solution)/shard_map/ppermute | solution.py:654
  54.4 3.3 %collective-permute-start.14 = (f32[4,8,128]{2,1,0:T(8,128)S(1)}, f32[4,8,128]{2,1,0:T(8,128)S(1)}, u32[]{:S(2)}, u32[]{:S(2)}) collective-permute-start(f32[4,8,128]{2,1,0:T(8,128)S(1)} %get-tuple-element.53), channel_id=1, source_target_pairs={{0,2},{2,0},{4,6},{6,4},{8,10},{10,8},{12,14},{14,12},{16,18},{18,... | collective-permute-start | bytes 49160 | tf_op jit(solution)/shard_map/ppermute | solution.py:654
  54.5 3.8 %collective-permute-start.15 = (f32[4,8,128]{2,1,0:T(8,128)S(1)}, f32[4,8,128]{2,1,0:T(8,128)S(1)}, u32[]{:S(2)}, u32[]{:S(2)}) collective-permute-start(f32[4,8,128]{2,1,0:T(8,128)S(1)} %get-tuple-element.54), channel_id=1, source_target_pairs={{0,4},{2,6},{4,0},{6,2},{8,12},{10,14},{12,8},{14,10},{16,20},{18,... | collective-permute-start | bytes 49160 | tf_op jit(solution)/shard_map/ppermute | solution.py:654
  55.6 3.2 %collective-permute-start.16 = (f32[4,8,128]{2,1,0:T(8,128)S(1)}, f32[4,8,128]{2,1,0:T(8,128)S(1)}, u32[]{:S(2)}, u32[]{:S(2)}) collective-permute-start(f32[4,8,128]{2,1,0:T(8,128)S(1)} %get-tuple-element.55), channel_id=1, source_target_pairs={{0,6},{2,4},{4,2},{6,0},{8,14},{10,12},{12,10},{14,8},{16,22},{18,... | collective-permute-start | bytes 49160 | tf_op jit(solution)/shard_map/ppermute | solution.py:654
  (6 other events, 15.7 us)

commit v12 on v11

--- a/solution.py
+++ b/solution.py
@@ -260,16 +260,22 @@
 
 def middle_rows(plan, w_ref, p_refs, own, own_force, g_ref, near, near_force, side, corner, y_ref, h_refs, n_refs):
     pad, rows, ct = plan.pad, plan.rows, plan.ct
-    outward, inward, last = (UP_SP, DOWN_SP), (DOWN_SP, UP_SP), (rows - 1, 0)
+    last = (rows - 1, 0)
     edge_terms, edge_new, corner_terms = [], [], []
-    for n in range(2):
+    is_first = lax.axis_index("span") == 0
+
+    def choose(n, above, below):
+        return jnp.where(is_first, above, below) if plan.ends == 1 else (above, below)[n]
+
+    for n in range(plan.ends):
+        outward = choose(n, matrix(plan, w_ref, UP_SP), matrix(plan, w_ref, DOWN_SP))
+        inward = choose(n, matrix(plan, w_ref, DOWN_SP), matrix(plan, w_ref, UP_SP))
         first, second, edge_force, edge_rate = side(n)
         corners = corner(n)
         every = dot3(w_ref[...], first)
-        edge_terms.append(every[outward[n] * pad : (outward[n] + 1) * pad])
-        corner_terms.append([dot3(matrix(plan, w_ref, outward[n]), c) for c in corners])
-        beyond = dot3(matrix(plan, w_ref, outward[n]), second)
-        within = dot3(matrix(plan, w_ref, inward[n]), jnp.concatenate([x.row(last[n]) for x in own], axis=1))
+        beyond = dot3(outward, second)
+        within = [choose(n, x.row(last[0]), x.row(last[1])) for x in own]
+        within = dot3(inward, jnp.concatenate(within, axis=1))
         from_low = dot3(matrix(plan, w_ref, DOWN_AZ), corners[0])
         from_high = dot3(matrix(plan, w_ref, UP_AZ), corners[1])
         new = []
@@ -284,7 +290,13 @@
             total = total + edge_rate(C_UP, a) * rolled(part(UP_AX), -1)
             total = total + edge_rate(C_DOWN, a) * rolled(part(DOWN_AX), 1)
             new.append(edge_force[:, at(a)] - total)
-        edge_new.append(dot3(matrix(plan, w_ref, outward[n]), jnp.concatenate(new, axis=1)))
+        of_edge = choose(n, *(every[block * pad : (block + 1) * pad] for block in (UP_SP, DOWN_SP)))
+        of_new = dot3(outward, jnp.concatenate(new, axis=1))
+        of_corners = dot3(outward, jnp.concatenate(corners, axis=1))
+        for keep in has_sides(plan) if plan.ends == 1 else (1.0,):
+            edge_terms.append(of_edge * keep)
+            edge_new.append(of_new * keep)
+            corner_terms.append([of_corners[:, at(a)] * keep for a in range(ct)])
 
     products = (
         Products(plan, w_ref, p_refs[0], DOWN_AZ).fill(near[0]), Products(plan, w_ref, p_refs[1], SPECTRAL).fill(near[1]),
@@ -328,24 +340,28 @@
 
 def sides_of(plan, side_ref, force_ref, seams_ref):
     pad, ct = plan.pad, plan.ct
-    keeps = has_sides(plan)
+    keeps = (1.0,) if plan.ends == 1 else has_sides(plan)
+    is_first = lax.axis_index("span") == 0
+
+    def inlet(n, e, a):
+        above, below = a * plan.rows + e, a * plan.rows + plan.rows - 1 - e
+        tile = seams_ref[1, 1 + n]
+        if plan.ends == 1:
+            return jnp.where(is_first, placed(tile, above), placed(tile, below))
+        return placed(tile, (above, below)[n])
 
     def read(n, ref, e, seam):
-        i = n if plan.ends == 2 else 0
-        value = ref[i, :pad, at(e * ct, ct)]
+        value = ref[n, :pad, at(e * ct, ct)]
         if seam:
-            r = e if n == 0 else plan.rows - 1 - e
-            tile = seams_ref[1, 1 + i]
-            scale = ref[i, pad + C_MASK : pad + C_MASK + 1, at(e * ct, ct)]
-            value = value + jnp.concatenate([placed(tile, a * plan.rows + r) for a in range(ct)], axis=1) * scale
+            scale = ref[n, pad + C_MASK : pad + C_MASK + 1, at(e * ct, ct)]
+            value = value + jnp.concatenate([inlet(n, e, a) for a in range(ct)], axis=1) * scale
         return value * keeps[n]
 
     def side(n):
-        i = n if plan.ends == 2 else 0
         same = side_ref is force_ref
 
         def rate(which, a):
-            return force_ref[i, pad + which : pad + which + 1, at(a)] * keeps[n]
+            return force_ref[n, pad + which : pad + which + 1, at(a)] * keeps[n]
 
         force = read(n, force_ref, 0, True)
         first = force if same else read(n, side_ref, 0, False)
@@ -355,17 +371,18 @@
 
 
 def corners_of(plan, c_refs, seams_ref):
-    keeps = has_sides(plan)
+    keeps = (1.0,) if plan.ends == 1 else has_sides(plan)
+    is_first = lax.axis_index("span") == 0
 
     def corner(n):
-        i = n if plan.ends == 2 else 0
         out = []
         for a, c_ref in enumerate(c_refs):
-            value = c_ref[i, : plan.pad]
+            value = c_ref[n, : plan.pad]
             if seams_ref is not None:
-                r = 0 if n == 0 else plan.rows - 1
-                scale = c_ref[i, plan.pad + C_MASK : plan.pad + C_MASK + 1]
-                value = value + placed(seams_ref[2 * a, 1 + i], a * plan.rows + r) * scale
+                tile = seams_ref[2 * a, 1 + n]
+                above, below = (placed(tile, a * plan.rows + r) for r in (0, plan.rows - 1))
+                inlet = jnp.where(is_first, above, below) if plan.ends == 1 else (above, below)[n]
+                value = value + inlet * c_ref[n, plan.pad + C_MASK : plan.pad + C_MASK + 1]
             out.append(value * keeps[n])
         return out
 
@@ -549,8 +566,8 @@
     *refs,
 ):
     pad = plan.pad
-    send_refs = refs[: plan.groups]
-    n0_ref, h0_ref, x1_ref, rates_ref, p0_ref, p1_ref, y_ref, h1_ref, n1_ref, turn_ref, send_ref = refs[plan.groups :]
+    send_refs = refs[:GROUP]
+    n0_ref, h0_ref, x1_ref, rates_ref, p0_ref, p1_ref, y_ref, h1_ref, n1_ref, turn_ref, send_ref = refs[GROUP:]
     own, force = two_layers(plan, x_ref, m_ref), two_layers(plan, f_ref, m_ref)
     low_force = Layer(plan, low_first, 0, None, seams_ref[0, 0], 0)
     high_force = Layer(plan, high_first, plan.slab, None, seams_ref[2, 0], 1)
@@ -597,10 +614,10 @@
     send_ref[...] = jnp.zeros_like(send_ref)
     for t in range(plan.insts):
         to = lax.rem(me + plan.shift[t], plan.sectors)
-        place = (lax.div(to, GROUP) ^ lax.div(me, GROUP)) * GROUP + lax.rem(to, GROUP)
+        place = (lax.rem(to, GROUP) ^ lax.rem(me, GROUP)) * plan.groups + (lax.div(to, GROUP) ^ lax.div(me, GROUP))
         send_ref[place, : plan.fields, : plan.width] = back[t * plan.fields : (t + 1) * plan.fields, : plan.width]
     for i, ref in enumerate(send_refs):
-        ref[...] = send_ref[i * GROUP : (i + 1) * GROUP]
+        ref[...] = send_ref[i * plan.groups : (i + 1) * plan.groups]
 
 
 def outer(plan, w_ref, rates_ref, n0_ref, h0_ref, x1_ref, far_ref, out_ref):
@@ -621,22 +638,21 @@
 
 
 def turn_panels(plan, *refs):
-    place = lax.rem(lax.axis_index("sector"), GROUP)
-    for j, out_ref in enumerate(refs[plan.groups :]):
-        for i, ref in enumerate(refs[: plan.groups]):
-            out_ref[i] = ref[place ^ j]
+    for i, out_ref in enumerate(refs[GROUP:]):
+        for j, ref in enumerate(refs[:GROUP]):
+            out_ref[j] = ref[i]
 
 
 def collect_panels(plan, *refs):
-    out_ref, tiles_ref, panels_ref = refs[GROUP:]
-    for j, ref in enumerate(refs[:GROUP]):
-        tiles_ref[j * plan.groups : (j + 1) * plan.groups] = ref[...]
+    out_ref, tiles_ref, panels_ref = refs[plan.groups :]
+    for i, ref in enumerate(refs[: plan.groups]):
+        tiles_ref[i * GROUP : (i + 1) * GROUP] = ref[...]
     me = lax.axis_index("sector")
     for t in range(plan.insts):
         source = lax.rem(me + (plan.sectors - plan.shift[t]), plan.sectors)
         j = lax.rem(source, GROUP) ^ lax.rem(me, GROUP)
         i = lax.div(source, GROUP) ^ lax.div(me, GROUP)
-        panels_ref[t * RATES : (t + 1) * RATES, :] = tiles_ref[j * plan.groups + i]
+        panels_ref[t * RATES : (t + 1) * RATES, :] = tiles_ref[i * GROUP + j]
     for f in range(plan.fields):
         tile = panels_ref[pl.ds(f, plan.insts, stride=RATES), : plan.width]
         out_ref[f] = jnp.transpose(tile)
@@ -725,9 +741,9 @@
     (g,) = call(bind(inner, plan), (whole,), products, flops=2_000_000_000)(matrices, m, force, x)
     far = call(bind(hold_far, plan), half)(x, side, c_high)
     far_low = swap(far, next_chip)
-    tiles = f32(GROUP, RATES, LANES)
+    tiles = f32(plan.groups, RATES, LANES)
     *back, n0, h0, x1, rates = call(
-        bind(middle, plan), (tiles,) * plan.groups + (half, half, half, f32(RATES, slab)),
+        bind(middle, plan), (tiles,) * GROUP + (half, half, half, f32(RATES, slab)),
         products + (
             vmem(pad, 2 * slab), vmem(pad, slab), vmem(pad, slab), vmem(LANES, LANES), vmem(sectors, RATES, LANES),
         ),
@@ -735,11 +751,11 @@
     )(
         matrices, m, force, x, g, low, high, side, c_low, c_high, low_first, high_first, side_first, seams, weight
     )
+    for j in range(1, GROUP):
+        back[j] = swap(back[j], [s ^ j for s in range(sectors)])
+    back = list(call(bind(turn_panels, plan), (f32(GROUP, RATES, LANES),) * plan.groups)(*back))
     for i in range(1, plan.groups):
         back[i] = swap(back[i], [(s // GROUP ^ i) * GROUP + s % GROUP for s in range(sectors)])
-    back = list(call(bind(turn_panels, plan), (f32(plan.groups, RATES, LANES),) * GROUP)(*back))
-    for j in range(1, GROUP):
-        back[j] = swap(back[j], [s ^ j for s in range(sectors)])
     sens = call(
         bind(collect_panels, plan), f32(fields, plan.width, insts),
         (vmem(sectors, RATES, LANES), vmem(insts * RATES, LANES)),

time: 59.9 us -> 61.3 us (1.023)
  waiting for transfers between devices: 12.5 us -> 14.4 us
    ppermute x11, waiting for transfers between devices: 2.98 us -> 4.86 us  [swap(): return lax.ppermute(array, 'sector', list(enumerate(partner)))]
  transfers between devices with their start and end apart: 18 -> 18, of which waited for: 7 -> 5; matrix products, arithmetic and copies ran while one was open for 0% -> 0% of each run, Pallas kernels for 15% -> 14%
where the time goes in v12:
time: 61.3 us; the launch traced here: 60.9 us
  starting transfers between devices  29.8 us (49%)
  waiting for transfers between devices  14.4 us (23%)
  Pallas kernels  12.5 us (20%)
  local copies, waits for them, and re-layouts  1.9 us (3%)
  other arithmetic  1.54 us (3%)
  between operations  0.85 us (1%)
    ppermute x11, starting transfers between devices, swap(): return lax.ppermute(array, 'sector', list(enumerate(partner)))  20 us
    ppermute x6, starting transfers between devices, beside(): return lax.ppermute(array, AXES, pairs(0))  7.05 us
    all_to_all x1, waiting for transfers between devices, on_device(): got = lax.all_to_all(sent, AXES, 0, 0, tiled=True)  5.64 us
    ppermute x11, waiting for transfers between devices, swap(): return lax.ppermute(array, 'sector', list(enumerate(partner)))  4.86 us
    ppermute x6, waiting for transfers between devices, beside(): return lax.ppermute(array, AXES, pairs(0))  3.89 us
    pallas_call x1, Pallas kernels, on_device(): call(bind(first_half, plan), (whole, half) + edges(pad), products + (vmem...  2.81 us
    all_to_all x1, starting transfers between devices, on_device(): got = lax.all_to_all(sent, AXES, 0, 0, tiled=True)  2.72 us
    pallas_call x1, Pallas kernels, on_device(): call(bind(middle, plan), (tiles,) * GROUP + (half, half, half, f32(RATES,...  2.72 us
  transfers between devices with their start and end apart: 18, of which 5 were waited for; matrix products, arithmetic and copies ran while one was open for 0% of the time, Pallas kernels for 14%

profile of v12, /device:TPU:0, one launch (start us, length us, event | category | flops | bytes accessed | tf_op | source)
XLA Modules:
  0.0 60.9 jit_solution(11907391357793546973)
XLA Ops:
  1.4 0.7 %pad_maximum_fusion.coef_ref = f32[96,128]{1,0:T(8,128)S(1)} fusion(f32[48,128]{1,0:T(8,128)} %bitcast.20, f32[16,128]{1,0:T(8,128)S(1)} %bitcast.21, f32[16,128]{1,0:T(8,128)S(1)} %bitcast.22, f32[16,128]{1,0:T(8,128)S(1)} %convert_bitcast_fusion), kind=kLoop, calls=%fused_computation | loop fusion | flops 36864 | bytes 98304 | tf_op jit(solution)/shard_map/concatenate | solution.py:714
  2.1 1.1 %copy-done = f32[11,7,2,8,128]{4,3,2,1,0:T(8,128)S(1)} copy-done((f32[11,7,2,8,128]{4,3,2,1,0:T(8,128)S(1)}, f32[11,7,2,8,128]{4,3,2,1,0:T(8,128)}, u32[]{:S(2)}) %copy-start) | copy-done | bytes 630808
  3.5 5.5 %collective-permute-start = (f32[88,2048]{1,0:T(8,128)S(1)}, f32[88,2048]{1,0:T(8,128)S(1)}, u32[]{:S(2)}, u32[]{:S(2)}) collective-permute-start(f32[88,2048]{1,0:T(8,128)S(1)} %get-tuple-element.31.m_ref), channel_id=1, source_target_pairs={{0,30},{2,4},{4,2},{6,8},{8,6},{10,12},{12,10},{14,16},{16,14},{18... | collective-permute-start | bytes 2162696 | tf_op jit(solution)/shard_map/ppermute | solution.py:670
  9.9 0.9 %shard_map.151 = f32[32,8,128]{2,1,0:T(8,128)} custom-call(f32[7,32,11]{2,1,0:T(8,128)S(1)} %bitcast.17, f32[11,32]{1,0:T(8,128)S(1)} %pad_maximum_fusion.1.both_ref), custom_call_target="tpu_custom_call" | custom-call | flops 2000000 | bytes 1000000 | tf_op jit(solution)/shard_map/pallas_call | solution.py:703
  10.8 2.7 %all-to-all-start = ((f32[32,8,128]{2,1,0:T(8,128)}), f32[32,8,128]{2,1,0:T(8,128)S(1)}, u32[]{:S(2)}, u32[]{:S(2)}) async-start(f32[32,8,128]{2,1,0:T(8,128)} %shard_map.151), calls=%async_computation | async-start | bytes 262144 | tf_op jit(solution)/shard_map/all_to_all | solution.py:709
  13.5 1.7 %collective-permute-start.2 = (f32[1,88,512]{2,1,0:T(8,128)S(1)}, f32[1,88,512]{2,1,0:T(8,128)S(1)}, u32[]{:S(2)}, u32[]{:S(2)}) collective-permute-start(f32[1,88,512]{2,1,0:T(8,128)S(1)} %get-tuple-element.34), channel_id=1, source_target_pairs={{0,1},{1,0},{2,3},{3,2},{4,5},{5,4},{6,7},{7,6},{8,9},{9,8},{10,11... | collective-permute-start | bytes 540680 | tf_op jit(solution)/shard_map/ppermute | solution.py:684
  15.2 3.9 %collective-permute-start.3 = (f32[1,88,128]{2,1,0:T(8,128)S(1)}, f32[1,88,128]{2,1,0:T(8,128)S(1)}, u32[]{:S(2)}, u32[]{:S(2)}) collective-permute-start(f32[1,88,128]{2,1,0:T(8,128)S(1)} %get-tuple-element.35), channel_id=1, source_target_pairs={{0,31},{1,30},{2,5},{3,4},{4,3},{5,2},{6,9},{7,8},{8,7},{9,6},{10,... | collective-permute-start | bytes 135176 | tf_op jit(solution)/shard_map/ppermute | solution.py:684
  19.1 1.1 %shard_map.149 = (bf16[560,240]{1,0:T(8,128)(2,1)S(1)}, bf16[80,240]{1,0:T(8,128)(2,1)S(1)}) custom-call(f32[3,7,7]{2,1,0:T(8,128)S(1)} %copy-done.5, f32[3,7,7]{2,1,0:T(8,128)S(1)} %copy-done.6, bf16[80,240]{1,0:T(8,128)(2,1)S(1)} %copy-done.3, f32[80,7]{1,0:T(8,128)S(1)} %copy-done.4, f32[7,240]{1,0:T(8,128)S(1)} %copy-done.7, f32[80,240]{1,0:T(8,128)S(1)} %copy-done.2), custom_call_target="tpu_custom_call" | custom-call | flops 2000000 | bytes 1000000 | tf_op jit(solution)/shard_map/pallas_call | solution.py:722
  20.2 5.6 %all-to-all-done.got_ref = f32[32,8,128]{2,1,0:T(8,128)S(1)} async-done(((f32[32,8,128]{2,1,0:T(8,128)}), f32[32,8,128]{2,1,0:T(8,128)S(1)}, u32[]{:S(2)}, u32[]{:S(2)}) %all-to-all-start) | async-done | bytes 131104 | tf_op jit(solution)/shard_map/all_to_all | solution.py:709
  25.9 1.7 %shard_map.152 = (f32[3,2,80,128]{3,2,1,0:T(8,128)S(1)}, f32[80,128]{1,0:T(8,128)S(1)}, f32[80,2048]{1,0:T(8,128)S(1)}, f32[80,2048]{1,0:T(8,128)S(1)}) custom-call(bf16[560,240]{1,0:T(8,128)(2,1)S(1)} %get-tuple-element.30.w_ref, f32[88,2048]{1,0:T(8,128)S(1)} %get-tuple-element.31.m_ref, f32[32,8,128]{2,1,0:T(8,128)S(1)} %all-to-all-done.got_ref), custom_call_target="tpu_custom_call" | custom-call | flops 2000000000 | bytes 1000000 | tf_op jit(solution)/shard_map/pallas_call | solution.py:727
  27.6 2.8 %shard_map.153 = (f32[80,2048]{1,0:T(8,128)S(1)}, f32[80,1024]{1,0:T(8,128)S(1)}, f32[1,80,512]{2,1,0:T(8,128)S(1)}, f32[1,80,128]{2,1,0:T(8,128)S(1)}, f32[1,80,128]{2,1,0:T(8,128)S(1)}) custom-call(bf16[560,240]{1,0:T(8,128)(2,1)S(1)} %get-tuple-element.30.w_ref, f32[88,2048]{1,0:T(8,128)S(1)} %get-tuple-element.31.m_ref, ...), custom_call_target="tpu_custom_call" | custom-call | flops 4000000000 | bytes 1000000 | tf_op jit(solution)/shard_map/pallas_call | solution.py:732
  30.5 4.6 %collective-permute-start.5 = (f32[80,1024]{1,0:T(8,128)S(1)}, f32[80,1024]{1,0:T(8,128)S(1)}, u32[]{:S(2)}, u32[]{:S(2)}) collective-permute-start(f32[80,1024]{1,0:T(8,128)S(1)} %get-tuple-element.39), channel_id=1, source_target_pairs={{0,30},{2,4},{4,2},{6,8},{8,6},{10,12},{12,10},{14,16},{16,14},{18... | collective-permute-start | bytes 983048 | tf_op jit(solution)/shard_map/ppermute | solution.py:670
  35.1 1.5 %collective-permute-start.7 = (f32[1,80,512]{2,1,0:T(8,128)S(1)}, f32[1,80,512]{2,1,0:T(8,128)S(1)}, u32[]{:S(2)}, u32[]{:S(2)}) collective-permute-start(f32[1,80,512]{2,1,0:T(8,128)S(1)} %get-tuple-element.40), channel_id=1, source_target_pairs={{0,1},{1,0},{2,3},{3,2},{4,5},{5,4},{6,7},{7,6},{8,9},{9,8},{10,11... | collective-permute-start | bytes 491528 | tf_op jit(solution)/shard_map/ppermute | solution.py:684
  36.6 0.8 %shard_map.154.g_ref = f32[80,2048]{1,0:T(8,128)S(1)} custom-call(bf16[560,240]{1,0:T(8,128)(2,1)S(1)} %get-tuple-element.30.w_ref, f32[88,2048]{1,0:T(8,128)S(1)} %get-tuple-element.31.m_ref, f32[80,2048]{1,0:T(8,128)S(1)} %get-tuple-element.32.f_ref, f32[80,2048]{1,0:T(8,128)S(1)} %get-tuple-element.38.x_ref), custom_call_target="tpu_custom_call" | custom-call | flops 2000000000 | bytes 1000000 | tf_op jit(solution)/shard_map/pallas_call | solution.py:741
  37.4 3.5 %collective-permute-done.9.c_high = f32[1,80,128]{2,1,0:T(8,128)S(1)} collective-permute-done((f32[1,80,128]{2,1,0:T(8,128)S(1)}, f32[1,80,128]{2,1,0:T(8,128)S(1)}, u32[]{:S(2)}, u32[]{:S(2)}) %collective-permute-start.9) | collective-permute-done | bytes 40992 | tf_op jit(solution)/shard_map/ppermute | solution.py:684
  41.3 3.5 %collective-permute-start.10 = (f32[80,1024]{1,0:T(8,128)S(1)}, f32[80,1024]{1,0:T(8,128)S(1)}, u32[]{:S(2)}, u32[]{:S(2)}) collective-permute-start(f32[80,1024]{1,0:T(8,128)S(1)} %shard_map.156), channel_id=1, source_target_pairs={{0,30},{2,4},{4,2},{6,8},{8,6},{10,12},{12,10},{14,16},{16,14},{18... | collective-permute-start | bytes 983048 | tf_op jit(solution)/shard_map/ppermute | solution.py:670
  44.9 2.7 %shard_map.155 = (f32[4,8,128]{2,1,0:T(8,128)S(1)}, f32[4,8,128]{2,1,0:T(8,128)S(1)}, f32[4,8,128]{2,1,0:T(8,128)S(1)}, f32[4,8,128]{2,1,0:T(8,128)S(1)}, f32[80...) custom-call(bf16[560,240]{1,0:T(8,128)(2,1)S(1)} %get-tuple-element.30.w_ref, ...), custom_call_target="tpu_custom_call" | custom-call | flops 4000000000 | bytes 1000000 | tf_op jit(solution)/shard_map/pallas_call | solution.py:745
  47.7 1.8 %collective-permute-start.13 = (f32[4,8,128]{2,1,0:T(8,128)S(1)}, f32[4,8,128]{2,1,0:T(8,128)S(1)}, u32[]{:S(2)}, u32[]{:S(2)}) collective-permute-start(f32[4,8,128]{2,1,0:T(8,128)S(1)} %get-tuple-element.51), channel_id=1, source_target_pairs={{0,6},{2,4},{4,2},{6,0},{8,14},{10,12},{12,10},{14,8},{16,22},{18,... | collective-permute-start | bytes 49160 | tf_op jit(solution)/shard_map/ppermute | solution.py:670
  49.5 2.9 %collective-permute-done.12.refs_2_ = f32[4,8,128]{2,1,0:T(8,128)S(1)} collective-permute-done((f32[4,8,128]{2,1,0:T(8,128)S(1)}, f32[4,8,128]{2,1,0:T(8,128)S(1)}, u32[]{:S(2)}, u32[]{:S(2)}) %collective-permute-start.12) | collective-permute-done | bytes 16416 | tf_op jit(solution)/shard_map/ppermute | solution.py:670
  52.5 2.1 %collective-permute-start.15 = (f32[4,8,128]{2,1,0:T(8,128)S(1)}, f32[4,8,128]{2,1,0:T(8,128)S(1)}, u32[]{:S(2)}, u32[]{:S(2)}) collective-permute-start(f32[4,8,128]{2,1,0:T(8,128)S(1)} %get-tuple-element.54), channel_id=1, source_target_pairs={{0,16},{2,18},{4,20},{6,22},{8,24},{10,26},{12,28},{14,30},{16,0},... | collective-permute-start | bytes 49160 | tf_op jit(solution)/shard_map/ppermute | solution.py:670
  54.6 2.3 %collective-permute-start.16 = (f32[4,8,128]{2,1,0:T(8,128)S(1)}, f32[4,8,128]{2,1,0:T(8,128)S(1)}, u32[]{:S(2)}, u32[]{:S(2)}) collective-permute-start(f32[4,8,128]{2,1,0:T(8,128)S(1)} %get-tuple-element.55), channel_id=1, source_target_pairs={{0,24},{2,26},{4,28},{6,30},{8,16},{10,18},{12,20},{14,22},{16,8},... | collective-permute-start | bytes 49160 | tf_op jit(solution)/shard_map/ppermute | solution.py:670
  56.9 1.3 %shard_map.157 = f32[1232,128]{1,0:T(8,128)} custom-call(bf16[80,240]{1,0:T(8,128)(2,1)S(1)} %get-tuple-element.29.w_ref, f32[8,1024]{1,0:T(8,128)S(1)} %get-tuple-element.44.rates_ref, f32[80,1024]{1,0:T(8,128)S(1)} %get-tuple-element.45.n0_ref, f32[80,1024]{1,0:T(8,128)S(1)} %get-tuple-element.46.h0_ref, f32[80,1024]{1,0:T(8,128)S(1)} %get-tuple-element.47.x1_ref, ...), custom_call_target="tpu_custom_call" | custom-call | flops 2000000 | bytes 1000000 | tf_op jit(solution)/shard_map/pallas_call | solution.py:763
  58.2 2.0 %collective-permute-done.16.refs_3_ = f32[4,8,128]{2,1,0:T(8,128)S(1)} collective-permute-done((f32[4,8,128]{2,1,0:T(8,128)S(1)}, f32[4,8,128]{2,1,0:T(8,128)S(1)}, u32[]{:S(2)}, u32[]{:S(2)}) %collective-permute-start.16) | collective-permute-done | bytes 16416 | tf_op jit(solution)/shard_map/ppermute | solution.py:670
  60.1 0.8 %shard_map.159 = f32[7,32,11]{2,1,0:T(8,128)} custom-call(f32[4,8,128]{2,1,0:T(8,128)S(1)} %get-tuple-element.52.refs_0_, f32[4,8,128]{2,1,0:T(8,128)S(1)} %collective-permute-done.14.refs_1_, f32[4,8,128]{2,1,0:T(8,128)S(1)} %collective-permute-done.15.refs_2_, f32[4,8,128]{2,1,0:T(8,128)S(1)} %collective-permute-done.16.refs_3_), custom_call_target="tpu_custom_call" | custom-call | flops 2000000 | bytes 1000000 | tf_op jit(solution)/shard_map/pallas_call | solution.py:759
  (53 shorter events, 2.7 us)
Async XLA Ops:
  3.5 24.1 %collective-permute-start = (f32[88,2048]{1,0:T(8,128)S(1)}, f32[88,2048]{1,0:T(8,128)S(1)}, u32[]{:S(2)}, u32[]{:S(2)}) collective-permute-start(f32[88,2048]{1,0:T(8,128)S(1)} %get-tuple-element.31.m_ref), channel_id=1, source_target_pairs={{0,30},{2,4},{4,2},{6,8},{8,6},{10,12},{12,10},{14,16},{16,14},{18... | collective-permute-start | bytes 2162696 | tf_op jit(solution)/shard_map/ppermute | solution.py:670
  9.0 18.7 %collective-permute-start.1 = (f32[88,2048]{1,0:T(8,128)S(1)}, f32[88,2048]{1,0:T(8,128)S(1)}, u32[]{:S(2)}, u32[]{:S(2)}) collective-permute-start(f32[88,2048]{1,0:T(8,128)S(1)} %get-tuple-element.31.m_ref), channel_id=1, source_target_pairs={{0,2},{2,0},{4,6},{6,4},{8,10},{10,8},{12,14},{14,12},{16,18},{18,... | collective-permute-start | bytes 2162696 | tf_op jit(solution)/shard_map/ppermute | solution.py:670
  10.7 8.3 %copy-start.2 = (f32[80,240]{1,0:T(8,128)S(1)}, f32[80,240]{1,0:T(8,128)}, u32[]{:S(2)}) copy-start(f32[80,240]{1,0:T(8,128)} %constant.16.clone.diagonal_ref) | copy-start | bytes 230404
  10.7 8.3 %copy-start.3 = (bf16[80,240]{1,0:T(8,128)(2,1)S(1)}, bf16[80,240]{1,0:T(8,128)(2,1)}, u32[]{:S(2)}) copy-start(bf16[80,240]{1,0:T(8,128)(2,1)} %constant.13.clone.spectral_ref) | copy-start | bytes 115204
  10.7 8.3 %copy-start.4 = (f32[80,7]{1,0:T(8,128)S(1)}, f32[80,7]{1,0:T(8,128)}, u32[]{:S(2)}) copy-start(f32[80,7]{1,0:T(8,128)} %constant.14.clone.rows_ref) | copy-start | bytes 6724
  10.7 8.3 %copy-start.5 = (f32[3,7,7]{2,1,0:T(8,128)S(1)}, f32[3,7,7]{2,1,0:T(8,128)}, u32[]{:S(2)}) copy-start(f32[3,7,7]{2,1,0:T(8,128)} %up_ref.1) | copy-start | bytes 1768
  10.7 8.3 %copy-start.6 = (f32[3,7,7]{2,1,0:T(8,128)S(1)}, f32[3,7,7]{2,1,0:T(8,128)}, u32[]{:S(2)}) copy-start(f32[3,7,7]{2,1,0:T(8,128)} %down_ref.1) | copy-start | bytes 1768
  10.8 8.3 %copy-start.7 = (f32[7,240]{1,0:T(8,128)S(1)}, f32[7,240]{1,0:T(8,128)}, u32[]{:S(2)}) copy-start(f32[7,240]{1,0:T(8,128)} %constant.15.clone.lanes_ref) | copy-start | bytes 20164
  10.8 15.1 %all-to-all-start = ((f32[32,8,128]{2,1,0:T(8,128)}), f32[32,8,128]{2,1,0:T(8,128)S(1)}, u32[]{:S(2)}, u32[]{:S(2)}) async-start(f32[32,8,128]{2,1,0:T(8,128)} %shard_map.151), calls=%async_computation | async-start | bytes 262144 | tf_op jit(solution)/shard_map/all_to_all | solution.py:709
  13.5 14.1 %collective-permute-start.2 = (f32[1,88,512]{2,1,0:T(8,128)S(1)}, f32[1,88,512]{2,1,0:T(8,128)S(1)}, u32[]{:S(2)}, u32[]{:S(2)}) collective-permute-start(f32[1,88,512]{2,1,0:T(8,128)S(1)} %get-tuple-element.34), channel_id=1, source_target_pairs={{0,1},{1,0},{2,3},{3,2},{4,5},{5,4},{6,7},{7,6},{8,9},{9,8},{10,11... | collective-permute-start | bytes 540680 | tf_op jit(solution)/shard_map/ppermute | solution.py:684
  15.2 12.4 %collective-permute-start.3 = (f32[1,88,128]{2,1,0:T(8,128)S(1)}, f32[1,88,128]{2,1,0:T(8,128)S(1)}, u32[]{:S(2)}, u32[]{:S(2)}) collective-permute-start(f32[1,88,128]{2,1,0:T(8,128)S(1)} %get-tuple-element.35), channel_id=1, source_target_pairs={{0,31},{1,30},{2,5},{3,4},{4,3},{5,2},{6,9},{7,8},{8,7},{9,6},{10,... | collective-permute-start | bytes 135176 | tf_op jit(solution)/shard_map/ppermute | solution.py:684
  19.0 8.6 %collective-permute-start.4 = (f32[1,88,128]{2,1,0:T(8,128)S(1)}, f32[1,88,128]{2,1,0:T(8,128)S(1)}, u32[]{:S(2)}, u32[]{:S(2)}) collective-permute-start(f32[1,88,128]{2,1,0:T(8,128)S(1)} %get-tuple-element.36), channel_id=1, source_target_pairs={{0,3},{1,2},{2,1},{3,0},{4,7},{5,6},{6,5},{7,4},{8,11},{9,10},{10,... | collective-permute-start | bytes 135176 | tf_op jit(solution)/shard_map/ppermute | solution.py:684
  30.5 14.4 %collective-permute-start.6 = (f32[80,2048]{1,0:T(8,128)S(1)}, f32[80,2048]{1,0:T(8,128)S(1)}, u32[]{:S(2)}, u32[]{:S(2)}) collective-permute-start(f32[80,2048]{1,0:T(8,128)S(1)} %get-tuple-element.38.x_ref), channel_id=1, source_target_pairs={{0,2},{2,0},{4,6},{6,4},{8,10},{10,8},{12,14},{14,12},{16,18},{18,... | collective-permute-start | bytes 1966088 | tf_op jit(solution)/shard_map/ppermute | solution.py:670
  30.5 14.4 %collective-permute-start.5 = (f32[80,1024]{1,0:T(8,128)S(1)}, f32[80,1024]{1,0:T(8,128)S(1)}, u32[]{:S(2)}, u32[]{:S(2)}) collective-permute-start(f32[80,1024]{1,0:T(8,128)S(1)} %get-tuple-element.39), channel_id=1, source_target_pairs={{0,30},{2,4},{4,2},{6,8},{8,6},{10,12},{12,10},{14,16},{16,14},{18... | collective-permute-start | bytes 983048 | tf_op jit(solution)/shard_map/ppermute | solution.py:670
  35.1 6.2 %collective-permute-start.7 = (f32[1,80,512]{2,1,0:T(8,128)S(1)}, f32[1,80,512]{2,1,0:T(8,128)S(1)}, u32[]{:S(2)}, u32[]{:S(2)}) collective-permute-start(f32[1,80,512]{2,1,0:T(8,128)S(1)} %get-tuple-element.40), channel_id=1, source_target_pairs={{0,1},{1,0},{2,3},{3,2},{4,5},{5,4},{6,7},{7,6},{8,9},{9,8},{10,11... | collective-permute-start | bytes 491528 | tf_op jit(solution)/shard_map/ppermute | solution.py:684
  36.6 8.3 %collective-permute-start.8 = (f32[1,80,128]{2,1,0:T(8,128)S(1)}, f32[1,80,128]{2,1,0:T(8,128)S(1)}, u32[]{:S(2)}, u32[]{:S(2)}) collective-permute-start(f32[1,80,128]{2,1,0:T(8,128)S(1)} %get-tuple-element.41), channel_id=1, source_target_pairs={{0,31},{1,30},{2,5},{3,4},{4,3},{5,2},{6,9},{7,8},{8,7},{9,6},{10,... | collective-permute-start | bytes 122888 | tf_op jit(solution)/shard_map/ppermute | solution.py:684
  36.6 4.3 %collective-permute-start.9 = (f32[1,80,128]{2,1,0:T(8,128)S(1)}, f32[1,80,128]{2,1,0:T(8,128)S(1)}, u32[]{:S(2)}, u32[]{:S(2)}) collective-permute-start(f32[1,80,128]{2,1,0:T(8,128)S(1)} %get-tuple-element.42), channel_id=1, source_target_pairs={{0,3},{1,2},{2,1},{3,0},{4,7},{5,6},{6,5},{7,4},{8,11},{9,10},{10,... | collective-permute-start | bytes 122888 | tf_op jit(solution)/shard_map/ppermute | solution.py:684
  41.3 15.5 %collective-permute-start.10 = (f32[80,1024]{1,0:T(8,128)S(1)}, f32[80,1024]{1,0:T(8,128)S(1)}, u32[]{:S(2)}, u32[]{:S(2)}) collective-permute-start(f32[80,1024]{1,0:T(8,128)S(1)} %shard_map.156), channel_id=1, source_target_pairs={{0,30},{2,4},{4,2},{6,8},{8,6},{10,12},{12,10},{14,16},{16,14},{18... | collective-permute-start | bytes 983048 | tf_op jit(solution)/shard_map/ppermute | solution.py:670
  47.6 1.9 %collective-permute-start.11 = (f32[4,8,128]{2,1,0:T(8,128)S(1)}, f32[4,8,128]{2,1,0:T(8,128)S(1)}, u32[]{:S(2)}, u32[]{:S(2)}) collective-permute-start(f32[4,8,128]{2,1,0:T(8,128)S(1)} %get-tuple-element.49), channel_id=1, source_target_pairs={{0,2},{2,0},{4,6},{6,4},{8,10},{10,8},{12,14},{14,12},{16,18},{18,... | collective-permute-start | bytes 49160 | tf_op jit(solution)/shard_map/ppermute | solution.py:670
  47.7 4.7 %collective-permute-start.12 = (f32[4,8,128]{2,1,0:T(8,128)S(1)}, f32[4,8,128]{2,1,0:T(8,128)S(1)}, u32[]{:S(2)}, u32[]{:S(2)}) collective-permute-start(f32[4,8,128]{2,1,0:T(8,128)S(1)} %get-tuple-element.50), channel_id=1, source_target_pairs={{0,4},{2,6},{4,0},{6,2},{8,12},{10,14},{12,8},{14,10},{16,20},{18,... | collective-permute-start | bytes 49160 | tf_op jit(solution)/shard_map/ppermute | solution.py:670
  47.7 4.7 %collective-permute-start.13 = (f32[4,8,128]{2,1,0:T(8,128)S(1)}, f32[4,8,128]{2,1,0:T(8,128)S(1)}, u32[]{:S(2)}, u32[]{:S(2)}) collective-permute-start(f32[4,8,128]{2,1,0:T(8,128)S(1)} %get-tuple-element.51), channel_id=1, source_target_pairs={{0,6},{2,4},{4,2},{6,0},{8,14},{10,12},{12,10},{14,8},{16,22},{18,... | collective-permute-start | bytes 49160 | tf_op jit(solution)/shard_map/ppermute | solution.py:670
  52.4 5.8 %collective-permute-start.14 = (f32[4,8,128]{2,1,0:T(8,128)S(1)}, f32[4,8,128]{2,1,0:T(8,128)S(1)}, u32[]{:S(2)}, u32[]{:S(2)}) collective-permute-start(f32[4,8,128]{2,1,0:T(8,128)S(1)} %get-tuple-element.53), channel_id=1, source_target_pairs={{0,8},{2,10},{4,12},{6,14},{8,0},{10,2},{12,4},{14,6},{16,24},{18,... | collective-permute-start | bytes 49160 | tf_op jit(solution)/shard_map/ppermute | solution.py:670
  52.5 5.7 %collective-permute-start.15 = (f32[4,8,128]{2,1,0:T(8,128)S(1)}, f32[4,8,128]{2,1,0:T(8,128)S(1)}, u32[]{:S(2)}, u32[]{:S(2)}) collective-permute-start(f32[4,8,128]{2,1,0:T(8,128)S(1)} %get-tuple-element.54), channel_id=1, source_target_pairs={{0,16},{2,18},{4,20},{6,22},{8,24},{10,26},{12,28},{14,30},{16,0},... | collective-permute-start | bytes 49160 | tf_op jit(solution)/shard_map/ppermute | solution.py:670
  54.6 5.5 %collective-permute-start.16 = (f32[4,8,128]{2,1,0:T(8,128)S(1)}, f32[4,8,128]{2,1,0:T(8,128)S(1)}, u32[]{:S(2)}, u32[]{:S(2)}) collective-permute-start(f32[4,8,128]{2,1,0:T(8,128)S(1)} %get-tuple-element.55), channel_id=1, source_target_pairs={{0,24},{2,26},{4,28},{6,30},{8,16},{10,18},{12,20},{14,22},{16,8},... | collective-permute-start | bytes 49160 | tf_op jit(solution)/shard_map/ppermute | solution.py:670
  (6 other events, 15.7 us)

commit v13 on v12

--- a/solution.py
+++ b/solution.py
@@ -10,7 +10,6 @@
 from jax.sharding import PartitionSpec as P
 
 SWEEPS = 4
-GROUP = 4
 DEPTH = 2
 LANES = 128
 CHUNK = 256
@@ -39,8 +38,6 @@
         assert len(set(self.shift)) == self.insts and self.cells * WINDOW == LANES and self.rows >= SWEEPS
         assert self.slab % CHUNK == 0 and 3 * self.pad <= 256 and 2 * self.ct * self.width == LANES
         assert sectors % 2 == 0
-        self.groups = sectors // GROUP
-        assert sectors % GROUP == 0 and self.groups & (self.groups - 1) == 0
         self.ends = 1 if spans == 2 else 2
         self.blocks = [-1, 0, 1]
         self.halves = [0, 1] if spans == 2 else [-1, 0, 1]
@@ -563,11 +560,9 @@
 def middle(
     plan, w_ref, m_ref, f_ref, x_ref, g_ref, low_ref, high_ref, side_ref, c_low, c_high,
     low_first, high_first, side_first, seams_ref, weight_ref,
-    *refs,
+    send_ref, n0_ref, h0_ref, x1_ref, rates_ref, p0_ref, p1_ref, y_ref, h1_ref, n1_ref, turn_ref,
 ):
     pad = plan.pad
-    send_refs = refs[:GROUP]
-    n0_ref, h0_ref, x1_ref, rates_ref, p0_ref, p1_ref, y_ref, h1_ref, n1_ref, turn_ref, send_ref = refs[GROUP:]
     own, force = two_layers(plan, x_ref, m_ref), two_layers(plan, f_ref, m_ref)
     low_force = Layer(plan, low_first, 0, None, seams_ref[0, 0], 0)
     high_force = Layer(plan, high_first, plan.slab, None, seams_ref[2, 0], 1)
@@ -614,10 +609,7 @@
     send_ref[...] = jnp.zeros_like(send_ref)
     for t in range(plan.insts):
         to = lax.rem(me + plan.shift[t], plan.sectors)
-        place = (lax.rem(to, GROUP) ^ lax.rem(me, GROUP)) * plan.groups + (lax.div(to, GROUP) ^ lax.div(me, GROUP))
-        send_ref[place, : plan.fields, : plan.width] = back[t * plan.fields : (t + 1) * plan.fields, : plan.width]
-    for i, ref in enumerate(send_refs):
-        ref[...] = send_ref[i * plan.groups : (i + 1) * plan.groups]
+        send_ref[to, : plan.fields, : plan.width] = back[t * plan.fields : (t + 1) * plan.fields, : plan.width]
 
 
 def outer(plan, w_ref, rates_ref, n0_ref, h0_ref, x1_ref, far_ref, out_ref):
@@ -637,22 +629,11 @@
     azimuthal(plan, w_ref, 0, near_chunk, lambda r, terms: put(0, r, h0_ref[:, at(r)] - rates_ref[1:2, at(r)] * terms))
 
 
-def turn_panels(plan, *refs):
-    for i, out_ref in enumerate(refs[GROUP:]):
-        for j, ref in enumerate(refs[:GROUP]):
-            out_ref[j] = ref[i]
-
-
-def collect_panels(plan, *refs):
-    out_ref, tiles_ref, panels_ref = refs[plan.groups :]
-    for i, ref in enumerate(refs[: plan.groups]):
-        tiles_ref[i * GROUP : (i + 1) * GROUP] = ref[...]
+def collect_panels(plan, got_ref, out_ref, panels_ref):
     me = lax.axis_index("sector")
     for t in range(plan.insts):
         source = lax.rem(me + (plan.sectors - plan.shift[t]), plan.sectors)
-        j = lax.rem(source, GROUP) ^ lax.rem(me, GROUP)
-        i = lax.div(source, GROUP) ^ lax.div(me, GROUP)
-        panels_ref[t * RATES : (t + 1) * RATES, :] = tiles_ref[i * GROUP + j]
+        panels_ref[t * RATES : (t + 1) * RATES, :] = got_ref[source]
     for f in range(plan.fields):
         tile = panels_ref[pl.ds(f, plan.insts, stride=RATES), : plan.width]
         out_ref[f] = jnp.transpose(tile)
@@ -741,25 +722,15 @@
     (g,) = call(bind(inner, plan), (whole,), products, flops=2_000_000_000)(matrices, m, force, x)
     far = call(bind(hold_far, plan), half)(x, side, c_high)
     far_low = swap(far, next_chip)
-    tiles = f32(plan.groups, RATES, LANES)
-    *back, n0, h0, x1, rates = call(
-        bind(middle, plan), (tiles,) * GROUP + (half, half, half, f32(RATES, slab)),
-        products + (
-            vmem(pad, 2 * slab), vmem(pad, slab), vmem(pad, slab), vmem(LANES, LANES), vmem(sectors, RATES, LANES),
-        ),
+    back, n0, h0, x1, rates = call(
+        bind(middle, plan), (f32(sectors, RATES, LANES), half, half, half, f32(RATES, slab)),
+        products + (vmem(pad, 2 * slab), vmem(pad, slab), vmem(pad, slab), vmem(LANES, LANES)),
         flops=4_000_000_000,
     )(
         matrices, m, force, x, g, low, high, side, c_low, c_high, low_first, high_first, side_first, seams, weight
     )
-    for j in range(1, GROUP):
-        back[j] = swap(back[j], [s ^ j for s in range(sectors)])
-    back = list(call(bind(turn_panels, plan), (f32(GROUP, RATES, LANES),) * plan.groups)(*back))
-    for i in range(1, plan.groups):
-        back[i] = swap(back[i], [(s // GROUP ^ i) * GROUP + s % GROUP for s in range(sectors)])
-    sens = call(
-        bind(collect_panels, plan), f32(fields, plan.width, insts),
-        (vmem(sectors, RATES, LANES), vmem(insts * RATES, LANES)),
-    )(*back)
+    returned = lax.all_to_all(back, "sector", 0, 0, tiled=True)
+    sens = call(bind(collect_panels, plan), f32(fields, plan.width, insts), (vmem(insts * RATES, LANES),))(returned)
     out = call(bind(outer, plan), f32(plan.tf * cells, LANES))(down, rates, n0, h0, x1, far_low)
     sens = jnp.transpose(sens.reshape(fields, plan.panels, plan.rows, insts), (3, 0, 1, 2))
     return out.reshape(rhs.shape), sens

time: 61.3 us -> 59.8 us (0.976)
  starting transfers between devices: 29.8 us -> 26.9 us
  waiting for transfers between devices: 14.4 us -> 15.1 us
    ppermute x11 -> x5, starting transfers between devices: 20 us -> 13.7 us  [swap(): return lax.ppermute(array, 'sector', list(enumerate(partner)))]
    all_to_all x0 -> x1, waiting for transfers between devices: none -> 5.54 us  [on_device(): returned = lax.all_to_all(back, 'sector', 0, 0, tiled=True)]
    ppermute x11 -> x5, waiting for transfers between devices: 4.86 us -> 0.01 us  [swap(): return lax.ppermute(array, 'sector', list(enumerate(partner)))]
    all_to_all x0 -> x1, starting transfers between devices: none -> 3.5 us  [on_device(): returned = lax.all_to_all(back, 'sector', 0, 0, tiled=True)]
    pallas_call x3 -> x2, Pallas kernels: 3.52 us -> 4.09 us  [the longest x1 3.32 us: on_device(): call(bind(middle, plan), (f32(sectors, RATES, LANES), half, half, half, f...]
    unnamed x24 -> x32, local copies, waits for them, and re-layouts: 1.74 us -> 1.76 us
  transfers between devices with their start and end apart: 18 -> 13, of which waited for: 5 -> 4; matrix products, arithmetic and copies ran while one was open for 0% -> 0% of each run, Pallas kernels for 14% -> 15%
where the time goes in v13:
time: 59.8 us; the launch traced here: 59.4 us
  starting transfers between devices  26.9 us (45%)
  waiting for transfers between devices  15.1 us (25%)
  Pallas kernels  13 us (22%)
  local copies, waits for them, and re-layouts  1.92 us (3%)
  other arithmetic  1.54 us (3%)
  between operations  0.88 us (1%)
    ppermute x5, starting transfers between devices, swap(): return lax.ppermute(array, 'sector', list(enumerate(partner)))  13.7 us
    ppermute x6, starting transfers between devices, beside(): return lax.ppermute(array, AXES, pairs(0))  7.05 us
    all_to_all x1, waiting for transfers between devices, on_device(): got = lax.all_to_all(sent, AXES, 0, 0, tiled=True)  5.64 us
    all_to_all x1, waiting for transfers between devices, on_device(): returned = lax.all_to_all(back, 'sector', 0, 0, tiled=True)  5.54 us
    ppermute x6, waiting for transfers between devices, beside(): return lax.ppermute(array, AXES, pairs(0))  3.87 us
    all_to_all x1, starting transfers between devices, on_device(): returned = lax.all_to_all(back, 'sector', 0, 0, tiled=True)  3.5 us
    pallas_call x1, Pallas kernels, on_device(): call(bind(middle, plan), (f32(sectors, RATES, LANES), half, half, half, f...  3.32 us
    pallas_call x1, Pallas kernels, on_device(): call(bind(first_half, plan), (whole, half) + edges(pad), products + (vmem...  2.79 us
  transfers between devices with their start and end apart: 13, of which 4 were waited for; matrix products, arithmetic and copies ran while one was open for 0% of the time, Pallas kernels for 15%

profile of v13, /device:TPU:0, one launch (start us, length us, event | category | flops | bytes accessed | tf_op | source)
XLA Modules:
  0.0 59.4 jit_solution(14281214806632074552)
XLA Ops:
  0.7 0.7 %convert_bitcast_fusion = f32[16,128]{1,0:T(8,128)S(1)} fusion(s32[2,8,128]{2,1,0:T(8,128)} %param.20), kind=kLoop, calls=%fused_computation.7 | loop fusion | flops 2048 | bytes 16384 | tf_op jit(solution)/shard_map/reshape | solution.py:696
  1.4 0.7 %pad_maximum_fusion.coef_ref = f32[96,128]{1,0:T(8,128)S(1)} fusion(f32[48,128]{1,0:T(8,128)} %bitcast.20, f32[16,128]{1,0:T(8,128)S(1)} %bitcast.21, f32[16,128]{1,0:T(8,128)S(1)} %bitcast.22, f32[16,128]{1,0:T(8,128)S(1)} %convert_bitcast_fusion), kind=kLoop, calls=%fused_computation | loop fusion | flops 36864 | bytes 98304 | tf_op jit(solution)/shard_map/concatenate | solution.py:695
  2.1 1.1 %copy-done = f32[11,7,2,8,128]{4,3,2,1,0:T(8,128)S(1)} copy-done((f32[11,7,2,8,128]{4,3,2,1,0:T(8,128)S(1)}, f32[11,7,2,8,128]{4,3,2,1,0:T(8,128)}, u32[]{:S(2)}) %copy-start) | copy-done | bytes 630808
  3.5 5.5 %collective-permute-start = (f32[88,2048]{1,0:T(8,128)S(1)}, f32[88,2048]{1,0:T(8,128)S(1)}, u32[]{:S(2)}, u32[]{:S(2)}) collective-permute-start(f32[88,2048]{1,0:T(8,128)S(1)} %get-tuple-element.24.m_ref), channel_id=1, source_target_pairs={{0,30},{2,4},{4,2},{6,8},{8,6},{10,12},{12,10},{14,16},{16,14},{18... | collective-permute-start | bytes 2162696 | tf_op jit(solution)/shard_map/ppermute | solution.py:651
  9.1 0.6 %copy-done.15 = s32[11,2,8]{0,2,1:T(8,128)S(1)} copy-done((s32[11,2,8]{0,2,1:T(8,128)S(1)}, s32[11,2,8]{0,2,1:T(8,128)}, u32[]{:S(2)}) %copy-start.15) | copy-done | bytes 728
  9.9 0.9 %shard_map.151 = f32[32,8,128]{2,1,0:T(8,128)} custom-call(f32[7,32,11]{2,1,0:T(8,128)S(1)} %bitcast.17, f32[11,32]{1,0:T(8,128)S(1)} %pad_maximum_fusion.1.both_ref), custom_call_target="tpu_custom_call" | custom-call | flops 2000000 | bytes 1000000 | tf_op jit(solution)/shard_map/pallas_call | solution.py:684
  10.8 2.7 %all-to-all-start = ((f32[32,8,128]{2,1,0:T(8,128)}), f32[32,8,128]{2,1,0:T(8,128)S(1)}, u32[]{:S(2)}, u32[]{:S(2)}) async-start(f32[32,8,128]{2,1,0:T(8,128)} %shard_map.151), calls=%async_computation | async-start | bytes 262144 | tf_op jit(solution)/shard_map/all_to_all | solution.py:690
  13.5 1.7 %collective-permute-start.2 = (f32[1,88,512]{2,1,0:T(8,128)S(1)}, f32[1,88,512]{2,1,0:T(8,128)S(1)}, u32[]{:S(2)}, u32[]{:S(2)}) collective-permute-start(f32[1,88,512]{2,1,0:T(8,128)S(1)} %get-tuple-element.27), channel_id=1, source_target_pairs={{0,1},{1,0},{2,3},{3,2},{4,5},{5,4},{6,7},{7,6},{8,9},{9,8},{10,11... | collective-permute-start | bytes 540680 | tf_op jit(solution)/shard_map/ppermute | solution.py:665
  15.2 3.9 %collective-permute-start.3 = (f32[1,88,128]{2,1,0:T(8,128)S(1)}, f32[1,88,128]{2,1,0:T(8,128)S(1)}, u32[]{:S(2)}, u32[]{:S(2)}) collective-permute-start(f32[1,88,128]{2,1,0:T(8,128)S(1)} %get-tuple-element.28), channel_id=1, source_target_pairs={{0,31},{1,30},{2,5},{3,4},{4,3},{5,2},{6,9},{7,8},{8,7},{9,6},{10,... | collective-permute-start | bytes 135176 | tf_op jit(solution)/shard_map/ppermute | solution.py:665
  19.1 1.1 %shard_map.149 = (bf16[560,240]{1,0:T(8,128)(2,1)S(1)}, bf16[80,240]{1,0:T(8,128)(2,1)S(1)}) custom-call(f32[3,7,7]{2,1,0:T(8,128)S(1)} %copy-done.5, f32[3,7,7]{2,1,0:T(8,128)S(1)} %copy-done.6, bf16[80,240]{1,0:T(8,128)(2,1)S(1)} %copy-done.3, f32[80,7]{1,0:T(8,128)S(1)} %copy-done.4, f32[7,240]{1,0:T(8,128)S(1)} %copy-done.7, f32[80,240]{1,0:T(8,128)S(1)} %copy-done.2), custom_call_target="tpu_custom_call" | custom-call | flops 2000000 | bytes 1000000 | tf_op jit(solution)/shard_map/pallas_call | solution.py:703
  20.2 5.6 %all-to-all-done.got_ref = f32[32,8,128]{2,1,0:T(8,128)S(1)} async-done(((f32[32,8,128]{2,1,0:T(8,128)}), f32[32,8,128]{2,1,0:T(8,128)S(1)}, u32[]{:S(2)}, u32[]{:S(2)}) %all-to-all-start) | async-done | bytes 131104 | tf_op jit(solution)/shard_map/all_to_all | solution.py:690
  25.9 1.7 %shard_map.152 = (f32[3,2,80,128]{3,2,1,0:T(8,128)S(1)}, f32[80,128]{1,0:T(8,128)S(1)}, f32[80,2048]{1,0:T(8,128)S(1)}, f32[80,2048]{1,0:T(8,128)S(1)}) custom-call(bf16[560,240]{1,0:T(8,128)(2,1)S(1)} %get-tuple-element.23.w_ref, f32[88,2048]{1,0:T(8,128)S(1)} %get-tuple-element.24.m_ref, f32[32,8,128]{2,1,0:T(8,128)S(1)} %all-to-all-done.got_ref), custom_call_target="tpu_custom_call" | custom-call | flops 2000000000 | bytes 1000000 | tf_op jit(solution)/shard_map/pallas_call | solution.py:708
  27.7 2.8 %shard_map.153 = (f32[80,2048]{1,0:T(8,128)S(1)}, f32[80,1024]{1,0:T(8,128)S(1)}, f32[1,80,512]{2,1,0:T(8,128)S(1)}, f32[1,80,128]{2,1,0:T(8,128)S(1)}, f32[1,80,128]{2,1,0:T(8,128)S(1)}) custom-call(bf16[560,240]{1,0:T(8,128)(2,1)S(1)} %get-tuple-element.23.w_ref, f32[88,2048]{1,0:T(8,128)S(1)} %get-tuple-element.24.m_ref, ...), custom_call_target="tpu_custom_call" | custom-call | flops 4000000000 | bytes 1000000 | tf_op jit(solution)/shard_map/pallas_call | solution.py:713
  30.5 4.6 %collective-permute-start.5 = (f32[80,1024]{1,0:T(8,128)S(1)}, f32[80,1024]{1,0:T(8,128)S(1)}, u32[]{:S(2)}, u32[]{:S(2)}) collective-permute-start(f32[80,1024]{1,0:T(8,128)S(1)} %get-tuple-element.32), channel_id=1, source_target_pairs={{0,30},{2,4},{4,2},{6,8},{8,6},{10,12},{12,10},{14,16},{16,14},{18... | collective-permute-start | bytes 983048 | tf_op jit(solution)/shard_map/ppermute | solution.py:651
  35.1 1.5 %collective-permute-start.7 = (f32[1,80,512]{2,1,0:T(8,128)S(1)}, f32[1,80,512]{2,1,0:T(8,128)S(1)}, u32[]{:S(2)}, u32[]{:S(2)}) collective-permute-start(f32[1,80,512]{2,1,0:T(8,128)S(1)} %get-tuple-element.33), channel_id=1, source_target_pairs={{0,1},{1,0},{2,3},{3,2},{4,5},{5,4},{6,7},{7,6},{8,9},{9,8},{10,11... | collective-permute-start | bytes 491528 | tf_op jit(solution)/shard_map/ppermute | solution.py:665
  36.6 0.8 %shard_map.154.g_ref = f32[80,2048]{1,0:T(8,128)S(1)} custom-call(bf16[560,240]{1,0:T(8,128)(2,1)S(1)} %get-tuple-element.23.w_ref, f32[88,2048]{1,0:T(8,128)S(1)} %get-tuple-element.24.m_ref, f32[80,2048]{1,0:T(8,128)S(1)} %get-tuple-element.25.f_ref, f32[80,2048]{1,0:T(8,128)S(1)} %get-tuple-element.31.x_ref), custom_call_target="tpu_custom_call" | custom-call | flops 2000000000 | bytes 1000000 | tf_op jit(solution)/shard_map/pallas_call | solution.py:722
  37.5 3.4 %collective-permute-done.9.c_high = f32[1,80,128]{2,1,0:T(8,128)S(1)} collective-permute-done((f32[1,80,128]{2,1,0:T(8,128)S(1)}, f32[1,80,128]{2,1,0:T(8,128)S(1)}, u32[]{:S(2)}, u32[]{:S(2)}) %collective-permute-start.9) | collective-permute-done | bytes 40992 | tf_op jit(solution)/shard_map/ppermute | solution.py:665
  40.9 0.4 collective-permute-done.7.side_ref
  41.4 3.5 %collective-permute-start.10 = (f32[80,1024]{1,0:T(8,128)S(1)}, f32[80,1024]{1,0:T(8,128)S(1)}, u32[]{:S(2)}, u32[]{:S(2)}) collective-permute-start(f32[80,1024]{1,0:T(8,128)S(1)} %shard_map.156), channel_id=1, source_target_pairs={{0,30},{2,4},{4,2},{6,8},{8,6},{10,12},{12,10},{14,16},{16,14},{18... | collective-permute-start | bytes 983048 | tf_op jit(solution)/shard_map/ppermute | solution.py:651
  44.9 3.3 %shard_map.155 = (f32[16,8,128]{2,1,0:T(8,128)}, f32[80,1024]{1,0:T(8,128)S(1)}, f32[80,1024]{1,0:T(8,128)S(1)}, f32[80,1024]{1,0:T(8,128)S(1)}, f32[8,1024]{1,0:T(8,128)S(1)}) custom-call(bf16[560,240]{1,0:T(8,128)(2,1)S(1)} %get-tuple-element.23.w_ref, f32[88,2048]{1,0:T(8,128)S(1)} %get-tuple-element.24.m_ref, f32[80,2048]{1,0:T(8,128)S(1)} %get-tuple-element.25.f_ref, ...), custom_call_target="tpu_custom_call" | custom-call | flops 4000000000 | bytes 1000000 | tf_op jit(solution)/shard_map/pallas_call | solution.py:725
  48.2 3.5 %all-to-all-start.1 = ((f32[16,8,128]{2,1,0:T(8,128)}), f32[16,8,128]{2,1,0:T(8,128)S(1)}, u32[]{:S(2)}, u32[]{:S(2)}) async-start(f32[16,8,128]{2,1,0:T(8,128)} %get-tuple-element.41), calls=%async_computation.1 | async-start | bytes 131072 | tf_op jit(solution)/shard_map/all_to_all | solution.py:732
  51.8 1.3 %shard_map.157 = f32[1232,128]{1,0:T(8,128)} custom-call(bf16[80,240]{1,0:T(8,128)(2,1)S(1)} %get-tuple-element.22.w_ref, f32[8,1024]{1,0:T(8,128)S(1)} %get-tuple-element.37.rates_ref, f32[80,1024]{1,0:T(8,128)S(1)} %get-tuple-element.38.n0_ref, f32[80,1024]{1,0:T(8,128)S(1)} %get-tuple-element.39.h0_ref, f32[80,1024]{1,0:T(8,128)S(1)} %get-tuple-element.40.x1_ref, ...), custom_call_target="tpu_custom_call" | custom-call | flops 2000000 | bytes 1000000 | tf_op jit(solution)/shard_map/pallas_call | solution.py:734
  53.1 5.5 %all-to-all-done.1.got_ref = f32[16,8,128]{2,1,0:T(8,128)S(1)} async-done(((f32[16,8,128]{2,1,0:T(8,128)}), f32[16,8,128]{2,1,0:T(8,128)S(1)}, u32[]{:S(2)}, u32[]{:S(2)}) %all-to-all-start.1) | async-done | bytes 65568 | tf_op jit(solution)/shard_map/all_to_all | solution.py:732
  58.6 0.8 %shard_map.158 = f32[7,32,11]{2,1,0:T(8,128)} custom-call(f32[16,8,128]{2,1,0:T(8,128)S(1)} %all-to-all-done.1.got_ref), custom_call_target="tpu_custom_call" | custom-call | flops 2000000 | bytes 1000000 | tf_op jit(solution)/shard_map/pallas_call | solution.py:733
  (50 shorter events, 0.8 us)
Async XLA Ops:
  3.2 5.8 %copy-start.14 = (f32[11,2,8]{0,2,1:T(8,128)S(1)}, f32[11,2,8]{0,2,1:T(8,128)}, u32[]{:S(2)}) copy-start(f32[11,2,8]{0,2,1:T(8,128)} %param.23) | copy-start | bytes 2116
  3.2 6.7 %copy-start.1 = (f32[11,7,4,8]{0,3,2,1:T(8,128)S(1)}, f32[11,7,4,8]{0,3,2,1:T(8,128)}, u32[]{:S(2)}) copy-start(f32[11,7,4,8]{0,3,2,1:T(8,128)} %param.21) | copy-start | bytes 29572
  3.5 24.2 %collective-permute-start = (f32[88,2048]{1,0:T(8,128)S(1)}, f32[88,2048]{1,0:T(8,128)S(1)}, u32[]{:S(2)}, u32[]{:S(2)}) collective-permute-start(f32[88,2048]{1,0:T(8,128)S(1)} %get-tuple-element.24.m_ref), channel_id=1, source_target_pairs={{0,30},{2,4},{4,2},{6,8},{8,6},{10,12},{12,10},{14,16},{16,14},{18... | collective-permute-start | bytes 2162696 | tf_op jit(solution)/shard_map/ppermute | solution.py:651
  9.0 18.7 %collective-permute-start.1 = (f32[88,2048]{1,0:T(8,128)S(1)}, f32[88,2048]{1,0:T(8,128)S(1)}, u32[]{:S(2)}, u32[]{:S(2)}) collective-permute-start(f32[88,2048]{1,0:T(8,128)S(1)} %get-tuple-element.24.m_ref), channel_id=1, source_target_pairs={{0,2},{2,0},{4,6},{6,4},{8,10},{10,8},{12,14},{14,12},{16,18},{18,... | collective-permute-start | bytes 2162696 | tf_op jit(solution)/shard_map/ppermute | solution.py:651
  10.7 8.3 %copy-start.2 = (f32[80,240]{1,0:T(8,128)S(1)}, f32[80,240]{1,0:T(8,128)}, u32[]{:S(2)}) copy-start(f32[80,240]{1,0:T(8,128)} %constant.16.clone.diagonal_ref) | copy-start | bytes 230404
  10.7 8.3 %copy-start.3 = (bf16[80,240]{1,0:T(8,128)(2,1)S(1)}, bf16[80,240]{1,0:T(8,128)(2,1)}, u32[]{:S(2)}) copy-start(bf16[80,240]{1,0:T(8,128)(2,1)} %constant.13.clone.spectral_ref) | copy-start | bytes 115204
  10.7 8.3 %copy-start.4 = (f32[80,7]{1,0:T(8,128)S(1)}, f32[80,7]{1,0:T(8,128)}, u32[]{:S(2)}) copy-start(f32[80,7]{1,0:T(8,128)} %constant.14.clone.rows_ref) | copy-start | bytes 6724
  10.7 8.3 %copy-start.5 = (f32[3,7,7]{2,1,0:T(8,128)S(1)}, f32[3,7,7]{2,1,0:T(8,128)}, u32[]{:S(2)}) copy-start(f32[3,7,7]{2,1,0:T(8,128)} %up_ref.1) | copy-start | bytes 1768
  10.7 8.3 %copy-start.6 = (f32[3,7,7]{2,1,0:T(8,128)S(1)}, f32[3,7,7]{2,1,0:T(8,128)}, u32[]{:S(2)}) copy-start(f32[3,7,7]{2,1,0:T(8,128)} %down_ref.1) | copy-start | bytes 1768
  10.8 8.3 %copy-start.7 = (f32[7,240]{1,0:T(8,128)S(1)}, f32[7,240]{1,0:T(8,128)}, u32[]{:S(2)}) copy-start(f32[7,240]{1,0:T(8,128)} %constant.15.clone.lanes_ref) | copy-start | bytes 20164
  10.8 15.1 %all-to-all-start = ((f32[32,8,128]{2,1,0:T(8,128)}), f32[32,8,128]{2,1,0:T(8,128)S(1)}, u32[]{:S(2)}, u32[]{:S(2)}) async-start(f32[32,8,128]{2,1,0:T(8,128)} %shard_map.151), calls=%async_computation | async-start | bytes 262144 | tf_op jit(solution)/shard_map/all_to_all | solution.py:690
  13.5 14.1 %collective-permute-start.2 = (f32[1,88,512]{2,1,0:T(8,128)S(1)}, f32[1,88,512]{2,1,0:T(8,128)S(1)}, u32[]{:S(2)}, u32[]{:S(2)}) collective-permute-start(f32[1,88,512]{2,1,0:T(8,128)S(1)} %get-tuple-element.27), channel_id=1, source_target_pairs={{0,1},{1,0},{2,3},{3,2},{4,5},{5,4},{6,7},{7,6},{8,9},{9,8},{10,11... | collective-permute-start | bytes 540680 | tf_op jit(solution)/shard_map/ppermute | solution.py:665
  15.2 12.4 %collective-permute-start.3 = (f32[1,88,128]{2,1,0:T(8,128)S(1)}, f32[1,88,128]{2,1,0:T(8,128)S(1)}, u32[]{:S(2)}, u32[]{:S(2)}) collective-permute-start(f32[1,88,128]{2,1,0:T(8,128)S(1)} %get-tuple-element.28), channel_id=1, source_target_pairs={{0,31},{1,30},{2,5},{3,4},{4,3},{5,2},{6,9},{7,8},{8,7},{9,6},{10,... | collective-permute-start | bytes 135176 | tf_op jit(solution)/shard_map/ppermute | solution.py:665
  19.0 8.6 %collective-permute-start.4 = (f32[1,88,128]{2,1,0:T(8,128)S(1)}, f32[1,88,128]{2,1,0:T(8,128)S(1)}, u32[]{:S(2)}, u32[]{:S(2)}) collective-permute-start(f32[1,88,128]{2,1,0:T(8,128)S(1)} %get-tuple-element.29), channel_id=1, source_target_pairs={{0,3},{1,2},{2,1},{3,0},{4,7},{5,6},{6,5},{7,4},{8,11},{9,10},{10,... | collective-permute-start | bytes 135176 | tf_op jit(solution)/shard_map/ppermute | solution.py:665
  27.6 2.8 %copy-start.10 = (f32[1,88,512]{2,1,0:T(8,128)}, f32[1,88,512]{2,1,0:T(8,128)S(1)}, u32[]{:S(2)}) copy-start(f32[1,88,512]{2,1,0:T(8,128)S(1)} %collective-permute-done.2.side_ref.side_first) | copy-start | bytes 540676
  30.5 14.4 %collective-permute-start.6 = (f32[80,2048]{1,0:T(8,128)S(1)}, f32[80,2048]{1,0:T(8,128)S(1)}, u32[]{:S(2)}, u32[]{:S(2)}) collective-permute-start(f32[80,2048]{1,0:T(8,128)S(1)} %get-tuple-element.31.x_ref), channel_id=1, source_target_pairs={{0,2},{2,0},{4,6},{6,4},{8,10},{10,8},{12,14},{14,12},{16,18},{18,... | collective-permute-start | bytes 1966088 | tf_op jit(solution)/shard_map/ppermute | solution.py:651
  30.5 14.4 %collective-permute-start.5 = (f32[80,1024]{1,0:T(8,128)S(1)}, f32[80,1024]{1,0:T(8,128)S(1)}, u32[]{:S(2)}, u32[]{:S(2)}) collective-permute-start(f32[80,1024]{1,0:T(8,128)S(1)} %get-tuple-element.32), channel_id=1, source_target_pairs={{0,30},{2,4},{4,2},{6,8},{8,6},{10,12},{12,10},{14,16},{16,14},{18... | collective-permute-start | bytes 983048 | tf_op jit(solution)/shard_map/ppermute | solution.py:651
  35.1 6.2 %collective-permute-start.7 = (f32[1,80,512]{2,1,0:T(8,128)S(1)}, f32[1,80,512]{2,1,0:T(8,128)S(1)}, u32[]{:S(2)}, u32[]{:S(2)}) collective-permute-start(f32[1,80,512]{2,1,0:T(8,128)S(1)} %get-tuple-element.33), channel_id=1, source_target_pairs={{0,1},{1,0},{2,3},{3,2},{4,5},{5,4},{6,7},{7,6},{8,9},{9,8},{10,11... | collective-permute-start | bytes 491528 | tf_op jit(solution)/shard_map/ppermute | solution.py:665
  36.6 8.3 %collective-permute-start.8 = (f32[1,80,128]{2,1,0:T(8,128)S(1)}, f32[1,80,128]{2,1,0:T(8,128)S(1)}, u32[]{:S(2)}, u32[]{:S(2)}) collective-permute-start(f32[1,80,128]{2,1,0:T(8,128)S(1)} %get-tuple-element.34), channel_id=1, source_target_pairs={{0,31},{1,30},{2,5},{3,4},{4,3},{5,2},{6,9},{7,8},{8,7},{9,6},{10,... | collective-permute-start | bytes 122888 | tf_op jit(solution)/shard_map/ppermute | solution.py:665
  36.6 4.3 %collective-permute-start.9 = (f32[1,80,128]{2,1,0:T(8,128)S(1)}, f32[1,80,128]{2,1,0:T(8,128)S(1)}, u32[]{:S(2)}, u32[]{:S(2)}) collective-permute-start(f32[1,80,128]{2,1,0:T(8,128)S(1)} %get-tuple-element.35), channel_id=1, source_target_pairs={{0,3},{1,2},{2,1},{3,0},{4,7},{5,6},{6,5},{7,4},{8,11},{9,10},{10,... | collective-permute-start | bytes 122888 | tf_op jit(solution)/shard_map/ppermute | solution.py:665
  37.4 7.5 %copy-start.9 = (f32[88,2048]{1,0:T(8,128)S(1)}, f32[88,2048]{1,0:T(8,128)}, u32[]{:S(2)}) copy-start(f32[88,2048]{1,0:T(8,128)} %copy-done.8) | copy-start | bytes 2162692
  37.4 7.5 %copy-start.11 = (f32[1,88,512]{2,1,0:T(8,128)S(1)}, f32[1,88,512]{2,1,0:T(8,128)}, u32[]{:S(2)}) copy-start(f32[1,88,512]{2,1,0:T(8,128)} %copy-done.10) | copy-start | bytes 540676
  41.4 10.4 %collective-permute-start.10 = (f32[80,1024]{1,0:T(8,128)S(1)}, f32[80,1024]{1,0:T(8,128)S(1)}, u32[]{:S(2)}, u32[]{:S(2)}) collective-permute-start(f32[80,1024]{1,0:T(8,128)S(1)} %shard_map.156), channel_id=1, source_target_pairs={{0,30},{2,4},{4,2},{6,8},{8,6},{10,12},{12,10},{14,16},{16,14},{18... | collective-permute-start | bytes 983048 | tf_op jit(solution)/shard_map/ppermute | solution.py:651
  48.2 10.4 %all-to-all-start.1 = ((f32[16,8,128]{2,1,0:T(8,128)}), f32[16,8,128]{2,1,0:T(8,128)S(1)}, u32[]{:S(2)}, u32[]{:S(2)}) async-start(f32[16,8,128]{2,1,0:T(8,128)} %get-tuple-element.41), calls=%async_computation.1 | async-start | bytes 131072 | tf_op jit(solution)/shard_map/all_to_all | solution.py:732
  (5 other events, 6.0 us)

commit v14 on v13

--- a/solution.py
+++ b/solution.py
@@ -16,7 +16,7 @@
 WINDOW = 8
 HIGHEST = lax.Precision.HIGHEST
 DOWN_AZ, SPECTRAL, UP_SP, DOWN_SP, UP_AX, DOWN_AX, UP_AZ = range(7)
-C_TIME, C_AZ, C_SP, C_UP, C_DOWN, C_MASK = range(6)
+C_TIME, C_AZ, C_SP, C_UP, C_DOWN, C_MASK, C_OTHER = range(7)
 RATES = 8
 AXES = ("sector", "span")
 
@@ -176,6 +176,8 @@
         self.rates = rates or (ref, start)
 
     def rate(self, which, r, count=1):
+        if isinstance(self.rates, Layer):
+            return self.rates.rate(which, r, count)
         ref, start = self.rates
         row = self.plan.pad + which
         return ref[row : row + 1, at(r, count, start)]
@@ -191,6 +193,23 @@
         if self.seam is None:
             return self.ref[: self.plan.pad, at(c * count, count, self.start)]
         return jnp.concatenate([self.row(c * count + part) for part in range(count)], axis=1)
+
+
+class Native(Layer):
+    def __init__(self, plan, ref, table, seam, layer, near):
+        super().__init__(plan, ref, 0, None, seam, layer)
+        self.table, self.near = table, near
+
+    def rate(self, which, r, count=1):
+        row = which if self.near else C_OTHER
+        return self.table[row : row + 1, at(r, count)]
+
+    def row(self, r):
+        plan = self.plan
+        there = jnp.where(parity() == 1, self.layer, plan.ct - 1 - self.layer) * plan.rows + r
+        field = self.ref[pl.ds(there, plan.tf, stride=plan.cells), :]
+        field = jnp.concatenate([field, jnp.zeros((plan.pad - plan.tf, LANES), jnp.float32)], axis=0)
+        return (field + placed(self.seam, self.layer * plan.rows + r)) * self.rate(C_MASK, r)
 
 
 def placed(tile, cell):
@@ -386,7 +405,7 @@
     return corner
 
 
-def prepare(plan, rhs_ref, coef_ref, m_ref, side_ref, c0_ref, c1_ref, rates_ref):
+def prepare(plan, rhs_ref, coef_ref, m_ref, table0_ref, table1_ref, side_ref, c0_ref, c1_ref, rates_ref):
     pad, cells = plan.pad, plan.cells
     mask, diag, time, *face = [coef_ref[cells * i : cells * (i + 1), :] for i in range(6)]
     scale = mask / diag
@@ -408,6 +427,9 @@
         field = jnp.concatenate([rhs_ref[pl.ds(there, plan.tf, stride=cells), :], tail], axis=0)
         m_ref[:pad, at(cell)] = field * table[C_MASK]
         m_ref[pad:, at(cell)] = jnp.concatenate(table + [rest], axis=0)
+        other = jnp.where(mirror == 0, plan.ct - 1 - a, a) * plan.rows + r
+        table = table + [rates_ref[C_MASK, pl.ds(other, 1), :], rest[:1]]
+        (table0_ref, table1_ref)[a][:, at(r)] = jnp.concatenate(table, axis=0)
     write_edges(plan, m_ref, side_ref, (c0_ref, c1_ref))
 
 
@@ -519,12 +541,12 @@
 
 
 def first_half(
-    plan, w_ref, m_ref, f_ref, g_ref, low_ref, high_ref, side_ref, c_low, c_high, seams_ref,
+    plan, w_ref, m_ref, f_ref, g_ref, low_ref, high_ref, low_table, high_table, side_ref, c_low, c_high, seams_ref,
     x_ref, near_ref, side_out, c0_ref, c1_ref, p0_ref, p1_ref, y_ref, h0_ref, h1_ref, n0_ref, n1_ref, inlet_ref,
 ):
     own = two_layers(plan, f_ref, m_ref)
-    low = two_layers(plan, low_ref, seam=seams_ref[0, 0])
-    high = two_layers(plan, high_ref, seam=seams_ref[2, 0])
+    low = [Native(plan, low_ref, low_table, seams_ref[0, 0], a, a == 0) for a in range(plan.ct)]
+    high = [Native(plan, high_ref, high_table, seams_ref[2, 0], a, a == 1) for a in range(plan.ct)]
     near = low[0], high[1]
     n_refs = n0_ref, n1_ref
     middle_rows(
@@ -559,14 +581,14 @@
 
 def middle(
     plan, w_ref, m_ref, f_ref, x_ref, g_ref, low_ref, high_ref, side_ref, c_low, c_high,
-    low_first, high_first, side_first, seams_ref, weight_ref,
+    low_first, high_first, low_table, high_table, side_first, seams_ref, weight_ref,
     send_ref, n0_ref, h0_ref, x1_ref, rates_ref, p0_ref, p1_ref, y_ref, h1_ref, n1_ref, turn_ref,
 ):
     pad = plan.pad
     own, force = two_layers(plan, x_ref, m_ref), two_layers(plan, f_ref, m_ref)
-    low_force = Layer(plan, low_first, 0, None, seams_ref[0, 0], 0)
-    high_force = Layer(plan, high_first, plan.slab, None, seams_ref[2, 0], 1)
-    near = Layer(plan, low_ref, 0, low_force.rates), Layer(plan, high_ref, plan.slab, high_force.rates)
+    low_force = Native(plan, low_first, low_table, seams_ref[0, 0], 0, True)
+    high_force = Native(plan, high_first, high_table, seams_ref[2, 0], 1, True)
+    near = Layer(plan, low_ref, 0, low_force), Layer(plan, high_ref, plan.slab, high_force)
     n_refs = n0_ref, n1_ref
     middle_rows(
         plan, w_ref, (p0_ref, p1_ref), own, force, g_ref, near, (low_force, high_force),
@@ -688,16 +710,20 @@
         ], axis=1),
     )
     got = lax.all_to_all(sent, AXES, 0, 0, tiled=True)
-    m, side, c0, c1 = call(
-        bind(prepare, plan), (f32(pad + RATES, plan.ct * slab),) + edges(pad + RATES), (vmem(6, cells, LANES),)
+    native = rhs.reshape(plan.tf * cells, LANES)
+    low_first, high_first = swap(native, next_chip), swap(native, next_core)
+    m, table0, table1, side, c0, c1 = call(
+        bind(prepare, plan),
+        (f32(pad + RATES, plan.ct * slab), f32(RATES, slab), f32(RATES, slab)) + edges(pad + RATES),
+        (vmem(6, cells, LANES),),
     )(
-        rhs.reshape(plan.tf * cells, LANES),
+        native,
         jnp.concatenate([
             wall_mask.astype(jnp.float32).reshape(cells, LANES), diag_coef.reshape(cells, LANES),
             time_coef.reshape(cells, LANES), face_coef.reshape(3 * cells, LANES),
         ]),
     )
-    low_first, high_first = swap(m, next_chip), swap(m, next_core)
+    low_table, high_table = swap(table0, next_chip), swap(table1, next_core)
     side_first = beside(plan, side, alone)
     c_low, c_high = beside(plan, c0, next_chip), beside(plan, c1, next_core)
     matrices, down = call(
@@ -714,7 +740,7 @@
         bind(first_half, plan), (whole, half) + edges(pad),
         products + (vmem(pad, 2 * slab),) + (vmem(pad, slab),) * 4 + (vmem(LANES, LANES),),
         flops=4_000_000_000,
-    )(matrices, m, force, g, low_first, high_first, side_first, c_low, c_high, seams)
+    )(matrices, m, force, g, low_first, high_first, low_table, high_table, side_first, c_low, c_high, seams)
 
     low, high = swap(near, next_chip), swap(x, next_core)
     side = beside(plan, side, alone)
@@ -727,7 +753,8 @@
         products + (vmem(pad, 2 * slab), vmem(pad, slab), vmem(pad, slab), vmem(LANES, LANES)),
         flops=4_000_000_000,
     )(
-        matrices, m, force, x, g, low, high, side, c_low, c_high, low_first, high_first, side_first, seams, weight
+        matrices, m, force, x, g, low, high, side, c_low, c_high, low_first, high_first, low_table, high_table, side_first,
+        seams, weight,
     )
     returned = lax.all_to_all(back, "sector", 0, 0, tiled=True)
     sens = call(bind(collect_panels, plan), f32(fields, plan.width, insts), (vmem(insts * RATES, LANES),))(returned)

time: 59.8 us -> 60 us (level)
  waiting for transfers between devices: 15.1 us -> 10.2 us
  starting transfers between devices: 26.9 us -> 30.5 us
  Pallas kernels: 13 us -> 14 us
  other arithmetic: 1.54 us -> 2.23 us
    all_to_all x1, waiting for transfers between devices: 5.64 us -> 0.01 us  [on_device(): got = lax.all_to_all(sent, AXES, 0, 0, tiled=True)]
    ppermute x5 -> x7, starting transfers between devices: 13.7 us -> 15.7 us  [swap(): return lax.ppermute(array, 'sector', list(enumerate(partner)))]
    ppermute x6, starting transfers between devices: 7.05 us -> 8.76 us  [beside(): return lax.ppermute(array, AXES, pairs(0))]
    unnamed x32 -> x24, local copies, waits for them, and re-layouts: 1.76 us -> 0.96 us
    ppermute x6, waiting for transfers between devices: 3.87 us -> 4.63 us  [beside(): return lax.ppermute(array, AXES, pairs(0))]
    reshape x1, other arithmetic: 0.01 us -> 0.7 us  [on_device(): lax.rem(owner, plan.panels).astype(jnp.float32).reshape(insts, cells)]
    reshape x1, local copies, waits for them, and re-layouts: 0.08 us -> 0.78 us  [on_device(): first_panel_share.reshape(insts, cells)]
    pallas_call x1, Pallas kernels: 0.28 us -> 0.96 us  [on_device(): call(bind(prepare, plan), (f32(pad + RATES, plan.ct * slab), f32(RATES, s...]
  transfers between devices with their start and end apart: 13 -> 15, of which waited for: 4 -> 4; matrix products, arithmetic and copies ran while one was open for 0% -> 5% of each run, Pallas kernels for 15% -> 17%
where the time goes in v14:
time: 60 us; the launch traced here: 59.6 us
  starting transfers between devices  30.5 us (51%)
  Pallas kernels  14 us (23%)
  waiting for transfers between devices  10.2 us (17%)
  other arithmetic  2.23 us (4%)
  local copies, waits for them, and re-layouts  1.82 us (3%)
  between operations  0.85 us (1%)
    ppermute x7, starting transfers between devices, swap(): return lax.ppermute(array, 'sector', list(enumerate(partner)))  15.7 us
    ppermute x6, starting transfers between devices, beside(): return lax.ppermute(array, AXES, pairs(0))  8.76 us
    all_to_all x1, waiting for transfers between devices, on_device(): returned = lax.all_to_all(back, 'sector', 0, 0, tiled=True)  5.54 us
    ppermute x6, waiting for transfers between devices, beside(): return lax.ppermute(array, AXES, pairs(0))  4.63 us
    all_to_all x1, starting transfers between devices, on_device(): returned = lax.all_to_all(back, 'sector', 0, 0, tiled=True)  3.5 us
    pallas_call x1, Pallas kernels, on_device(): call(bind(middle, plan), (f32(sectors, RATES, LANES), half, half, half, f...  3.41 us
    pallas_call x1, Pallas kernels, on_device(): call(bind(first_half, plan), (whole, half) + edges(pad), products + (vmem...  3.01 us
    all_to_all x1, starting transfers between devices, on_device(): got = lax.all_to_all(sent, AXES, 0, 0, tiled=True)  2.57 us
  transfers between devices with their start and end apart: 15, of which 4 were waited for; matrix products, arithmetic and copies ran while one was open for 5% of the time, Pallas kernels for 17%

profile of v14, /device:TPU:0, one launch (start us, length us, event | category | flops | bytes accessed | tf_op | source)
XLA Modules:
  0.0 59.6 jit_solution(7394017831205239490)
XLA Ops:
  0.6 5.5 %collective-permute-start = (f32[1232,128]{1,0:T(8,128)}, f32[1232,128]{1,0:T(8,128)S(1)}, u32[]{:S(2)}, u32[]{:S(2)}) collective-permute-start(f32[1232,128]{1,0:T(8,128)} %bitcast.16), channel_id=1, source_target_pairs={{0,30},{2,4},{4,2},{6,8},{8,6},{10,12},{12,10},{14,16},{16,14},{18... | collective-permute-start | bytes 1892360 | tf_op jit(solution)/shard_map/ppermute | solution.py:673
  6.2 0.8 %copy.19 = f32[11,16]{1,0:T(8,128)S(1)} copy(f32[11,16]{0,1:T(8,128)} %bitcast.25) | data formatting | bytes 1408 | tf_op jit(solution)/shard_map/reshape | solution.py:709
  7.8 0.9 %copy-done.1 = f32[11,7,4,8]{0,3,2,1:T(8,128)S(1)} copy-done((f32[11,7,4,8]{0,3,2,1:T(8,128)S(1)}, f32[11,7,4,8]{0,3,2,1:T(8,128)}, u32[]{:S(2)}) %copy-start.1) | copy-done | bytes 9880
  8.7 0.9 %shard_map.151 = f32[32,8,128]{2,1,0:T(8,128)} custom-call(f32[7,32,11]{2,1,0:T(8,128)S(1)} %bitcast.19, f32[11,32]{1,0:T(8,128)S(1)} %pad_maximum_fusion.1.both_ref), custom_call_target="tpu_custom_call" | custom-call | flops 2000000 | bytes 1000000 | tf_op jit(solution)/shard_map/pallas_call | solution.py:706
  9.6 2.6 %all-to-all-start = ((f32[32,8,128]{2,1,0:T(8,128)}), f32[32,8,128]{2,1,0:T(8,128)S(1)}, u32[]{:S(2)}, u32[]{:S(2)}) async-start(f32[32,8,128]{2,1,0:T(8,128)} %shard_map.151), calls=%async_computation | async-start | bytes 262144 | tf_op jit(solution)/shard_map/all_to_all | solution.py:712
  13.7 1.0 %shard_map.150 = (f32[88,2048]{1,0:T(8,128)S(1)}, f32[8,1024]{1,0:T(8,128)S(1)}, f32[8,1024]{1,0:T(8,128)S(1)}, f32[1,88,512]{2,1,0:T(8,128)}, f32[1,88,128]{2,1,0:T(8,128)S(1)}, /*index=5*/f32[1,88,128]{2,1,0:T(8,128)S(1)}) custom-call(f32[1232,128]{1,0:T(8,128)S(1)} %bitcast.18, f32[96,128]{1,0:T(8,128)S(1)} %pad_maximum_fusion.coef_ref), custom_call_target="tpu_custom_call" | custom-call | flops 2000000 | bytes 1000000 | tf_op jit(solution)/shard_map/pallas_call | solution.py:715
  14.6 4.3 %collective-permute-start.2 = (f32[8,1024]{1,0:T(8,128)S(1)}, f32[8,1024]{1,0:T(8,128)S(1)}, u32[]{:S(2)}, u32[]{:S(2)}) collective-permute-start(f32[8,1024]{1,0:T(8,128)S(1)} %get-tuple-element.29), channel_id=1, source_target_pairs={{0,30},{2,4},{4,2},{6,8},{8,6},{10,12},{12,10},{14,16},{16,14},{18... | collective-permute-start | bytes 98312 | tf_op jit(solution)/shard_map/ppermute | solution.py:673
  18.9 1.5 %collective-permute-start.4 = (f32[1,88,512]{2,1,0:T(8,128)}, f32[1,88,512]{2,1,0:T(8,128)S(1)}, u32[]{:S(2)}, u32[]{:S(2)}) collective-permute-start(f32[1,88,512]{2,1,0:T(8,128)} %get-tuple-element.31), channel_id=1, source_target_pairs={{0,1},{1,0},{2,3},{3,2},{4,5},{5,4},{6,7},{7,6},{8,9},{9,8},{10,11... | collective-permute-start | bytes 540680 | tf_op jit(solution)/shard_map/ppermute | solution.py:687
  20.4 1.1 %shard_map.149 = (bf16[560,240]{1,0:T(8,128)(2,1)S(1)}, bf16[80,240]{1,0:T(8,128)(2,1)S(1)}) custom-call(f32[3,7,7]{2,1,0:T(8,128)S(1)} %copy-done.5, f32[3,7,7]{2,1,0:T(8,128)S(1)} %copy-done.6, bf16[80,240]{1,0:T(8,128)(2,1)S(1)} %copy-done.3, f32[80,7]{1,0:T(8,128)S(1)} %copy-done.4, f32[7,240]{1,0:T(8,128)S(1)} %copy-done.7, f32[80,240]{1,0:T(8,128)S(1)} %copy-done.2), custom_call_target="tpu_custom_call" | custom-call | flops 2000000 | bytes 1000000 | tf_op jit(solution)/shard_map/pallas_call | solution.py:729
  21.6 4.3 %collective-permute-start.5 = (f32[1,88,128]{2,1,0:T(8,128)S(1)}, f32[1,88,128]{2,1,0:T(8,128)S(1)}, u32[]{:S(2)}, u32[]{:S(2)}) collective-permute-start(f32[1,88,128]{2,1,0:T(8,128)S(1)} %get-tuple-element.32), channel_id=1, source_target_pairs={{0,31},{1,30},{2,5},{3,4},{4,3},{5,2},{6,9},{7,8},{8,7},{9,6},{10,... | collective-permute-start | bytes 135176 | tf_op jit(solution)/shard_map/ppermute | solution.py:687
  25.9 1.7 %shard_map.152 = (f32[3,2,80,128]{3,2,1,0:T(8,128)S(1)}, f32[80,128]{1,0:T(8,128)S(1)}, f32[80,2048]{1,0:T(8,128)S(1)}, f32[80,2048]{1,0:T(8,128)S(1)}) custom-call(bf16[560,240]{1,0:T(8,128)(2,1)S(1)} %get-tuple-element.25.w_ref, f32[88,2048]{1,0:T(8,128)S(1)} %get-tuple-element.26.m_ref, f32[32,8,128]{2,1,0:T(8,128)S(1)} %all-to-all-done.got_ref), custom_call_target="tpu_custom_call" | custom-call | flops 2000000000 | bytes 1000000 | tf_op jit(solution)/shard_map/pallas_call | solution.py:734
  27.6 1.1 %collective-permute-done.5.c_low = f32[1,88,128]{2,1,0:T(8,128)S(1)} collective-permute-done((f32[1,88,128]{2,1,0:T(8,128)S(1)}, f32[1,88,128]{2,1,0:T(8,128)S(1)}, u32[]{:S(2)}, u32[]{:S(2)}) %collective-permute-start.5) | collective-permute-done | bytes 45088 | tf_op jit(solution)/shard_map/ppermute | solution.py:687
  29.4 3.0 %shard_map.153 = (f32[80,2048]{1,0:T(8,128)S(1)}, f32[80,1024]{1,0:T(8,128)S(1)}, f32[1,80,512]{2,1,0:T(8,128)S(1)}, f32[1,80,128]{2,1,0:T(8,128)S(1)}, f32[1,80,128]{2,1,0:T(8,128)S(1)}) custom-call(bf16[560,240]{1,0:T(8,128)(2,1)S(1)} %get-tuple-element.25.w_ref, f32[88,2048]{1,0:T(8,128)S(1)} %get-tuple-element.26.m_ref, ...), custom_call_target="tpu_custom_call" | custom-call | flops 4000000000 | bytes 1000000 | tf_op jit(solution)/shard_map/pallas_call | solution.py:739
  32.5 2.7 %collective-permute-start.7 = (f32[80,1024]{1,0:T(8,128)S(1)}, f32[80,1024]{1,0:T(8,128)S(1)}, u32[]{:S(2)}, u32[]{:S(2)}) collective-permute-start(f32[80,1024]{1,0:T(8,128)S(1)} %get-tuple-element.36), channel_id=1, source_target_pairs={{0,30},{2,4},{4,2},{6,8},{8,6},{10,12},{12,10},{14,16},{16,14},{18... | collective-permute-start | bytes 983048 | tf_op jit(solution)/shard_map/ppermute | solution.py:673
  35.2 1.5 %collective-permute-start.9 = (f32[1,80,512]{2,1,0:T(8,128)S(1)}, f32[1,80,512]{2,1,0:T(8,128)S(1)}, u32[]{:S(2)}, u32[]{:S(2)}) collective-permute-start(f32[1,80,512]{2,1,0:T(8,128)S(1)} %get-tuple-element.37), channel_id=1, source_target_pairs={{0,1},{1,0},{2,3},{3,2},{4,5},{5,4},{6,7},{7,6},{8,9},{9,8},{10,11... | collective-permute-start | bytes 491528 | tf_op jit(solution)/shard_map/ppermute | solution.py:687
  36.7 1.5 %collective-permute-start.10 = (f32[1,80,128]{2,1,0:T(8,128)S(1)}, f32[1,80,128]{2,1,0:T(8,128)S(1)}, u32[]{:S(2)}, u32[]{:S(2)}) collective-permute-start(f32[1,80,128]{2,1,0:T(8,128)S(1)} %get-tuple-element.38), channel_id=1, source_target_pairs={{0,31},{1,30},{2,5},{3,4},{4,3},{5,2},{6,9},{7,8},{8,7},{9,6},{10,... | collective-permute-start | bytes 122888 | tf_op jit(solution)/shard_map/ppermute | solution.py:687
  38.2 0.8 %shard_map.154.g_ref = f32[80,2048]{1,0:T(8,128)S(1)} custom-call(bf16[560,240]{1,0:T(8,128)(2,1)S(1)} %get-tuple-element.25.w_ref, f32[88,2048]{1,0:T(8,128)S(1)} %get-tuple-element.26.m_ref, f32[80,2048]{1,0:T(8,128)S(1)} %get-tuple-element.27.f_ref, f32[80,2048]{1,0:T(8,128)S(1)} %get-tuple-element.35.x_ref), custom_call_target="tpu_custom_call" | custom-call | flops 2000000000 | bytes 1000000 | tf_op jit(solution)/shard_map/pallas_call | solution.py:748
  39.0 2.9 %collective-permute-done.11.c_high = f32[1,80,128]{2,1,0:T(8,128)S(1)} collective-permute-done((f32[1,80,128]{2,1,0:T(8,128)S(1)}, f32[1,80,128]{2,1,0:T(8,128)S(1)}, u32[]{:S(2)}, u32[]{:S(2)}) %collective-permute-start.11) | collective-permute-done | bytes 40992 | tf_op jit(solution)/shard_map/ppermute | solution.py:687
  41.9 3.1 %collective-permute-start.12 = (f32[80,1024]{1,0:T(8,128)S(1)}, f32[80,1024]{1,0:T(8,128)S(1)}, u32[]{:S(2)}, u32[]{:S(2)}) collective-permute-start(f32[80,1024]{1,0:T(8,128)S(1)} %shard_map.156), channel_id=1, source_target_pairs={{0,30},{2,4},{4,2},{6,8},{8,6},{10,12},{12,10},{14,16},{16,14},{18... | collective-permute-start | bytes 983048 | tf_op jit(solution)/shard_map/ppermute | solution.py:673
  45.0 3.4 %shard_map.155 = (f32[16,8,128]{2,1,0:T(8,128)}, f32[80,1024]{1,0:T(8,128)S(1)}, f32[80,1024]{1,0:T(8,128)S(1)}, f32[80,1024]{1,0:T(8,128)S(1)}, f32[8,1024]{1,0:T(8,128)S(1)}) custom-call(bf16[560,240]{1,0:T(8,128)(2,1)S(1)} %get-tuple-element.25.w_ref, f32[88,2048]{1,0:T(8,128)S(1)} %get-tuple-element.26.m_ref, f32[80,2048]{1,0:T(8,128)S(1)} %get-tuple-element.27.f_ref, ...), custom_call_target="tpu_custom_call" | custom-call | flops 4000000000 | bytes 1000000 | tf_op jit(solution)/shard_map/pallas_call | solution.py:751
  48.4 3.5 %all-to-all-start.1 = ((f32[16,8,128]{2,1,0:T(8,128)}), f32[16,8,128]{2,1,0:T(8,128)S(1)}, u32[]{:S(2)}, u32[]{:S(2)}) async-start(f32[16,8,128]{2,1,0:T(8,128)} %get-tuple-element.45), calls=%async_computation.1 | async-start | bytes 131072 | tf_op jit(solution)/shard_map/all_to_all | solution.py:759
  51.9 1.3 %shard_map.157 = f32[1232,128]{1,0:T(8,128)} custom-call(bf16[80,240]{1,0:T(8,128)(2,1)S(1)} %get-tuple-element.24.w_ref, f32[8,1024]{1,0:T(8,128)S(1)} %get-tuple-element.41.rates_ref, f32[80,1024]{1,0:T(8,128)S(1)} %get-tuple-element.42.n0_ref, f32[80,1024]{1,0:T(8,128)S(1)} %get-tuple-element.43.h0_ref, f32[80,1024]{1,0:T(8,128)S(1)} %get-tuple-element.44.x1_ref, ...), custom_call_target="tpu_custom_call" | custom-call | flops 2000000 | bytes 1000000 | tf_op jit(solution)/shard_map/pallas_call | solution.py:761
  53.3 5.5 %all-to-all-done.1.got_ref = f32[16,8,128]{2,1,0:T(8,128)S(1)} async-done(((f32[16,8,128]{2,1,0:T(8,128)}), f32[16,8,128]{2,1,0:T(8,128)S(1)}, u32[]{:S(2)}, u32[]{:S(2)}) %all-to-all-start.1) | async-done | bytes 65568 | tf_op jit(solution)/shard_map/all_to_all | solution.py:759
  58.8 0.8 %shard_map.158 = f32[7,32,11]{2,1,0:T(8,128)} custom-call(f32[16,8,128]{2,1,0:T(8,128)S(1)} %all-to-all-done.1.got_ref), custom_call_target="tpu_custom_call" | custom-call | flops 2000000 | bytes 1000000 | tf_op jit(solution)/shard_map/pallas_call | solution.py:760
  (46 shorter events, 3.2 us)
Async XLA Ops:
  0.6 13.0 %copy-start = (f32[11,7,2,8,128]{4,3,2,1,0:T(8,128)S(1)}, f32[11,7,2,8,128]{4,3,2,1,0:T(8,128)}, u32[]{:S(2)}) copy-start(f32[11,7,2,8,128]{4,3,2,1,0:T(8,128)} %param.14) | copy-start | bytes 1892356
  0.6 28.7 %collective-permute-start = (f32[1232,128]{1,0:T(8,128)}, f32[1232,128]{1,0:T(8,128)S(1)}, u32[]{:S(2)}, u32[]{:S(2)}) collective-permute-start(f32[1232,128]{1,0:T(8,128)} %bitcast.16), channel_id=1, source_target_pairs={{0,30},{2,4},{4,2},{6,8},{8,6},{10,12},{12,10},{14,16},{16,14},{18... | collective-permute-start | bytes 1892360 | tf_op jit(solution)/shard_map/ppermute | solution.py:673
  6.1 23.2 %collective-permute-start.1 = (f32[1232,128]{1,0:T(8,128)}, f32[1232,128]{1,0:T(8,128)S(1)}, u32[]{:S(2)}, u32[]{:S(2)}) collective-permute-start(f32[1232,128]{1,0:T(8,128)} %bitcast.17), channel_id=1, source_target_pairs={{0,2},{2,0},{4,6},{6,4},{8,10},{10,8},{12,14},{14,12},{16,18},{18,... | collective-permute-start | bytes 1892360 | tf_op jit(solution)/shard_map/ppermute | solution.py:673
  9.6 16.3 %all-to-all-start = ((f32[32,8,128]{2,1,0:T(8,128)}), f32[32,8,128]{2,1,0:T(8,128)S(1)}, u32[]{:S(2)}, u32[]{:S(2)}) async-start(f32[32,8,128]{2,1,0:T(8,128)} %shard_map.151), calls=%async_computation | async-start | bytes 262144 | tf_op jit(solution)/shard_map/all_to_all | solution.py:712
  13.6 6.8 %copy-start.2 = (f32[80,240]{1,0:T(8,128)S(1)}, f32[80,240]{1,0:T(8,128)}, u32[]{:S(2)}) copy-start(f32[80,240]{1,0:T(8,128)} %constant.16.clone.diagonal_ref) | copy-start | bytes 230404
  13.6 6.8 %copy-start.3 = (bf16[80,240]{1,0:T(8,128)(2,1)S(1)}, bf16[80,240]{1,0:T(8,128)(2,1)}, u32[]{:S(2)}) copy-start(bf16[80,240]{1,0:T(8,128)(2,1)} %constant.13.clone.spectral_ref) | copy-start | bytes 115204
  13.6 6.8 %copy-start.4 = (f32[80,7]{1,0:T(8,128)S(1)}, f32[80,7]{1,0:T(8,128)}, u32[]{:S(2)}) copy-start(f32[80,7]{1,0:T(8,128)} %constant.14.clone.rows_ref) | copy-start | bytes 6724
  13.6 6.8 %copy-start.5 = (f32[3,7,7]{2,1,0:T(8,128)S(1)}, f32[3,7,7]{2,1,0:T(8,128)}, u32[]{:S(2)}) copy-start(f32[3,7,7]{2,1,0:T(8,128)} %up_ref.1) | copy-start | bytes 1768
  13.6 6.8 %copy-start.6 = (f32[3,7,7]{2,1,0:T(8,128)S(1)}, f32[3,7,7]{2,1,0:T(8,128)}, u32[]{:S(2)}) copy-start(f32[3,7,7]{2,1,0:T(8,128)} %down_ref.1) | copy-start | bytes 1768
  13.6 6.8 %copy-start.7 = (f32[7,240]{1,0:T(8,128)S(1)}, f32[7,240]{1,0:T(8,128)}, u32[]{:S(2)}) copy-start(f32[7,240]{1,0:T(8,128)} %constant.15.clone.lanes_ref) | copy-start | bytes 20164
  14.6 6.9 %collective-permute-start.2 = (f32[8,1024]{1,0:T(8,128)S(1)}, f32[8,1024]{1,0:T(8,128)S(1)}, u32[]{:S(2)}, u32[]{:S(2)}) collective-permute-start(f32[8,1024]{1,0:T(8,128)S(1)} %get-tuple-element.29), channel_id=1, source_target_pairs={{0,30},{2,4},{4,2},{6,8},{8,6},{10,12},{12,10},{14,16},{16,14},{18... | collective-permute-start | bytes 98312 | tf_op jit(solution)/shard_map/ppermute | solution.py:673
  18.9 7.0 %collective-permute-start.3 = (f32[8,1024]{1,0:T(8,128)S(1)}, f32[8,1024]{1,0:T(8,128)S(1)}, u32[]{:S(2)}, u32[]{:S(2)}) collective-permute-start(f32[8,1024]{1,0:T(8,128)S(1)} %get-tuple-element.30), channel_id=1, source_target_pairs={{0,2},{2,0},{4,6},{6,4},{8,10},{10,8},{12,14},{14,12},{16,18},{18,... | collective-permute-start | bytes 98312 | tf_op jit(solution)/shard_map/ppermute | solution.py:673
  18.9 10.4 %collective-permute-start.4 = (f32[1,88,512]{2,1,0:T(8,128)}, f32[1,88,512]{2,1,0:T(8,128)S(1)}, u32[]{:S(2)}, u32[]{:S(2)}) collective-permute-start(f32[1,88,512]{2,1,0:T(8,128)} %get-tuple-element.31), channel_id=1, source_target_pairs={{0,1},{1,0},{2,3},{3,2},{4,5},{5,4},{6,7},{7,6},{8,9},{9,8},{10,11... | collective-permute-start | bytes 540680 | tf_op jit(solution)/shard_map/ppermute | solution.py:687
  21.6 7.1 %collective-permute-start.5 = (f32[1,88,128]{2,1,0:T(8,128)S(1)}, f32[1,88,128]{2,1,0:T(8,128)S(1)}, u32[]{:S(2)}, u32[]{:S(2)}) collective-permute-start(f32[1,88,128]{2,1,0:T(8,128)S(1)} %get-tuple-element.32), channel_id=1, source_target_pairs={{0,31},{1,30},{2,5},{3,4},{4,3},{5,2},{6,9},{7,8},{8,7},{9,6},{10,... | collective-permute-start | bytes 135176 | tf_op jit(solution)/shard_map/ppermute | solution.py:687
  25.9 3.5 %collective-permute-start.6 = (f32[1,88,128]{2,1,0:T(8,128)S(1)}, f32[1,88,128]{2,1,0:T(8,128)S(1)}, u32[]{:S(2)}, u32[]{:S(2)}) collective-permute-start(f32[1,88,128]{2,1,0:T(8,128)S(1)} %get-tuple-element.33), channel_id=1, source_target_pairs={{0,3},{1,2},{2,1},{3,0},{4,7},{5,6},{6,5},{7,4},{8,11},{9,10},{10,... | collective-permute-start | bytes 135176 | tf_op jit(solution)/shard_map/ppermute | solution.py:687
  32.4 12.6 %collective-permute-start.8 = (f32[80,2048]{1,0:T(8,128)S(1)}, f32[80,2048]{1,0:T(8,128)S(1)}, u32[]{:S(2)}, u32[]{:S(2)}) collective-permute-start(f32[80,2048]{1,0:T(8,128)S(1)} %get-tuple-element.35.x_ref), channel_id=1, source_target_pairs={{0,2},{2,0},{4,6},{6,4},{8,10},{10,8},{12,14},{14,12},{16,18},{18,... | collective-permute-start | bytes 1966088 | tf_op jit(solution)/shard_map/ppermute | solution.py:673
  32.5 12.5 %collective-permute-start.7 = (f32[80,1024]{1,0:T(8,128)S(1)}, f32[80,1024]{1,0:T(8,128)S(1)}, u32[]{:S(2)}, u32[]{:S(2)}) collective-permute-start(f32[80,1024]{1,0:T(8,128)S(1)} %get-tuple-element.36), channel_id=1, source_target_pairs={{0,30},{2,4},{4,2},{6,8},{8,6},{10,12},{12,10},{14,16},{16,14},{18... | collective-permute-start | bytes 983048 | tf_op jit(solution)/shard_map/ppermute | solution.py:673
  35.2 6.6 %collective-permute-start.9 = (f32[1,80,512]{2,1,0:T(8,128)S(1)}, f32[1,80,512]{2,1,0:T(8,128)S(1)}, u32[]{:S(2)}, u32[]{:S(2)}) collective-permute-start(f32[1,80,512]{2,1,0:T(8,128)S(1)} %get-tuple-element.37), channel_id=1, source_target_pairs={{0,1},{1,0},{2,3},{3,2},{4,5},{5,4},{6,7},{7,6},{8,9},{9,8},{10,11... | collective-permute-start | bytes 491528 | tf_op jit(solution)/shard_map/ppermute | solution.py:687
  36.7 8.3 %collective-permute-start.10 = (f32[1,80,128]{2,1,0:T(8,128)S(1)}, f32[1,80,128]{2,1,0:T(8,128)S(1)}, u32[]{:S(2)}, u32[]{:S(2)}) collective-permute-start(f32[1,80,128]{2,1,0:T(8,128)S(1)} %get-tuple-element.38), channel_id=1, source_target_pairs={{0,31},{1,30},{2,5},{3,4},{4,3},{5,2},{6,9},{7,8},{8,7},{9,6},{10,... | collective-permute-start | bytes 122888 | tf_op jit(solution)/shard_map/ppermute | solution.py:687
  38.2 3.7 %collective-permute-start.11 = (f32[1,80,128]{2,1,0:T(8,128)S(1)}, f32[1,80,128]{2,1,0:T(8,128)S(1)}, u32[]{:S(2)}, u32[]{:S(2)}) collective-permute-start(f32[1,80,128]{2,1,0:T(8,128)S(1)} %get-tuple-element.39), channel_id=1, source_target_pairs={{0,3},{1,2},{2,1},{3,0},{4,7},{5,6},{6,5},{7,4},{8,11},{9,10},{10,... | collective-permute-start | bytes 122888 | tf_op jit(solution)/shard_map/ppermute | solution.py:687
  39.0 6.0 %copy-start.9 = (f32[1232,128]{1,0:T(8,128)S(1)}, f32[1232,128]{1,0:T(8,128)}, u32[]{:S(2)}) copy-start(f32[1232,128]{1,0:T(8,128)} %copy-done.8) | copy-start | bytes 1892356
  39.0 6.0 %copy-start.11 = (f32[1,88,512]{2,1,0:T(8,128)S(1)}, f32[1,88,512]{2,1,0:T(8,128)}, u32[]{:S(2)}) copy-start(f32[1,88,512]{2,1,0:T(8,128)} %copy-done.10) | copy-start | bytes 540676
  41.9 10.0 %collective-permute-start.12 = (f32[80,1024]{1,0:T(8,128)S(1)}, f32[80,1024]{1,0:T(8,128)S(1)}, u32[]{:S(2)}, u32[]{:S(2)}) collective-permute-start(f32[80,1024]{1,0:T(8,128)S(1)} %shard_map.156), channel_id=1, source_target_pairs={{0,30},{2,4},{4,2},{6,8},{8,6},{10,12},{12,10},{14,16},{16,14},{18... | collective-permute-start | bytes 983048 | tf_op jit(solution)/shard_map/ppermute | solution.py:673
  48.4 10.4 %all-to-all-start.1 = ((f32[16,8,128]{2,1,0:T(8,128)}), f32[16,8,128]{2,1,0:T(8,128)S(1)}, u32[]{:S(2)}, u32[]{:S(2)}) async-start(f32[16,8,128]{2,1,0:T(8,128)} %get-tuple-element.45), calls=%async_computation.1 | async-start | bytes 131072 | tf_op jit(solution)/shard_map/all_to_all | solution.py:759
  (3 other events, 7.0 us)

commit v15 on v14

--- a/solution.py
+++ b/solution.py
@@ -209,7 +209,9 @@
         there = jnp.where(parity() == 1, self.layer, plan.ct - 1 - self.layer) * plan.rows + r
         field = self.ref[pl.ds(there, plan.tf, stride=plan.cells), :]
         field = jnp.concatenate([field, jnp.zeros((plan.pad - plan.tf, LANES), jnp.float32)], axis=0)
-        return (field + placed(self.seam, self.layer * plan.rows + r)) * self.rate(C_MASK, r)
+        if self.seam is not None:
+            field = field + placed(self.seam, self.layer * plan.rows + r)
+        return field * self.rate(C_MASK, r)
 
 
 def placed(tile, cell):
@@ -392,20 +394,22 @@
 
     def corner(n):
         out = []
-        for a, c_ref in enumerate(c_refs):
-            value = c_ref[n, : plan.pad]
-            if seams_ref is not None:
+        for a in range(plan.ct):
+            if seams_ref is None:
+                value = c_refs[a][n, : plan.pad]
+            else:
+                value = c_refs[n, : plan.pad, at(a)]
                 tile = seams_ref[2 * a, 1 + n]
                 above, below = (placed(tile, a * plan.rows + r) for r in (0, plan.rows - 1))
                 inlet = jnp.where(is_first, above, below) if plan.ends == 1 else (above, below)[n]
-                value = value + inlet * c_ref[n, plan.pad + C_MASK : plan.pad + C_MASK + 1]
+                value = value + inlet * c_refs[n, plan.pad + C_MASK : plan.pad + C_MASK + 1, at(a)]
             out.append(value * keeps[n])
         return out
 
     return corner
 
 
-def prepare(plan, rhs_ref, coef_ref, m_ref, table0_ref, table1_ref, side_ref, c0_ref, c1_ref, rates_ref):
+def prepare(plan, rhs_ref, coef_ref, m_ref, table0_ref, table1_ref, side_ref, rates_ref):
     pad, cells = plan.pad, plan.cells
     mask, diag, time, *face = [coef_ref[cells * i : cells * (i + 1), :] for i in range(6)]
     scale = mask / diag
@@ -430,7 +434,7 @@
         other = jnp.where(mirror == 0, plan.ct - 1 - a, a) * plan.rows + r
         table = table + [rates_ref[C_MASK, pl.ds(other, 1), :], rest[:1]]
         (table0_ref, table1_ref)[a][:, at(r)] = jnp.concatenate(table, axis=0)
-    write_edges(plan, m_ref, side_ref, (c0_ref, c1_ref))
+    write_edges(plan, m_ref, side_ref, None)
 
 
 def write_edges(plan, x_ref, side_ref, c_refs):
@@ -441,8 +445,22 @@
             ends = [jnp.where(first, high, low)] if plan.ends == 1 else [low, high]
             for n, end in enumerate(ends):
                 side_ref[n, :, at(e * plan.ct + a)] = end
-                if e == 0:
+                if e == 0 and c_refs:
                     c_refs[a][n] = end
+
+
+def corner_rows(plan, low_ref, high_ref, low_table, high_table, c_ref):
+    first = lax.axis_index("span") == 0
+    near = Native(plan, low_ref, low_table, None, 0, True), Native(plan, high_ref, high_table, None, 1, True)
+    for a, layer in enumerate(near):
+        ends = []
+        for r in (0, plan.rows - 1):
+            rates = [layer.rate(C_MASK, r) if i == C_MASK else jnp.zeros((1, LANES), jnp.float32) for i in range(RATES)]
+            ends.append(jnp.concatenate([layer.row(r)] + rates, axis=0))
+        if plan.ends == 1:
+            ends = [jnp.where(first, ends[1], ends[0])]
+        for n, end in enumerate(ends):
+            c_ref[n, :, at(a)] = end
 
 
 def stack_matrices(plan, up_ref, down_ref, spectral_ref, rows_ref, lanes_ref, diagonal_ref, out_ref, down_out):
@@ -541,7 +559,7 @@
 
 
 def first_half(
-    plan, w_ref, m_ref, f_ref, g_ref, low_ref, high_ref, low_table, high_table, side_ref, c_low, c_high, seams_ref,
+    plan, w_ref, m_ref, f_ref, g_ref, low_ref, high_ref, low_table, high_table, side_ref, corner_ref, seams_ref,
     x_ref, near_ref, side_out, c0_ref, c1_ref, p0_ref, p1_ref, y_ref, h0_ref, h1_ref, n0_ref, n1_ref, inlet_ref,
 ):
     own = two_layers(plan, f_ref, m_ref)
@@ -551,7 +569,7 @@
     n_refs = n0_ref, n1_ref
     middle_rows(
         plan, w_ref, (p0_ref, p1_ref), own, own, g_ref, near, near, sides_of(plan, side_ref, side_ref, seams_ref),
-        corners_of(plan, (c_low, c_high), seams_ref), y_ref, (h0_ref, h1_ref), n_refs,
+        corners_of(plan, corner_ref, seams_ref), y_ref, (h0_ref, h1_ref), n_refs,
     )
     lane = lane_index(plan.pad)
     inlet_ref[...] = jnp.zeros_like(inlet_ref)
@@ -712,9 +730,9 @@
     got = lax.all_to_all(sent, AXES, 0, 0, tiled=True)
     native = rhs.reshape(plan.tf * cells, LANES)
     low_first, high_first = swap(native, next_chip), swap(native, next_core)
-    m, table0, table1, side, c0, c1 = call(
+    m, table0, table1, side = call(
         bind(prepare, plan),
-        (f32(pad + RATES, plan.ct * slab), f32(RATES, slab), f32(RATES, slab)) + edges(pad + RATES),
+        (f32(pad + RATES, plan.ct * slab), f32(RATES, slab), f32(RATES, slab)) + edges(pad + RATES)[:1],
         (vmem(6, cells, LANES),),
     )(
         native,
@@ -725,7 +743,10 @@
     )
     low_table, high_table = swap(table0, next_chip), swap(table1, next_core)
     side_first = beside(plan, side, alone)
-    c_low, c_high = beside(plan, c0, next_chip), beside(plan, c1, next_core)
+    corner = call(bind(corner_rows, plan), f32(ends, pad + RATES, plan.ct * LANES))(
+        low_first, high_first, low_table, high_table
+    )
+    corner = beside(plan, corner, alone)
     matrices, down = call(
         bind(stack_matrices, plan),
         [jax.ShapeDtypeStruct((count * pad, 3 * pad), jnp.bfloat16) for count in (7, 1)],
@@ -740,7 +761,7 @@
         bind(first_half, plan), (whole, half) + edges(pad),
         products + (vmem(pad, 2 * slab),) + (vmem(pad, slab),) * 4 + (vmem(LANES, LANES),),
         flops=4_000_000_000,
-    )(matrices, m, force, g, low_first, high_first, low_table, high_table, side_first, c_low, c_high, seams)
+    )(matrices, m, force, g, low_first, high_first, low_table, high_table, side_first, corner, seams)
 
     low, high = swap(near, next_chip), swap(x, next_core)
     side = beside(plan, side, alone)

time: 60 us -> 58.5 us (0.975)
  starting transfers between devices: 30.5 us -> 27.2 us
  waiting for transfers between devices: 10.2 us -> 12.2 us
    ppermute x6 -> x5, starting transfers between devices: 8.76 us -> 4.97 us  [beside(): return lax.ppermute(array, AXES, pairs(0))]
    ppermute x6 -> x5, waiting for transfers between devices: 4.63 us -> 6.62 us  [beside(): return lax.ppermute(array, AXES, pairs(0))]
    pallas_call x1, Pallas kernels: 0.96 us -> 0.28 us  [on_device(): call(bind(prepare, plan), (f32(pad + RATES, plan.ct * slab), f32(RATES, s...]
  transfers between devices with their start and end apart: 15 -> 14, of which waited for: 4 -> 4; matrix products, arithmetic and copies ran while one was open for 5% -> 5% of each run, Pallas kernels for 17% -> 17%
where the time goes in v15:
time: 58.5 us; the launch traced here: 58 us
  starting transfers between devices  27.2 us (46%)
  Pallas kernels  13.7 us (23%)
  waiting for transfers between devices  12.2 us (21%)
  other arithmetic  2.23 us (4%)
  local copies, waits for them, and re-layouts  1.82 us (3%)
  between operations  0.87 us (1%)
    ppermute x7, starting transfers between devices, swap(): return lax.ppermute(array, 'sector', list(enumerate(partner)))  16.2 us
    ppermute x5, waiting for transfers between devices, beside(): return lax.ppermute(array, AXES, pairs(0))  6.62 us
    all_to_all x1, waiting for transfers between devices, on_device(): returned = lax.all_to_all(back, 'sector', 0, 0, tiled=True)  5.54 us
    ppermute x5, starting transfers between devices, beside(): return lax.ppermute(array, AXES, pairs(0))  4.97 us
    pallas_call x1, Pallas kernels, on_device(): call(bind(middle, plan), (f32(sectors, RATES, LANES), half, half, half, f...  3.52 us
    all_to_all x1, starting transfers between devices, on_device(): returned = lax.all_to_all(back, 'sector', 0, 0, tiled=True)  3.5 us
    pallas_call x1, Pallas kernels, on_device(): call(bind(first_half, plan), (whole, half) + edges(pad), products + (vmem...  3.15 us
    all_to_all x1, starting transfers between devices, on_device(): got = lax.all_to_all(sent, AXES, 0, 0, tiled=True)  2.58 us
  transfers between devices with their start and end apart: 14, of which 4 were waited for; matrix products, arithmetic and copies ran while one was open for 5% of the time, Pallas kernels for 17%

profile of v15, /device:TPU:0, one launch (start us, length us, event | category | flops | bytes accessed | tf_op | source)
XLA Modules:
  0.0 58.0 jit_solution(10282515084358265237)
XLA Ops:
  0.6 5.5 %collective-permute-start = (f32[1232,128]{1,0:T(8,128)}, f32[1232,128]{1,0:T(8,128)S(1)}, u32[]{:S(2)}, u32[]{:S(2)}) collective-permute-start(f32[1232,128]{1,0:T(8,128)} %bitcast.16), channel_id=1, source_target_pairs={{0,30},{2,4},{4,2},{6,8},{8,6},{10,12},{12,10},{14,16},{16,14},{18... | collective-permute-start | bytes 1892360 | tf_op jit(solution)/shard_map/ppermute | solution.py:691
  6.2 0.8 %copy.19 = f32[11,16]{1,0:T(8,128)S(1)} copy(f32[11,16]{0,1:T(8,128)} %bitcast.25) | data formatting | bytes 1408 | tf_op jit(solution)/shard_map/reshape | solution.py:727
  7.8 0.9 %copy-done.1 = f32[11,7,4,8]{0,3,2,1:T(8,128)S(1)} copy-done((f32[11,7,4,8]{0,3,2,1:T(8,128)S(1)}, f32[11,7,4,8]{0,3,2,1:T(8,128)}, u32[]{:S(2)}) %copy-start.1) | copy-done | bytes 9880
  8.7 0.9 %shard_map.151 = f32[32,8,128]{2,1,0:T(8,128)} custom-call(f32[7,32,11]{2,1,0:T(8,128)S(1)} %bitcast.19, f32[11,32]{1,0:T(8,128)S(1)} %pad_maximum_fusion.1.both_ref), custom_call_target="tpu_custom_call" | custom-call | flops 2000000 | bytes 1000000 | tf_op jit(solution)/shard_map/pallas_call | solution.py:724
  9.6 2.6 %all-to-all-start = ((f32[32,8,128]{2,1,0:T(8,128)}), f32[32,8,128]{2,1,0:T(8,128)S(1)}, u32[]{:S(2)}, u32[]{:S(2)}) async-start(f32[32,8,128]{2,1,0:T(8,128)} %shard_map.151), calls=%async_computation | async-start | bytes 262144 | tf_op jit(solution)/shard_map/all_to_all | solution.py:730
  14.0 4.4 %collective-permute-start.2 = (f32[8,1024]{1,0:T(8,128)S(1)}, f32[8,1024]{1,0:T(8,128)S(1)}, u32[]{:S(2)}, u32[]{:S(2)}) collective-permute-start(f32[8,1024]{1,0:T(8,128)S(1)} %get-tuple-element.27), channel_id=1, source_target_pairs={{0,30},{2,4},{4,2},{6,8},{8,6},{10,12},{12,10},{14,16},{16,14},{18... | collective-permute-start | bytes 98312 | tf_op jit(solution)/shard_map/ppermute | solution.py:691
  18.3 1.5 %collective-permute-start.4 = (f32[1,88,512]{2,1,0:T(8,128)S(1)}, f32[1,88,512]{2,1,0:T(8,128)S(1)}, u32[]{:S(2)}, u32[]{:S(2)}) collective-permute-start(f32[1,88,512]{2,1,0:T(8,128)S(1)} %get-tuple-element.29), channel_id=1, source_target_pairs={{0,1},{1,0},{2,3},{3,2},{4,5},{5,4},{6,7},{7,6},{8,9},{9,8},{10,11... | collective-permute-start | bytes 540680 | tf_op jit(solution)/shard_map/ppermute | solution.py:705
  19.8 1.1 %shard_map.149 = (bf16[560,240]{1,0:T(8,128)(2,1)S(1)}, bf16[80,240]{1,0:T(8,128)(2,1)S(1)}) custom-call(f32[3,7,7]{2,1,0:T(8,128)S(1)} %copy-done.5, f32[3,7,7]{2,1,0:T(8,128)S(1)} %copy-done.6, bf16[80,240]{1,0:T(8,128)(2,1)S(1)} %copy-done.3, f32[80,7]{1,0:T(8,128)S(1)} %copy-done.4, f32[7,240]{1,0:T(8,128)S(1)} %copy-done.7, f32[80,240]{1,0:T(8,128)S(1)} %copy-done.2), custom_call_target="tpu_custom_call" | custom-call | flops 2000000 | bytes 1000000 | tf_op jit(solution)/shard_map/pallas_call | solution.py:750
  21.1 0.9 %collective-permute-start.5 = (f32[1,88,256]{2,1,0:T(8,128)S(1)}, f32[1,88,256]{2,1,0:T(8,128)S(1)}, u32[]{:S(2)}, u32[]{:S(2)}) collective-permute-start(f32[1,88,256]{2,1,0:T(8,128)S(1)} %shard_map.153), channel_id=1, source_target_pairs={{0,1},{1,0},{2,3},{3,2},{4,5},{5,4},{6,7},{7,6},{8,9},{9,8},{10,11... | collective-permute-start | bytes 270344 | tf_op jit(solution)/shard_map/ppermute | solution.py:705
  22.0 1.7 %shard_map.152 = (f32[3,2,80,128]{3,2,1,0:T(8,128)S(1)}, f32[80,128]{1,0:T(8,128)S(1)}, f32[80,2048]{1,0:T(8,128)S(1)}, f32[80,2048]{1,0:T(8,128)S(1)}) custom-call(bf16[560,240]{1,0:T(8,128)(2,1)S(1)} %get-tuple-element.23.w_ref, f32[88,2048]{1,0:T(8,128)S(1)} %get-tuple-element.24.m_ref, f32[32,8,128]{2,1,0:T(8,128)S(1)} %all-to-all-done.got_ref), custom_call_target="tpu_custom_call" | custom-call | flops 2000000000 | bytes 1000000 | tf_op jit(solution)/shard_map/pallas_call | solution.py:755
  23.7 2.0 %collective-permute-done.4.side_ref.side_first = f32[1,88,512]{2,1,0:T(8,128)S(1)} collective-permute-done((f32[1,88,512]{2,1,0:T(8,128)S(1)}, f32[1,88,512]{2,1,0:T(8,128)S(1)}, u32[]{:S(2)}, u32[]{:S(2)}) %collective-permute-start.4) | collective-permute-done | bytes 180256 | tf_op jit(solution)/shard_map/ppermute | solution.py:705
  25.7 1.5 %collective-permute-done.5.corner_ref = f32[1,88,256]{2,1,0:T(8,128)S(1)} collective-permute-done((f32[1,88,256]{2,1,0:T(8,128)S(1)}, f32[1,88,256]{2,1,0:T(8,128)S(1)}, u32[]{:S(2)}, u32[]{:S(2)}) %collective-permute-start.5) | collective-permute-done | bytes 90144 | tf_op jit(solution)/shard_map/ppermute | solution.py:705
  27.2 3.2 %shard_map.154 = (f32[80,2048]{1,0:T(8,128)S(1)}, f32[80,1024]{1,0:T(8,128)S(1)}, f32[1,80,512]{2,1,0:T(8,128)S(1)}, f32[1,80,128]{2,1,0:T(8,128)S(1)}, f32[1,80,128]{2,1,0:T(8,128)S(1)}) custom-call(bf16[560,240]{1,0:T(8,128)(2,1)S(1)} %get-tuple-element.23.w_ref, f32[88,2048]{1,0:T(8,128)S(1)} %get-tuple-element.24.m_ref, ...), custom_call_target="tpu_custom_call" | custom-call | flops 4000000000 | bytes 1000000 | tf_op jit(solution)/shard_map/pallas_call | solution.py:760
  30.4 3.1 %collective-permute-start.6 = (f32[80,1024]{1,0:T(8,128)S(1)}, f32[80,1024]{1,0:T(8,128)S(1)}, u32[]{:S(2)}, u32[]{:S(2)}) collective-permute-start(f32[80,1024]{1,0:T(8,128)S(1)} %get-tuple-element.32), channel_id=1, source_target_pairs={{0,30},{2,4},{4,2},{6,8},{8,6},{10,12},{12,10},{14,16},{16,14},{18... | collective-permute-start | bytes 983048 | tf_op jit(solution)/shard_map/ppermute | solution.py:691
  33.5 1.5 %collective-permute-start.8 = (f32[1,80,512]{2,1,0:T(8,128)S(1)}, f32[1,80,512]{2,1,0:T(8,128)S(1)}, u32[]{:S(2)}, u32[]{:S(2)}) collective-permute-start(f32[1,80,512]{2,1,0:T(8,128)S(1)} %get-tuple-element.33), channel_id=1, source_target_pairs={{0,1},{1,0},{2,3},{3,2},{4,5},{5,4},{6,7},{7,6},{8,9},{9,8},{10,11... | collective-permute-start | bytes 491528 | tf_op jit(solution)/shard_map/ppermute | solution.py:705
  35.0 1.1 %collective-permute-start.9 = (f32[1,80,128]{2,1,0:T(8,128)S(1)}, f32[1,80,128]{2,1,0:T(8,128)S(1)}, u32[]{:S(2)}, u32[]{:S(2)}) collective-permute-start(f32[1,80,128]{2,1,0:T(8,128)S(1)} %get-tuple-element.34), channel_id=1, source_target_pairs={{0,31},{1,30},{2,5},{3,4},{4,3},{5,2},{6,9},{7,8},{8,7},{9,6},{10,... | collective-permute-start | bytes 122888 | tf_op jit(solution)/shard_map/ppermute | solution.py:705
  36.1 0.8 %shard_map.155.g_ref = f32[80,2048]{1,0:T(8,128)S(1)} custom-call(bf16[560,240]{1,0:T(8,128)(2,1)S(1)} %get-tuple-element.23.w_ref, f32[88,2048]{1,0:T(8,128)S(1)} %get-tuple-element.24.m_ref, f32[80,2048]{1,0:T(8,128)S(1)} %get-tuple-element.25.f_ref, f32[80,2048]{1,0:T(8,128)S(1)} %get-tuple-element.31.x_ref), custom_call_target="tpu_custom_call" | custom-call | flops 2000000000 | bytes 1000000 | tf_op jit(solution)/shard_map/pallas_call | solution.py:769
  37.0 3.1 %collective-permute-done.10.c_high = f32[1,80,128]{2,1,0:T(8,128)S(1)} collective-permute-done((f32[1,80,128]{2,1,0:T(8,128)S(1)}, f32[1,80,128]{2,1,0:T(8,128)S(1)}, u32[]{:S(2)}, u32[]{:S(2)}) %collective-permute-start.10) | collective-permute-done | bytes 40992 | tf_op jit(solution)/shard_map/ppermute | solution.py:705
  40.1 3.2 %collective-permute-start.11 = (f32[80,1024]{1,0:T(8,128)S(1)}, f32[80,1024]{1,0:T(8,128)S(1)}, u32[]{:S(2)}, u32[]{:S(2)}) collective-permute-start(f32[80,1024]{1,0:T(8,128)S(1)} %shard_map.157), channel_id=1, source_target_pairs={{0,30},{2,4},{4,2},{6,8},{8,6},{10,12},{12,10},{14,16},{16,14},{18... | collective-permute-start | bytes 983048 | tf_op jit(solution)/shard_map/ppermute | solution.py:691
  43.3 3.5 %shard_map.156 = (f32[16,8,128]{2,1,0:T(8,128)}, f32[80,1024]{1,0:T(8,128)S(1)}, f32[80,1024]{1,0:T(8,128)S(1)}, f32[80,1024]{1,0:T(8,128)S(1)}, f32[8,1024]{1,0:T(8,128)S(1)}) custom-call(bf16[560,240]{1,0:T(8,128)(2,1)S(1)} %get-tuple-element.23.w_ref, f32[88,2048]{1,0:T(8,128)S(1)} %copy-done.9, f32[80,2048]{1,0:T(8,128)S(1)} %get-tuple-element.25.f_ref, ...), custom_call_target="tpu_custom_call" | custom-call | flops 4000000000 | bytes 1000000 | tf_op jit(solution)/shard_map/pallas_call | solution.py:772
  46.8 3.5 %all-to-all-start.1 = ((f32[16,8,128]{2,1,0:T(8,128)}), f32[16,8,128]{2,1,0:T(8,128)S(1)}, u32[]{:S(2)}, u32[]{:S(2)}) async-start(f32[16,8,128]{2,1,0:T(8,128)} %get-tuple-element.41), calls=%async_computation.1 | async-start | bytes 131072 | tf_op jit(solution)/shard_map/all_to_all | solution.py:780
  50.4 1.3 %shard_map.158 = f32[1232,128]{1,0:T(8,128)} custom-call(bf16[80,240]{1,0:T(8,128)(2,1)S(1)} %get-tuple-element.22.w_ref, f32[8,1024]{1,0:T(8,128)S(1)} %get-tuple-element.37.rates_ref, f32[80,1024]{1,0:T(8,128)S(1)} %get-tuple-element.38.n0_ref, f32[80,1024]{1,0:T(8,128)S(1)} %get-tuple-element.39.h0_ref, f32[80,1024]{1,0:T(8,128)S(1)} %get-tuple-element.40.x1_ref, ...), custom_call_target="tpu_custom_call" | custom-call | flops 2000000 | bytes 1000000 | tf_op jit(solution)/shard_map/pallas_call | solution.py:782
  51.7 5.5 %all-to-all-done.1.got_ref = f32[16,8,128]{2,1,0:T(8,128)S(1)} async-done(((f32[16,8,128]{2,1,0:T(8,128)}), f32[16,8,128]{2,1,0:T(8,128)S(1)}, u32[]{:S(2)}, u32[]{:S(2)}) %all-to-all-start.1) | async-done | bytes 65568 | tf_op jit(solution)/shard_map/all_to_all | solution.py:780
  57.2 0.8 %shard_map.159 = f32[7,32,11]{2,1,0:T(8,128)} custom-call(f32[16,8,128]{2,1,0:T(8,128)S(1)} %all-to-all-done.1.got_ref), custom_call_target="tpu_custom_call" | custom-call | flops 2000000 | bytes 1000000 | tf_op jit(solution)/shard_map/pallas_call | solution.py:781
  (45 shorter events, 2.9 us)
Async XLA Ops:
  0.6 13.0 %copy-start = (f32[11,7,2,8,128]{4,3,2,1,0:T(8,128)S(1)}, f32[11,7,2,8,128]{4,3,2,1,0:T(8,128)}, u32[]{:S(2)}) copy-start(f32[11,7,2,8,128]{4,3,2,1,0:T(8,128)} %param.14) | copy-start | bytes 1892356
  0.6 20.4 %collective-permute-start = (f32[1232,128]{1,0:T(8,128)}, f32[1232,128]{1,0:T(8,128)S(1)}, u32[]{:S(2)}, u32[]{:S(2)}) collective-permute-start(f32[1232,128]{1,0:T(8,128)} %bitcast.16), channel_id=1, source_target_pairs={{0,30},{2,4},{4,2},{6,8},{8,6},{10,12},{12,10},{14,16},{16,14},{18... | collective-permute-start | bytes 1892360 | tf_op jit(solution)/shard_map/ppermute | solution.py:691
  6.1 14.9 %collective-permute-start.1 = (f32[1232,128]{1,0:T(8,128)}, f32[1232,128]{1,0:T(8,128)S(1)}, u32[]{:S(2)}, u32[]{:S(2)}) collective-permute-start(f32[1232,128]{1,0:T(8,128)} %bitcast.17), channel_id=1, source_target_pairs={{0,2},{2,0},{4,6},{6,4},{8,10},{10,8},{12,14},{14,12},{16,18},{18,... | collective-permute-start | bytes 1892360 | tf_op jit(solution)/shard_map/ppermute | solution.py:691
  9.6 12.4 %all-to-all-start = ((f32[32,8,128]{2,1,0:T(8,128)}), f32[32,8,128]{2,1,0:T(8,128)S(1)}, u32[]{:S(2)}, u32[]{:S(2)}) async-start(f32[32,8,128]{2,1,0:T(8,128)} %shard_map.151), calls=%async_computation | async-start | bytes 262144 | tf_op jit(solution)/shard_map/all_to_all | solution.py:730
  13.6 6.2 %copy-start.2 = (f32[80,240]{1,0:T(8,128)S(1)}, f32[80,240]{1,0:T(8,128)}, u32[]{:S(2)}) copy-start(f32[80,240]{1,0:T(8,128)} %constant.16.clone.diagonal_ref) | copy-start | bytes 230404
  13.6 6.2 %copy-start.3 = (bf16[80,240]{1,0:T(8,128)(2,1)S(1)}, bf16[80,240]{1,0:T(8,128)(2,1)}, u32[]{:S(2)}) copy-start(bf16[80,240]{1,0:T(8,128)(2,1)} %constant.13.clone.spectral_ref) | copy-start | bytes 115204
  13.6 6.2 %copy-start.4 = (f32[80,7]{1,0:T(8,128)S(1)}, f32[80,7]{1,0:T(8,128)}, u32[]{:S(2)}) copy-start(f32[80,7]{1,0:T(8,128)} %constant.14.clone.rows_ref) | copy-start | bytes 6724
  13.6 6.2 %copy-start.5 = (f32[3,7,7]{2,1,0:T(8,128)S(1)}, f32[3,7,7]{2,1,0:T(8,128)}, u32[]{:S(2)}) copy-start(f32[3,7,7]{2,1,0:T(8,128)} %up_ref.1) | copy-start | bytes 1768
  13.6 6.2 %copy-start.6 = (f32[3,7,7]{2,1,0:T(8,128)S(1)}, f32[3,7,7]{2,1,0:T(8,128)}, u32[]{:S(2)}) copy-start(f32[3,7,7]{2,1,0:T(8,128)} %down_ref.1) | copy-start | bytes 1768
  13.7 6.2 %copy-start.7 = (f32[7,240]{1,0:T(8,128)S(1)}, f32[7,240]{1,0:T(8,128)}, u32[]{:S(2)}) copy-start(f32[7,240]{1,0:T(8,128)} %constant.15.clone.lanes_ref) | copy-start | bytes 20164
  14.0 22.2 %copy-start.8 = (f32[88,2048]{1,0:T(8,128)}, f32[88,2048]{1,0:T(8,128)S(1)}, u32[]{:S(2)}) copy-start(f32[88,2048]{1,0:T(8,128)S(1)} %get-tuple-element.24.m_ref) | copy-start | bytes 2162692
  14.0 7.0 %collective-permute-start.2 = (f32[8,1024]{1,0:T(8,128)S(1)}, f32[8,1024]{1,0:T(8,128)S(1)}, u32[]{:S(2)}, u32[]{:S(2)}) collective-permute-start(f32[8,1024]{1,0:T(8,128)S(1)} %get-tuple-element.27), channel_id=1, source_target_pairs={{0,30},{2,4},{4,2},{6,8},{8,6},{10,12},{12,10},{14,16},{16,14},{18... | collective-permute-start | bytes 98312 | tf_op jit(solution)/shard_map/ppermute | solution.py:691
  18.3 2.7 %collective-permute-start.3 = (f32[8,1024]{1,0:T(8,128)S(1)}, f32[8,1024]{1,0:T(8,128)S(1)}, u32[]{:S(2)}, u32[]{:S(2)}) collective-permute-start(f32[8,1024]{1,0:T(8,128)S(1)} %get-tuple-element.28), channel_id=1, source_target_pairs={{0,2},{2,0},{4,6},{6,4},{8,10},{10,8},{12,14},{14,12},{16,18},{18,... | collective-permute-start | bytes 98312 | tf_op jit(solution)/shard_map/ppermute | solution.py:691
  18.3 7.3 %collective-permute-start.4 = (f32[1,88,512]{2,1,0:T(8,128)S(1)}, f32[1,88,512]{2,1,0:T(8,128)S(1)}, u32[]{:S(2)}, u32[]{:S(2)}) collective-permute-start(f32[1,88,512]{2,1,0:T(8,128)S(1)} %get-tuple-element.29), channel_id=1, source_target_pairs={{0,1},{1,0},{2,3},{3,2},{4,5},{5,4},{6,7},{7,6},{8,9},{9,8},{10,11... | collective-permute-start | bytes 540680 | tf_op jit(solution)/shard_map/ppermute | solution.py:705
  21.1 6.1 %collective-permute-start.5 = (f32[1,88,256]{2,1,0:T(8,128)S(1)}, f32[1,88,256]{2,1,0:T(8,128)S(1)}, u32[]{:S(2)}, u32[]{:S(2)}) collective-permute-start(f32[1,88,256]{2,1,0:T(8,128)S(1)} %shard_map.153), channel_id=1, source_target_pairs={{0,1},{1,0},{2,3},{3,2},{4,5},{5,4},{6,7},{7,6},{8,9},{9,8},{10,11... | collective-permute-start | bytes 270344 | tf_op jit(solution)/shard_map/ppermute | solution.py:705
  30.4 12.9 %collective-permute-start.7 = (f32[80,2048]{1,0:T(8,128)S(1)}, f32[80,2048]{1,0:T(8,128)S(1)}, u32[]{:S(2)}, u32[]{:S(2)}) collective-permute-start(f32[80,2048]{1,0:T(8,128)S(1)} %get-tuple-element.31.x_ref), channel_id=1, source_target_pairs={{0,2},{2,0},{4,6},{6,4},{8,10},{10,8},{12,14},{14,12},{16,18},{18,... | collective-permute-start | bytes 1966088 | tf_op jit(solution)/shard_map/ppermute | solution.py:691
  30.4 12.9 %collective-permute-start.6 = (f32[80,1024]{1,0:T(8,128)S(1)}, f32[80,1024]{1,0:T(8,128)S(1)}, u32[]{:S(2)}, u32[]{:S(2)}) collective-permute-start(f32[80,1024]{1,0:T(8,128)S(1)} %get-tuple-element.32), channel_id=1, source_target_pairs={{0,30},{2,4},{4,2},{6,8},{8,6},{10,12},{12,10},{14,16},{16,14},{18... | collective-permute-start | bytes 983048 | tf_op jit(solution)/shard_map/ppermute | solution.py:691
  33.5 6.5 %collective-permute-start.8 = (f32[1,80,512]{2,1,0:T(8,128)S(1)}, f32[1,80,512]{2,1,0:T(8,128)S(1)}, u32[]{:S(2)}, u32[]{:S(2)}) collective-permute-start(f32[1,80,512]{2,1,0:T(8,128)S(1)} %get-tuple-element.33), channel_id=1, source_target_pairs={{0,1},{1,0},{2,3},{3,2},{4,5},{5,4},{6,7},{7,6},{8,9},{9,8},{10,11... | collective-permute-start | bytes 491528 | tf_op jit(solution)/shard_map/ppermute | solution.py:705
  35.0 8.3 %collective-permute-start.9 = (f32[1,80,128]{2,1,0:T(8,128)S(1)}, f32[1,80,128]{2,1,0:T(8,128)S(1)}, u32[]{:S(2)}, u32[]{:S(2)}) collective-permute-start(f32[1,80,128]{2,1,0:T(8,128)S(1)} %get-tuple-element.34), channel_id=1, source_target_pairs={{0,31},{1,30},{2,5},{3,4},{4,3},{5,2},{6,9},{7,8},{8,7},{9,6},{10,... | collective-permute-start | bytes 122888 | tf_op jit(solution)/shard_map/ppermute | solution.py:705
  36.1 3.9 %collective-permute-start.10 = (f32[1,80,128]{2,1,0:T(8,128)S(1)}, f32[1,80,128]{2,1,0:T(8,128)S(1)}, u32[]{:S(2)}, u32[]{:S(2)}) collective-permute-start(f32[1,80,128]{2,1,0:T(8,128)S(1)} %get-tuple-element.35), channel_id=1, source_target_pairs={{0,3},{1,2},{2,1},{3,0},{4,7},{5,6},{6,5},{7,4},{8,11},{9,10},{10,... | collective-permute-start | bytes 122888 | tf_op jit(solution)/shard_map/ppermute | solution.py:705
  36.9 6.4 %copy-start.9 = (f32[88,2048]{1,0:T(8,128)S(1)}, f32[88,2048]{1,0:T(8,128)}, u32[]{:S(2)}) copy-start(f32[88,2048]{1,0:T(8,128)} %copy-done.8) | copy-start | bytes 2162692
  37.0 6.4 %copy-start.11 = (f32[1,88,512]{2,1,0:T(8,128)S(1)}, f32[1,88,512]{2,1,0:T(8,128)}, u32[]{:S(2)}) copy-start(f32[1,88,512]{2,1,0:T(8,128)} %copy-done.10) | copy-start | bytes 540676
  40.1 10.2 %collective-permute-start.11 = (f32[80,1024]{1,0:T(8,128)S(1)}, f32[80,1024]{1,0:T(8,128)S(1)}, u32[]{:S(2)}, u32[]{:S(2)}) collective-permute-start(f32[80,1024]{1,0:T(8,128)S(1)} %shard_map.157), channel_id=1, source_target_pairs={{0,30},{2,4},{4,2},{6,8},{8,6},{10,12},{12,10},{14,16},{16,14},{18... | collective-permute-start | bytes 983048 | tf_op jit(solution)/shard_map/ppermute | solution.py:691
  46.8 10.4 %all-to-all-start.1 = ((f32[16,8,128]{2,1,0:T(8,128)}), f32[16,8,128]{2,1,0:T(8,128)S(1)}, u32[]{:S(2)}, u32[]{:S(2)}) async-start(f32[16,8,128]{2,1,0:T(8,128)} %get-tuple-element.41), calls=%async_computation.1 | async-start | bytes 131072 | tf_op jit(solution)/shard_map/all_to_all | solution.py:780
  (2 other events, 5.6 us)

commit v16 on v15

--- a/solution.py
+++ b/solution.py
@@ -479,13 +479,14 @@
     down_out[...] = matrix(plan, out_ref, DOWN_AZ)
 
 
-def send_panels(plan, stator_ref, both_ref, out_ref, panels_ref):
+def send_panels(plan, stator_ref, both_ref, table_ref, out_ref, panels_ref):
     me = lax.axis_index("sector")
     for f in range(plan.fields):
         panels_ref[pl.ds(f, plan.insts, stride=RATES), : plan.width] = jnp.transpose(stator_ref[f])
     out_ref[...] = jnp.zeros_like(out_ref)
     for t, (row, start) in enumerate(plan.weight_at):
-        both = jnp.broadcast_to(both_ref[t : t + 1, :][None], (out_ref.shape[0], 1, plan.width))
+        both = both_ref[t : t + 1, :] + 0.0 * table_ref[0:1, 0:1]
+        both = jnp.broadcast_to(both[None], (out_ref.shape[0], 1, plan.width))
         out_ref[:, row : row + 1, start : start + plan.width] = both
     for o, slots in enumerate(plan.slots):
         to = lax.rem(me + (plan.sectors - o), plan.sectors) * plan.spans
@@ -720,14 +721,6 @@
     def edges(rows):
         return f32(ends, rows, DEPTH * plan.ct * LANES), f32(ends, rows, LANES), f32(ends, rows, LANES)
 
-    stator = jnp.transpose(stator_adj, (1, 2, 3, 0)).reshape(fields, plan.width, insts)
-    sent = call(bind(send_panels, plan), f32(sectors * spans, RATES, LANES), (vmem(insts * RATES, LANES),))(
-        stator,
-        jnp.concatenate([
-            lax.rem(owner, plan.panels).astype(jnp.float32).reshape(insts, cells), first_panel_share.reshape(insts, cells),
-        ], axis=1),
-    )
-    got = lax.all_to_all(sent, AXES, 0, 0, tiled=True)
     native = rhs.reshape(plan.tf * cells, LANES)
     low_first, high_first = swap(native, next_chip), swap(native, next_core)
     m, table0, table1, side = call(
@@ -742,6 +735,15 @@
         ]),
     )
     low_table, high_table = swap(table0, next_chip), swap(table1, next_core)
+    stator = jnp.transpose(stator_adj, (1, 2, 3, 0)).reshape(fields, plan.width, insts)
+    sent = call(bind(send_panels, plan), f32(sectors * spans, RATES, LANES), (vmem(insts * RATES, LANES),))(
+        stator,
+        jnp.concatenate([
+            lax.rem(owner, plan.panels).astype(jnp.float32).reshape(insts, cells), first_panel_share.reshape(insts, cells),
+        ], axis=1),
+        table0,
+    )
+    got = lax.all_to_all(sent, AXES, 0, 0, tiled=True)
     side_first = beside(plan, side, alone)
     corner = call(bind(corner_rows, plan), f32(ends, pad + RATES, plan.ct * LANES))(
         low_first, high_first, low_table, high_table

time: 58.5 us -> 58.5 us (level)
  other arithmetic: 2.23 us -> 0.09 us
  local copies, waits for them, and re-layouts: 1.82 us -> 3.85 us
  starting transfers between devices: 27.2 us -> 27.9 us
  waiting for transfers between devices: 12.2 us -> 11.6 us
    unnamed x24 -> x30, local copies, waits for them, and re-layouts: 0.96 us -> 2.97 us
    ppermute x5, waiting for transfers between devices: 6.62 us -> 5.07 us  [beside(): return lax.ppermute(array, AXES, pairs(0))]
    ppermute x7, waiting for transfers between devices: 0.02 us -> 0.97 us  [swap(): return lax.ppermute(array, 'sector', list(enumerate(partner)))]
    ppermute x5, starting transfers between devices: 4.97 us -> 5.76 us  [beside(): return lax.ppermute(array, AXES, pairs(0))]
    concatenate x1, other arithmetic: 0.74 us -> 0.01 us  [on_device(): jnp.concatenate([wall_mask.astype(jnp.float32).reshape(cells, LANES), dia...]
    reshape x1, other arithmetic: 0.7 us -> 0.01 us  [on_device(): wall_mask.astype(jnp.float32).reshape(cells, LANES)]
    reshape x1, other arithmetic: 0.7 us -> 0.01 us  [on_device(): lax.rem(owner, plan.panels).astype(jnp.float32).reshape(insts, cells)]
  transfers between devices with their start and end apart: 14 -> 14, of which waited for: 4 -> 5; matrix products, arithmetic and copies ran while one was open for 5% -> 2% of each run, Pallas kernels for 17% -> 17%
where the time goes in v16:
time: 58.5 us; the launch traced here: 57.9 us
  starting transfers between devices  27.9 us (48%)
  Pallas kernels  13.7 us (23%)
  waiting for transfers between devices  11.6 us (20%)
  local copies, waits for them, and re-layouts  3.85 us (7%)
  between operations  0.81 us (1%)
    ppermute x7, starting transfers between devices, swap(): return lax.ppermute(array, 'sector', list(enumerate(partner)))  15.9 us
    ppermute x5, starting transfers between devices, beside(): return lax.ppermute(array, AXES, pairs(0))  5.76 us
    all_to_all x1, waiting for transfers between devices, on_device(): returned = lax.all_to_all(back, 'sector', 0, 0, tiled=True)  5.54 us
    ppermute x5, waiting for transfers between devices, beside(): return lax.ppermute(array, AXES, pairs(0))  5.07 us
    pallas_call x1, Pallas kernels, on_device(): call(bind(middle, plan), (f32(sectors, RATES, LANES), half, half, half, f...  3.53 us
    all_to_all x1, starting transfers between devices, on_device(): returned = lax.all_to_all(back, 'sector', 0, 0, tiled=True)  3.5 us
    pallas_call x1, Pallas kernels, on_device(): call(bind(first_half, plan), (whole, half) + edges(pad), products + (vmem...  3.13 us
    unnamed x30, local copies, waits for them, and re-layouts  2.97 us
  transfers between devices with their start and end apart: 14, of which 5 were waited for; matrix products, arithmetic and copies ran while one was open for 2% of the time, Pallas kernels for 17%

profile of v16, /device:TPU:0, one launch (start us, length us, event | category | flops | bytes accessed | tf_op | source)
XLA Modules:
  0.0 57.9 jit_solution(15466021337719155168)
XLA Ops:
  0.6 5.5 %collective-permute-start = (f32[1232,128]{1,0:T(8,128)}, f32[1232,128]{1,0:T(8,128)S(1)}, u32[]{:S(2)}, u32[]{:S(2)}) collective-permute-start(f32[1232,128]{1,0:T(8,128)} %bitcast.16), channel_id=1, source_target_pairs={{0,30},{2,4},{4,2},{6,8},{8,6},{10,12},{12,10},{14,16},{16,14},{18... | collective-permute-start | bytes 1892360 | tf_op jit(solution)/shard_map/ppermute | solution.py:692
  6.1 0.8 %copy.19 = f32[11,16]{1,0:T(8,128)S(1)} copy(f32[11,16]{0,1:T(8,128)} %bitcast.25) | data formatting | bytes 1408 | tf_op jit(solution)/shard_map/reshape | solution.py:742
  8.4 1.1 %copy-done = f32[11,7,2,8,128]{4,3,2,1,0:T(8,128)S(1)} copy-done((f32[11,7,2,8,128]{4,3,2,1,0:T(8,128)S(1)}, f32[11,7,2,8,128]{4,3,2,1,0:T(8,128)}, u32[]{:S(2)}) %copy-start) | copy-done | bytes 630808
  10.4 0.9 %shard_map.151 = f32[32,8,128]{2,1,0:T(8,128)} custom-call(f32[7,32,11]{2,1,0:T(8,128)S(1)} %bitcast.19, f32[11,32]{1,0:T(8,128)S(1)} %pad_maximum_fusion.1.both_ref, f32[8,1024]{1,0:T(8,128)S(1)} %get-tuple-element.25.table_ref), custom_call_target="tpu_custom_call" | custom-call | flops 2000000 | bytes 1000000 | tf_op jit(solution)/shard_map/pallas_call | solution.py:739
  11.3 2.7 %all-to-all-start = ((f32[32,8,128]{2,1,0:T(8,128)}), f32[32,8,128]{2,1,0:T(8,128)S(1)}, u32[]{:S(2)}, u32[]{:S(2)}) async-start(f32[32,8,128]{2,1,0:T(8,128)} %shard_map.151), calls=%async_computation | async-start | bytes 262144 | tf_op jit(solution)/shard_map/all_to_all | solution.py:746
  14.0 4.4 %collective-permute-start.2 = (f32[8,1024]{1,0:T(8,128)S(1)}, f32[8,1024]{1,0:T(8,128)S(1)}, u32[]{:S(2)}, u32[]{:S(2)}) collective-permute-start(f32[8,1024]{1,0:T(8,128)S(1)} %get-tuple-element.25.table_ref), channel_id=1, source_target_pairs={{0,30},{2,4},{4,2},{6,8},{8,6},{10,12},{12,10},{14,16},{16,14},{18... | collective-permute-start | bytes 98312 | tf_op jit(solution)/shard_map/ppermute | solution.py:692
  18.4 1.5 %collective-permute-start.4 = (f32[1,88,512]{2,1,0:T(8,128)S(1)}, f32[1,88,512]{2,1,0:T(8,128)S(1)}, u32[]{:S(2)}, u32[]{:S(2)}) collective-permute-start(f32[1,88,512]{2,1,0:T(8,128)S(1)} %get-tuple-element.29), channel_id=1, source_target_pairs={{0,1},{1,0},{2,3},{3,2},{4,5},{5,4},{6,7},{7,6},{8,9},{9,8},{10,11... | collective-permute-start | bytes 540680 | tf_op jit(solution)/shard_map/ppermute | solution.py:706
  19.9 1.1 %shard_map.149 = (bf16[560,240]{1,0:T(8,128)(2,1)S(1)}, bf16[80,240]{1,0:T(8,128)(2,1)S(1)}) custom-call(f32[3,7,7]{2,1,0:T(8,128)S(1)} %copy-done.5, f32[3,7,7]{2,1,0:T(8,128)S(1)} %copy-done.6, bf16[80,240]{1,0:T(8,128)(2,1)S(1)} %copy-done.3, f32[80,7]{1,0:T(8,128)S(1)} %copy-done.4, f32[7,240]{1,0:T(8,128)S(1)} %copy-done.7, f32[80,240]{1,0:T(8,128)S(1)} %copy-done.2), custom_call_target="tpu_custom_call" | custom-call | flops 2000000 | bytes 1000000 | tf_op jit(solution)/shard_map/pallas_call | solution.py:752
  21.1 1.0 %collective-permute-done.2.low_table = f32[8,1024]{1,0:T(8,128)S(1)} collective-permute-done((f32[8,1024]{1,0:T(8,128)S(1)}, f32[8,1024]{1,0:T(8,128)S(1)}, u32[]{:S(2)}, u32[]{:S(2)}) %collective-permute-start.2) | collective-permute-done | bytes 32800 | tf_op jit(solution)/shard_map/ppermute | solution.py:692
  22.1 1.5 %collective-permute-start.5 = (f32[1,88,256]{2,1,0:T(8,128)S(1)}, f32[1,88,256]{2,1,0:T(8,128)S(1)}, u32[]{:S(2)}, u32[]{:S(2)}) collective-permute-start(f32[1,88,256]{2,1,0:T(8,128)S(1)} %shard_map.153), channel_id=1, source_target_pairs={{0,1},{1,0},{2,3},{3,2},{4,5},{5,4},{6,7},{7,6},{8,9},{9,8},{10,11... | collective-permute-start | bytes 270344 | tf_op jit(solution)/shard_map/ppermute | solution.py:706
  23.6 1.7 %shard_map.152 = (f32[3,2,80,128]{3,2,1,0:T(8,128)S(1)}, f32[80,128]{1,0:T(8,128)S(1)}, f32[80,2048]{1,0:T(8,128)S(1)}, f32[80,2048]{1,0:T(8,128)S(1)}) custom-call(bf16[560,240]{1,0:T(8,128)(2,1)S(1)} %get-tuple-element.23.w_ref, f32[88,2048]{1,0:T(8,128)S(1)} %get-tuple-element.24.m_ref, f32[32,8,128]{2,1,0:T(8,128)S(1)} %all-to-all-done.got_ref), custom_call_target="tpu_custom_call" | custom-call | flops 2000000000 | bytes 1000000 | tf_op jit(solution)/shard_map/pallas_call | solution.py:757
  25.8 1.6 %collective-permute-done.5.corner_ref = f32[1,88,256]{2,1,0:T(8,128)S(1)} collective-permute-done((f32[1,88,256]{2,1,0:T(8,128)S(1)}, f32[1,88,256]{2,1,0:T(8,128)S(1)}, u32[]{:S(2)}, u32[]{:S(2)}) %collective-permute-start.5) | collective-permute-done | bytes 90144 | tf_op jit(solution)/shard_map/ppermute | solution.py:706
  27.3 3.1 %shard_map.154 = (f32[80,2048]{1,0:T(8,128)S(1)}, f32[80,1024]{1,0:T(8,128)S(1)}, f32[1,80,512]{2,1,0:T(8,128)S(1)}, f32[1,80,128]{2,1,0:T(8,128)S(1)}, f32[1,80,128]{2,1,0:T(8,128)S(1)}) custom-call(bf16[560,240]{1,0:T(8,128)(2,1)S(1)} %get-tuple-element.23.w_ref, f32[88,2048]{1,0:T(8,128)S(1)} %get-tuple-element.24.m_ref, ...), custom_call_target="tpu_custom_call" | custom-call | flops 4000000000 | bytes 1000000 | tf_op jit(solution)/shard_map/pallas_call | solution.py:762
  30.5 3.0 %collective-permute-start.6 = (f32[80,1024]{1,0:T(8,128)S(1)}, f32[80,1024]{1,0:T(8,128)S(1)}, u32[]{:S(2)}, u32[]{:S(2)}) collective-permute-start(f32[80,1024]{1,0:T(8,128)S(1)} %get-tuple-element.32), channel_id=1, source_target_pairs={{0,30},{2,4},{4,2},{6,8},{8,6},{10,12},{12,10},{14,16},{16,14},{18... | collective-permute-start | bytes 983048 | tf_op jit(solution)/shard_map/ppermute | solution.py:692
  33.5 1.5 %collective-permute-start.8 = (f32[1,80,512]{2,1,0:T(8,128)S(1)}, f32[1,80,512]{2,1,0:T(8,128)S(1)}, u32[]{:S(2)}, u32[]{:S(2)}) collective-permute-start(f32[1,80,512]{2,1,0:T(8,128)S(1)} %get-tuple-element.33), channel_id=1, source_target_pairs={{0,1},{1,0},{2,3},{3,2},{4,5},{5,4},{6,7},{7,6},{8,9},{9,8},{10,11... | collective-permute-start | bytes 491528 | tf_op jit(solution)/shard_map/ppermute | solution.py:706
  35.0 1.2 %collective-permute-start.9 = (f32[1,80,128]{2,1,0:T(8,128)S(1)}, f32[1,80,128]{2,1,0:T(8,128)S(1)}, u32[]{:S(2)}, u32[]{:S(2)}) collective-permute-start(f32[1,80,128]{2,1,0:T(8,128)S(1)} %get-tuple-element.34), channel_id=1, source_target_pairs={{0,31},{1,30},{2,5},{3,4},{4,3},{5,2},{6,9},{7,8},{8,7},{9,6},{10,... | collective-permute-start | bytes 122888 | tf_op jit(solution)/shard_map/ppermute | solution.py:706
  36.2 0.8 %shard_map.155.g_ref = f32[80,2048]{1,0:T(8,128)S(1)} custom-call(bf16[560,240]{1,0:T(8,128)(2,1)S(1)} %get-tuple-element.23.w_ref, f32[88,2048]{1,0:T(8,128)S(1)} %get-tuple-element.24.m_ref, f32[80,2048]{1,0:T(8,128)S(1)} %get-tuple-element.26.f_ref, f32[80,2048]{1,0:T(8,128)S(1)} %get-tuple-element.31.x_ref), custom_call_target="tpu_custom_call" | custom-call | flops 2000000000 | bytes 1000000 | tf_op jit(solution)/shard_map/pallas_call | solution.py:771
  37.0 3.1 %collective-permute-done.10.c_high = f32[1,80,128]{2,1,0:T(8,128)S(1)} collective-permute-done((f32[1,80,128]{2,1,0:T(8,128)S(1)}, f32[1,80,128]{2,1,0:T(8,128)S(1)}, u32[]{:S(2)}, u32[]{:S(2)}) %collective-permute-start.10) | collective-permute-done | bytes 40992 | tf_op jit(solution)/shard_map/ppermute | solution.py:706
  40.2 3.1 %collective-permute-start.11 = (f32[80,1024]{1,0:T(8,128)S(1)}, f32[80,1024]{1,0:T(8,128)S(1)}, u32[]{:S(2)}, u32[]{:S(2)}) collective-permute-start(f32[80,1024]{1,0:T(8,128)S(1)} %shard_map.157), channel_id=1, source_target_pairs={{0,30},{2,4},{4,2},{6,8},{8,6},{10,12},{12,10},{14,16},{16,14},{18... | collective-permute-start | bytes 983048 | tf_op jit(solution)/shard_map/ppermute | solution.py:692
  43.3 3.5 %shard_map.156 = (f32[16,8,128]{2,1,0:T(8,128)}, f32[80,1024]{1,0:T(8,128)S(1)}, f32[80,1024]{1,0:T(8,128)S(1)}, f32[80,1024]{1,0:T(8,128)S(1)}, f32[8,1024]{1,0:T(8,128)S(1)}) custom-call(bf16[560,240]{1,0:T(8,128)(2,1)S(1)} %get-tuple-element.23.w_ref, f32[88,2048]{1,0:T(8,128)S(1)} %copy-done.9, f32[80,2048]{1,0:T(8,128)S(1)} %get-tuple-element.26.f_ref, ...), custom_call_target="tpu_custom_call" | custom-call | flops 4000000000 | bytes 1000000 | tf_op jit(solution)/shard_map/pallas_call | solution.py:774
  46.8 3.5 %all-to-all-start.1 = ((f32[16,8,128]{2,1,0:T(8,128)}), f32[16,8,128]{2,1,0:T(8,128)S(1)}, u32[]{:S(2)}, u32[]{:S(2)}) async-start(f32[16,8,128]{2,1,0:T(8,128)} %get-tuple-element.41), calls=%async_computation.1 | async-start | bytes 131072 | tf_op jit(solution)/shard_map/all_to_all | solution.py:782
  50.3 1.3 %shard_map.158 = f32[1232,128]{1,0:T(8,128)} custom-call(bf16[80,240]{1,0:T(8,128)(2,1)S(1)} %get-tuple-element.22.w_ref, f32[8,1024]{1,0:T(8,128)S(1)} %get-tuple-element.37.rates_ref, f32[80,1024]{1,0:T(8,128)S(1)} %get-tuple-element.38.n0_ref, f32[80,1024]{1,0:T(8,128)S(1)} %get-tuple-element.39.h0_ref, f32[80,1024]{1,0:T(8,128)S(1)} %get-tuple-element.40.x1_ref, ...), custom_call_target="tpu_custom_call" | custom-call | flops 2000000 | bytes 1000000 | tf_op jit(solution)/shard_map/pallas_call | solution.py:784
  51.6 5.5 %all-to-all-done.1.got_ref = f32[16,8,128]{2,1,0:T(8,128)S(1)} async-done(((f32[16,8,128]{2,1,0:T(8,128)}), f32[16,8,128]{2,1,0:T(8,128)S(1)}, u32[]{:S(2)}, u32[]{:S(2)}) %all-to-all-start.1) | async-done | bytes 65568 | tf_op jit(solution)/shard_map/all_to_all | solution.py:782
  57.2 0.8 %shard_map.159 = f32[7,32,11]{2,1,0:T(8,128)} custom-call(f32[16,8,128]{2,1,0:T(8,128)S(1)} %all-to-all-done.1.got_ref), custom_call_target="tpu_custom_call" | custom-call | flops 2000000 | bytes 1000000 | tf_op jit(solution)/shard_map/pallas_call | solution.py:783
  (51 shorter events, 2.9 us)
Async XLA Ops:
  0.6 21.4 %collective-permute-start = (f32[1232,128]{1,0:T(8,128)}, f32[1232,128]{1,0:T(8,128)S(1)}, u32[]{:S(2)}, u32[]{:S(2)}) collective-permute-start(f32[1232,128]{1,0:T(8,128)} %bitcast.16), channel_id=1, source_target_pairs={{0,30},{2,4},{4,2},{6,8},{8,6},{10,12},{12,10},{14,16},{16,14},{18... | collective-permute-start | bytes 1892360 | tf_op jit(solution)/shard_map/ppermute | solution.py:692
  6.1 15.9 %collective-permute-start.1 = (f32[1232,128]{1,0:T(8,128)}, f32[1232,128]{1,0:T(8,128)S(1)}, u32[]{:S(2)}, u32[]{:S(2)}) collective-permute-start(f32[1232,128]{1,0:T(8,128)} %bitcast.17), channel_id=1, source_target_pairs={{0,2},{2,0},{4,6},{6,4},{8,10},{10,8},{12,14},{14,12},{16,18},{18,... | collective-permute-start | bytes 1892360 | tf_op jit(solution)/shard_map/ppermute | solution.py:692
  8.4 1.1 %copy-start = (f32[11,7,2,8,128]{4,3,2,1,0:T(8,128)S(1)}, f32[11,7,2,8,128]{4,3,2,1,0:T(8,128)}, u32[]{:S(2)}) copy-start(f32[11,7,2,8,128]{4,3,2,1,0:T(8,128)} %param.14) | copy-start | bytes 1892356
  9.5 0.9 %copy-start.1 = (f32[11,7,4,8]{0,3,2,1:T(8,128)S(1)}, f32[11,7,4,8]{0,3,2,1:T(8,128)}, u32[]{:S(2)}) copy-start(f32[11,7,4,8]{0,3,2,1:T(8,128)} %param.21) | copy-start | bytes 29572
  9.7 26.5 %copy-start.8 = (f32[88,2048]{1,0:T(8,128)}, f32[88,2048]{1,0:T(8,128)S(1)}, u32[]{:S(2)}) copy-start(f32[88,2048]{1,0:T(8,128)S(1)} %get-tuple-element.24.m_ref) | copy-start | bytes 2162692
  11.3 8.6 %copy-start.2 = (f32[80,240]{1,0:T(8,128)S(1)}, f32[80,240]{1,0:T(8,128)}, u32[]{:S(2)}) copy-start(f32[80,240]{1,0:T(8,128)} %constant.16.clone.diagonal_ref) | copy-start | bytes 230404
  11.3 8.6 %copy-start.3 = (bf16[80,240]{1,0:T(8,128)(2,1)S(1)}, bf16[80,240]{1,0:T(8,128)(2,1)}, u32[]{:S(2)}) copy-start(bf16[80,240]{1,0:T(8,128)(2,1)} %constant.13.clone.spectral_ref) | copy-start | bytes 115204
  11.3 8.6 %copy-start.4 = (f32[80,7]{1,0:T(8,128)S(1)}, f32[80,7]{1,0:T(8,128)}, u32[]{:S(2)}) copy-start(f32[80,7]{1,0:T(8,128)} %constant.14.clone.rows_ref) | copy-start | bytes 6724
  11.3 8.6 %copy-start.5 = (f32[3,7,7]{2,1,0:T(8,128)S(1)}, f32[3,7,7]{2,1,0:T(8,128)}, u32[]{:S(2)}) copy-start(f32[3,7,7]{2,1,0:T(8,128)} %up_ref.1) | copy-start | bytes 1768
  11.3 8.6 %copy-start.6 = (f32[3,7,7]{2,1,0:T(8,128)S(1)}, f32[3,7,7]{2,1,0:T(8,128)}, u32[]{:S(2)}) copy-start(f32[3,7,7]{2,1,0:T(8,128)} %down_ref.1) | copy-start | bytes 1768
  11.3 8.6 %copy-start.7 = (f32[7,240]{1,0:T(8,128)S(1)}, f32[7,240]{1,0:T(8,128)}, u32[]{:S(2)}) copy-start(f32[7,240]{1,0:T(8,128)} %constant.15.clone.lanes_ref) | copy-start | bytes 20164
  11.3 12.3 %all-to-all-start = ((f32[32,8,128]{2,1,0:T(8,128)}), f32[32,8,128]{2,1,0:T(8,128)S(1)}, u32[]{:S(2)}, u32[]{:S(2)}) async-start(f32[32,8,128]{2,1,0:T(8,128)} %shard_map.151), calls=%async_computation | async-start | bytes 262144 | tf_op jit(solution)/shard_map/all_to_all | solution.py:746
  14.0 8.0 %collective-permute-start.2 = (f32[8,1024]{1,0:T(8,128)S(1)}, f32[8,1024]{1,0:T(8,128)S(1)}, u32[]{:S(2)}, u32[]{:S(2)}) collective-permute-start(f32[8,1024]{1,0:T(8,128)S(1)} %get-tuple-element.25.table_ref), channel_id=1, source_target_pairs={{0,30},{2,4},{4,2},{6,8},{8,6},{10,12},{12,10},{14,16},{16,14},{18... | collective-permute-start | bytes 98312 | tf_op jit(solution)/shard_map/ppermute | solution.py:692
  18.4 3.6 %collective-permute-start.3 = (f32[8,1024]{1,0:T(8,128)S(1)}, f32[8,1024]{1,0:T(8,128)S(1)}, u32[]{:S(2)}, u32[]{:S(2)}) collective-permute-start(f32[8,1024]{1,0:T(8,128)S(1)} %get-tuple-element.28), channel_id=1, source_target_pairs={{0,2},{2,0},{4,6},{6,4},{8,10},{10,8},{12,14},{14,12},{16,18},{18,... | collective-permute-start | bytes 98312 | tf_op jit(solution)/shard_map/ppermute | solution.py:692
  18.4 7.3 %collective-permute-start.4 = (f32[1,88,512]{2,1,0:T(8,128)S(1)}, f32[1,88,512]{2,1,0:T(8,128)S(1)}, u32[]{:S(2)}, u32[]{:S(2)}) collective-permute-start(f32[1,88,512]{2,1,0:T(8,128)S(1)} %get-tuple-element.29), channel_id=1, source_target_pairs={{0,1},{1,0},{2,3},{3,2},{4,5},{5,4},{6,7},{7,6},{8,9},{9,8},{10,11... | collective-permute-start | bytes 540680 | tf_op jit(solution)/shard_map/ppermute | solution.py:706
  22.1 5.2 %collective-permute-start.5 = (f32[1,88,256]{2,1,0:T(8,128)S(1)}, f32[1,88,256]{2,1,0:T(8,128)S(1)}, u32[]{:S(2)}, u32[]{:S(2)}) collective-permute-start(f32[1,88,256]{2,1,0:T(8,128)S(1)} %shard_map.153), channel_id=1, source_target_pairs={{0,1},{1,0},{2,3},{3,2},{4,5},{5,4},{6,7},{7,6},{8,9},{9,8},{10,11... | collective-permute-start | bytes 270344 | tf_op jit(solution)/shard_map/ppermute | solution.py:706
  30.5 12.8 %collective-permute-start.7 = (f32[80,2048]{1,0:T(8,128)S(1)}, f32[80,2048]{1,0:T(8,128)S(1)}, u32[]{:S(2)}, u32[]{:S(2)}) collective-permute-start(f32[80,2048]{1,0:T(8,128)S(1)} %get-tuple-element.31.x_ref), channel_id=1, source_target_pairs={{0,2},{2,0},{4,6},{6,4},{8,10},{10,8},{12,14},{14,12},{16,18},{18,... | collective-permute-start | bytes 1966088 | tf_op jit(solution)/shard_map/ppermute | solution.py:692
  30.5 12.7 %collective-permute-start.6 = (f32[80,1024]{1,0:T(8,128)S(1)}, f32[80,1024]{1,0:T(8,128)S(1)}, u32[]{:S(2)}, u32[]{:S(2)}) collective-permute-start(f32[80,1024]{1,0:T(8,128)S(1)} %get-tuple-element.32), channel_id=1, source_target_pairs={{0,30},{2,4},{4,2},{6,8},{8,6},{10,12},{12,10},{14,16},{16,14},{18... | collective-permute-start | bytes 983048 | tf_op jit(solution)/shard_map/ppermute | solution.py:692
  33.5 6.6 %collective-permute-start.8 = (f32[1,80,512]{2,1,0:T(8,128)S(1)}, f32[1,80,512]{2,1,0:T(8,128)S(1)}, u32[]{:S(2)}, u32[]{:S(2)}) collective-permute-start(f32[1,80,512]{2,1,0:T(8,128)S(1)} %get-tuple-element.33), channel_id=1, source_target_pairs={{0,1},{1,0},{2,3},{3,2},{4,5},{5,4},{6,7},{7,6},{8,9},{9,8},{10,11... | collective-permute-start | bytes 491528 | tf_op jit(solution)/shard_map/ppermute | solution.py:706
  35.0 8.3 %collective-permute-start.9 = (f32[1,80,128]{2,1,0:T(8,128)S(1)}, f32[1,80,128]{2,1,0:T(8,128)S(1)}, u32[]{:S(2)}, u32[]{:S(2)}) collective-permute-start(f32[1,80,128]{2,1,0:T(8,128)S(1)} %get-tuple-element.34), channel_id=1, source_target_pairs={{0,31},{1,30},{2,5},{3,4},{4,3},{5,2},{6,9},{7,8},{8,7},{9,6},{10,... | collective-permute-start | bytes 122888 | tf_op jit(solution)/shard_map/ppermute | solution.py:706
  36.2 3.9 %collective-permute-start.10 = (f32[1,80,128]{2,1,0:T(8,128)S(1)}, f32[1,80,128]{2,1,0:T(8,128)S(1)}, u32[]{:S(2)}, u32[]{:S(2)}) collective-permute-start(f32[1,80,128]{2,1,0:T(8,128)S(1)} %get-tuple-element.35), channel_id=1, source_target_pairs={{0,3},{1,2},{2,1},{3,0},{4,7},{5,6},{6,5},{7,4},{8,11},{9,10},{10,... | collective-permute-start | bytes 122888 | tf_op jit(solution)/shard_map/ppermute | solution.py:706
  37.0 6.2 %copy-start.9 = (f32[88,2048]{1,0:T(8,128)S(1)}, f32[88,2048]{1,0:T(8,128)}, u32[]{:S(2)}) copy-start(f32[88,2048]{1,0:T(8,128)} %copy-done.8) | copy-start | bytes 2162692
  40.2 10.1 %collective-permute-start.11 = (f32[80,1024]{1,0:T(8,128)S(1)}, f32[80,1024]{1,0:T(8,128)S(1)}, u32[]{:S(2)}, u32[]{:S(2)}) collective-permute-start(f32[80,1024]{1,0:T(8,128)S(1)} %shard_map.157), channel_id=1, source_target_pairs={{0,30},{2,4},{4,2},{6,8},{8,6},{10,12},{12,10},{14,16},{16,14},{18... | collective-permute-start | bytes 983048 | tf_op jit(solution)/shard_map/ppermute | solution.py:692
  46.8 10.4 %all-to-all-start.1 = ((f32[16,8,128]{2,1,0:T(8,128)}), f32[16,8,128]{2,1,0:T(8,128)S(1)}, u32[]{:S(2)}, u32[]{:S(2)}) async-start(f32[16,8,128]{2,1,0:T(8,128)} %get-tuple-element.41), calls=%async_computation.1 | async-start | bytes 131072 | tf_op jit(solution)/shard_map/all_to_all | solution.py:782
  (5 other events, 3.6 us)

commit v17 on v16

--- a/solution.py
+++ b/solution.py
@@ -741,7 +741,7 @@
         jnp.concatenate([
             lax.rem(owner, plan.panels).astype(jnp.float32).reshape(insts, cells), first_panel_share.reshape(insts, cells),
         ], axis=1),
-        table0,
+        high_table,
     )
     got = lax.all_to_all(sent, AXES, 0, 0, tiled=True)
     side_first = beside(plan, side, alone)

time: 58.5 us -> 58.4 us (level)
  local copies, waits for them, and re-layouts: 3.85 us -> 1.91 us
  other arithmetic: 0.09 us -> 1.53 us
  starting transfers between devices: 27.9 us -> 28.7 us
    ppermute x7, starting transfers between devices: 15.9 us -> 17.3 us  [swap(): return lax.ppermute(array, 'sector', list(enumerate(partner)))]
    unnamed x30 -> x28, local copies, waits for them, and re-layouts: 2.97 us -> 1.75 us
    concatenate x1, other arithmetic: 0.01 us -> 0.74 us  [on_device(): jnp.concatenate([wall_mask.astype(jnp.float32).reshape(cells, LANES), dia...]
    reshape x1, local copies, waits for them, and re-layouts: 0.79 us -> 0.08 us  [on_device(): first_panel_share.reshape(insts, cells)]
    reshape x1, other arithmetic: 0.01 us -> 0.7 us  [on_device(): wall_mask.astype(jnp.float32).reshape(cells, LANES)]
    ppermute x5, starting transfers between devices: 5.76 us -> 5.17 us  [beside(): return lax.ppermute(array, AXES, pairs(0))]
  transfers between devices with their start and end apart: 14 -> 14, of which waited for: 5 -> 4; matrix products, arithmetic and copies ran while one was open for 2% -> 3% of each run, Pallas kernels for 17% -> 17%
where the time goes in v17:
time: 58.4 us; the launch traced here: 57.9 us
  starting transfers between devices  28.7 us (49%)
  Pallas kernels  13.7 us (23%)
  waiting for transfers between devices  11.3 us (19%)
  local copies, waits for them, and re-layouts  1.91 us (3%)
  other arithmetic  1.53 us (3%)
  between operations  0.82 us (1%)
    ppermute x7, starting transfers between devices, swap(): return lax.ppermute(array, 'sector', list(enumerate(partner)))  17.3 us
    all_to_all x1, waiting for transfers between devices, on_device(): returned = lax.all_to_all(back, 'sector', 0, 0, tiled=True)  5.54 us
    ppermute x5, starting transfers between devices, beside(): return lax.ppermute(array, AXES, pairs(0))  5.17 us
    ppermute x5, waiting for transfers between devices, beside(): return lax.ppermute(array, AXES, pairs(0))  4.73 us
    pallas_call x1, Pallas kernels, on_device(): call(bind(middle, plan), (f32(sectors, RATES, LANES), half, half, half, f...  3.52 us
    all_to_all x1, starting transfers between devices, on_device(): returned = lax.all_to_all(back, 'sector', 0, 0, tiled=True)  3.5 us
    pallas_call x1, Pallas kernels, on_device(): call(bind(first_half, plan), (whole, half) + edges(pad), products + (vmem...  3.12 us
    all_to_all x1, starting transfers between devices, on_device(): got = lax.all_to_all(sent, AXES, 0, 0, tiled=True)  2.72 us
  transfers between devices with their start and end apart: 14, of which 4 were waited for; matrix products, arithmetic and copies ran while one was open for 3% of the time, Pallas kernels for 17%

profile of v17, /device:TPU:0, one launch (start us, length us, event | category | flops | bytes accessed | tf_op | source)
XLA Modules:
  0.0 57.9 jit_solution(17337528608681604081)
XLA Ops:
  0.7 5.5 %collective-permute-start.1 = (f32[1232,128]{1,0:T(8,128)}, f32[1232,128]{1,0:T(8,128)S(1)}, u32[]{:S(2)}, u32[]{:S(2)}) collective-permute-start(f32[1232,128]{1,0:T(8,128)} %bitcast.16), channel_id=1, source_target_pairs={{0,30},{2,4},{4,2},{6,8},{8,6},{10,12},{12,10},{14,16},{16,14},{18... | collective-permute-start | bytes 1892360 | tf_op jit(solution)/shard_map/ppermute | solution.py:692
  6.2 0.7 %convert_bitcast_fusion = f32[16,128]{1,0:T(8,128)S(1)} fusion(s32[2,8,128]{2,1,0:T(8,128)} %param.20), kind=kLoop, calls=%fused_computation.7 | loop fusion | flops 2048 | bytes 16384 | tf_op jit(solution)/shard_map/reshape | solution.py:733
  6.9 0.7 %pad_maximum_fusion.coef_ref = f32[96,128]{1,0:T(8,128)S(1)} fusion(f32[48,128]{1,0:T(8,128)} %bitcast.22, f32[16,128]{1,0:T(8,128)S(1)} %bitcast.23, f32[16,128]{1,0:T(8,128)S(1)} %bitcast.24, f32[16,128]{1,0:T(8,128)S(1)} %convert_bitcast_fusion), kind=kLoop, calls=%fused_computation | loop fusion | flops 36864 | bytes 98304 | tf_op jit(solution)/shard_map/concatenate | solution.py:732
  7.6 1.1 %copy-done = f32[11,7,2,8,128]{4,3,2,1,0:T(8,128)S(1)} copy-done((f32[11,7,2,8,128]{4,3,2,1,0:T(8,128)S(1)}, f32[11,7,2,8,128]{4,3,2,1,0:T(8,128)}, u32[]{:S(2)}) %copy-start) | copy-done | bytes 630808
  10.4 0.9 %shard_map.151 = f32[32,8,128]{2,1,0:T(8,128)} custom-call(f32[7,32,11]{2,1,0:T(8,128)S(1)} %bitcast.19, f32[11,32]{1,0:T(8,128)S(1)} %pad_maximum_fusion.1.both_ref, f32[8,1024]{1,0:T(8,128)S(1)} %collective-permute-done.table_ref.high_table), custom_call_target="tpu_custom_call" | custom-call | flops 2000000 | bytes 1000000 | tf_op jit(solution)/shard_map/pallas_call | solution.py:739
  11.4 2.7 %all-to-all-start = ((f32[32,8,128]{2,1,0:T(8,128)}), f32[32,8,128]{2,1,0:T(8,128)S(1)}, u32[]{:S(2)}, u32[]{:S(2)}) async-start(f32[32,8,128]{2,1,0:T(8,128)} %shard_map.151), calls=%async_computation | async-start | bytes 262144 | tf_op jit(solution)/shard_map/all_to_all | solution.py:746
  14.1 4.4 %collective-permute-start.3 = (f32[8,1024]{1,0:T(8,128)S(1)}, f32[8,1024]{1,0:T(8,128)S(1)}, u32[]{:S(2)}, u32[]{:S(2)}) collective-permute-start(f32[8,1024]{1,0:T(8,128)S(1)} %get-tuple-element.28), channel_id=1, source_target_pairs={{0,30},{2,4},{4,2},{6,8},{8,6},{10,12},{12,10},{14,16},{16,14},{18... | collective-permute-start | bytes 98312 | tf_op jit(solution)/shard_map/ppermute | solution.py:692
  18.5 1.5 %collective-permute-start.4 = (f32[1,88,512]{2,1,0:T(8,128)S(1)}, f32[1,88,512]{2,1,0:T(8,128)S(1)}, u32[]{:S(2)}, u32[]{:S(2)}) collective-permute-start(f32[1,88,512]{2,1,0:T(8,128)S(1)} %get-tuple-element.29), channel_id=1, source_target_pairs={{0,1},{1,0},{2,3},{3,2},{4,5},{5,4},{6,7},{7,6},{8,9},{9,8},{10,11... | collective-permute-start | bytes 540680 | tf_op jit(solution)/shard_map/ppermute | solution.py:706
  20.0 1.1 %shard_map.149 = (bf16[560,240]{1,0:T(8,128)(2,1)S(1)}, bf16[80,240]{1,0:T(8,128)(2,1)S(1)}) custom-call(f32[3,7,7]{2,1,0:T(8,128)S(1)} %copy-done.5, f32[3,7,7]{2,1,0:T(8,128)S(1)} %copy-done.6, bf16[80,240]{1,0:T(8,128)(2,1)S(1)} %copy-done.3, f32[80,7]{1,0:T(8,128)S(1)} %copy-done.4, f32[7,240]{1,0:T(8,128)S(1)} %copy-done.7, f32[80,240]{1,0:T(8,128)S(1)} %copy-done.2), custom_call_target="tpu_custom_call" | custom-call | flops 2000000 | bytes 1000000 | tf_op jit(solution)/shard_map/pallas_call | solution.py:752
  21.1 1.0 %collective-permute-done.3.low_table = f32[8,1024]{1,0:T(8,128)S(1)} collective-permute-done((f32[8,1024]{1,0:T(8,128)S(1)}, f32[8,1024]{1,0:T(8,128)S(1)}, u32[]{:S(2)}, u32[]{:S(2)}) %collective-permute-start.3) | collective-permute-done | bytes 32800 | tf_op jit(solution)/shard_map/ppermute | solution.py:692
  22.2 1.5 %collective-permute-start.5 = (f32[1,88,256]{2,1,0:T(8,128)S(1)}, f32[1,88,256]{2,1,0:T(8,128)S(1)}, u32[]{:S(2)}, u32[]{:S(2)}) collective-permute-start(f32[1,88,256]{2,1,0:T(8,128)S(1)} %shard_map.153), channel_id=1, source_target_pairs={{0,1},{1,0},{2,3},{3,2},{4,5},{5,4},{6,7},{7,6},{8,9},{9,8},{10,11... | collective-permute-start | bytes 270344 | tf_op jit(solution)/shard_map/ppermute | solution.py:706
  23.7 1.7 %shard_map.152 = (f32[3,2,80,128]{3,2,1,0:T(8,128)S(1)}, f32[80,128]{1,0:T(8,128)S(1)}, f32[80,2048]{1,0:T(8,128)S(1)}, f32[80,2048]{1,0:T(8,128)S(1)}) custom-call(bf16[560,240]{1,0:T(8,128)(2,1)S(1)} %get-tuple-element.23.w_ref, f32[88,2048]{1,0:T(8,128)S(1)} %get-tuple-element.24.m_ref, f32[32,8,128]{2,1,0:T(8,128)S(1)} %all-to-all-done.got_ref), custom_call_target="tpu_custom_call" | custom-call | flops 2000000000 | bytes 1000000 | tf_op jit(solution)/shard_map/pallas_call | solution.py:757
  25.4 1.3 %collective-permute-done.5.corner_ref = f32[1,88,256]{2,1,0:T(8,128)S(1)} collective-permute-done((f32[1,88,256]{2,1,0:T(8,128)S(1)}, f32[1,88,256]{2,1,0:T(8,128)S(1)}, u32[]{:S(2)}, u32[]{:S(2)}) %collective-permute-start.5) | collective-permute-done | bytes 90144 | tf_op jit(solution)/shard_map/ppermute | solution.py:706
  26.8 3.1 %shard_map.154 = (f32[80,2048]{1,0:T(8,128)S(1)}, f32[80,1024]{1,0:T(8,128)S(1)}, f32[1,80,512]{2,1,0:T(8,128)S(1)}, f32[1,80,128]{2,1,0:T(8,128)S(1)}, f32[1,80,128]{2,1,0:T(8,128)S(1)}) custom-call(bf16[560,240]{1,0:T(8,128)(2,1)S(1)} %get-tuple-element.23.w_ref, f32[88,2048]{1,0:T(8,128)S(1)} %get-tuple-element.24.m_ref, ...), custom_call_target="tpu_custom_call" | custom-call | flops 4000000000 | bytes 1000000 | tf_op jit(solution)/shard_map/pallas_call | solution.py:762
  29.9 3.5 %collective-permute-start.6 = (f32[80,1024]{1,0:T(8,128)S(1)}, f32[80,1024]{1,0:T(8,128)S(1)}, u32[]{:S(2)}, u32[]{:S(2)}) collective-permute-start(f32[80,1024]{1,0:T(8,128)S(1)} %get-tuple-element.32), channel_id=1, source_target_pairs={{0,30},{2,4},{4,2},{6,8},{8,6},{10,12},{12,10},{14,16},{16,14},{18... | collective-permute-start | bytes 983048 | tf_op jit(solution)/shard_map/ppermute | solution.py:692
  33.5 1.5 %collective-permute-start.8 = (f32[1,80,512]{2,1,0:T(8,128)S(1)}, f32[1,80,512]{2,1,0:T(8,128)S(1)}, u32[]{:S(2)}, u32[]{:S(2)}) collective-permute-start(f32[1,80,512]{2,1,0:T(8,128)S(1)} %get-tuple-element.33), channel_id=1, source_target_pairs={{0,1},{1,0},{2,3},{3,2},{4,5},{5,4},{6,7},{7,6},{8,9},{9,8},{10,11... | collective-permute-start | bytes 491528 | tf_op jit(solution)/shard_map/ppermute | solution.py:706
  35.6 0.8 %shard_map.155.g_ref = f32[80,2048]{1,0:T(8,128)S(1)} custom-call(bf16[560,240]{1,0:T(8,128)(2,1)S(1)} %get-tuple-element.23.w_ref, f32[88,2048]{1,0:T(8,128)S(1)} %get-tuple-element.24.m_ref, f32[80,2048]{1,0:T(8,128)S(1)} %get-tuple-element.26.f_ref, f32[80,2048]{1,0:T(8,128)S(1)} %get-tuple-element.31.x_ref), custom_call_target="tpu_custom_call" | custom-call | flops 2000000000 | bytes 1000000 | tf_op jit(solution)/shard_map/pallas_call | solution.py:771
  36.4 3.4 %collective-permute-done.10.c_high = f32[1,80,128]{2,1,0:T(8,128)S(1)} collective-permute-done((f32[1,80,128]{2,1,0:T(8,128)S(1)}, f32[1,80,128]{2,1,0:T(8,128)S(1)}, u32[]{:S(2)}, u32[]{:S(2)}) %collective-permute-start.10) | collective-permute-done | bytes 40992 | tf_op jit(solution)/shard_map/ppermute | solution.py:706
  39.9 3.3 %collective-permute-start.11 = (f32[80,1024]{1,0:T(8,128)S(1)}, f32[80,1024]{1,0:T(8,128)S(1)}, u32[]{:S(2)}, u32[]{:S(2)}) collective-permute-start(f32[80,1024]{1,0:T(8,128)S(1)} %shard_map.157), channel_id=1, source_target_pairs={{0,30},{2,4},{4,2},{6,8},{8,6},{10,12},{12,10},{14,16},{16,14},{18... | collective-permute-start | bytes 983048 | tf_op jit(solution)/shard_map/ppermute | solution.py:692
  43.3 3.5 %shard_map.156 = (f32[16,8,128]{2,1,0:T(8,128)}, f32[80,1024]{1,0:T(8,128)S(1)}, f32[80,1024]{1,0:T(8,128)S(1)}, f32[80,1024]{1,0:T(8,128)S(1)}, f32[8,1024]{1,0:T(8,128)S(1)}) custom-call(bf16[560,240]{1,0:T(8,128)(2,1)S(1)} %get-tuple-element.23.w_ref, f32[88,2048]{1,0:T(8,128)S(1)} %copy-done.9, f32[80,2048]{1,0:T(8,128)S(1)} %get-tuple-element.26.f_ref, ...), custom_call_target="tpu_custom_call" | custom-call | flops 4000000000 | bytes 1000000 | tf_op jit(solution)/shard_map/pallas_call | solution.py:774
  46.8 3.5 %all-to-all-start.1 = ((f32[16,8,128]{2,1,0:T(8,128)}), f32[16,8,128]{2,1,0:T(8,128)S(1)}, u32[]{:S(2)}, u32[]{:S(2)}) async-start(f32[16,8,128]{2,1,0:T(8,128)} %get-tuple-element.41), calls=%async_computation.1 | async-start | bytes 131072 | tf_op jit(solution)/shard_map/all_to_all | solution.py:782
  50.3 1.3 %shard_map.158 = f32[1232,128]{1,0:T(8,128)} custom-call(bf16[80,240]{1,0:T(8,128)(2,1)S(1)} %get-tuple-element.22.w_ref, f32[8,1024]{1,0:T(8,128)S(1)} %get-tuple-element.37.rates_ref, f32[80,1024]{1,0:T(8,128)S(1)} %get-tuple-element.38.n0_ref, f32[80,1024]{1,0:T(8,128)S(1)} %get-tuple-element.39.h0_ref, f32[80,1024]{1,0:T(8,128)S(1)} %get-tuple-element.40.x1_ref, ...), custom_call_target="tpu_custom_call" | custom-call | flops 2000000 | bytes 1000000 | tf_op jit(solution)/shard_map/pallas_call | solution.py:784
  51.6 5.5 %all-to-all-done.1.got_ref = f32[16,8,128]{2,1,0:T(8,128)S(1)} async-done(((f32[16,8,128]{2,1,0:T(8,128)}), f32[16,8,128]{2,1,0:T(8,128)S(1)}, u32[]{:S(2)}, u32[]{:S(2)}) %all-to-all-start.1) | async-done | bytes 65568 | tf_op jit(solution)/shard_map/all_to_all | solution.py:782
  57.2 0.8 %shard_map.159 = f32[7,32,11]{2,1,0:T(8,128)} custom-call(f32[16,8,128]{2,1,0:T(8,128)S(1)} %all-to-all-done.1.got_ref), custom_call_target="tpu_custom_call" | custom-call | flops 2000000 | bytes 1000000 | tf_op jit(solution)/shard_map/pallas_call | solution.py:783
  (49 shorter events, 2.6 us)
Async XLA Ops:
  0.6 6.2 %copy-start.10 = (f32[2,8,128]{2,1,0:T(8,128)S(1)}, f32[2,8,128]{2,1,0:T(8,128)}, u32[]{:S(2)}) copy-start(f32[2,8,128]{2,1,0:T(8,128)} %param.17) | copy-start | bytes 24580
  0.6 6.2 %copy-start.11 = (f32[2,8,128]{2,1,0:T(8,128)S(1)}, f32[2,8,128]{2,1,0:T(8,128)}, u32[]{:S(2)}) copy-start(f32[2,8,128]{2,1,0:T(8,128)} %param.15) | copy-start | bytes 24580
  0.7 21.4 %collective-permute-start.1 = (f32[1232,128]{1,0:T(8,128)}, f32[1232,128]{1,0:T(8,128)S(1)}, u32[]{:S(2)}, u32[]{:S(2)}) collective-permute-start(f32[1232,128]{1,0:T(8,128)} %bitcast.16), channel_id=1, source_target_pairs={{0,30},{2,4},{4,2},{6,8},{8,6},{10,12},{12,10},{14,16},{16,14},{18... | collective-permute-start | bytes 1892360 | tf_op jit(solution)/shard_map/ppermute | solution.py:692
  6.2 15.9 %collective-permute-start.2 = (f32[1232,128]{1,0:T(8,128)}, f32[1232,128]{1,0:T(8,128)S(1)}, u32[]{:S(2)}, u32[]{:S(2)}) collective-permute-start(f32[1232,128]{1,0:T(8,128)} %bitcast.17), channel_id=1, source_target_pairs={{0,2},{2,0},{4,6},{6,4},{8,10},{10,8},{12,14},{14,12},{16,18},{18,... | collective-permute-start | bytes 1892360 | tf_op jit(solution)/shard_map/ppermute | solution.py:692
  9.0 26.6 %copy-start.8 = (f32[88,2048]{1,0:T(8,128)}, f32[88,2048]{1,0:T(8,128)S(1)}, u32[]{:S(2)}) copy-start(f32[88,2048]{1,0:T(8,128)S(1)} %get-tuple-element.24.m_ref) | copy-start | bytes 2162692
  9.0 1.4 %collective-permute-start = (f32[8,1024]{1,0:T(8,128)S(1)}, f32[8,1024]{1,0:T(8,128)S(1)}, u32[]{:S(2)}, u32[]{:S(2)}) collective-permute-start(f32[8,1024]{1,0:T(8,128)S(1)} %get-tuple-element.25), channel_id=1, source_target_pairs={{0,2},{2,0},{4,6},{6,4},{8,10},{10,8},{12,14},{14,12},{16,18},{18,... | collective-permute-start | bytes 98312 | tf_op jit(solution)/shard_map/ppermute | solution.py:692
  11.3 8.6 %copy-start.2 = (f32[80,240]{1,0:T(8,128)S(1)}, f32[80,240]{1,0:T(8,128)}, u32[]{:S(2)}) copy-start(f32[80,240]{1,0:T(8,128)} %constant.16.clone.diagonal_ref) | copy-start | bytes 230404
  11.4 8.6 %copy-start.3 = (bf16[80,240]{1,0:T(8,128)(2,1)S(1)}, bf16[80,240]{1,0:T(8,128)(2,1)}, u32[]{:S(2)}) copy-start(bf16[80,240]{1,0:T(8,128)(2,1)} %constant.13.clone.spectral_ref) | copy-start | bytes 115204
  11.4 8.6 %copy-start.4 = (f32[80,7]{1,0:T(8,128)S(1)}, f32[80,7]{1,0:T(8,128)}, u32[]{:S(2)}) copy-start(f32[80,7]{1,0:T(8,128)} %constant.14.clone.rows_ref) | copy-start | bytes 6724
  11.4 8.6 %copy-start.5 = (f32[3,7,7]{2,1,0:T(8,128)S(1)}, f32[3,7,7]{2,1,0:T(8,128)}, u32[]{:S(2)}) copy-start(f32[3,7,7]{2,1,0:T(8,128)} %up_ref.1) | copy-start | bytes 1768
  11.4 8.6 %copy-start.6 = (f32[3,7,7]{2,1,0:T(8,128)S(1)}, f32[3,7,7]{2,1,0:T(8,128)}, u32[]{:S(2)}) copy-start(f32[3,7,7]{2,1,0:T(8,128)} %down_ref.1) | copy-start | bytes 1768
  11.4 8.6 %copy-start.7 = (f32[7,240]{1,0:T(8,128)S(1)}, f32[7,240]{1,0:T(8,128)}, u32[]{:S(2)}) copy-start(f32[7,240]{1,0:T(8,128)} %constant.15.clone.lanes_ref) | copy-start | bytes 20164
  11.4 12.3 %all-to-all-start = ((f32[32,8,128]{2,1,0:T(8,128)}), f32[32,8,128]{2,1,0:T(8,128)S(1)}, u32[]{:S(2)}, u32[]{:S(2)}) async-start(f32[32,8,128]{2,1,0:T(8,128)} %shard_map.151), calls=%async_computation | async-start | bytes 262144 | tf_op jit(solution)/shard_map/all_to_all | solution.py:746
  14.1 8.0 %collective-permute-start.3 = (f32[8,1024]{1,0:T(8,128)S(1)}, f32[8,1024]{1,0:T(8,128)S(1)}, u32[]{:S(2)}, u32[]{:S(2)}) collective-permute-start(f32[8,1024]{1,0:T(8,128)S(1)} %get-tuple-element.28), channel_id=1, source_target_pairs={{0,30},{2,4},{4,2},{6,8},{8,6},{10,12},{12,10},{14,16},{16,14},{18... | collective-permute-start | bytes 98312 | tf_op jit(solution)/shard_map/ppermute | solution.py:692
  18.5 6.9 %collective-permute-start.4 = (f32[1,88,512]{2,1,0:T(8,128)S(1)}, f32[1,88,512]{2,1,0:T(8,128)S(1)}, u32[]{:S(2)}, u32[]{:S(2)}) collective-permute-start(f32[1,88,512]{2,1,0:T(8,128)S(1)} %get-tuple-element.29), channel_id=1, source_target_pairs={{0,1},{1,0},{2,3},{3,2},{4,5},{5,4},{6,7},{7,6},{8,9},{9,8},{10,11... | collective-permute-start | bytes 540680 | tf_op jit(solution)/shard_map/ppermute | solution.py:706
  22.2 4.6 %collective-permute-start.5 = (f32[1,88,256]{2,1,0:T(8,128)S(1)}, f32[1,88,256]{2,1,0:T(8,128)S(1)}, u32[]{:S(2)}, u32[]{:S(2)}) collective-permute-start(f32[1,88,256]{2,1,0:T(8,128)S(1)} %shard_map.153), channel_id=1, source_target_pairs={{0,1},{1,0},{2,3},{3,2},{4,5},{5,4},{6,7},{7,6},{8,9},{9,8},{10,11... | collective-permute-start | bytes 270344 | tf_op jit(solution)/shard_map/ppermute | solution.py:706
  29.9 13.4 %collective-permute-start.7 = (f32[80,2048]{1,0:T(8,128)S(1)}, f32[80,2048]{1,0:T(8,128)S(1)}, u32[]{:S(2)}, u32[]{:S(2)}) collective-permute-start(f32[80,2048]{1,0:T(8,128)S(1)} %get-tuple-element.31.x_ref), channel_id=1, source_target_pairs={{0,2},{2,0},{4,6},{6,4},{8,10},{10,8},{12,14},{14,12},{16,18},{18,... | collective-permute-start | bytes 1966088 | tf_op jit(solution)/shard_map/ppermute | solution.py:692
  29.9 13.3 %collective-permute-start.6 = (f32[80,1024]{1,0:T(8,128)S(1)}, f32[80,1024]{1,0:T(8,128)S(1)}, u32[]{:S(2)}, u32[]{:S(2)}) collective-permute-start(f32[80,1024]{1,0:T(8,128)S(1)} %get-tuple-element.32), channel_id=1, source_target_pairs={{0,30},{2,4},{4,2},{6,8},{8,6},{10,12},{12,10},{14,16},{16,14},{18... | collective-permute-start | bytes 983048 | tf_op jit(solution)/shard_map/ppermute | solution.py:692
  33.5 6.4 %collective-permute-start.8 = (f32[1,80,512]{2,1,0:T(8,128)S(1)}, f32[1,80,512]{2,1,0:T(8,128)S(1)}, u32[]{:S(2)}, u32[]{:S(2)}) collective-permute-start(f32[1,80,512]{2,1,0:T(8,128)S(1)} %get-tuple-element.33), channel_id=1, source_target_pairs={{0,1},{1,0},{2,3},{3,2},{4,5},{5,4},{6,7},{7,6},{8,9},{9,8},{10,11... | collective-permute-start | bytes 491528 | tf_op jit(solution)/shard_map/ppermute | solution.py:706
  35.0 8.3 %collective-permute-start.9 = (f32[1,80,128]{2,1,0:T(8,128)S(1)}, f32[1,80,128]{2,1,0:T(8,128)S(1)}, u32[]{:S(2)}, u32[]{:S(2)}) collective-permute-start(f32[1,80,128]{2,1,0:T(8,128)S(1)} %get-tuple-element.34), channel_id=1, source_target_pairs={{0,31},{1,30},{2,5},{3,4},{4,3},{5,2},{6,9},{7,8},{8,7},{9,6},{10,... | collective-permute-start | bytes 122888 | tf_op jit(solution)/shard_map/ppermute | solution.py:706
  35.6 4.2 %collective-permute-start.10 = (f32[1,80,128]{2,1,0:T(8,128)S(1)}, f32[1,80,128]{2,1,0:T(8,128)S(1)}, u32[]{:S(2)}, u32[]{:S(2)}) collective-permute-start(f32[1,80,128]{2,1,0:T(8,128)S(1)} %get-tuple-element.35), channel_id=1, source_target_pairs={{0,3},{1,2},{2,1},{3,0},{4,7},{5,6},{6,5},{7,4},{8,11},{9,10},{10,... | collective-permute-start | bytes 122888 | tf_op jit(solution)/shard_map/ppermute | solution.py:706
  36.4 6.8 %copy-start.9 = (f32[88,2048]{1,0:T(8,128)S(1)}, f32[88,2048]{1,0:T(8,128)}, u32[]{:S(2)}) copy-start(f32[88,2048]{1,0:T(8,128)} %copy-done.8) | copy-start | bytes 2162692
  39.9 10.4 %collective-permute-start.11 = (f32[80,1024]{1,0:T(8,128)S(1)}, f32[80,1024]{1,0:T(8,128)S(1)}, u32[]{:S(2)}, u32[]{:S(2)}) collective-permute-start(f32[80,1024]{1,0:T(8,128)S(1)} %shard_map.157), channel_id=1, source_target_pairs={{0,30},{2,4},{4,2},{6,8},{8,6},{10,12},{12,10},{14,16},{16,14},{18... | collective-permute-start | bytes 983048 | tf_op jit(solution)/shard_map/ppermute | solution.py:692
  46.8 10.4 %all-to-all-start.1 = ((f32[16,8,128]{2,1,0:T(8,128)}), f32[16,8,128]{2,1,0:T(8,128)S(1)}, u32[]{:S(2)}, u32[]{:S(2)}) async-start(f32[16,8,128]{2,1,0:T(8,128)} %get-tuple-element.41), calls=%async_computation.1 | async-start | bytes 131072 | tf_op jit(solution)/shard_map/all_to_all | solution.py:782
  (4 other events, 4.4 us)

commit v18 on v15

--- a/solution.py
+++ b/solution.py
@@ -148,6 +148,12 @@
     return jnp.dot(a, b, precision=HIGHEST, preferred_element_type=jnp.float32)
 
 
+def cell_rows(plan, ref, there):
+    whole = plan.tf // 8 * 8
+    rest = [ref[pl.ds(there + plan.cells * i, 1), :] for i in range(whole, plan.tf)]
+    return jnp.concatenate([ref[pl.ds(there, whole, stride=plan.cells), :]] + rest, axis=0)
+
+
 def lane_index(rows):
     return lax.broadcasted_iota(jnp.int32, (rows, LANES), 1)
 
@@ -207,7 +213,7 @@
     def row(self, r):
         plan = self.plan
         there = jnp.where(parity() == 1, self.layer, plan.ct - 1 - self.layer) * plan.rows + r
-        field = self.ref[pl.ds(there, plan.tf, stride=plan.cells), :]
+        field = cell_rows(plan, self.ref, there)
         field = jnp.concatenate([field, jnp.zeros((plan.pad - plan.tf, LANES), jnp.float32)], axis=0)
         if self.seam is not None:
             field = field + placed(self.seam, self.layer * plan.rows + r)
@@ -428,7 +434,7 @@
         a, r = divmod(cell, plan.rows)
         there = jnp.where(mirror == 0, a, plan.ct - 1 - a) * plan.rows + r
         table = [rates_ref[i, pl.ds(there, 1), :] for i in range(6)]
-        field = jnp.concatenate([rhs_ref[pl.ds(there, plan.tf, stride=cells), :], tail], axis=0)
+        field = jnp.concatenate([cell_rows(plan, rhs_ref, there), tail], axis=0)
         m_ref[:pad, at(cell)] = field * table[C_MASK]
         m_ref[pad:, at(cell)] = jnp.concatenate(table + [rest], axis=0)
         other = jnp.where(mirror == 0, plan.ct - 1 - a, a) * plan.rows + r
@@ -657,7 +663,10 @@
 
     def put(a, r, value):
         there = jnp.where(mirror == 0, a, plan.ct - 1 - a) * plan.rows + r
-        out_ref[pl.ds(there, plan.tf, stride=plan.cells), :] = value[: plan.tf]
+        whole = plan.tf // 8 * 8
+        out_ref[pl.ds(there, whole, stride=plan.cells), :] = value[:whole]
+        for i in range(whole, plan.tf):
+            out_ref[pl.ds(there + plan.cells * i, 1), :] = value[i : i + 1]
 
     for r in range(plan.rows):
         put(1, r, x1_ref[:, at(r)])

time: 58.5 us -> 58.5 us (level)
  no operation moved by 1% of the time
where the time goes in v18:
time: 58.5 us; the launch traced here: 58 us
  starting transfers between devices  27.2 us (46%)
  Pallas kernels  13.7 us (23%)
  waiting for transfers between devices  12.2 us (21%)
  other arithmetic  2.23 us (4%)
  local copies, waits for them, and re-layouts  1.82 us (3%)
  between operations  0.87 us (1%)
    ppermute x7, starting transfers between devices, swap(): return lax.ppermute(array, 'sector', list(enumerate(partner)))  16.1 us
    ppermute x5, waiting for transfers between devices, beside(): return lax.ppermute(array, AXES, pairs(0))  6.61 us
    all_to_all x1, waiting for transfers between devices, on_device(): returned = lax.all_to_all(back, 'sector', 0, 0, tiled=True)  5.54 us
    ppermute x5, starting transfers between devices, beside(): return lax.ppermute(array, AXES, pairs(0))  5.01 us
    pallas_call x1, Pallas kernels, on_device(): call(bind(middle, plan), (f32(sectors, RATES, LANES), half, half, half, f...  3.54 us
    all_to_all x1, starting transfers between devices, on_device(): returned = lax.all_to_all(back, 'sector', 0, 0, tiled=True)  3.5 us
    pallas_call x1, Pallas kernels, on_device(): call(bind(first_half, plan), (whole, half) + edges(pad), products + (vmem...  3.14 us
    all_to_all x1, starting transfers between devices, on_device(): got = lax.all_to_all(sent, AXES, 0, 0, tiled=True)  2.58 us
  transfers between devices with their start and end apart: 14, of which 4 were waited for; matrix products, arithmetic and copies ran while one was open for 5% of the time, Pallas kernels for 17%

profile of v18, /device:TPU:0, one launch (start us, length us, event | category | flops | bytes accessed | tf_op | source)
XLA Modules:
  0.0 58.0 jit_solution(10490386109640412790)
XLA Ops:
  0.6 5.5 %collective-permute-start = (f32[1232,128]{1,0:T(8,128)}, f32[1232,128]{1,0:T(8,128)S(1)}, u32[]{:S(2)}, u32[]{:S(2)}) collective-permute-start(f32[1232,128]{1,0:T(8,128)} %bitcast.16), channel_id=1, source_target_pairs={{0,30},{2,4},{4,2},{6,8},{8,6},{10,12},{12,10},{14,16},{16,14},{18... | collective-permute-start | bytes 1892360 | tf_op jit(solution)/shard_map/ppermute | solution.py:700
  6.2 0.8 %copy.19 = f32[11,16]{1,0:T(8,128)S(1)} copy(f32[11,16]{0,1:T(8,128)} %bitcast.25) | data formatting | bytes 1408 | tf_op jit(solution)/shard_map/reshape | solution.py:736
  7.8 0.9 %copy-done.1 = f32[11,7,4,8]{0,3,2,1:T(8,128)S(1)} copy-done((f32[11,7,4,8]{0,3,2,1:T(8,128)S(1)}, f32[11,7,4,8]{0,3,2,1:T(8,128)}, u32[]{:S(2)}) %copy-start.1) | copy-done | bytes 9880
  8.7 0.9 %shard_map.151 = f32[32,8,128]{2,1,0:T(8,128)} custom-call(f32[7,32,11]{2,1,0:T(8,128)S(1)} %bitcast.19, f32[11,32]{1,0:T(8,128)S(1)} %pad_maximum_fusion.1.both_ref), custom_call_target="tpu_custom_call" | custom-call | flops 2000000 | bytes 1000000 | tf_op jit(solution)/shard_map/pallas_call | solution.py:733
  9.6 2.6 %all-to-all-start = ((f32[32,8,128]{2,1,0:T(8,128)}), f32[32,8,128]{2,1,0:T(8,128)S(1)}, u32[]{:S(2)}, u32[]{:S(2)}) async-start(f32[32,8,128]{2,1,0:T(8,128)} %shard_map.151), calls=%async_computation | async-start | bytes 262144 | tf_op jit(solution)/shard_map/all_to_all | solution.py:739
  14.0 4.4 %collective-permute-start.2 = (f32[8,1024]{1,0:T(8,128)S(1)}, f32[8,1024]{1,0:T(8,128)S(1)}, u32[]{:S(2)}, u32[]{:S(2)}) collective-permute-start(f32[8,1024]{1,0:T(8,128)S(1)} %get-tuple-element.27), channel_id=1, source_target_pairs={{0,30},{2,4},{4,2},{6,8},{8,6},{10,12},{12,10},{14,16},{16,14},{18... | collective-permute-start | bytes 98312 | tf_op jit(solution)/shard_map/ppermute | solution.py:700
  18.4 1.5 %collective-permute-start.4 = (f32[1,88,512]{2,1,0:T(8,128)S(1)}, f32[1,88,512]{2,1,0:T(8,128)S(1)}, u32[]{:S(2)}, u32[]{:S(2)}) collective-permute-start(f32[1,88,512]{2,1,0:T(8,128)S(1)} %get-tuple-element.29), channel_id=1, source_target_pairs={{0,1},{1,0},{2,3},{3,2},{4,5},{5,4},{6,7},{7,6},{8,9},{9,8},{10,11... | collective-permute-start | bytes 540680 | tf_op jit(solution)/shard_map/ppermute | solution.py:714
  19.9 1.1 %shard_map.149 = (bf16[560,240]{1,0:T(8,128)(2,1)S(1)}, bf16[80,240]{1,0:T(8,128)(2,1)S(1)}) custom-call(f32[3,7,7]{2,1,0:T(8,128)S(1)} %copy-done.5, f32[3,7,7]{2,1,0:T(8,128)S(1)} %copy-done.6, bf16[80,240]{1,0:T(8,128)(2,1)S(1)} %copy-done.3, f32[80,7]{1,0:T(8,128)S(1)} %copy-done.4, f32[7,240]{1,0:T(8,128)S(1)} %copy-done.7, f32[80,240]{1,0:T(8,128)S(1)} %copy-done.2), custom_call_target="tpu_custom_call" | custom-call | flops 2000000 | bytes 1000000 | tf_op jit(solution)/shard_map/pallas_call | solution.py:759
  21.1 0.9 %collective-permute-start.5 = (f32[1,88,256]{2,1,0:T(8,128)S(1)}, f32[1,88,256]{2,1,0:T(8,128)S(1)}, u32[]{:S(2)}, u32[]{:S(2)}) collective-permute-start(f32[1,88,256]{2,1,0:T(8,128)S(1)} %shard_map.153), channel_id=1, source_target_pairs={{0,1},{1,0},{2,3},{3,2},{4,5},{5,4},{6,7},{7,6},{8,9},{9,8},{10,11... | collective-permute-start | bytes 270344 | tf_op jit(solution)/shard_map/ppermute | solution.py:714
  22.0 1.7 %shard_map.152 = (f32[3,2,80,128]{3,2,1,0:T(8,128)S(1)}, f32[80,128]{1,0:T(8,128)S(1)}, f32[80,2048]{1,0:T(8,128)S(1)}, f32[80,2048]{1,0:T(8,128)S(1)}) custom-call(bf16[560,240]{1,0:T(8,128)(2,1)S(1)} %get-tuple-element.23.w_ref, f32[88,2048]{1,0:T(8,128)S(1)} %get-tuple-element.24.m_ref, f32[32,8,128]{2,1,0:T(8,128)S(1)} %all-to-all-done.got_ref), custom_call_target="tpu_custom_call" | custom-call | flops 2000000000 | bytes 1000000 | tf_op jit(solution)/shard_map/pallas_call | solution.py:764
  23.7 2.0 %collective-permute-done.4.side_ref.side_first = f32[1,88,512]{2,1,0:T(8,128)S(1)} collective-permute-done((f32[1,88,512]{2,1,0:T(8,128)S(1)}, f32[1,88,512]{2,1,0:T(8,128)S(1)}, u32[]{:S(2)}, u32[]{:S(2)}) %collective-permute-start.4) | collective-permute-done | bytes 180256 | tf_op jit(solution)/shard_map/ppermute | solution.py:714
  25.7 1.5 %collective-permute-done.5.corner_ref = f32[1,88,256]{2,1,0:T(8,128)S(1)} collective-permute-done((f32[1,88,256]{2,1,0:T(8,128)S(1)}, f32[1,88,256]{2,1,0:T(8,128)S(1)}, u32[]{:S(2)}, u32[]{:S(2)}) %collective-permute-start.5) | collective-permute-done | bytes 90144 | tf_op jit(solution)/shard_map/ppermute | solution.py:714
  27.3 3.1 %shard_map.154 = (f32[80,2048]{1,0:T(8,128)S(1)}, f32[80,1024]{1,0:T(8,128)S(1)}, f32[1,80,512]{2,1,0:T(8,128)S(1)}, f32[1,80,128]{2,1,0:T(8,128)S(1)}, f32[1,80,128]{2,1,0:T(8,128)S(1)}) custom-call(bf16[560,240]{1,0:T(8,128)(2,1)S(1)} %get-tuple-element.23.w_ref, f32[88,2048]{1,0:T(8,128)S(1)} %get-tuple-element.24.m_ref, ...), custom_call_target="tpu_custom_call" | custom-call | flops 4000000000 | bytes 1000000 | tf_op jit(solution)/shard_map/pallas_call | solution.py:769
  30.5 3.1 %collective-permute-start.6 = (f32[80,1024]{1,0:T(8,128)S(1)}, f32[80,1024]{1,0:T(8,128)S(1)}, u32[]{:S(2)}, u32[]{:S(2)}) collective-permute-start(f32[80,1024]{1,0:T(8,128)S(1)} %get-tuple-element.32), channel_id=1, source_target_pairs={{0,30},{2,4},{4,2},{6,8},{8,6},{10,12},{12,10},{14,16},{16,14},{18... | collective-permute-start | bytes 983048 | tf_op jit(solution)/shard_map/ppermute | solution.py:700
  33.5 1.5 %collective-permute-start.8 = (f32[1,80,512]{2,1,0:T(8,128)S(1)}, f32[1,80,512]{2,1,0:T(8,128)S(1)}, u32[]{:S(2)}, u32[]{:S(2)}) collective-permute-start(f32[1,80,512]{2,1,0:T(8,128)S(1)} %get-tuple-element.33), channel_id=1, source_target_pairs={{0,1},{1,0},{2,3},{3,2},{4,5},{5,4},{6,7},{7,6},{8,9},{9,8},{10,11... | collective-permute-start | bytes 491528 | tf_op jit(solution)/shard_map/ppermute | solution.py:714
  35.0 1.1 %collective-permute-start.9 = (f32[1,80,128]{2,1,0:T(8,128)S(1)}, f32[1,80,128]{2,1,0:T(8,128)S(1)}, u32[]{:S(2)}, u32[]{:S(2)}) collective-permute-start(f32[1,80,128]{2,1,0:T(8,128)S(1)} %get-tuple-element.34), channel_id=1, source_target_pairs={{0,31},{1,30},{2,5},{3,4},{4,3},{5,2},{6,9},{7,8},{8,7},{9,6},{10,... | collective-permute-start | bytes 122888 | tf_op jit(solution)/shard_map/ppermute | solution.py:714
  36.2 0.8 %shard_map.155.g_ref = f32[80,2048]{1,0:T(8,128)S(1)} custom-call(bf16[560,240]{1,0:T(8,128)(2,1)S(1)} %get-tuple-element.23.w_ref, f32[88,2048]{1,0:T(8,128)S(1)} %get-tuple-element.24.m_ref, f32[80,2048]{1,0:T(8,128)S(1)} %get-tuple-element.25.f_ref, f32[80,2048]{1,0:T(8,128)S(1)} %get-tuple-element.31.x_ref), custom_call_target="tpu_custom_call" | custom-call | flops 2000000000 | bytes 1000000 | tf_op jit(solution)/shard_map/pallas_call | solution.py:778
  37.0 3.1 %collective-permute-done.10.c_high = f32[1,80,128]{2,1,0:T(8,128)S(1)} collective-permute-done((f32[1,80,128]{2,1,0:T(8,128)S(1)}, f32[1,80,128]{2,1,0:T(8,128)S(1)}, u32[]{:S(2)}, u32[]{:S(2)}) %collective-permute-start.10) | collective-permute-done | bytes 40992 | tf_op jit(solution)/shard_map/ppermute | solution.py:714
  40.2 3.1 %collective-permute-start.11 = (f32[80,1024]{1,0:T(8,128)S(1)}, f32[80,1024]{1,0:T(8,128)S(1)}, u32[]{:S(2)}, u32[]{:S(2)}) collective-permute-start(f32[80,1024]{1,0:T(8,128)S(1)} %shard_map.157), channel_id=1, source_target_pairs={{0,30},{2,4},{4,2},{6,8},{8,6},{10,12},{12,10},{14,16},{16,14},{18... | collective-permute-start | bytes 983048 | tf_op jit(solution)/shard_map/ppermute | solution.py:700
  43.3 3.5 %shard_map.156 = (f32[16,8,128]{2,1,0:T(8,128)}, f32[80,1024]{1,0:T(8,128)S(1)}, f32[80,1024]{1,0:T(8,128)S(1)}, f32[80,1024]{1,0:T(8,128)S(1)}, f32[8,1024]{1,0:T(8,128)S(1)}) custom-call(bf16[560,240]{1,0:T(8,128)(2,1)S(1)} %get-tuple-element.23.w_ref, f32[88,2048]{1,0:T(8,128)S(1)} %copy-done.9, f32[80,2048]{1,0:T(8,128)S(1)} %get-tuple-element.25.f_ref, ...), custom_call_target="tpu_custom_call" | custom-call | flops 4000000000 | bytes 1000000 | tf_op jit(solution)/shard_map/pallas_call | solution.py:781
  46.9 3.5 %all-to-all-start.1 = ((f32[16,8,128]{2,1,0:T(8,128)}), f32[16,8,128]{2,1,0:T(8,128)S(1)}, u32[]{:S(2)}, u32[]{:S(2)}) async-start(f32[16,8,128]{2,1,0:T(8,128)} %get-tuple-element.41), calls=%async_computation.1 | async-start | bytes 131072 | tf_op jit(solution)/shard_map/all_to_all | solution.py:789
  50.4 1.3 %shard_map.158 = f32[1232,128]{1,0:T(8,128)} custom-call(bf16[80,240]{1,0:T(8,128)(2,1)S(1)} %get-tuple-element.22.w_ref, f32[8,1024]{1,0:T(8,128)S(1)} %get-tuple-element.37.rates_ref, f32[80,1024]{1,0:T(8,128)S(1)} %get-tuple-element.38.n0_ref, f32[80,1024]{1,0:T(8,128)S(1)} %get-tuple-element.39.h0_ref, f32[80,1024]{1,0:T(8,128)S(1)} %get-tuple-element.40.x1_ref, ...), custom_call_target="tpu_custom_call" | custom-call | flops 2000000 | bytes 1000000 | tf_op jit(solution)/shard_map/pallas_call | solution.py:791
  51.7 5.5 %all-to-all-done.1.got_ref = f32[16,8,128]{2,1,0:T(8,128)S(1)} async-done(((f32[16,8,128]{2,1,0:T(8,128)}), f32[16,8,128]{2,1,0:T(8,128)S(1)}, u32[]{:S(2)}, u32[]{:S(2)}) %all-to-all-start.1) | async-done | bytes 65568 | tf_op jit(solution)/shard_map/all_to_all | solution.py:789
  57.2 0.8 %shard_map.159 = f32[7,32,11]{2,1,0:T(8,128)} custom-call(f32[16,8,128]{2,1,0:T(8,128)S(1)} %all-to-all-done.1.got_ref), custom_call_target="tpu_custom_call" | custom-call | flops 2000000 | bytes 1000000 | tf_op jit(solution)/shard_map/pallas_call | solution.py:790
  (45 shorter events, 2.9 us)
Async XLA Ops:
  0.6 13.0 %copy-start = (f32[11,7,2,8,128]{4,3,2,1,0:T(8,128)S(1)}, f32[11,7,2,8,128]{4,3,2,1,0:T(8,128)}, u32[]{:S(2)}) copy-start(f32[11,7,2,8,128]{4,3,2,1,0:T(8,128)} %param.14) | copy-start | bytes 1892356
  0.6 20.4 %collective-permute-start = (f32[1232,128]{1,0:T(8,128)}, f32[1232,128]{1,0:T(8,128)S(1)}, u32[]{:S(2)}, u32[]{:S(2)}) collective-permute-start(f32[1232,128]{1,0:T(8,128)} %bitcast.16), channel_id=1, source_target_pairs={{0,30},{2,4},{4,2},{6,8},{8,6},{10,12},{12,10},{14,16},{16,14},{18... | collective-permute-start | bytes 1892360 | tf_op jit(solution)/shard_map/ppermute | solution.py:700
  6.1 14.9 %collective-permute-start.1 = (f32[1232,128]{1,0:T(8,128)}, f32[1232,128]{1,0:T(8,128)S(1)}, u32[]{:S(2)}, u32[]{:S(2)}) collective-permute-start(f32[1232,128]{1,0:T(8,128)} %bitcast.17), channel_id=1, source_target_pairs={{0,2},{2,0},{4,6},{6,4},{8,10},{10,8},{12,14},{14,12},{16,18},{18,... | collective-permute-start | bytes 1892360 | tf_op jit(solution)/shard_map/ppermute | solution.py:700
  9.6 12.5 %all-to-all-start = ((f32[32,8,128]{2,1,0:T(8,128)}), f32[32,8,128]{2,1,0:T(8,128)S(1)}, u32[]{:S(2)}, u32[]{:S(2)}) async-start(f32[32,8,128]{2,1,0:T(8,128)} %shard_map.151), calls=%async_computation | async-start | bytes 262144 | tf_op jit(solution)/shard_map/all_to_all | solution.py:739
  13.6 6.3 %copy-start.2 = (f32[80,240]{1,0:T(8,128)S(1)}, f32[80,240]{1,0:T(8,128)}, u32[]{:S(2)}) copy-start(f32[80,240]{1,0:T(8,128)} %constant.16.clone.diagonal_ref) | copy-start | bytes 230404
  13.6 6.3 %copy-start.3 = (bf16[80,240]{1,0:T(8,128)(2,1)S(1)}, bf16[80,240]{1,0:T(8,128)(2,1)}, u32[]{:S(2)}) copy-start(bf16[80,240]{1,0:T(8,128)(2,1)} %constant.13.clone.spectral_ref) | copy-start | bytes 115204
  13.6 6.2 %copy-start.4 = (f32[80,7]{1,0:T(8,128)S(1)}, f32[80,7]{1,0:T(8,128)}, u32[]{:S(2)}) copy-start(f32[80,7]{1,0:T(8,128)} %constant.14.clone.rows_ref) | copy-start | bytes 6724
  13.6 6.2 %copy-start.5 = (f32[3,7,7]{2,1,0:T(8,128)S(1)}, f32[3,7,7]{2,1,0:T(8,128)}, u32[]{:S(2)}) copy-start(f32[3,7,7]{2,1,0:T(8,128)} %up_ref.1) | copy-start | bytes 1768
  13.6 6.2 %copy-start.6 = (f32[3,7,7]{2,1,0:T(8,128)S(1)}, f32[3,7,7]{2,1,0:T(8,128)}, u32[]{:S(2)}) copy-start(f32[3,7,7]{2,1,0:T(8,128)} %down_ref.1) | copy-start | bytes 1768
  13.7 6.2 %copy-start.7 = (f32[7,240]{1,0:T(8,128)S(1)}, f32[7,240]{1,0:T(8,128)}, u32[]{:S(2)}) copy-start(f32[7,240]{1,0:T(8,128)} %constant.15.clone.lanes_ref) | copy-start | bytes 20164
  14.0 22.2 %copy-start.8 = (f32[88,2048]{1,0:T(8,128)}, f32[88,2048]{1,0:T(8,128)S(1)}, u32[]{:S(2)}) copy-start(f32[88,2048]{1,0:T(8,128)S(1)} %get-tuple-element.24.m_ref) | copy-start | bytes 2162692
  14.0 7.0 %collective-permute-start.2 = (f32[8,1024]{1,0:T(8,128)S(1)}, f32[8,1024]{1,0:T(8,128)S(1)}, u32[]{:S(2)}, u32[]{:S(2)}) collective-permute-start(f32[8,1024]{1,0:T(8,128)S(1)} %get-tuple-element.27), channel_id=1, source_target_pairs={{0,30},{2,4},{4,2},{6,8},{8,6},{10,12},{12,10},{14,16},{16,14},{18... | collective-permute-start | bytes 98312 | tf_op jit(solution)/shard_map/ppermute | solution.py:700
  18.4 2.7 %collective-permute-start.3 = (f32[8,1024]{1,0:T(8,128)S(1)}, f32[8,1024]{1,0:T(8,128)S(1)}, u32[]{:S(2)}, u32[]{:S(2)}) collective-permute-start(f32[8,1024]{1,0:T(8,128)S(1)} %get-tuple-element.28), channel_id=1, source_target_pairs={{0,2},{2,0},{4,6},{6,4},{8,10},{10,8},{12,14},{14,12},{16,18},{18,... | collective-permute-start | bytes 98312 | tf_op jit(solution)/shard_map/ppermute | solution.py:700
  18.4 7.3 %collective-permute-start.4 = (f32[1,88,512]{2,1,0:T(8,128)S(1)}, f32[1,88,512]{2,1,0:T(8,128)S(1)}, u32[]{:S(2)}, u32[]{:S(2)}) collective-permute-start(f32[1,88,512]{2,1,0:T(8,128)S(1)} %get-tuple-element.29), channel_id=1, source_target_pairs={{0,1},{1,0},{2,3},{3,2},{4,5},{5,4},{6,7},{7,6},{8,9},{9,8},{10,11... | collective-permute-start | bytes 540680 | tf_op jit(solution)/shard_map/ppermute | solution.py:714
  21.1 6.1 %collective-permute-start.5 = (f32[1,88,256]{2,1,0:T(8,128)S(1)}, f32[1,88,256]{2,1,0:T(8,128)S(1)}, u32[]{:S(2)}, u32[]{:S(2)}) collective-permute-start(f32[1,88,256]{2,1,0:T(8,128)S(1)} %shard_map.153), channel_id=1, source_target_pairs={{0,1},{1,0},{2,3},{3,2},{4,5},{5,4},{6,7},{7,6},{8,9},{9,8},{10,11... | collective-permute-start | bytes 270344 | tf_op jit(solution)/shard_map/ppermute | solution.py:714
  30.4 12.9 %collective-permute-start.7 = (f32[80,2048]{1,0:T(8,128)S(1)}, f32[80,2048]{1,0:T(8,128)S(1)}, u32[]{:S(2)}, u32[]{:S(2)}) collective-permute-start(f32[80,2048]{1,0:T(8,128)S(1)} %get-tuple-element.31.x_ref), channel_id=1, source_target_pairs={{0,2},{2,0},{4,6},{6,4},{8,10},{10,8},{12,14},{14,12},{16,18},{18,... | collective-permute-start | bytes 1966088 | tf_op jit(solution)/shard_map/ppermute | solution.py:700
  30.5 12.8 %collective-permute-start.6 = (f32[80,1024]{1,0:T(8,128)S(1)}, f32[80,1024]{1,0:T(8,128)S(1)}, u32[]{:S(2)}, u32[]{:S(2)}) collective-permute-start(f32[80,1024]{1,0:T(8,128)S(1)} %get-tuple-element.32), channel_id=1, source_target_pairs={{0,30},{2,4},{4,2},{6,8},{8,6},{10,12},{12,10},{14,16},{16,14},{18... | collective-permute-start | bytes 983048 | tf_op jit(solution)/shard_map/ppermute | solution.py:700
  33.5 6.6 %collective-permute-start.8 = (f32[1,80,512]{2,1,0:T(8,128)S(1)}, f32[1,80,512]{2,1,0:T(8,128)S(1)}, u32[]{:S(2)}, u32[]{:S(2)}) collective-permute-start(f32[1,80,512]{2,1,0:T(8,128)S(1)} %get-tuple-element.33), channel_id=1, source_target_pairs={{0,1},{1,0},{2,3},{3,2},{4,5},{5,4},{6,7},{7,6},{8,9},{9,8},{10,11... | collective-permute-start | bytes 491528 | tf_op jit(solution)/shard_map/ppermute | solution.py:714
  35.0 8.3 %collective-permute-start.9 = (f32[1,80,128]{2,1,0:T(8,128)S(1)}, f32[1,80,128]{2,1,0:T(8,128)S(1)}, u32[]{:S(2)}, u32[]{:S(2)}) collective-permute-start(f32[1,80,128]{2,1,0:T(8,128)S(1)} %get-tuple-element.34), channel_id=1, source_target_pairs={{0,31},{1,30},{2,5},{3,4},{4,3},{5,2},{6,9},{7,8},{8,7},{9,6},{10,... | collective-permute-start | bytes 122888 | tf_op jit(solution)/shard_map/ppermute | solution.py:714
  36.2 3.9 %collective-permute-start.10 = (f32[1,80,128]{2,1,0:T(8,128)S(1)}, f32[1,80,128]{2,1,0:T(8,128)S(1)}, u32[]{:S(2)}, u32[]{:S(2)}) collective-permute-start(f32[1,80,128]{2,1,0:T(8,128)S(1)} %get-tuple-element.35), channel_id=1, source_target_pairs={{0,3},{1,2},{2,1},{3,0},{4,7},{5,6},{6,5},{7,4},{8,11},{9,10},{10,... | collective-permute-start | bytes 122888 | tf_op jit(solution)/shard_map/ppermute | solution.py:714
  37.0 6.3 %copy-start.9 = (f32[88,2048]{1,0:T(8,128)S(1)}, f32[88,2048]{1,0:T(8,128)}, u32[]{:S(2)}) copy-start(f32[88,2048]{1,0:T(8,128)} %copy-done.8) | copy-start | bytes 2162692
  37.0 6.3 %copy-start.11 = (f32[1,88,512]{2,1,0:T(8,128)S(1)}, f32[1,88,512]{2,1,0:T(8,128)}, u32[]{:S(2)}) copy-start(f32[1,88,512]{2,1,0:T(8,128)} %copy-done.10) | copy-start | bytes 540676
  40.2 10.2 %collective-permute-start.11 = (f32[80,1024]{1,0:T(8,128)S(1)}, f32[80,1024]{1,0:T(8,128)S(1)}, u32[]{:S(2)}, u32[]{:S(2)}) collective-permute-start(f32[80,1024]{1,0:T(8,128)S(1)} %shard_map.157), channel_id=1, source_target_pairs={{0,30},{2,4},{4,2},{6,8},{8,6},{10,12},{12,10},{14,16},{16,14},{18... | collective-permute-start | bytes 983048 | tf_op jit(solution)/shard_map/ppermute | solution.py:700
  46.9 10.4 %all-to-all-start.1 = ((f32[16,8,128]{2,1,0:T(8,128)}), f32[16,8,128]{2,1,0:T(8,128)S(1)}, u32[]{:S(2)}, u32[]{:S(2)}) async-start(f32[16,8,128]{2,1,0:T(8,128)} %get-tuple-element.41), calls=%async_computation.1 | async-start | bytes 131072 | tf_op jit(solution)/shard_map/all_to_all | solution.py:789
  (2 other events, 5.6 us)
